TPU v7x, 32 devices: a whole 2x2x4 slice. The times are simulated.
32 devices in a mesh: blk: 8 (over y, x, core), head: 4 (over z).
Axes of the slice: x: 2, y: 2, z: 4, core: 2. Of those that a mesh axis runs over, the one named last changes fastest.
Arguments:
- tokens: bfloat16 [2, 2048, 2048], P(None, ('blk', 'head')), may hold values from -6 to 6
- cotangent: bfloat16 [2, 2048, 2048], P(None, ('blk', 'head')), may hold values from -6 to 6
- segments: int32 [2, 2048], P(None, ('blk', 'head')), may hold values from 0 to 127, as said below
- padding: int32 [2, 2048], P(None, ('blk', 'head')), may hold values from 0 to 1, as said below
- query_weight: bfloat16 [2048, 2048], P('blk', 'head'), may hold values from -0.125 to 0.125
- key_weight: bfloat16 [2048, 2048], P('blk', 'head'), may hold values from -0.125 to 0.125
- value_weight: bfloat16 [2048, 2048], P('blk', 'head'), may hold values from -0.125 to 0.125
- output_weight: bfloat16 [2048, 2048], P('head', 'blk'), may hold values from -0.125 to 0.125
- query_gain: float32 [2048], P('head'), may hold values from 0.1 to 1.9
- key_gain: float32 [2048], P('head'), may hold values from 0.1 to 1.9
- attn_gain: float32 [2048], replicated, may hold values from 0.1 to 1.9
- gate_weight: bfloat16 [2048, 8192], P('blk', 'head'), may hold values from -0.125 to 0.125
- up_weight: bfloat16 [2048, 8192], P('blk', 'head'), may hold values from -0.125 to 0.125
- down_weight: bfloat16 [8192, 2048], P('head', 'blk'), may hold values from -0.0625 to 0.0625
- ffn_gain: float32 [2048], replicated, may hold values from 0.1 to 1.9
Outputs:
- output: bfloat16 [2, 2048, 2048], P(None, ('blk', 'head'))
- input_grad: float32 [2, 2048, 2048], P(None, ('blk', 'head'))
- query_weight_grad: float32 [2048, 2048], P('blk', 'head')
- key_weight_grad: float32 [2048, 2048], P('blk', 'head')
- value_weight_grad: float32 [2048, 2048], P('blk', 'head')
- output_weight_grad: float32 [2048, 2048], P('head', 'blk')
- query_gain_grad: float32 [2048], P('head')
- key_gain_grad: float32 [2048], P('head')
- attn_gain_grad: float32 [2048], replicated
- gate_weight_grad: float32 [2048, 8192], P('blk', 'head')
- up_weight_grad: float32 [2048, 8192], P('blk', 'head')
- down_weight_grad: float32 [8192, 2048], P('head', 'blk')
- ffn_gain_grad: float32 [2048], replicated
Inputs may be any that keep to these rules, and one draw needn't show every extreme that they name: `segments`: along each sequence the ids never fall; a document is a run of equal ids. `padding`: in each sequence a trailing run of 1 to fewer than 512 positions is 0, all others 1.
All inputs are finite; a program needn't handle non-finite values.
Results may differ from a plain program's by a relative error of at most 0.025.
Values may be sent and summed in bfloat16 or wider, within the bound.
No kernel may reach another device: no remote copies, remote signals or barrier semaphores. Data moves between devices by JAX's collectives and lax.ppermute only.
A program may use at most 192 MiB of HBM per device.

v0:
```python
import jax
import jax.numpy as jnp
from jax import lax
from jax.sharding import PartitionSpec as P

HD = 128


epsilon = 1e-06
theta = 500000.0


def rms_scale(values):
    return lax.rsqrt(jnp.mean(values * values, axis=-1, keepdims=True) + epsilon)


def dot_plain(left_side, right_side):
    return jnp.dot(left_side, right_side, preferred_element_type=jnp.float32)


def dot_right_t(left_side, right_side):
    return lax.dot_general(
        left_side, right_side, (((1,), (1,)), ((), ())), preferred_element_type=jnp.float32
    )


def dot_left_t(left_side, right_side):
    return lax.dot_general(
        left_side, right_side, (((0,), (0,)), ((), ())), preferred_element_type=jnp.float32
    )


def rotary_tables(first_row, row_count):
    half_size = HD // 2
    positions = (first_row + jnp.arange(row_count, dtype=jnp.int32)).astype(jnp.float32)
    inverse = theta ** (-2.0 * jnp.arange(half_size, dtype=jnp.int32).astype(jnp.float32) / HD)
    angles = positions[:, None] * inverse[None, :]
    angles = jnp.concatenate([angles, angles], axis=1)
    return (jnp.cos(angles)[:, None, :], jnp.sin(angles)[:, None, :])


def rotate(head_rows, cosine, sine_table):
    half_size = head_rows.shape[-1] // 2
    turned = jnp.concatenate([-head_rows[..., half_size:], head_rows[..., :half_size]], axis=-1)
    return head_rows * cosine + turned * sine_table


def unrotate(grad_rows, cosine, sine_table):
    half_size = grad_rows.shape[-1] // 2
    shifted = grad_rows * sine_table
    turned = jnp.concatenate([shifted[..., half_size:], -shifted[..., :half_size]], axis=-1)
    return grad_rows * cosine + turned


def allowed_mask(query_pos, query_seg, key_pos, key_seg, key_pad):
    same_doc = query_seg[:, None] == key_seg[None, :]
    causal = key_pos[None, :] <= query_pos[:, None]
    live = (key_pad[None, :] == 1) | (key_pos[None, :] == query_pos[:, None])
    return same_doc & causal & live


def block_scores(query_view, key_rows, allowed):
    scores = jnp.einsum(
        "qhd,khd->hqk", query_view, key_rows, preferred_element_type=jnp.float32
    ) * HD ** (-0.5)
    return jnp.where(allowed[None], scores, -jnp.inf)


def split_blocks(key_all, value_all, seg_all, pad_all, row_count):
    blocks = key_all.shape[0] // row_count
    block_shape = (blocks, row_count) + key_all.shape[1:]
    offsets = jnp.arange(blocks, dtype=jnp.int32) * row_count
    return (
        key_all.reshape(block_shape),
        value_all.reshape(block_shape),
        seg_all.reshape(blocks, row_count),
        pad_all.reshape(blocks, row_count),
        offsets,
    )


def collect(values):
    return lax.all_gather(values, "head", axis=0, tiled=True)


def reduce_rows(term_fn, row_count):
    return lax.psum_scatter(
        term_fn(jnp.int32(0), row_count * lax.axis_size("head")).astype(jnp.bfloat16),
        "head",
        scatter_dimension=0,
        tiled=True,
    ).astype(jnp.float32)


def head_sums(first_sum, second_sum):
    return lax.psum((first_sum, second_sum), "head")


def gather_attention(query_weight, key_weight, value_weight, output_weight):
    return (
        lax.all_gather(query_weight, "blk", axis=0, tiled=True),
        lax.all_gather(key_weight, "blk", axis=0, tiled=True),
        lax.all_gather(value_weight, "blk", axis=0, tiled=True),
        lax.all_gather(output_weight, "blk", axis=1, tiled=True),
    )


def gather_ffn(gate_weight, up_weight, down_weight):
    return (
        lax.all_gather(gate_weight, "blk", axis=0, tiled=True),
        lax.all_gather(up_weight, "blk", axis=0, tiled=True),
        lax.all_gather(down_weight, "blk", axis=1, tiled=True),
    )


def attention_forward(query_view, query_pos, query_seg, key_all, value_all, seg_all, pad_all):
    row_count = query_view.shape[0]
    heads_local = query_view.shape[1]
    stacked = split_blocks(key_all, value_all, seg_all, pad_all, row_count)

    def measure(running, key_block):
        key_rows, value_rows, key_seg, key_pad, offset = key_block
        key_pos = offset + jnp.arange(row_count, dtype=jnp.int32)
        row_top, row_total = running
        scores = block_scores(
            query_view, key_rows, allowed_mask(query_pos, query_seg, key_pos, key_seg, key_pad)
        )
        new_top = jnp.maximum(row_top, jnp.max(scores, axis=-1))
        new_total = row_total * jnp.exp(row_top - new_top) + jnp.sum(
            jnp.exp(scores - new_top[..., None]), axis=-1
        )
        return ((new_top, new_total), None)

    start_top = jnp.full((heads_local, row_count), -1e30, jnp.float32)
    start_total = jnp.zeros((heads_local, row_count), jnp.float32)
    row_top, row_total = lax.scan(measure, (start_top, start_total), stacked)[0]

    def accumulate(running, key_block):
        key_rows, value_rows, key_seg, key_pad, offset = key_block
        key_pos = offset + jnp.arange(row_count, dtype=jnp.int32)
        scores = block_scores(
            query_view, key_rows, allowed_mask(query_pos, query_seg, key_pos, key_seg, key_pad)
        )
        prob_rows = (jnp.exp(scores - row_top[..., None]) / row_total[..., None]).astype(
            jnp.bfloat16
        )
        return (
            running
            + jnp.einsum("hqk,khd->qhd", prob_rows, value_rows, preferred_element_type=jnp.float32),
            None,
        )

    start_heads = jnp.zeros((row_count, heads_local, HD), jnp.float32)
    mixed_heads = lax.scan(accumulate, start_heads, stacked)[0]
    return (mixed_heads, row_top, row_total)


def query_gradient(
    query_view,
    grad_view,
    query_pos,
    query_seg,
    row_top,
    row_total,
    row_delta,
    key_all,
    value_all,
    seg_all,
    pad_all,
):
    row_count = query_view.shape[0]
    heads_local = query_view.shape[1]
    stacked = split_blocks(key_all, value_all, seg_all, pad_all, row_count)

    def step_fn(running, key_block):
        key_rows, value_rows, key_seg, key_pad, offset = key_block
        key_pos = offset + jnp.arange(row_count, dtype=jnp.int32)
        scores = block_scores(
            query_view, key_rows, allowed_mask(query_pos, query_seg, key_pos, key_seg, key_pad)
        )
        prob_rows = jnp.exp(scores - row_top[..., None]) / row_total[..., None]
        grad_probs = jnp.einsum(
            "qhd,khd->hqk", grad_view, value_rows, preferred_element_type=jnp.float32
        )
        grad_scores = (prob_rows * (grad_probs - row_delta[..., None])).astype(jnp.bfloat16)
        new_grad = running + jnp.einsum(
            "hqk,khd->qhd", grad_scores, key_rows, preferred_element_type=jnp.float32
        )
        grad_keys = jnp.einsum(
            "hqk,qhd->khd", grad_scores, query_view, preferred_element_type=jnp.float32
        )
        grad_values = jnp.einsum(
            "hqk,qhd->khd",
            prob_rows.astype(jnp.bfloat16),
            grad_view,
            preferred_element_type=jnp.float32,
        )
        return (new_grad, jnp.concatenate([grad_keys, grad_values], axis=1))

    start_grad = jnp.zeros((row_count, heads_local, HD), jnp.float32)
    grad_query, key_terms = lax.scan(step_fn, start_grad, stacked)
    return (grad_query, key_terms.reshape(key_terms.shape[0] * row_count, 2 * heads_local * HD))


def on_device(
    tokens,
    cotangent,
    segments,
    padding,
    query_weight,
    key_weight,
    value_weight,
    output_weight,
    query_gain,
    key_gain,
    attn_gain,
    gate_weight,
    up_weight,
    down_weight,
    ffn_gain,
):
    micro_count = tokens.shape[0]
    local_rows = tokens.shape[1]
    model_width = tokens.shape[2]
    group_rows = local_rows * lax.axis_size("head")
    feature_width = query_weight.shape[1]
    heads_local = feature_width // HD
    hidden_width = gate_weight.shape[1]
    score_scale = HD ** (-0.5)
    first_row = lax.axis_index("blk") * group_rows
    query_pos = first_row + jnp.arange(group_rows, dtype=jnp.int32)
    cosine, sine_table = rotary_tables(first_row, group_rows)
    query_acc = jnp.zeros((model_width, feature_width), jnp.float32)
    key_acc = jnp.zeros((model_width, feature_width), jnp.float32)
    value_acc = jnp.zeros((model_width, feature_width), jnp.float32)
    output_acc = jnp.zeros((feature_width, model_width), jnp.float32)
    gate_acc = jnp.zeros((model_width, hidden_width), jnp.float32)
    up_acc = jnp.zeros((model_width, hidden_width), jnp.float32)
    down_acc = jnp.zeros((hidden_width, model_width), jnp.float32)
    query_gain_acc = jnp.zeros((feature_width,), jnp.float32)
    key_gain_acc = jnp.zeros((feature_width,), jnp.float32)
    attn_gain_acc = jnp.zeros((model_width,), jnp.float32)
    ffn_gain_acc = jnp.zeros((model_width,), jnp.float32)
    outputs = []
    input_grads = []
    for batch_index in range(micro_count):
        attn_set = gather_attention(query_weight, key_weight, value_weight, output_weight)
        query_full, key_full, value_full, output_full = attn_set
        token_local = tokens[batch_index]
        token_rows, seg_rows, pad_rows = (
            lax.all_gather(token_local, "head", axis=0, tiled=True),
            lax.all_gather(segments[batch_index], "head", axis=0, tiled=True),
            lax.all_gather(padding[batch_index], "head", axis=0, tiled=True),
        )
        raw_query = dot_plain(token_rows, query_full)
        raw_key = dot_plain(token_rows, key_full)
        value_low = dot_plain(token_rows, value_full).astype(jnp.bfloat16)
        query_total, key_total = head_sums(
            jnp.sum(raw_query * raw_query, axis=1), jnp.sum(raw_key * raw_key, axis=1)
        )
        query_scale = lax.rsqrt(query_total / model_width + epsilon)[:, None]
        key_scale = lax.rsqrt(key_total / model_width + epsilon)[:, None]
        query_hat = raw_query * query_scale
        key_hat = raw_key * key_scale
        query_view = rotate(
            (query_hat * query_gain).reshape(group_rows, heads_local, HD), cosine, sine_table
        ).astype(jnp.bfloat16)
        key_view = rotate(
            (key_hat * key_gain).reshape(group_rows, heads_local, HD), cosine, sine_table
        ).astype(jnp.bfloat16)
        value_view = value_low.reshape(group_rows, heads_local, HD)
        key_all, value_all, seg_all, pad_all = (
            lax.all_gather(key_view, "blk", axis=0, tiled=True),
            lax.all_gather(value_view, "blk", axis=0, tiled=True),
            lax.all_gather(seg_rows, "blk", axis=0, tiled=True),
            lax.all_gather(pad_rows, "blk", axis=0, tiled=True),
        )
        mixed_heads, row_top, row_total = attention_forward(
            query_view, query_pos, seg_rows, key_all, value_all, seg_all, pad_all
        )
        mixed_low = mixed_heads.reshape(group_rows, feature_width).astype(jnp.bfloat16)

        def attn_term(offset, row_count):
            return dot_plain(mixed_low, output_full)

        attn_rows = reduce_rows(attn_term, local_rows)
        attn_scale = rms_scale(attn_rows)
        attn_hat = attn_rows * attn_scale
        hidden = token_local.astype(jnp.float32) + attn_hat * attn_gain
        ffn_set = gather_ffn(gate_weight, up_weight, down_weight)
        gate_full, up_full, down_full = ffn_set
        hidden_rows = collect(hidden.astype(jnp.bfloat16))
        gate_values = dot_plain(hidden_rows, gate_full)
        up_values = dot_plain(hidden_rows, up_full)
        sigmoid_gate = jax.nn.sigmoid(gate_values)
        silu_gate = gate_values * sigmoid_gate
        middle = (silu_gate * up_values).astype(jnp.bfloat16)

        def down_term(offset, row_count):
            return dot_plain(middle, down_full)

        down_rows = reduce_rows(down_term, local_rows)
        down_scale = rms_scale(down_rows)
        down_hat = down_rows * down_scale
        outputs.append((hidden + down_hat * ffn_gain).astype(jnp.bfloat16))
        grad_out = cotangent[batch_index].astype(jnp.float32)
        ffn_gain_acc = ffn_gain_acc + jnp.sum(grad_out * down_hat, axis=0)
        grad_norm = grad_out * ffn_gain
        grad_down = (
            down_scale
            * (grad_norm - down_hat * jnp.mean(grad_norm * down_hat, axis=1, keepdims=True))
        ).astype(jnp.bfloat16)
        gate_full, up_full, down_full = gather_ffn(gate_weight, up_weight, down_weight)
        grad_down_rows = collect(grad_down)
        grad_middle = dot_right_t(grad_down_rows, down_full)
        down_acc = down_acc + dot_left_t(middle, grad_down_rows)
        grad_up = (grad_middle * silu_gate).astype(jnp.bfloat16)
        grad_gate = (
            grad_middle * up_values * sigmoid_gate * (1.0 + gate_values * (1.0 - sigmoid_gate))
        ).astype(jnp.bfloat16)
        gate_acc = gate_acc + dot_left_t(hidden_rows, grad_gate)
        up_acc = up_acc + dot_left_t(hidden_rows, grad_up)

        def hidden_term(offset, row_count):
            return dot_right_t(grad_gate, gate_full) + dot_right_t(grad_up, up_full)

        grad_hidden = reduce_rows(hidden_term, local_rows) + grad_out
        attn_gain_acc = attn_gain_acc + jnp.sum(grad_hidden * attn_hat, axis=0)
        grad_norm = grad_hidden * attn_gain
        grad_attn = (
            attn_scale
            * (grad_norm - attn_hat * jnp.mean(grad_norm * attn_hat, axis=1, keepdims=True))
        ).astype(jnp.bfloat16)
        query_full, key_full, value_full, output_full = gather_attention(
            query_weight, key_weight, value_weight, output_weight
        )
        grad_attn_rows = collect(grad_attn)
        grad_mixed = dot_right_t(grad_attn_rows, output_full).astype(jnp.bfloat16)
        output_acc = output_acc + dot_left_t(mixed_low, grad_attn_rows)
        grad_view = grad_mixed.reshape(group_rows, heads_local, HD)
        row_delta = jnp.sum(grad_view.astype(jnp.float32) * mixed_heads, axis=2).T
        grad_query, key_terms = query_gradient(
            query_view,
            grad_view,
            query_pos,
            seg_rows,
            row_top,
            row_total,
            row_delta,
            key_all,
            value_all,
            seg_all,
            pad_all,
        )
        own_terms = lax.psum_scatter(
            key_terms.astype(jnp.bfloat16), "blk", scatter_dimension=0, tiled=True
        ).astype(jnp.float32)
        grad_key_flat = own_terms[:, :feature_width]
        grad_value_flat = own_terms[:, feature_width:]
        grad_query_norm = unrotate(grad_query * score_scale, cosine, sine_table).reshape(
            group_rows, feature_width
        )
        grad_key_norm = unrotate(
            grad_key_flat.reshape(group_rows, heads_local, HD) * score_scale, cosine, sine_table
        ).reshape(group_rows, feature_width)
        query_gain_acc = query_gain_acc + jnp.sum(grad_query_norm * query_hat, axis=0)
        key_gain_acc = key_gain_acc + jnp.sum(grad_key_norm * key_hat, axis=0)
        grad_query_hat = grad_query_norm * query_gain
        grad_key_hat = grad_key_norm * key_gain
        query_dot, key_dot = head_sums(
            jnp.sum(grad_query_hat * query_hat, axis=1), jnp.sum(grad_key_hat * key_hat, axis=1)
        )
        grad_raw_query = (
            query_scale * (grad_query_hat - query_hat * (query_dot / model_width)[:, None])
        ).astype(jnp.bfloat16)
        grad_raw_key = (
            key_scale * (grad_key_hat - key_hat * (key_dot / model_width)[:, None])
        ).astype(jnp.bfloat16)
        grad_value_low = grad_value_flat.astype(jnp.bfloat16)
        query_acc = query_acc + dot_left_t(token_rows, grad_raw_query)
        key_acc = key_acc + dot_left_t(token_rows, grad_raw_key)
        value_acc = value_acc + dot_left_t(token_rows, grad_value_low)

        def input_term(offset, row_count):
            return (
                dot_right_t(grad_raw_query, query_full)
                + dot_right_t(grad_raw_key, key_full)
                + dot_right_t(grad_value_low, value_full)
            )

        input_grads.append(reduce_rows(input_term, local_rows) + grad_hidden)
    reduced = (
        lax.psum_scatter(
            query_acc.astype(jnp.bfloat16), "blk", scatter_dimension=0, tiled=True
        ).astype(jnp.float32),
        lax.psum_scatter(
            key_acc.astype(jnp.bfloat16), "blk", scatter_dimension=0, tiled=True
        ).astype(jnp.float32),
        lax.psum_scatter(
            value_acc.astype(jnp.bfloat16), "blk", scatter_dimension=0, tiled=True
        ).astype(jnp.float32),
        lax.psum_scatter(
            output_acc.astype(jnp.bfloat16), "blk", scatter_dimension=1, tiled=True
        ).astype(jnp.float32),
        lax.psum_scatter(
            gate_acc.astype(jnp.bfloat16), "blk", scatter_dimension=0, tiled=True
        ).astype(jnp.float32),
        lax.psum_scatter(
            up_acc.astype(jnp.bfloat16), "blk", scatter_dimension=0, tiled=True
        ).astype(jnp.float32),
        lax.psum_scatter(
            down_acc.astype(jnp.bfloat16), "blk", scatter_dimension=1, tiled=True
        ).astype(jnp.float32),
    )
    head_offset = lax.axis_index("head") * feature_width
    zeros_full = jnp.zeros((model_width,), jnp.float32)
    query_full_gain = lax.dynamic_update_slice_in_dim(zeros_full, query_gain_acc, head_offset, 0)
    key_full_gain = lax.dynamic_update_slice_in_dim(zeros_full, key_gain_acc, head_offset, 0)
    gains = lax.psum((query_full_gain, key_full_gain, attn_gain_acc, ffn_gain_acc), ("blk", "head"))
    query_gain_grad = lax.dynamic_slice_in_dim(gains[0], head_offset, feature_width, 0)
    key_gain_grad = lax.dynamic_slice_in_dim(gains[1], head_offset, feature_width, 0)
    return (
        jnp.stack(outputs),
        jnp.stack(input_grads),
        reduced[0],
        reduced[1],
        reduced[2],
        reduced[3],
        query_gain_grad,
        key_gain_grad,
        gains[2],
        reduced[4],
        reduced[5],
        reduced[6],
        gains[3],
    )


def solution(mesh):
    return jax.shard_map(
        on_device,
        mesh=mesh,
        in_specs=(
            P(None, ("blk", "head"), None),
            P(None, ("blk", "head"), None),
            P(None, ("blk", "head")),
            P(None, ("blk", "head")),
            P("blk", "head"),
            P("blk", "head"),
            P("blk", "head"),
            P("head", "blk"),
            P("head"),
            P("head"),
            P(),
            P("blk", "head"),
            P("blk", "head"),
            P("head", "blk"),
            P(),
        ),
        out_specs=(
            P(None, ("blk", "head"), None),
            P(None, ("blk", "head"), None),
            P("blk", "head"),
            P("blk", "head"),
            P("blk", "head"),
            P("head", "blk"),
            P("head"),
            P("head"),
            P(),
            P("blk", "head"),
            P("blk", "head"),
            P("head", "blk"),
            P(),
        ),
        check_vma=False,
    )
```

profile of v0, /device:TPU:0, one launch (start us, length us, event | category | flops | bytes accessed | tf_op | source)
XLA Modules:
  0.0 1513.3 jit_solution(2241600453066559844)
XLA Ops:
  13.2 27.6 %all-gather.64.cloned.1.call-done = bf16[1,256,2048]{2,1,0:T(8,128)(2,1)} async-done(((bf16[1,64,2048]{2,1,0:T(8,128)(2,1)}), bf16[1,256,2048]{2,1,0:T(8,128)(2,1)}) %all-gather.64.cloned.1.call-update) | async-done | bytes 1048592 | tf_op jit(solution)/shard_map/all_gather | solution.py:251
  40.8 29.3 %all-gather.38.cloned.1.call-done = bf16[2048,512]{1,0:T(8,128)(2,1)} async-done(((bf16[256,512]{1,0:T(8,128)(2,1)}), bf16[2048,512]{1,0:T(8,128)(2,1)}) %all-gather.38.cloned.1.call-update) | async-done | bytes 2097168 | tf_op jit(solution)/shard_map/all_gather | solution.py:101
  72.8 27.1 %all-gather.34.cloned.1.call-done = bf16[2048,512]{1,0:T(8,128)(2,1)} async-done(((bf16[256,512]{1,0:T(8,128)(2,1)}), bf16[2048,512]{1,0:T(8,128)(2,1)}) %all-gather.34.cloned.1.call-update) | async-done | bytes 2097168 | tf_op jit(solution)/shard_map/all_gather | solution.py:102
  103.0 26.9 %all-gather.66.cloned.1.call-done = bf16[1,256,2048]{2,1,0:T(8,128)(2,1)} async-done(((bf16[1,64,2048]{2,1,0:T(8,128)(2,1)}), bf16[1,256,2048]{2,1,0:T(8,128)(2,1)}) %all-gather.66.cloned.1.call-update) | async-done | bytes 1048592 | tf_op jit(solution)/shard_map/all_gather | solution.py:251
  134.3 10.3 all-reduce.7
  149.2 9.9 all-gather.30.cloned.1.call-done
  164.6 8.3 all-reduce.4
  172.9 8.8 all-gather.2
  182.9 7.9 all-gather.4
  191.6 8.9 all-gather.7
  201.1 7.9 all-gather.9
  217.2 23.7 %while.74 = (s32[]{:T(128)}, f32[4,256]{1,0:T(4,128)S(1)}, f32[4,256]{1,0:T(4,128)S(1)}, s32[256]{0:T(256)S(1)}, s32[8,256]{1,0:T(8,128)S(1)}, /*index=5*/s32[8]...) while((s32[]{:T(128)}, f32[4,256]{1,0:T(4,128)S(1)}, ...), condition=%wide.region_7.8_spmd.clone, body=%wide.region_4.7_spmd.clone.sunk | while | flops 68818688 | bytes 2815656 | solution.py:136
  244.1 23.7 %while.76 = (s32[]{:T(128)}, f32[4,256]{1,0:T(4,128)S(1)}, f32[4,256]{1,0:T(4,128)S(1)}, s32[256]{0:T(256)S(1)}, s32[8,256]{1,0:T(8,128)S(1)}, /*index=5*/s32[8]...) while((s32[]{:T(128)}, f32[4,256]{1,0:T(4,128)S(1)}, ...), condition=%wide.region_21.22_spmd.clone, body=%wide.region_18.21_spmd.clone.sunk | while | flops 68818688 | bytes 2815656 | solution.py:136
  267.9 35.3 %while.75 = (s32[]{:T(128)}, f32[256,4,128]{0,2,1:T(8,128)S(1)}, bf16[8,256,4,128]{3,1,0,2:T(8,128)(2,1)}, s32[256]{0:T(256)S(1)}, s32[8,256]{1,0:T(8,128)S(1)},...) while((s32[]{:T(128)}, f32[256,4,128]{0,2,1:T(8,128)S(1)}, ...), condition=%wide.region_9.10_spmd.clone, body=%wide.region_8.9_spmd.clone.sunk | while | flops 136184576 | bytes 3032763 | solution.py:154
  310.0 42.0 %while.77 = (s32[]{:T(128)}, f32[256,4,128]{0,2,1:T(8,128)}, bf16[8,256,4,128]{3,1,0,2:T(8,128)(2,1)}, s32[256]{0:T(256)S(1)}, s32[8,256]{1,0:T(8,128)S(1)}, /*i...) while((s32[]{:T(128)}, f32[256,4,128]{0,2,1:T(8,128)}, ...), condition=%wide.region_23.24_spmd.clone, body=%wide.region_22.23_spmd.clone.sunk | while | flops 136184576 | bytes 3032763 | solution.py:154
  356.7 26.2 %reduce-scatter.22.cloned.1.call-done = bf16[64,2048]{1,0:T(8,128)(2,1)} async-done(((bf16[256,2048]{1,0:T(8,128)(2,1)}), bf16[64,2048]{1,0:T(8,128)(2,1)}) %reduce-scatter.22.cloned.1.call-update) | async-done | bytes 262160 | tf_op jit(solution)/shard_map/reduce_scatter | solution.py:87
  388.5 24.3 %all-gather.42.cloned.1.call-done = bf16[256,2048]{1,0:T(8,128)(2,1)} async-done(((bf16[64,2048]{1,0:T(8,128)(2,1)}), bf16[256,2048]{1,0:T(8,128)(2,1)}) %all-gather.42.cloned.1.call-update) | async-done | bytes 1048592 | tf_op jit(solution)/shard_map/all_gather | solution.py:83
  412.8 55.7 %all-gather.44.cloned.1.call-done = bf16[2048,2048]{1,0:T(8,128)(2,1)} async-done(((bf16[256,2048]{1,0:T(8,128)(2,1)}), bf16[2048,2048]{1,0:T(8,128)(2,1)}) %all-gather.44.cloned.1.call-update) | async-done | bytes 8388624 | tf_op jit(solution)/shard_map/all_gather | solution.py:110
  475.8 48.8 %all-gather.46.cloned.1.call-done = bf16[2048,2048]{1,0:T(8,128)(2,1)} async-done(((bf16[256,2048]{1,0:T(8,128)(2,1)}), bf16[2048,2048]{1,0:T(8,128)(2,1)}) %all-gather.46.cloned.1.call-update) | async-done | bytes 8388624 | tf_op jit(solution)/shard_map/all_gather | solution.py:111
  524.6 8.5 multiply_convert_fusion.5
  533.1 49.3 %all-gather.48.cloned.1.call-done = bf16[2048,2048]{1,0:T(8,128)(2,1)} async-done(((bf16[2048,256]{1,0:T(8,128)(2,1)}), bf16[2048,2048]{1,0:T(8,128)(2,1)}) %all-gather.48.cloned.1.call-update) | async-done | bytes 8388624 | tf_op jit(solution)/shard_map/all_gather | solution.py:112
  589.7 22.1 %all-gather.54.cloned.1.call-done = bf16[256,2048]{1,0:T(8,128)(2,1)} async-done(((bf16[64,2048]{1,0:T(8,128)(2,1)}), bf16[256,2048]{1,0:T(8,128)(2,1)}) %all-gather.54.cloned.1.call-update) | async-done | bytes 1048592 | tf_op jit(solution)/shard_map/all_gather | solution.py:83
  617.9 8.1 multiply_convert_fusion.4
  630.5 10.0 reduce-scatter.20.cloned.1.call-done
  641.7 27.1 %reduce-scatter.24.cloned.1.call-done = bf16[64,2048]{1,0:T(8,128)(2,1)} async-done(((bf16[256,2048]{1,0:T(8,128)(2,1)}), bf16[64,2048]{1,0:T(8,128)(2,1)}) %reduce-scatter.24.cloned.1.call-update) | async-done | bytes 262160 | tf_op jit(solution)/shard_map/reduce_scatter | solution.py:87
  675.1 25.7 %all-gather.60.cloned.1.call-done = bf16[256,2048]{1,0:T(8,128)(2,1)} async-done(((bf16[64,2048]{1,0:T(8,128)(2,1)}), bf16[256,2048]{1,0:T(8,128)(2,1)}) %all-gather.60.cloned.1.call-update) | async-done | bytes 1048592 | tf_op jit(solution)/shard_map/all_gather | solution.py:83
  722.6 7.8 all-gather.56.cloned.1.call-done
  751.6 7.8 reduce-scatter.32.cloned.1.call-done
  759.4 28.8 %reduce-scatter.26.cloned.1.call-done = bf16[64,2048]{1,0:T(8,128)(2,1)} async-done(((bf16[256,2048]{1,0:T(8,128)(2,1)}), bf16[64,2048]{1,0:T(8,128)(2,1)}) %reduce-scatter.26.cloned.1.call-update) | async-done | bytes 262160 | tf_op jit(solution)/shard_map/reduce_scatter | solution.py:87
  793.6 25.7 %all-gather.62.cloned.1.call-done = bf16[256,2048]{1,0:T(8,128)(2,1)} async-done(((bf16[64,2048]{1,0:T(8,128)(2,1)}), bf16[256,2048]{1,0:T(8,128)(2,1)}) %all-gather.62.cloned.1.call-update) | async-done | bytes 1048592 | tf_op jit(solution)/shard_map/all_gather | solution.py:83
  821.5 27.4 %all-gather.58.cloned.1.call-done = bf16[256,2048]{1,0:T(8,128)(2,1)} async-done(((bf16[64,2048]{1,0:T(8,128)(2,1)}), bf16[256,2048]{1,0:T(8,128)(2,1)}) %all-gather.58.cloned.1.call-update) | async-done | bytes 1048592 | tf_op jit(solution)/shard_map/all_gather | solution.py:83
  854.8 61.7 %while.79 = (s32[]{:T(128)}, f32[256,4,128]{0,2,1:T(8,128)}, bf16[8,256,8,128]{3,1,2,0:T(8,128)(2,1)}, bf16[8,256,4,128]{3,1,2,0:T(8,128)(2,1)}, s32[256]{0:T(25...) while((s32[]{:T(128)}, f32[256,4,128]{0,2,1:T(8,128)}, ...), condition=%wide.region_45.46_spmd.clone, body=%wide.region_44.45_spmd.clone.sunk | while | flops 339346176 | bytes 9328347 | solution.py:201
  928.7 54.9 %while.78 = (s32[]{:T(128)}, f32[256,4,128]{0,2,1:T(8,128)S(1)}, bf16[8,256,8,128]{3,1,2,0:T(8,128)(2,1)}, bf16[8,256,4,128]{3,1,2,0:T(8,128)(2,1)}, s32[256]{0:...) while((s32[]{:T(128)}, f32[256,4,128]{0,2,1:T(8,128)S(1)}, ...), condition=%wide.region_33.34_spmd.clone, body=%wide.region_32.33_spmd.clone.sunk | while | flops 339346176 | bytes 9328347 | solution.py:201
  998.6 44.2 %reduce-scatter.28.cloned.1.call-done = bf16[256,1024]{1,0:T(8,128)(2,1)} async-done(((bf16[2048,1024]{1,0:T(8,128)(2,1)}), bf16[256,1024]{1,0:T(8,128)(2,1)}) %reduce-scatter.28.cloned.1.call-update) | async-done | bytes 524304 | tf_op jit(solution)/shard_map/reduce_scatter | solution.py:355
  1054.8 11.9 all-reduce.6
  1080.1 9.5 fusion.212
  1089.6 11.5 add_convert_fusion.2
  1101.4 9.5 fusion.213
  1110.9 11.5 add_convert_fusion.1
  1124.0 8.2 fusion.214
  1132.1 11.6 add_convert_fusion
  1158.2 38.1 %all-reduce.5 = (f32[2048]{0:T(1024)S(1)}, f32[2048]{0:T(1024)S(1)}, f32[2048]{0:T(1024)}, f32[2048]{0:T(1024)}) all-reduce(f32[2048]{0:T(1024)S(1)} %add_dynamic-update-slice_fusion.1, f32[2048]{0:T(1024)S(1)} %add_dynamic-update-slice_fusion, f32[2048]{0:T(1024)S(1)} %add.375, ...), channel_id=1, replica_groups=mesh['blk'=8,'head'=4] {'blk','head'}, use_global_device_ids=true, to_apply=%region_58.59 | all-reduce | flops 8192 | bytes 65536 | tf_op jit(solution)/shard_map/psum | solution.py:419
  1199.9 21.2 %reduce-scatter.46.cloned.1.call-done = bf16[256,2048]{1,0:T(8,128)(2,1)} async-done(((bf16[2048,2048]{1,0:T(8,128)(2,1)}), bf16[256,2048]{1,0:T(8,128)(2,1)}) %reduce-scatter.46.cloned.1.call-update) | async-done | bytes 1048592 | tf_op jit(solution)/shard_map/reduce_scatter | solution.py:405
  1223.8 72.0 %reduce-scatter.48.cloned.1.call-done = bf16[256,2048]{1,0:T(8,128)(2,1)} async-done(((bf16[2048,2048]{1,0:T(8,128)(2,1)}), bf16[256,2048]{1,0:T(8,128)(2,1)}) %reduce-scatter.48.cloned.1.call-update) | async-done | bytes 1048592 | tf_op jit(solution)/shard_map/reduce_scatter | solution.py:408
  1298.6 72.2 %reduce-scatter.50.cloned.1.call-done = bf16[2048,256]{1,0:T(8,128)(2,1)} async-done(((bf16[2048,2048]{1,0:T(8,128)(2,1)}), bf16[2048,256]{1,0:T(8,128)(2,1)}) %reduce-scatter.50.cloned.1.call-update) | async-done | bytes 1048592 | tf_op jit(solution)/shard_map/reduce_scatter | solution.py:411
  1373.5 41.8 %reduce-scatter.38.cloned.1.call-done = bf16[256,512]{0,1:T(8,128)(2,1)} async-done(((bf16[2048,512]{0,1:T(8,128)(2,1)}), bf16[256,512]{0,1:T(8,128)(2,1)}) %reduce-scatter.38.cloned.1.call-update) | async-done | bytes 262160 | tf_op jit(solution)/shard_map/reduce_scatter | solution.py:393
  1417.2 43.0 %reduce-scatter.40.cloned.1.call-done = bf16[256,512]{0,1:T(8,128)(2,1)} async-done(((bf16[2048,512]{0,1:T(8,128)(2,1)}), bf16[256,512]{0,1:T(8,128)(2,1)}) %reduce-scatter.40.cloned.1.call-update) | async-done | bytes 262160 | tf_op jit(solution)/shard_map/reduce_scatter | solution.py:396
  1462.1 42.5 %reduce-scatter.42.cloned.1.call-done = bf16[256,512]{0,1:T(8,128)(2,1)} async-done(((bf16[2048,512]{0,1:T(8,128)(2,1)}), bf16[256,512]{0,1:T(8,128)(2,1)}) %reduce-scatter.42.cloned.1.call-update) | async-done | bytes 262160 | tf_op jit(solution)/shard_map/reduce_scatter | solution.py:399
  (893 shorter events, 469.0 us)
Async XLA Ops:
  7.2 33.6 %all-gather.64.cloned.1.call-start = ((), (), s32[]{:S(2)}) async-start(), calls=%async_computation.51 | async-start | bytes 1310720 | tf_op jit(solution)/shard_map/all_gather | solution.py:251
  9.1 61.0 %all-gather.38.cloned.1.call-start = ((), (), s32[]{:S(2)}) async-start(), calls=%async_computation.21 | async-start | bytes 2359296 | tf_op jit(solution)/shard_map/all_gather | solution.py:101
  9.9 90.1 %all-gather.34.cloned.1.call-start = ((), (), s32[]{:S(2)}) async-start(), calls=%async_computation.19 | async-start | bytes 2359296 | tf_op jit(solution)/shard_map/all_gather | solution.py:102
  10.6 119.3 %all-gather.66.cloned.1.call-start = ((), (), s32[]{:S(2)}) async-start(), calls=%async_computation.52 | async-start | bytes 1310720 | tf_op jit(solution)/shard_map/all_gather | solution.py:251
  11.2 147.9 %all-gather.30.cloned.1.call-start = ((), (), s32[]{:S(2)}) async-start(), calls=%async_computation.17 | async-start | bytes 2359296 | tf_op jit(solution)/shard_map/all_gather | solution.py:103
  11.8 202.2 %all-gather.36.cloned.1.call-start = ((), (), s32[]{:S(2)}) async-start(), calls=%async_computation.20 | async-start | bytes 2359296 | tf_op jit(solution)/shard_map/all_gather | solution.py:273
  40.8 59.1 %copy-start.3 = (bf16[1,256,2048]{2,1,0:T(8,128)(2,1)S(1)}, bf16[1,256,2048]{2,1,0:T(8,128)(2,1)}, u32[]{:S(2)}) copy-start(bf16[1,256,2048]{2,1,0:T(8,128)(2,1)} %all-gather.64.cloned.1.call-done) | copy-start | bytes 3145732
  72.8 71.8 %copy-start.14 = (f32[256,512]{1,0:T(8,128)}, f32[256,512]{1,0:T(8,128)S(1)}, u32[]{:S(2)}) copy-start(f32[256,512]{1,0:T(8,128)S(1)} %get-tuple-element.1099) | copy-start | bytes 1572868
  148.4 92.6 %all-gather.52.cloned.1.call-start = ((), (), s32[]{:S(2)}) async-start(), calls=%async_computation.30 | async-start | bytes 2359296 | tf_op jit(solution)/shard_map/all_gather | solution.py:273
  149.1 118.7 %all-gather.32.cloned.1.call-start = ((), (), s32[]{:S(2)}) async-start(), calls=%async_computation.18 | async-start | bytes 2359296 | tf_op jit(solution)/shard_map/all_gather | solution.py:274
  162.1 141.1 %all-gather.40.cloned.1.call-start = ((), (), s32[]{:S(2)}) async-start(), calls=%async_computation.22 | async-start | bytes 2359296 | tf_op jit(solution)/shard_map/all_gather | solution.py:104
  162.9 147.1 %all-gather.50.cloned.1.call-start = ((), (), s32[]{:S(2)}) async-start(), calls=%async_computation.29 | async-start | bytes 2359296 | tf_op jit(solution)/shard_map/all_gather | solution.py:274
  213.9 141.7 %reduce-scatter.18.cloned.1.call-start = ((), (), s32[]{:S(2)}) async-start(), calls=%async_computation.23 | async-start | bytes 1310720 | tf_op jit(solution)/shard_map/reduce_scatter | solution.py:87
  306.8 76.1 %reduce-scatter.22.cloned.1.call-start = ((), (), s32[]{:S(2)}) async-start(), calls=%async_computation.31 | async-start | bytes 1310720 | tf_op jit(solution)/shard_map/reduce_scatter | solution.py:87
  310.0 43.8 %copy-start.12 = (bf16[512,2048]{1,0:T(8,128)(2,1)S(1)}, bf16[512,2048]{1,0:T(8,128)(2,1)}, u32[]{:S(2)}) copy-start(bf16[512,2048]{1,0:T(8,128)(2,1)} %all-gather.40.cloned.1.call-done) | copy-start | bytes 6291460
  353.8 30.2 %copy-start.71 = (f32[2048]{0:T(1024)S(1)}, f32[2048]{0:T(1024)}, u32[]{:S(2)}) copy-start(f32[2048]{0:T(1024)} %param.37) | copy-start | bytes 24580
  355.5 57.3 %all-gather.42.cloned.1.call-start = ((), (), s32[]{:S(2)}) async-start(), calls=%async_computation.24 | async-start | bytes 1310720 | tf_op jit(solution)/shard_map/all_gather | solution.py:83
  386.1 82.4 %all-gather.44.cloned.1.call-start = ((), (), s32[]{:S(2)}) async-start(), calls=%async_computation.25 | async-start | bytes 9437184 | tf_op jit(solution)/shard_map/all_gather | solution.py:110
  386.7 138.0 %all-gather.46.cloned.1.call-start = ((), (), s32[]{:S(2)}) async-start(), calls=%async_computation.26 | async-start | bytes 9437184 | tf_op jit(solution)/shard_map/all_gather | solution.py:111
  387.3 195.1 %all-gather.48.cloned.1.call-start = ((), (), s32[]{:S(2)}) async-start(), calls=%async_computation.27 | async-start | bytes 9437184 | tf_op jit(solution)/shard_map/all_gather | solution.py:112
  387.8 223.9 %all-gather.54.cloned.1.call-start = ((), (), s32[]{:S(2)}) async-start(), calls=%async_computation.32 | async-start | bytes 1310720 | tf_op jit(solution)/shard_map/all_gather | solution.py:83
  388.4 252.1 %reduce-scatter.20.cloned.1.call-start = ((), (), s32[]{:S(2)}) async-start(), calls=%async_computation.28 | async-start | bytes 1310720 | tf_op jit(solution)/shard_map/reduce_scatter | solution.py:87
  589.4 79.3 %reduce-scatter.24.cloned.1.call-start = ((), (), s32[]{:S(2)}) async-start(), calls=%async_computation.33 | async-start | bytes 1310720 | tf_op jit(solution)/shard_map/reduce_scatter | solution.py:87
  627.1 42.8 %copy-start.1 = (bf16[2,64,2048]{2,1,0:T(8,128)(2,1)S(1)}, bf16[2,64,2048]{2,1,0:T(8,128)(2,1)}, u32[]{:S(2)}) copy-start(bf16[2,64,2048]{2,1,0:T(8,128)(2,1)} %param.28) | copy-start | bytes 1572868
  627.1 42.8 %copy-start.70 = (f32[2048]{0:T(1024)S(1)}, f32[2048]{0:T(1024)}, u32[]{:S(2)}) copy-start(f32[2048]{0:T(1024)} %param.41) | copy-start | bytes 24580
  630.5 70.4 %all-gather.60.cloned.1.call-start = ((), (), s32[]{:S(2)}) async-start(), calls=%async_computation.39 | async-start | bytes 1310720 | tf_op jit(solution)/shard_map/all_gather | solution.py:83
  674.1 56.4 %all-gather.56.cloned.1.call-start = ((), (), s32[]{:S(2)}) async-start(), calls=%async_computation.34 | async-start | bytes 1310720 | tf_op jit(solution)/shard_map/all_gather | solution.py:83
  674.8 84.6 %reduce-scatter.32.cloned.1.call-start = ((), (), s32[]{:S(2)}) async-start(), calls=%async_computation.40 | async-start | bytes 1310720 | tf_op jit(solution)/shard_map/reduce_scatter | solution.py:87
  722.1 66.1 %reduce-scatter.26.cloned.1.call-start = ((), (), s32[]{:S(2)}) async-start(), calls=%async_computation.35 | async-start | bytes 1310720 | tf_op jit(solution)/shard_map/reduce_scatter | solution.py:87
  744.7 43.5 %copy-start.23 = (bf16[64,2048]{1,0:T(8,128)(2,1)S(1)}, bf16[64,2048]{1,0:T(8,128)(2,1)}, u32[]{:S(2)}) copy-start(bf16[64,2048]{1,0:T(8,128)(2,1)} %reduce-scatter.18.cloned.1.call-done) | copy-start | bytes 786436
  751.6 67.7 %all-gather.62.cloned.1.call-start = ((), (), s32[]{:S(2)}) async-start(), calls=%async_computation.41 | async-start | bytes 1310720 | tf_op jit(solution)/shard_map/all_gather | solution.py:83
  792.6 56.3 %all-gather.58.cloned.1.call-start = ((), (), s32[]{:S(2)}) async-start(), calls=%async_computation.36 | async-start | bytes 1310720 | tf_op jit(solution)/shard_map/all_gather | solution.py:83
  793.3 204.0 %reduce-scatter.34.cloned.1.call-start = ((), (), s32[]{:S(2)}) async-start(), calls=%async_computation.42 | async-start | bytes 4718592 | tf_op jit(solution)/shard_map/reduce_scatter | solution.py:355
  821.5 30.3 %copy-start.42 = (f32[256,4,128]{0,2,1:T(8,128)S(1)}, f32[256,4,128]{0,2,1:T(8,128)}, u32[]{:S(2)}) copy-start(f32[256,4,128]{0,2,1:T(8,128)} %get-tuple-element.404) | copy-start | bytes 1572868
  924.6 118.2 %reduce-scatter.28.cloned.1.call-start = ((), (), s32[]{:S(2)}) async-start(), calls=%async_computation.37 | async-start | bytes 4718592 | tf_op jit(solution)/shard_map/reduce_scatter | solution.py:355
  991.7 164.5 %reduce-scatter.44.cloned.1.call-start = ((), (), s32[]{:S(2)}) async-start(), calls=%async_computation.47 | async-start | bytes 2359296 | tf_op jit(solution)/shard_map/reduce_scatter | solution.py:402
  997.2 46.8 %copy-start = (f32[256,4,128]{0,2,1:T(8,128)S(1)}, f32[256,4,128]{0,2,1:T(8,128)}, u32[]{:S(2)}) copy-start(f32[256,4,128]{0,2,1:T(8,128)} %get-tuple-element.407) | copy-start | bytes 1572868
  997.2 200.3 %reduce-scatter.30.cloned.1.call-start = ((), (), s32[]{:S(2)}) async-start(), calls=%async_computation.38 | async-start | bytes 1310720 | tf_op jit(solution)/shard_map/reduce_scatter | solution.py:87
  1074.1 123.5 %reduce-scatter.36.cloned.1.call-start = ((), (), s32[]{:S(2)}) async-start(), calls=%async_computation.43 | async-start | bytes 1310720 | tf_op jit(solution)/shard_map/reduce_scatter | solution.py:87
  1080.0 141.0 %reduce-scatter.46.cloned.1.call-start = ((), (), s32[]{:S(2)}) async-start(), calls=%async_computation.48 | async-start | bytes 9437184 | tf_op jit(solution)/shard_map/reduce_scatter | solution.py:405
  1101.2 194.7 %reduce-scatter.48.cloned.1.call-start = ((), (), s32[]{:S(2)}) async-start(), calls=%async_computation.49 | async-start | bytes 9437184 | tf_op jit(solution)/shard_map/reduce_scatter | solution.py:408
  1122.4 248.4 %reduce-scatter.50.cloned.1.call-start = ((), (), s32[]{:S(2)}) async-start(), calls=%async_computation.50 | async-start | bytes 9437184 | tf_op jit(solution)/shard_map/reduce_scatter | solution.py:411
  1143.8 271.6 %reduce-scatter.38.cloned.1.call-start = ((), (), s32[]{:S(2)}) async-start(), calls=%async_computation.44 | async-start | bytes 2359296 | tf_op jit(solution)/shard_map/reduce_scatter | solution.py:393
  1148.1 312.1 %reduce-scatter.40.cloned.1.call-start = ((), (), s32[]{:S(2)}) async-start(), calls=%async_computation.45 | async-start | bytes 2359296 | tf_op jit(solution)/shard_map/reduce_scatter | solution.py:396
  1151.1 353.6 %reduce-scatter.42.cloned.1.call-start = ((), (), s32[]{:S(2)}) async-start(), calls=%async_computation.46 | async-start | bytes 2359296 | tf_op jit(solution)/shard_map/reduce_scatter | solution.py:399
  1154.2 43.3 %copy-start.2 = (bf16[2,64,2048]{2,1,0:T(8,128)(2,1)S(1)}, bf16[2,64,2048]{2,1,0:T(8,128)(2,1)}, u32[]{:S(2)}) copy-start(bf16[2,64,2048]{2,1,0:T(8,128)(2,1)} %param.28) | copy-start | bytes 1572868
  1154.2 43.3 %copy-start.34 = (bf16[64,2048]{1,0:T(8,128)(2,1)S(1)}, bf16[64,2048]{1,0:T(8,128)(2,1)}, u32[]{:S(2)}) copy-start(bf16[64,2048]{1,0:T(8,128)(2,1)} %reduce-scatter.32.cloned.1.call-done) | copy-start | bytes 786436
  1154.2 43.3 %copy-start.36 = (bf16[64,2048]{1,0:T(8,128)(2,1)S(1)}, bf16[64,2048]{1,0:T(8,128)(2,1)}, u32[]{:S(2)}) copy-start(bf16[64,2048]{1,0:T(8,128)(2,1)} %reduce-scatter.26.cloned.1.call-done) | copy-start | bytes 786436
  (80 other events, 369.0 us)
Sparse Core Ops, SparseCore 0:
  10.2 30.6 all-gather.63
  42.7 27.3 all-gather.37
  72.0 27.8 all-gather.33
  101.9 27.9 all-gather.65
  131.6 27.3 all-gather.29
  161.4 27.9 all-gather.35
  191.8 27.9 all-gather.51
  222.3 27.9 all-gather.31
  252.1 28.1 all-gather.39
  282.1 27.8 all-gather.49
  312.9 27.1 reduce-scatter.17
  355.6 27.1 reduce-scatter.21
  386.2 26.5 all-gather.41
  414.6 53.8 all-gather.43
  470.2 54.3 all-gather.45
  526.4 55.9 all-gather.47
  583.8 27.9 all-gather.53
  613.9 26.6 reduce-scatter.19
  642.9 25.7 reduce-scatter.23
  674.2 26.5 all-gather.59
  703.0 27.4 all-gather.55
  732.7 26.6 reduce-scatter.31
  762.4 25.7 reduce-scatter.25
  792.7 26.5 all-gather.61
  821.4 27.4 all-gather.57
  924.7 50.8 reduce-scatter.33
  991.8 50.9 reduce-scatter.27
  1046.6 41.1 reduce-scatter.43
  1090.8 27.1 reduce-scatter.29
  1120.7 25.7 reduce-scatter.35
  1150.4 70.6 reduce-scatter.45
  1224.5 71.2 reduce-scatter.47
  1299.5 71.2 reduce-scatter.49
  1374.1 41.2 reduce-scatter.37
  1419.0 41.2 reduce-scatter.39
  1463.4 41.2 reduce-scatter.41
where the time goes:
time: 1530 us; the launch traced here: 1510 us
  waiting for transfers between devices  855 us (56%)
  matrix products  322 us (21%)
  local copies, waits for them, and re-layouts  109 us (7%)
  other arithmetic  102 us (7%)
  blocking collectives  102 us (7%)
  between operations  16.7 us (1%)
    all_gather x6, waiting for transfers between devices, collect(): return lax.all_gather(values, 'head', axis=0, tiled=True)  133 us
    reduce_scatter x8, waiting for transfers between devices, reduce_rows(): lax.psum_scatter(term_fn(jnp.int32(0), row_count * lax.axis_size('head'))...  99.9 us
    dot_general x14, matrix products, dot_left_t(): lax.dot_general(left_side, right_side, (((0,), (0,)), ((), ())), preferre...  73.2 us
    reduce_scatter x1, waiting for transfers between devices, on_device(): lax.psum_scatter(down_acc.astype(jnp.bfloat16), 'blk', scatter_dimension=...  72.2 us
    reduce_scatter x1, waiting for transfers between devices, on_device(): lax.psum_scatter(up_acc.astype(jnp.bfloat16), 'blk', scatter_dimension=0,...  72 us
    dot_general x14, matrix products, dot_plain(): return jnp.dot(left_side, right_side, preferred_element_type=jnp.float32)  60.4 us
    all_gather x1, waiting for transfers between devices, gather_ffn(): lax.all_gather(gate_weight, 'blk', axis=0, tiled=True)  55.7 us
    dot_general x14, matrix products, dot_right_t(): lax.dot_general(left_side, right_side, (((1,), (1,)), ((), ())), preferre...  54.9 us
  transfers between devices with their start and end apart: 36, of which 27 were waited for; matrix products, arithmetic and copies ran while one was open for 28% of the time, Pallas kernels for 0%

commit v1 on v0

v1 whole, which is shorter than its diff:
```python
import functools

import jax
import jax.numpy as jnp
from jax import lax
from jax.experimental import pallas as pl
from jax.experimental.pallas import tpu as pltpu
from jax.sharding import PartitionSpec as P

HD = 128

epsilon = 1e-06
theta = 500000.0
score_scale = HD ** (-0.5)
hidden_score = -1e30
low = jnp.bfloat16
full = jnp.float32
vmem_grant = 56 * 1024 * 1024


def dot_plain(left_side, right_side):
    return jnp.dot(left_side, right_side, preferred_element_type=full)


def dot_right_t(left_side, right_side):
    return lax.dot_general(
        left_side, right_side, (((1,), (1,)), ((), ())), preferred_element_type=full
    )


def dot_left_t(left_side, right_side):
    return lax.dot_general(
        left_side, right_side, (((0,), (0,)), ((), ())), preferred_element_type=full
    )


def rms_scale(values):
    return lax.rsqrt(jnp.mean(values * values, axis=-1, keepdims=True) + epsilon)


def xor_pairs(size, mask):
    return [(i, i ^ mask) for i in range(size)]


def gather_slots(values, axis):
    size = lax.axis_size(axis)
    return [values] + [lax.ppermute(values, axis, xor_pairs(size, s)) for s in range(1, size)]


def exchange_slots(slots, axis):
    size = lax.axis_size(axis)
    return [slots[0]] + [
        lax.ppermute(slots[s], axis, xor_pairs(size, s)) for s in range(1, size)
    ]


def gather_rows(values):
    return jnp.concatenate(gather_slots(values, "head"), axis=0)


def reduce_rows(partial_rows):
    size = lax.axis_size("head")
    rows = partial_rows.shape[0] // size
    slots = [partial_rows[s * rows : (s + 1) * rows] for s in range(size)]
    arrived = exchange_slots([slot.astype(low) for slot in slots], "head")
    return sum(slot.astype(full) for slot in arrived)


def sum_heads(values):
    size = lax.axis_size("head")
    total = None
    for s, arrived in enumerate(gather_slots(values, "head")):
        slots = jnp.split(arrived, size, axis=1)
        ordered = jnp.concatenate([slots[t ^ s] for t in range(size)], axis=1)
        total = ordered if total is None else total + ordered
    return total


def rotary_tables(positions):
    half_size = HD // 2
    inverse = theta ** (-2.0 * jnp.arange(half_size, dtype=jnp.int32).astype(full) / HD)
    angles = positions.astype(full)[:, None] * inverse[None, :]
    cosine, sine = jnp.cos(angles), jnp.sin(angles)
    return (
        jnp.concatenate([cosine, cosine], axis=1),
        jnp.concatenate([-sine, sine], axis=1),
    )


def whole(shape):
    return pl.BlockSpec(shape, lambda: (0,) * len(shape))


def call_whole(body, outs, *args, scalars=1, scratch=(), flops=0):
    moved = sum(a.size * a.dtype.itemsize for a in args) + sum(
        o.size * o.dtype.itemsize for o in outs
    )
    return pl.pallas_call(
        body,
        out_shape=outs,
        in_specs=[pl.BlockSpec(memory_space=pltpu.SMEM)] * scalars
        + [pl.BlockSpec(memory_space=pltpu.VMEM)] * (len(args) - scalars),
        out_specs=[pl.BlockSpec(memory_space=pltpu.VMEM)] * len(outs),
        scratch_shapes=list(scratch),
        compiler_params=pltpu.CompilerParams(vmem_limit_bytes=vmem_grant),
        cost_estimate=pl.CostEstimate(flops=flops, bytes_accessed=moved, transcendentals=0),
    )(*args)


def shape_of(shape, dtype):
    return jax.ShapeDtypeStruct(shape, dtype)


def send_views(me, raw, scale, gains, tables, blocks, rows, heads_local):
    micro_count = blocks // heads_local
    width = heads_local * HD

    def body(me_ref, *refs):
        raw_refs = refs[:micro_count]
        scale_ref, gain_ref, cos_ref, sin_ref = refs[micro_count : micro_count + 4]
        out_refs = refs[micro_count + 4 :]
        cosine, sine = cos_ref[...], sin_ref[...]
        for s in range(blocks):
            target = me_ref[0] ^ s
            column = pl.multiple_of((target % heads_local) * HD, HD)

            def piece(micro):
                for part in range(2):
                    values = raw_refs[micro][:, pl.ds(part * width + column, HD)]
                    factor = scale_ref[:, 2 * micro + part : 2 * micro + part + 1]
                    values = values * factor * gain_ref[part : part + 1, pl.ds(column, HD)]
                    turned = values * cosine + pltpu.roll(values, HD // 2, 1) * sine
                    out_refs[s][:, part * HD : (part + 1) * HD] = turned.astype(low)
                out_refs[s][:, 2 * HD :] = raw_refs[micro][
                    :, pl.ds(2 * width + column, HD)
                ].astype(low)

            for micro in range(micro_count):
                pl.when(target // heads_local == micro)(functools.partial(piece, micro))

    return call_whole(
        body,
        [shape_of((rows, 3 * HD), low)] * blocks,
        me,
        *raw,
        scale,
        gains,
        *tables,
    )


def masked_scores(k_rows, q_rows, key_seg, query_seg, key_pos=None, query_pos=None):
    scores = dot_right_t(k_rows, q_rows) * score_scale
    allowed = key_seg == query_seg
    if key_pos is not None:
        allowed = (allowed & (key_pos <= query_pos)) | (key_pos == query_pos)
    return jnp.where(allowed, scores, hidden_score)


def attention_forward(me, slots, key_seg, key_pos, query_seg, query_pos):
    blocks = len(slots)
    rows = slots[0].shape[0]
    length = blocks * rows

    def body(me_ref, *refs):
        slot_refs = refs[:blocks]
        ks_ref, kp_ref, qs_ref, qp_ref = refs[blocks : blocks + 4]
        out_refs = refs[blocks + 4 : 2 * blocks + 4]
        mixed_ref, norm_ref, q_all, k_all, v_all = refs[2 * blocks + 4 :]
        for s in range(blocks):
            place = pl.ds(pl.multiple_of((me_ref[0] ^ s) * rows, rows), rows)
            q_all[place, :] = slot_refs[s][:, :HD]
            k_all[place, :] = slot_refs[s][:, HD : 2 * HD]
            v_all[place, :] = slot_refs[s][:, 2 * HD :]
        for i in range(blocks):
            here = slice(i * rows, (i + 1) * rows)
            q_rows = q_all[here, :]
            query_seg_row = qs_ref[:, here]
            parts = [
                masked_scores(
                    k_all[here, :], q_rows, ks_ref[here, :], query_seg_row, kp_ref[here, :], qp_ref[:, here]
                )
            ]
            spans = [here]
            if i > 0:
                past = slice(0, i * rows)
                parts.append(masked_scores(k_all[past, :], q_rows, ks_ref[past, :], query_seg_row))
                spans.append(past)
            top = functools.reduce(
                jnp.maximum, [jnp.max(part, axis=0, keepdims=True) for part in parts]
            )
            total = jnp.zeros((1, rows), full)
            summed = jnp.zeros((HD, rows), full)
            for part, span in zip(parts, spans):
                expanded = jnp.exp(part - top)
                total = total + jnp.sum(expanded, axis=0, keepdims=True)
                summed = summed + dot_left_t(v_all[span, :], expanded.astype(low))
            mixed_ref[here, :] = jnp.transpose(summed / total)
            norm_ref[:, here] = top + jnp.log(total)
        for s in range(blocks):
            place = pl.ds(pl.multiple_of((me_ref[0] ^ s) * rows, rows), rows)
            out_refs[s][...] = mixed_ref[place, :].astype(low)

    return call_whole(
        body,
        [shape_of((rows, HD), low)] * blocks
        + [shape_of((length, HD), full), shape_of((1, length), full)],
        me,
        *slots,
        key_seg,
        key_pos,
        query_seg,
        query_pos,
        scratch=[pltpu.VMEM((length, HD), low)] * 3,
        flops=2 * length * length * HD,
    )


def attention_backward(me, slots, grad_slots, mixed, norm, key_seg, key_pos, query_seg, query_pos):
    blocks = len(slots)
    rows = slots[0].shape[0]
    length = blocks * rows

    def body(me_ref, *refs):
        slot_refs = refs[:blocks]
        grad_refs = refs[blocks : 2 * blocks]
        mixed_ref, norm_ref, ks_ref, kp_ref, qs_ref, qp_ref = refs[2 * blocks : 2 * blocks + 6]
        out_refs = refs[2 * blocks + 6 : 3 * blocks + 6]
        q_all, k_all, v_all, g_all, dq_all, dk_all, dv_all = refs[3 * blocks + 6 :]
        for s in range(blocks):
            place = pl.ds(pl.multiple_of((me_ref[0] ^ s) * rows, rows), rows)
            q_all[place, :] = slot_refs[s][:, :HD]
            k_all[place, :] = slot_refs[s][:, HD : 2 * HD]
            v_all[place, :] = slot_refs[s][:, 2 * HD :]
            g_all[place, :] = grad_refs[s][...]
        for i in range(blocks):
            here = slice(i * rows, (i + 1) * rows)
            q_rows = q_all[here, :]
            g_rows = g_all[here, :]
            query_seg_row = qs_ref[:, here]
            norm_row = norm_ref[:, here]
            delta = jnp.sum(
                jnp.transpose(g_rows.astype(full) * mixed_ref[here, :]), axis=0, keepdims=True
            )
            spans = [here] + ([slice(0, i * rows)] if i > 0 else [])
            grad_query = jnp.zeros((HD, rows), full)
            for n, span in enumerate(spans):
                k_rows = k_all[span, :]
                if n == 0:
                    scores = masked_scores(
                        k_rows, q_rows, ks_ref[span, :], query_seg_row, kp_ref[span, :], qp_ref[:, here]
                    )
                else:
                    scores = masked_scores(k_rows, q_rows, ks_ref[span, :], query_seg_row)
                weights = jnp.exp(scores - norm_row)
                grad_probs = dot_right_t(v_all[span, :], g_rows)
                grad_scores = (weights * (grad_probs - delta)).astype(low)
                key_term = dot_plain(grad_scores, q_rows)
                value_term = dot_plain(weights.astype(low), g_rows)
                if n == 0:
                    dk_all[span, :] = key_term
                    dv_all[span, :] = value_term
                else:
                    dk_all[span, :] += key_term
                    dv_all[span, :] += value_term
                grad_query = grad_query + dot_left_t(k_rows, grad_scores)
            dq_all[here, :] = jnp.transpose(grad_query)
        for s in range(blocks):
            place = pl.ds(pl.multiple_of((me_ref[0] ^ s) * rows, rows), rows)
            out_refs[s][:, :HD] = (dq_all[place, :] * score_scale).astype(low)
            out_refs[s][:, HD : 2 * HD] = (dk_all[place, :] * score_scale).astype(low)
            out_refs[s][:, 2 * HD :] = dv_all[place, :].astype(low)

    return call_whole(
        body,
        [shape_of((rows, 3 * HD), low)] * blocks,
        me,
        *slots,
        *grad_slots,
        mixed,
        norm,
        key_seg,
        key_pos,
        query_seg,
        query_pos,
        scratch=[pltpu.VMEM((length, HD), low)] * 4 + [pltpu.VMEM((length, HD), full)] * 3,
        flops=5 * length * length * HD,
    )


def assemble_mixed(me, slots, micro_count, heads_local):
    rows = slots[0].shape[0]
    blocks = len(slots)

    def body(me_ref, *refs):
        out_ref = refs[blocks]
        for s in range(blocks):
            source = me_ref[0] ^ s
            column = pl.multiple_of((source % heads_local) * HD, HD)
            out_ref[source // heads_local, :, pl.ds(column, HD)] = refs[s][...]

    return call_whole(
        body, [shape_of((micro_count, rows, heads_local * HD), low)], me, *slots
    )[0]


def split_mixed(me, mixed, blocks, heads_local):
    micro_count, rows = mixed.shape[:2]

    def body(me_ref, mixed_ref, *out_refs):
        for s in range(blocks):
            target = me_ref[0] ^ s
            column = pl.multiple_of((target % heads_local) * HD, HD)
            out_refs[s][...] = mixed_ref[target // heads_local, :, pl.ds(column, HD)]

    return call_whole(body, [shape_of((rows, HD), low)] * blocks, me, mixed)


def receive_grads(me, slots, tables, micro_count, heads_local):
    rows = slots[0].shape[0]
    blocks = len(slots)
    width = heads_local * HD

    def body(me_ref, *refs):
        cos_ref, sin_ref, norm_ref, value_ref = refs[blocks:]
        cosine, sine = cos_ref[...], sin_ref[...]
        for s in range(blocks):
            source = me_ref[0] ^ s
            micro = source // heads_local
            column = pl.multiple_of((source % heads_local) * HD, HD)
            for part in range(2):
                grads = refs[s][:, part * HD : (part + 1) * HD].astype(full)
                turned = grads * cosine - pltpu.roll(grads, HD // 2, 1) * sine
                norm_ref[micro, :, pl.ds(part * width + column, HD)] = turned
            value_ref[micro, :, pl.ds(column, HD)] = refs[s][:, 2 * HD :]

    return call_whole(
        body,
        [
            shape_of((micro_count, rows, 2 * width), full),
            shape_of((micro_count, rows, width), low),
        ],
        me,
        *slots,
        *tables,
    )


def turn(values, tables):
    return values * tables[0][:, None, :] + jnp.roll(values, HD // 2, axis=-1) * tables[1][:, None, :]


def turn_back(grads, tables):
    return grads * tables[0][:, None, :] - jnp.roll(grads, HD // 2, axis=-1) * tables[1][:, None, :]


def block_scores(query_view, key_rows, query_mark, key_mark):
    scores = score_scale * jnp.einsum(
        "qhd,khd->hqk", query_view, key_rows, preferred_element_type=full
    )
    query_seg, query_pos = query_mark
    key_seg, key_pos = key_mark
    allowed = (query_seg[:, None] == key_seg[None, :]) & (key_pos[None, :] <= query_pos[:, None])
    allowed = allowed | (key_pos[None, :] == query_pos[:, None])
    return jnp.where(allowed[None], scores, hidden_score)


def gathered_forward(query_view, query_mark, stacked):
    rows, heads = query_view.shape[:2]

    def step(running, block):
        key_rows, value_rows, key_seg, key_pos = block
        top, total, summed = running
        scores = block_scores(query_view, key_rows, query_mark, (key_seg, key_pos))
        new_top = jnp.maximum(top, jnp.max(scores, axis=-1))
        shrink = jnp.exp(top - new_top)
        expanded = jnp.where(scores > hidden_score, jnp.exp(scores - new_top[..., None]), 0.0)
        new_total = total * shrink + jnp.sum(expanded, axis=-1)
        new_summed = summed * shrink[..., None] + jnp.einsum(
            "hqk,khd->hqd", expanded.astype(low), value_rows, preferred_element_type=full
        )
        return ((new_top, new_total, new_summed), None)

    start = (
        jnp.full((heads, rows), hidden_score, full),
        jnp.zeros((heads, rows), full),
        jnp.zeros((heads, rows, HD), full),
    )
    top, total, summed = lax.scan(step, start, stacked)[0]
    return jnp.swapaxes(summed / total[..., None], 0, 1), top + jnp.log(total)


def gathered_backward(query_view, grad_view, mixed, norm, query_mark, stacked):
    delta = jnp.sum(grad_view.astype(full) * mixed, axis=2).T

    def step(running, block):
        key_rows, value_rows, key_seg, key_pos = block
        scores = block_scores(query_view, key_rows, query_mark, (key_seg, key_pos))
        weights = jnp.exp(scores - norm[..., None])
        grad_probs = jnp.einsum("qhd,khd->hqk", grad_view, value_rows, preferred_element_type=full)
        grad_scores = (weights * (grad_probs - delta[..., None])).astype(low)
        grad_query = running + jnp.einsum(
            "hqk,khd->qhd", grad_scores, key_rows, preferred_element_type=full
        )
        grad_keys = jnp.einsum("hqk,qhd->khd", grad_scores, query_view, preferred_element_type=full)
        grad_values = jnp.einsum(
            "hqk,qhd->khd", weights.astype(low), grad_view, preferred_element_type=full
        )
        return (
            grad_query,
            jnp.concatenate([grad_keys * score_scale, grad_values], axis=1).astype(low),
        )

    grad_query, key_terms = lax.scan(step, jnp.zeros(query_view.shape, full), stacked)
    return grad_query * score_scale, key_terms


class GatheredAttention:
    def __init__(self, raw, scales, gains, tables, codes, blocks, rows, positions):
        self.tables, self.rows = tables, rows
        width = gains.shape[1]
        shape = (rows, width // HD, HD)
        self.sets = []
        for m, values in enumerate(raw):
            views = []
            for part in range(2):
                cut = values[:, part * width : (part + 1) * width]
                normed = cut * scales[:, 2 * m + part : 2 * m + part + 1] * gains[part]
                views.append(turn(normed.reshape(shape), tables).astype(low))
            value_view = values[:, 2 * width :].astype(low).reshape(shape)
            seg_all = (codes[m] // 2).reshape(blocks, rows)
            key_seg = jnp.where(codes[m] % 2 == 1, codes[m] // 2, -1).reshape(blocks, rows)
            place = lax.axis_index("blk")
            mark = tuple(
                lax.dynamic_index_in_dim(mark, place, 0, keepdims=False)
                for mark in (seg_all, positions)
            )
            stacked = (
                lax.all_gather(views[1], "blk"),
                lax.all_gather(value_view, "blk"),
                key_seg,
                positions,
            )
            self.sets.append((views[0], mark, stacked))

    def forward(self):
        results = [gathered_forward(*one) for one in self.sets]
        self.kept = results
        return jnp.stack(
            [mixed.reshape(self.rows, -1).astype(low) for mixed, norm in results]
        )

    def backward(self, grad_mixed):
        norms, values = [], []
        for m, (view, mark, stacked) in enumerate(self.sets):
            grad_query, terms = gathered_backward(
                view, grad_mixed[m].reshape(view.shape), *self.kept[m], mark, stacked
            )
            own = lax.psum_scatter(terms, "blk", scatter_dimension=0, tiled=False)
            heads = view.shape[1]
            both = [turn_back(grad_query, self.tables)]
            both.append(turn_back(own[:, :heads].astype(full), self.tables))
            norms.append(jnp.concatenate([g.reshape(self.rows, -1) for g in both], axis=1))
            values.append(own[:, heads:].reshape(self.rows, -1))
        return jnp.stack(norms), jnp.stack(values)


class ExchangedAttention:
    def __init__(self, raw, scales, gains, tables, codes, blocks, rows, positions):
        self.blocks, self.tables = blocks, tables
        self.heads = gains.shape[1] // HD
        self.micro_count = len(raw)
        place = lax.axis_index("blk")
        self.me = place.astype(jnp.int32).reshape(1)
        self.slots = exchange_slots(
            send_views(self.me, raw, scales, gains, tables, blocks, rows, self.heads), "blk"
        )
        codes = lax.dynamic_index_in_dim(codes, place // self.heads, 0, keepdims=False)
        seg_all = codes // 2
        seg_key = jnp.where(codes % 2 == 1, seg_all, -1)
        pos_all = positions.reshape(-1)
        self.marks = (seg_key[:, None], pos_all[:, None], seg_all[None, :], pos_all[None, :])

    def forward(self):
        results = attention_forward(self.me, self.slots, *self.marks)
        self.kept = results[self.blocks :]
        return assemble_mixed(
            self.me,
            exchange_slots(results[: self.blocks], "blk"),
            self.micro_count,
            self.heads,
        )

    def backward(self, grad_mixed):
        grad_slots = exchange_slots(
            split_mixed(self.me, grad_mixed, self.blocks, self.heads), "blk"
        )
        back_slots = exchange_slots(
            attention_backward(self.me, self.slots, grad_slots, *self.kept, *self.marks), "blk"
        )
        return receive_grads(self.me, back_slots, self.tables, self.micro_count, self.heads)


def on_device(
    tokens,
    cotangent,
    segments,
    padding,
    query_weight,
    key_weight,
    value_weight,
    output_weight,
    query_gain,
    key_gain,
    attn_gain,
    gate_weight,
    up_weight,
    down_weight,
    ffn_gain,
):
    micro_count, local_rows, model_width = tokens.shape
    blocks = lax.axis_size("blk")
    head_size = lax.axis_size("head")
    group_rows = local_rows * head_size
    width = query_weight.shape[1]
    heads_local = width // HD
    hidden_width = gate_weight.shape[1]
    micros = range(micro_count)
    block_index = lax.axis_index("blk")
    head_index = lax.axis_index("head")
    slot_owner = head_index ^ jnp.arange(head_size, dtype=jnp.int32)
    group_order = (
        slot_owner[:, None] * local_rows + jnp.arange(local_rows, dtype=jnp.int32)[None, :]
    ).reshape(group_rows)
    tables = rotary_tables(block_index * group_rows + group_order)

    qkv_full = lax.all_gather(
        jnp.concatenate([query_weight, key_weight, value_weight], axis=1), "blk", axis=0, tiled=True
    )
    output_full_t = lax.all_gather(output_weight.T, "blk", axis=0, tiled=True)
    gate_up_full = lax.all_gather(
        jnp.concatenate([gate_weight, up_weight], axis=1), "blk", axis=0, tiled=True
    )
    down_full_t = lax.all_gather(down_weight.T, "blk", axis=0, tiled=True)

    codes = lax.all_gather(segments * 2 + padding, ("blk", "head"), axis=1, tiled=True)
    token_rows = [gather_rows(tokens[m]) for m in micros]
    raw = [dot_plain(token_rows[m], qkv_full) for m in micros]
    squares = jnp.stack(
        [
            jnp.sum(jnp.square(raw[m][:, part * width : (part + 1) * width]), axis=1)
            for m in micros
            for part in range(2)
        ]
    )
    scale_rows = lax.rsqrt(sum_heads(squares) / model_width + epsilon)
    scales = scale_rows.T
    gains_qk = jnp.stack([query_gain, key_gain])

    codes = codes.reshape(micro_count, blocks, head_size, local_rows)[:, :, slot_owner, :]
    positions = jnp.arange(blocks, dtype=jnp.int32)[:, None] * group_rows + group_order[None, :]
    exchanged = blocks == micro_count * heads_local and blocks & (blocks - 1) == 0
    attention = (ExchangedAttention if exchanged else GatheredAttention)(
        raw,
        scales,
        gains_qk,
        tables,
        codes.reshape(micro_count, -1),
        blocks,
        group_rows,
        positions,
    )
    mixed = attention.forward()

    outputs, hidden_rows_all, middle_all, grad_down_all, grad_gu_all = [], [], [], [], []
    grad_hidden_all, grad_attn_all = [], []
    attn_gain_grad = jnp.zeros((model_width,), full)
    ffn_gain_grad = jnp.zeros((model_width,), full)
    for m in micros:
        attn_rows = reduce_rows(dot_right_t(mixed[m], output_full_t))
        attn_scale = rms_scale(attn_rows)
        attn_hat = attn_rows * attn_scale
        hidden = tokens[m].astype(full) + attn_hat * attn_gain
        hidden_rows = gather_rows(hidden.astype(low))
        gate_up = dot_plain(hidden_rows, gate_up_full)
        gate_values, up_values = gate_up[:, :hidden_width], gate_up[:, hidden_width:]
        sigmoid_gate = jax.nn.sigmoid(gate_values)
        silu_gate = gate_values * sigmoid_gate
        middle = (silu_gate * up_values).astype(low)
        down_rows = reduce_rows(dot_right_t(middle, down_full_t))
        down_scale = rms_scale(down_rows)
        down_hat = down_rows * down_scale
        outputs.append((hidden + down_hat * ffn_gain).astype(low))
        grad_out = cotangent[m].astype(full)
        ffn_gain_grad = ffn_gain_grad + jnp.sum(grad_out * down_hat, axis=0)
        grad_norm = grad_out * ffn_gain
        grad_down = (
            down_scale
            * (grad_norm - down_hat * jnp.mean(grad_norm * down_hat, axis=1, keepdims=True))
        ).astype(low)
        grad_down_rows = gather_rows(grad_down)
        grad_middle = dot_plain(grad_down_rows, down_full_t)
        grad_gu = jnp.concatenate(
            [
                (
                    grad_middle * up_values * sigmoid_gate * (1.0 + gate_values * (1.0 - sigmoid_gate))
                ).astype(low),
                (grad_middle * silu_gate).astype(low),
            ],
            axis=1,
        )
        grad_hidden = reduce_rows(dot_right_t(grad_gu, gate_up_full)) + grad_out
        attn_gain_grad = attn_gain_grad + jnp.sum(grad_hidden * attn_hat, axis=0)
        grad_norm = grad_hidden * attn_gain
        grad_attn = (
            attn_scale
            * (grad_norm - attn_hat * jnp.mean(grad_norm * attn_hat, axis=1, keepdims=True))
        ).astype(low)
        hidden_rows_all.append(hidden_rows)
        middle_all.append(middle)
        grad_down_all.append(grad_down_rows)
        grad_gu_all.append(grad_gu)
        grad_hidden_all.append(grad_hidden)
        grad_attn_all.append(gather_rows(grad_attn))

    def joined(pieces):
        return jnp.concatenate(pieces, axis=0)

    def to_owner(values):
        return lax.psum_scatter(
            values.astype(low), "blk", scatter_dimension=0, tiled=True
        ).astype(full)

    grad_down_both = joined(grad_down_all)
    grad_attn_both = joined(grad_attn_all)
    down_grad = to_owner(dot_left_t(grad_down_both, joined(middle_all))).T
    gate_up_grad = to_owner(dot_left_t(joined(hidden_rows_all), joined(grad_gu_all)))

    grad_mixed = dot_plain(grad_attn_both, output_full_t).astype(low)
    output_grad = to_owner(
        dot_left_t(grad_attn_both, mixed.reshape(micro_count * group_rows, width))
    ).T
    grad_qk_norm, grad_value = attention.backward(
        grad_mixed.reshape(micro_count, group_rows, width)
    )

    gain_row = jnp.concatenate([query_gain, key_gain])
    hats, grad_hats, dots = [], [], []
    qk_gain_grad = jnp.zeros((2 * width,), full)
    for m in micros:
        scale_cols = jnp.concatenate(
            [
                jnp.broadcast_to(scales[:, 2 * m + part : 2 * m + part + 1], (group_rows, width))
                for part in range(2)
            ],
            axis=1,
        )
        hat = raw[m][:, : 2 * width] * scale_cols
        grad_hat = grad_qk_norm[m] * gain_row
        qk_gain_grad = qk_gain_grad + jnp.sum(grad_qk_norm[m] * hat, axis=0)
        for part in range(2):
            cut = slice(part * width, (part + 1) * width)
            dots.append(jnp.sum(grad_hat[:, cut] * hat[:, cut], axis=1))
        hats.append((hat, scale_cols))
        grad_hats.append(grad_hat)
    mean_dots = (sum_heads(jnp.stack(dots)) / model_width).T
    input_grads, grad_qkv_all = [], []
    for m in micros:
        hat, scale_cols = hats[m]
        dot_cols = jnp.concatenate(
            [
                jnp.broadcast_to(mean_dots[:, 2 * m + part : 2 * m + part + 1], (group_rows, width))
                for part in range(2)
            ],
            axis=1,
        )
        grad_raw = (scale_cols * (grad_hats[m] - hat * dot_cols)).astype(low)
        grad_qkv = jnp.concatenate([grad_raw, grad_value[m]], axis=1)
        grad_qkv_all.append(grad_qkv)
        input_grads.append(reduce_rows(dot_right_t(grad_qkv, qkv_full)) + grad_hidden_all[m])
    qkv_grad = to_owner(dot_left_t(joined(token_rows), joined(grad_qkv_all)))

    ffn_gain_grad, attn_gain_grad = lax.psum((ffn_gain_grad, attn_gain_grad), ("blk", "head"))
    qk_gain_grad = lax.psum(qk_gain_grad, "blk")
    return (
        jnp.stack(outputs),
        jnp.stack(input_grads),
        qkv_grad[:, :width],
        qkv_grad[:, width : 2 * width],
        qkv_grad[:, 2 * width :],
        output_grad,
        qk_gain_grad[:width],
        qk_gain_grad[width:],
        attn_gain_grad,
        gate_up_grad[:, :hidden_width],
        gate_up_grad[:, hidden_width:],
        down_grad,
        ffn_gain_grad,
    )


def solution(mesh):
    return jax.shard_map(
        on_device,
        mesh=mesh,
        in_specs=(
            P(None, ("blk", "head"), None),
            P(None, ("blk", "head"), None),
            P(None, ("blk", "head")),
            P(None, ("blk", "head")),
            P("blk", "head"),
            P("blk", "head"),
            P("blk", "head"),
            P("head", "blk"),
            P("head"),
            P("head"),
            P(),
            P("blk", "head"),
            P("blk", "head"),
            P("head", "blk"),
            P(),
        ),
        out_specs=(
            P(None, ("blk", "head"), None),
            P(None, ("blk", "head"), None),
            P("blk", "head"),
            P("blk", "head"),
            P("blk", "head"),
            P("head", "blk"),
            P("head"),
            P("head"),
            P(),
            P("blk", "head"),
            P("blk", "head"),
            P("head", "blk"),
            P(),
        ),
        check_vma=False,
    )
```

time: 1530 us -> 861 us (0.56)
  waiting for transfers between devices: 855 us -> 338 us
  matrix products: 322 us -> 124 us
  starting transfers between devices: 3.32 us -> 126 us
  other arithmetic: 102 us -> 29.8 us
  local copies, waits for them, and re-layouts: 109 us -> 41.3 us
  blocking collectives: 102 us -> 146 us
  Pallas kernels: 0 us -> 33 us
    all_gather x19 -> x4, waiting for transfers between devices: 411 us -> 0.05 us  [the longest x1 0.02 us: on_device(): lax.all_gather(jnp.concatenate([query_weight, key_weight, value_weight],...]
    reduce_scatter x17 -> x4, waiting for transfers between devices: 437 us -> 127 us  [to_owner(): lax.psum_scatter(values.astype(low), 'blk', scatter_dimension=0, tiled=True)]
    ppermute x0 -> x82, waiting for transfers between devices: none -> 210 us  [the longest x52 137 us: exchange_slots(): lax.ppermute(slots[s], axis, xor_pairs(size, s))]
    dot_general x126 -> x7, matrix products: 194 us -> 42.5 us  [dot_plain(): return jnp.dot(left_side, right_side, preferred_element_type=full)]
    ppermute x0 -> x82, starting transfers between devices: none -> 126 us  [the longest x52 66.3 us: exchange_slots(): lax.ppermute(slots[s], axis, xor_pairs(size, s))]
    all_gather x5 -> x1, blocking collectives: 41.8 us -> 95.9 us  [on_device(): lax.all_gather(segments * 2 + padding, ('blk', 'head'), axis=1, tiled=True)]
    dynamic_slice x130 -> x0, local copies, waits for them, and re-layouts: 48.9 us -> none  [the longest x128 47.6 us: attention_forward(): row_top, row_total = lax.scan(measure, (start_top, start_total), stacked)[0]]
    dot_general x14 -> x4, matrix products: 73.2 us -> 36.5 us  [dot_left_t(): lax.dot_general(left_side, right_side, (((0,), (0,)), ((), ())), preferre...]
  transfers between devices with their start and end apart: 36 -> 90, of which waited for: 27 -> 40; matrix products, arithmetic and copies ran while one was open for 28% -> 20% of each run, Pallas kernels for 0% -> 2%
where the time goes in v1:
time: 861 us; the launch traced here: 855 us
  waiting for transfers between devices  338 us (39%)
  blocking collectives  146 us (17%)
  starting transfers between devices  126 us (15%)
  matrix products  124 us (14%)
  local copies, waits for them, and re-layouts  41.3 us (5%)
  Pallas kernels  33 us (4%)
  other arithmetic  29.8 us (3%)
  between operations  15.9 us (2%)
    ppermute x52, waiting for transfers between devices, exchange_slots(): lax.ppermute(slots[s], axis, xor_pairs(size, s))  137 us
    reduce_scatter x4, waiting for transfers between devices, to_owner(): lax.psum_scatter(values.astype(low), 'blk', scatter_dimension=0, tiled=True)  127 us
    all_gather x1, blocking collectives, on_device(): lax.all_gather(segments * 2 + padding, ('blk', 'head'), axis=1, tiled=True)  95.9 us
    ppermute x30, waiting for transfers between devices, gather_slots(): lax.ppermute(values, axis, xor_pairs(size, s))  72.3 us
    ppermute x52, starting transfers between devices, exchange_slots(): lax.ppermute(slots[s], axis, xor_pairs(size, s))  66.3 us
    ppermute x30, starting transfers between devices, gather_slots(): lax.ppermute(values, axis, xor_pairs(size, s))  59.8 us
    dot_general x8, matrix products, dot_right_t(): lax.dot_general(left_side, right_side, (((1,), (1,)), ((), ())), preferre...  45 us
    dot_general x7, matrix products, dot_plain(): return jnp.dot(left_side, right_side, preferred_element_type=full)  42.5 us
  transfers between devices with their start and end apart: 90, of which 40 were waited for; matrix products, arithmetic and copies ran while one was open for 20% of the time, Pallas kernels for 2%

profile of v1, /device:TPU:0, one launch (start us, length us, event | category | flops | bytes accessed | tf_op | source)
XLA Modules:
  0.0 854.6 jit_solution(6130807504633906189)
XLA Ops:
  12.8 5.1 collective-permute-start.2
  24.0 95.9 %all-gather = s32[32,64,2]{1,2,0:T(2,128)S(1)} all-gather(s32[1,64,2]{1,2,0:T(2,128)S(1)} %add_bitcast_fusion.3), channel_id=1, replica_groups=mesh['blk'=8,'head'=4] {'blk','head'}, dimensions={0}, use_global_device_ids=true | all-gather | bytes 16896 | tf_op jit(solution)/shard_map/all_gather | solution.py:546
  121.5 4.8 fusion.35.refs_1_
  138.1 5.6 shard_map.246
  150.4 5.6 collective-permute-done.10.refs_2_
  158.0 5.7 collective-permute-done.11.refs_3_
  163.7 6.6 collective-permute-done.13.refs_5_
  173.9 7.7 collective-permute-done.15.refs_7_
  182.3 8.8 %shard_map.247 = (bf16[256,128]{1,0:T(8,128)(2,1)}, bf16[256,128]{1,0:T(8,128)(2,1)}, bf16[256,128]{1,0:T(8,128)(2,1)}, bf16[256,128]{1,0:T(8,128)(2,1)}, bf16[2...) custom-call(s32[1]{0:T(128)} %bitcast.1.me_ref, ...), custom_call_target="tpu_custom_call" | custom-call | flops 1073741824 | bytes 3186692 | tf_op jit(solution)/shard_map/pallas_call | solution.py:98
  219.0 10.9 %collective-permute-start.32 = (bf16[64,2048]{1,0:T(8,128)(2,1)S(1)}, bf16[64,2048]{1,0:T(8,128)(2,1)S(1)}, u32[]{:S(2)}, u32[]{:S(2)}) collective-permute-start(bf16[64,2048]{1,0:T(8,128)(2,1)S(1)} %get-tuple-element.225), channel_id=1, source_target_pairs={{0,1},{1,0},{2,3},{3,2},{4,5},{5,4},{6,7},{7,6},{8,9},{9,8},{10,11... | collective-permute-start | bytes 786440 | tf_op jit(solution)/shard_map/ppermute | solution.py:53
  229.8 15.8 %collective-permute-done.24 = bf16[64,2048]{1,0:T(8,128)(2,1)S(1)} collective-permute-done((bf16[64,2048]{1,0:T(8,128)(2,1)S(1)}, bf16[64,2048]{1,0:T(8,128)(2,1)S(1)}, u32[]{:S(2)}, u32[]{:S(2)}) %collective-permute-start.24) | collective-permute-done | bytes 262176 | tf_op jit(solution)/shard_map/ppermute | solution.py:53
  248.6 14.4 %collective-permute-start.26 = (bf16[64,2048]{1,0:T(8,128)(2,1)S(1)}, bf16[64,2048]{1,0:T(8,128)(2,1)S(1)}, u32[]{:S(2)}, u32[]{:S(2)}) collective-permute-start(bf16[64,2048]{1,0:T(8,128)(2,1)S(1)} %get-tuple-element.183), channel_id=1, source_target_pairs={{0,1},{1,0},{2,3},{3,2},{4,5},{5,4},{6,7},{7,6},{8,9},{9,8},{10,11... | collective-permute-start | bytes 786440 | tf_op jit(solution)/shard_map/ppermute | solution.py:47
  263.0 5.1 collective-permute-done.33
  268.4 4.3 collective-permute-done.26
  272.7 5.4 collective-permute-done.27
  283.6 8.6 %fusion.43 = f32[256,4096]{1,0:T(8,128)S(1)} fusion(bf16[2048,4096]{1,0:T(8,128)(2,1)} %all-gather.10.cloned.1.call-done, bf16[64,2048]{1,0:T(8,128)(2,1)S(1)} %collective-permute-done.28, bf16[64,2048]{1,0:T(8,128)(2,1)S(1)} %collective-permute-done.27, bf16[64,2048]{1,0:T(8,128)(2,1)S(1)} %collective-permute-done.26, bf16[64,2048]{1,0:T(8,128)(2,1)S(1)} %copy-done.65), kind=kOutput, calls=%fused_computation.74 | convolution fusion | flops 4299161600 | bytes 22020096 | tf_op jit(solution)/shard_map/dot_general | solution.py:22
  294.9 6.1 convolution_convert_fusion.11
  305.5 8.4 fusion.51
  323.0 14.9 %collective-permute-done.30 = bf16[64,2048]{1,0:T(8,128)(2,1)S(1)} collective-permute-done((bf16[64,2048]{1,0:T(8,128)(2,1)S(1)}, bf16[64,2048]{1,0:T(8,128)(2,1)S(1)}, u32[]{:S(2)}, u32[]{:S(2)}) %collective-permute-start.30) | collective-permute-done | bytes 262176 | tf_op jit(solution)/shard_map/ppermute | solution.py:53
  338.2 9.5 %collective-permute-done.39 = bf16[64,2048]{1,0:T(8,128)(2,1)S(1)} collective-permute-done((bf16[64,2048]{1,0:T(8,128)(2,1)S(1)}, bf16[64,2048]{1,0:T(8,128)(2,1)S(1)}, u32[]{:S(2)}, u32[]{:S(2)}) %collective-permute-start.39) | collective-permute-done | bytes 262176 | tf_op jit(solution)/shard_map/ppermute | solution.py:53
  353.1 7.1 collective-permute-done.41
  360.2 14.3 %collective-permute-done.42 = bf16[64,2048]{1,0:T(8,128)(2,1)S(1)} collective-permute-done((bf16[64,2048]{1,0:T(8,128)(2,1)S(1)}, bf16[64,2048]{1,0:T(8,128)(2,1)S(1)}, u32[]{:S(2)}, u32[]{:S(2)}) %collective-permute-start.42) | collective-permute-done | bytes 262176 | tf_op jit(solution)/shard_map/ppermute | solution.py:47
  381.2 7.6 multiply_convert_fusion.3
  388.8 10.9 %convolution_convert_fusion.5 = bf16[256,2048]{1,0:T(8,128)(2,1)S(1)} fusion(bf16[2048,4096]{1,0:T(8,128)(2,1)} %all-gather.10.cloned.1.call-done, bf16[256,2048]{1,0:T(8,128)(2,1)} %get-tuple-element.199, bf16[256,2048]{1,0:T(8,128)(2,1)} %get-tuple-element.198), kind=kOutput, calls=%fused_computation.13 | convolution fusion | flops 4299685888 | bytes 19922944 | tf_op jit(solution)/shard_map/dot_general | solution.py:26
  405.0 9.2 %multiply_convert_fusion.1 = (bf16[256,2048]{1,0:T(8,128)(2,1)}, bf16[256,2048]{1,0:T(8,128)(2,1)}) fusion(f32[256,4096]{1,0:T(8,128)} %copy-done.26, bf16[2048,2048]{0,1:T(8,128)(2,1)} %all-gather.12.cloned.1.call-done, bf16[64,2048]{1,0:T(8,128)(2,1)} %collective-permute-done.52, bf16[64,2048]{1,0:T(8,128)(2,1)} %collective-permute-done.51, ...), kind=kOutput, calls=%fused_computation.32 | convolution fusion | flops 2158493696 | bytes 15728640 | tf_op jit(solution)/shard_map/dot_general | solution.py:22
  414.2 11.9 %convolution_convert_fusion.4 = bf16[256,2048]{1,0:T(8,128)(2,1)} fusion(bf16[2048,4096]{1,0:T(8,128)(2,1)} %all-gather.10.cloned.1.call-done, bf16[256,2048]{1,0:T(8,128)(2,1)} %get-tuple-element.201, bf16[256,2048]{1,0:T(8,128)(2,1)} %get-tuple-element.200), kind=kOutput, calls=%fused_computation.12 | convolution fusion | flops 4299685888 | bytes 19922944 | tf_op jit(solution)/shard_map/dot_general | solution.py:26
  432.1 6.3 collective-permute-done.55
  438.4 10.5 %collective-permute-done.54 = bf16[64,2048]{1,0:T(8,128)(2,1)S(1)} collective-permute-done((bf16[64,2048]{1,0:T(8,128)(2,1)S(1)}, bf16[64,2048]{1,0:T(8,128)(2,1)S(1)}, u32[]{:S(2)}, u32[]{:S(2)}) %collective-permute-start.54) | collective-permute-done | bytes 262176 | tf_op jit(solution)/shard_map/ppermute | solution.py:53
  460.4 14.0 %collective-permute-done.48 = bf16[64,2048]{1,0:T(8,128)(2,1)S(1)} collective-permute-done((bf16[64,2048]{1,0:T(8,128)(2,1)S(1)}, bf16[64,2048]{1,0:T(8,128)(2,1)S(1)}, u32[]{:S(2)}, u32[]{:S(2)}) %collective-permute-start.48) | collective-permute-done | bytes 262176 | tf_op jit(solution)/shard_map/ppermute | solution.py:47
  474.6 4.1 collective-permute-start.56
  482.6 5.3 collective-permute-done.56
  487.9 11.7 %collective-permute-done.57 = bf16[64,2048]{1,0:T(8,128)(2,1)S(1)} collective-permute-done((bf16[64,2048]{1,0:T(8,128)(2,1)S(1)}, bf16[64,2048]{1,0:T(8,128)(2,1)S(1)}, u32[]{:S(2)}, u32[]{:S(2)}) %collective-permute-start.57) | collective-permute-done | bytes 262176 | tf_op jit(solution)/shard_map/ppermute | solution.py:47
  515.3 11.0 %shard_map.250 = (bf16[256,384]{1,0:T(8,128)(2,1)}, bf16[256,384]{1,0:T(8,128)(2,1)}, bf16[256,384]{1,0:T(8,128)(2,1)}, bf16[256,384]{1,0:T(8,128)(2,1)}, bf16[2...) custom-call(s32[1]{0:T(128)} %bitcast.1.me_ref, ...), custom_call_target="tpu_custom_call" | custom-call | flops 2684354560 | bytes 4759556 | tf_op jit(solution)/shard_map/pallas_call | solution.py:98
  537.9 11.1 %collective-permute-done.70.refs_5_ = bf16[256,384]{1,0:T(8,128)(2,1)} collective-permute-done((bf16[256,384]{1,0:T(8,128)(2,1)}, bf16[256,384]{1,0:T(8,128)(2,1)}, u32[]{:S(2)}, u32[]{:S(2)}) %collective-permute-start.70) | collective-permute-done | bytes 196640 | tf_op jit(solution)/shard_map/ppermute | solution.py:53
  548.9 3.7 shard_map.251
  555.9 3.7 collective-permute-start.73
  571.1 9.1 %convolution_convert_fusion.2 = bf16[2048,1536]{1,0:T(8,128)(2,1)} fusion(bf16[512,2048]{1,0:T(8,128)(2,1)S(1)} %copy-done.79, bf16[256,512]{1,0:T(8,128)(2,1)S(1)} %get-tuple-element.246, bf16[256,1024]{1,0:T(8,128)(2,1)S(1)} %fusion.78, bf16[256,512]{1,0:T(8,128)(2,1)S(1)} %get-tuple-element.245, bf16[256,1024]{1,0:T(8,128)(2,1)S(1)} %get-tuple-element.202), kind=kOutput, calls=%fused_computation.3 | convolution fusion | flops 3230662656 | bytes 9961472 | tf_op jit(solution)/shard_map/dot_general | solution.py:32
  585.5 8.4 convolution_convert_fusion.1
  596.1 16.0 %convolution_convert_fusion = bf16[2048,4096]{1,0:T(8,128)(2,1)} fusion(bf16[512,2048]{1,0:T(8,128)(2,1)S(1)} %constant_dynamic-update-slice_fusion.16, bf16[256,2048]{1,0:T(8,128)(2,1)} %get-tuple-element.201, bf16[256,2048]{1,0:T(8,128)(2,1)} %get-tuple-element.200, bf16[256,2048]{1,0:T(8,128)(2,1)} %get-tuple-element.199, ...), kind=kOutput, calls=%fused_computation.1 | convolution fusion | flops 8615100416 | bytes 23068672 | tf_op jit(solution)/shard_map/dot_general | solution.py:32
  613.8 37.8 %all-reduce = (f32[2048]{0:T(1024)}, f32[2048]{0:T(1024)}) all-reduce(f32[2048]{0:T(1024)S(1)} %add.359, f32[2048]{0:T(1024)S(1)} %add.360), channel_id=1, replica_groups=mesh['blk'=8,'head'=4] {'blk','head'}, use_global_device_ids=true, to_apply=%region_23.24 | all-reduce | flops 4096 | bytes 32768 | tf_op jit(solution)/shard_map/psum | solution.py:683
  651.6 4.7 convolution_convert_fusion.8
  661.5 5.7 convolution_convert_fusion.9
  671.1 12.2 %psum.21 = f32[1024]{0:T(1024)S(1)} all-reduce(f32[1024]{0:T(1024)S(1)} %add.358), channel_id=1, replica_groups=mesh['blk'=8,'head'=4] {'blk'}, use_global_device_ids=true, to_apply=%region_20.21 | all-reduce | flops 1024 | bytes 8192 | tf_op jit(solution)/shard_map/psum | solution.py:684
  685.5 9.8 %collective-permute-done.80 = bf16[64,2048]{1,0:T(8,128)(2,1)} collective-permute-done((bf16[64,2048]{1,0:T(8,128)(2,1)}, bf16[64,2048]{1,0:T(8,128)(2,1)}, u32[]{:S(2)}, u32[]{:S(2)}) %collective-permute-start.80) | collective-permute-done | bytes 262176 | tf_op jit(solution)/shard_map/ppermute | solution.py:53
  696.6 9.9 %collective-permute-done.77 = bf16[64,2048]{1,0:T(8,128)(2,1)} collective-permute-done((bf16[64,2048]{1,0:T(8,128)(2,1)}, bf16[64,2048]{1,0:T(8,128)(2,1)}, u32[]{:S(2)}, u32[]{:S(2)}) %collective-permute-start.77) | collective-permute-done | bytes 262176 | tf_op jit(solution)/shard_map/ppermute | solution.py:53
  713.0 10.5 %reduce-scatter.11.cloned.1.call-done = bf16[256,2048]{1,0:T(8,128)(2,1)} async-done(((bf16[2048,2048]{1,0:T(8,128)(2,1)}), bf16[256,2048]{1,0:T(8,128)(2,1)}) %reduce-scatter.11.cloned.1.call-update) | async-done | bytes 1048592 | tf_op jit(solution)/shard_map/reduce_scatter | solution.py:630
  726.8 116.7 %reduce-scatter.9.cloned.1.call-done = bf16[256,4096]{1,0:T(8,128)(2,1)} async-done(((bf16[2048,4096]{1,0:T(8,128)(2,1)}), bf16[256,4096]{1,0:T(8,128)(2,1)}) %reduce-scatter.9.cloned.1.call-update) | async-done | bytes 2097168 | tf_op jit(solution)/shard_map/reduce_scatter | solution.py:630
  843.5 4.1 fusion.143
  (501 shorter events, 202.3 us)
Async XLA Ops:
  7.2 114.3 %all-gather.6.cloned.1.call-start = ((), (), s32[]{:S(2)}) async-start(), calls=%async_computation.4 | async-start | bytes 7077888 | tf_op jit(solution)/shard_map/all_gather | solution.py:537
  9.4 195.8 %all-gather.8.cloned.1.call-start = ((), (), s32[]{:S(2)}) async-start(), calls=%async_computation.5 | async-start | bytes 2359296 | tf_op jit(solution)/shard_map/all_gather | solution.py:540
  10.2 273.4 %all-gather.10.cloned.1.call-start = ((), (), s32[]{:S(2)}) async-start(), calls=%async_computation.6 | async-start | bytes 18874368 | tf_op jit(solution)/shard_map/all_gather | solution.py:541
  11.8 283.1 %all-gather.12.cloned.1.call-start = ((), (), s32[]{:S(2)}) async-start(), calls=%async_computation.7 | async-start | bytes 9437184 | tf_op jit(solution)/shard_map/all_gather | solution.py:544
  12.4 696.3 %reduce-scatter.7.cloned.1.call-start = ((), (), s32[]{:S(2)}) async-start(), calls=%async_computation.9 | async-start | bytes 2359296 | tf_op jit(solution)/shard_map/reduce_scatter | solution.py:630
  12.8 113.7 %collective-permute-start.2 = (bf16[64,2048]{1,0:T(8,128)(2,1)S(1)}, bf16[64,2048]{1,0:T(8,128)(2,1)S(1)}, u32[]{:S(2)}, u32[]{:S(2)}) collective-permute-start(bf16[64,2048]{1,0:T(8,128)(2,1)S(1)} %get-tuple-element.248), channel_id=1, source_target_pairs={{0,3},{1,2},{2,1},{3,0},{4,7},{5,6},{6,5},{7,4},{8,11},{9,10},{10,... | collective-permute-start | bytes 786440 | tf_op jit(solution)/shard_map/ppermute | solution.py:47
  17.9 108.6 %collective-permute-start.1 = (bf16[64,2048]{1,0:T(8,128)(2,1)S(1)}, bf16[64,2048]{1,0:T(8,128)(2,1)S(1)}, u32[]{:S(2)}, u32[]{:S(2)}) collective-permute-start(bf16[64,2048]{1,0:T(8,128)(2,1)S(1)} %get-tuple-element.248), channel_id=1, source_target_pairs={{0,2},{1,3},{2,0},{3,1},{4,6},{5,7},{6,4},{7,5},{8,10},{9,11},{10,... | collective-permute-start | bytes 786440 | tf_op jit(solution)/shard_map/ppermute | solution.py:47
  17.9 103.5 %collective-permute-start.5 = (bf16[64,2048]{1,0:T(8,128)(2,1)S(1)}, bf16[64,2048]{1,0:T(8,128)(2,1)S(1)}, u32[]{:S(2)}, u32[]{:S(2)}) collective-permute-start(bf16[64,2048]{1,0:T(8,128)(2,1)S(1)} %get-tuple-element.247), channel_id=1, source_target_pairs={{0,3},{1,2},{2,1},{3,0},{4,7},{5,6},{6,5},{7,4},{8,11},{9,10},{10,... | collective-permute-start | bytes 786440 | tf_op jit(solution)/shard_map/ppermute | solution.py:47
  19.8 101.6 %collective-permute-start.4 = (bf16[64,2048]{1,0:T(8,128)(2,1)S(1)}, bf16[64,2048]{1,0:T(8,128)(2,1)S(1)}, u32[]{:S(2)}, u32[]{:S(2)}) collective-permute-start(bf16[64,2048]{1,0:T(8,128)(2,1)S(1)} %get-tuple-element.247), channel_id=1, source_target_pairs={{0,2},{1,3},{2,0},{3,1},{4,6},{5,7},{6,4},{7,5},{8,10},{9,11},{10,... | collective-permute-start | bytes 786440 | tf_op jit(solution)/shard_map/ppermute | solution.py:47
  20.9 100.6 %collective-permute-start.3 = (bf16[64,2048]{1,0:T(8,128)(2,1)S(1)}, bf16[64,2048]{1,0:T(8,128)(2,1)S(1)}, u32[]{:S(2)}, u32[]{:S(2)}) collective-permute-start(bf16[64,2048]{1,0:T(8,128)(2,1)S(1)} %get-tuple-element.247), channel_id=1, source_target_pairs={{0,1},{1,0},{2,3},{3,2},{4,5},{5,4},{6,7},{7,6},{8,9},{9,8},{10,11... | collective-permute-start | bytes 786440 | tf_op jit(solution)/shard_map/ppermute | solution.py:47
  149.2 21.2 %collective-permute-start.13 = (bf16[256,384]{1,0:T(8,128)(2,1)}, bf16[256,384]{1,0:T(8,128)(2,1)S(1)}, u32[]{:S(2)}, u32[]{:S(2)}) collective-permute-start(bf16[256,384]{1,0:T(8,128)(2,1)} %get-tuple-element.54), channel_id=1, source_target_pairs={{0,20},{4,16},{8,28},{12,24},{16,4},{20,0},{24,12},{28,8},{1,21},{... | collective-permute-start | bytes 589832 | tf_op jit(solution)/shard_map/ppermute | solution.py:53
  149.2 24.7 %collective-permute-start.14 = (bf16[256,384]{1,0:T(8,128)(2,1)}, bf16[256,384]{1,0:T(8,128)(2,1)S(1)}, u32[]{:S(2)}, u32[]{:S(2)}) collective-permute-start(bf16[256,384]{1,0:T(8,128)(2,1)} %get-tuple-element.55), channel_id=1, source_target_pairs={{0,24},{4,28},{8,16},{12,20},{16,8},{20,12},{24,0},{28,4},{1,25},{... | collective-permute-start | bytes 589832 | tf_op jit(solution)/shard_map/ppermute | solution.py:53
  156.0 25.7 %collective-permute-start.15 = (bf16[256,384]{1,0:T(8,128)(2,1)S(1)}, bf16[256,384]{1,0:T(8,128)(2,1)S(1)}, u32[]{:S(2)}, u32[]{:S(2)}) collective-permute-start(bf16[256,384]{1,0:T(8,128)(2,1)S(1)} %copy-done.92), channel_id=1, source_target_pairs={{0,28},{4,24},{8,20},{12,16},{16,12},{20,8},{24,4},{28,0},{1,29},{... | collective-permute-start | bytes 589832 | tf_op jit(solution)/shard_map/ppermute | solution.py:53
  211.1 34.5 %collective-permute-start.24 = (bf16[64,2048]{1,0:T(8,128)(2,1)S(1)}, bf16[64,2048]{1,0:T(8,128)(2,1)S(1)}, u32[]{:S(2)}, u32[]{:S(2)}) collective-permute-start(bf16[64,2048]{1,0:T(8,128)(2,1)S(1)} %get-tuple-element.230), channel_id=1, source_target_pairs={{0,2},{1,3},{2,0},{3,1},{4,6},{5,7},{6,4},{7,5},{8,10},{9,11},{10,... | collective-permute-start | bytes 786440 | tf_op jit(solution)/shard_map/ppermute | solution.py:53
  211.1 34.5 %collective-permute-start.23 = (bf16[64,2048]{1,0:T(8,128)(2,1)S(1)}, bf16[64,2048]{1,0:T(8,128)(2,1)S(1)}, u32[]{:S(2)}, u32[]{:S(2)}) collective-permute-start(bf16[64,2048]{1,0:T(8,128)(2,1)S(1)} %get-tuple-element.228), channel_id=1, source_target_pairs={{0,1},{1,0},{2,3},{3,2},{4,5},{5,4},{6,7},{7,6},{8,9},{9,8},{10,11... | collective-permute-start | bytes 786440 | tf_op jit(solution)/shard_map/ppermute | solution.py:53
  213.1 35.5 %collective-permute-start.34 = (bf16[64,2048]{1,0:T(8,128)(2,1)S(1)}, bf16[64,2048]{1,0:T(8,128)(2,1)S(1)}, u32[]{:S(2)}, u32[]{:S(2)}) collective-permute-start(bf16[64,2048]{1,0:T(8,128)(2,1)S(1)} %get-tuple-element.226), channel_id=1, source_target_pairs={{0,3},{1,2},{2,1},{3,0},{4,7},{5,6},{6,5},{7,4},{8,11},{9,10},{10,... | collective-permute-start | bytes 786440 | tf_op jit(solution)/shard_map/ppermute | solution.py:53
  216.4 51.7 %collective-permute-start.33 = (bf16[64,2048]{1,0:T(8,128)(2,1)S(1)}, bf16[64,2048]{1,0:T(8,128)(2,1)S(1)}, u32[]{:S(2)}, u32[]{:S(2)}) collective-permute-start(bf16[64,2048]{1,0:T(8,128)(2,1)S(1)} %get-tuple-element.227), channel_id=1, source_target_pairs={{0,2},{1,3},{2,0},{3,1},{4,6},{5,7},{6,4},{7,5},{8,10},{9,11},{10,... | collective-permute-start | bytes 786440 | tf_op jit(solution)/shard_map/ppermute | solution.py:53
  219.0 49.2 %collective-permute-start.32 = (bf16[64,2048]{1,0:T(8,128)(2,1)S(1)}, bf16[64,2048]{1,0:T(8,128)(2,1)S(1)}, u32[]{:S(2)}, u32[]{:S(2)}) collective-permute-start(bf16[64,2048]{1,0:T(8,128)(2,1)S(1)} %get-tuple-element.225), channel_id=1, source_target_pairs={{0,1},{1,0},{2,3},{3,2},{4,5},{5,4},{6,7},{7,6},{8,9},{9,8},{10,11... | collective-permute-start | bytes 786440 | tf_op jit(solution)/shard_map/ppermute | solution.py:53
  246.1 32.1 %collective-permute-start.28 = (bf16[64,2048]{1,0:T(8,128)(2,1)S(1)}, bf16[64,2048]{1,0:T(8,128)(2,1)S(1)}, u32[]{:S(2)}, u32[]{:S(2)}) collective-permute-start(bf16[64,2048]{1,0:T(8,128)(2,1)S(1)} %get-tuple-element.183), channel_id=1, source_target_pairs={{0,3},{1,2},{2,1},{3,0},{4,7},{5,6},{6,5},{7,4},{8,11},{9,10},{10,... | collective-permute-start | bytes 786440 | tf_op jit(solution)/shard_map/ppermute | solution.py:47
  248.5 29.6 %collective-permute-start.27 = (bf16[64,2048]{1,0:T(8,128)(2,1)S(1)}, bf16[64,2048]{1,0:T(8,128)(2,1)S(1)}, u32[]{:S(2)}, u32[]{:S(2)}) collective-permute-start(bf16[64,2048]{1,0:T(8,128)(2,1)S(1)} %get-tuple-element.183), channel_id=1, source_target_pairs={{0,2},{1,3},{2,0},{3,1},{4,6},{5,7},{6,4},{7,5},{8,10},{9,11},{10,... | collective-permute-start | bytes 786440 | tf_op jit(solution)/shard_map/ppermute | solution.py:47
  248.6 24.1 %collective-permute-start.26 = (bf16[64,2048]{1,0:T(8,128)(2,1)S(1)}, bf16[64,2048]{1,0:T(8,128)(2,1)S(1)}, u32[]{:S(2)}, u32[]{:S(2)}) collective-permute-start(bf16[64,2048]{1,0:T(8,128)(2,1)S(1)} %get-tuple-element.183), channel_id=1, source_target_pairs={{0,1},{1,0},{2,3},{3,2},{4,5},{5,4},{6,7},{7,6},{8,9},{9,8},{10,11... | collective-permute-start | bytes 786440 | tf_op jit(solution)/shard_map/ppermute | solution.py:47
  279.1 24.5 %collective-permute-start.37 = (bf16[64,2048]{1,0:T(8,128)(2,1)}, bf16[64,2048]{1,0:T(8,128)(2,1)S(1)}, u32[]{:S(2)}, u32[]{:S(2)}) collective-permute-start(bf16[64,2048]{1,0:T(8,128)(2,1)} %get-tuple-element.181), channel_id=1, source_target_pairs={{0,3},{1,2},{2,1},{3,0},{4,7},{5,6},{6,5},{7,4},{8,11},{9,10},{10,... | collective-permute-start | bytes 786440 | tf_op jit(solution)/shard_map/ppermute | solution.py:47
  281.7 23.8 %collective-permute-start.36 = (bf16[64,2048]{1,0:T(8,128)(2,1)}, bf16[64,2048]{1,0:T(8,128)(2,1)S(1)}, u32[]{:S(2)}, u32[]{:S(2)}) collective-permute-start(bf16[64,2048]{1,0:T(8,128)(2,1)} %get-tuple-element.181), channel_id=1, source_target_pairs={{0,2},{1,3},{2,0},{3,1},{4,6},{5,7},{6,4},{7,5},{8,10},{9,11},{10,... | collective-permute-start | bytes 786440 | tf_op jit(solution)/shard_map/ppermute | solution.py:47
  281.7 23.8 %collective-permute-start.35 = (bf16[64,2048]{1,0:T(8,128)(2,1)}, bf16[64,2048]{1,0:T(8,128)(2,1)S(1)}, u32[]{:S(2)}, u32[]{:S(2)}) collective-permute-start(bf16[64,2048]{1,0:T(8,128)(2,1)} %get-tuple-element.181), channel_id=1, source_target_pairs={{0,1},{1,0},{2,3},{3,2},{4,5},{5,4},{6,7},{7,6},{8,9},{9,8},{10,11... | collective-permute-start | bytes 786440 | tf_op jit(solution)/shard_map/ppermute | solution.py:47
  303.6 34.3 %collective-permute-start.30 = (bf16[64,2048]{1,0:T(8,128)(2,1)S(1)}, bf16[64,2048]{1,0:T(8,128)(2,1)S(1)}, u32[]{:S(2)}, u32[]{:S(2)}) collective-permute-start(bf16[64,2048]{1,0:T(8,128)(2,1)S(1)} %get-tuple-element.221), channel_id=1, source_target_pairs={{0,2},{1,3},{2,0},{3,1},{4,6},{5,7},{6,4},{7,5},{8,10},{9,11},{10,... | collective-permute-start | bytes 786440 | tf_op jit(solution)/shard_map/ppermute | solution.py:53
  303.6 34.3 %collective-permute-start.29 = (bf16[64,2048]{1,0:T(8,128)(2,1)S(1)}, bf16[64,2048]{1,0:T(8,128)(2,1)S(1)}, u32[]{:S(2)}, u32[]{:S(2)}) collective-permute-start(bf16[64,2048]{1,0:T(8,128)(2,1)S(1)} %get-tuple-element.219), channel_id=1, source_target_pairs={{0,1},{1,0},{2,3},{3,2},{4,5},{5,4},{6,7},{7,6},{8,9},{9,8},{10,11... | collective-permute-start | bytes 786440 | tf_op jit(solution)/shard_map/ppermute | solution.py:53
  321.1 26.6 %collective-permute-start.39 = (bf16[64,2048]{1,0:T(8,128)(2,1)S(1)}, bf16[64,2048]{1,0:T(8,128)(2,1)S(1)}, u32[]{:S(2)}, u32[]{:S(2)}) collective-permute-start(bf16[64,2048]{1,0:T(8,128)(2,1)S(1)} %get-tuple-element.224), channel_id=1, source_target_pairs={{0,2},{1,3},{2,0},{3,1},{4,6},{5,7},{6,4},{7,5},{8,10},{9,11},{10,... | collective-permute-start | bytes 786440 | tf_op jit(solution)/shard_map/ppermute | solution.py:53
  321.1 26.6 %collective-permute-start.38 = (bf16[64,2048]{1,0:T(8,128)(2,1)S(1)}, bf16[64,2048]{1,0:T(8,128)(2,1)S(1)}, u32[]{:S(2)}, u32[]{:S(2)}) collective-permute-start(bf16[64,2048]{1,0:T(8,128)(2,1)S(1)} %get-tuple-element.222), channel_id=1, source_target_pairs={{0,1},{1,0},{2,3},{3,2},{4,5},{5,4},{6,7},{7,6},{8,9},{9,8},{10,11... | collective-permute-start | bytes 786440 | tf_op jit(solution)/shard_map/ppermute | solution.py:53
  349.7 24.9 %collective-permute-start.43 = (bf16[64,2048]{1,0:T(8,128)(2,1)S(1)}, bf16[64,2048]{1,0:T(8,128)(2,1)S(1)}, u32[]{:S(2)}, u32[]{:S(2)}) collective-permute-start(bf16[64,2048]{1,0:T(8,128)(2,1)S(1)} %get-tuple-element.179), channel_id=1, source_target_pairs={{0,3},{1,2},{2,1},{3,0},{4,7},{5,6},{6,5},{7,4},{8,11},{9,10},{10,... | collective-permute-start | bytes 786440 | tf_op jit(solution)/shard_map/ppermute | solution.py:47
  351.2 23.3 %collective-permute-start.42 = (bf16[64,2048]{1,0:T(8,128)(2,1)S(1)}, bf16[64,2048]{1,0:T(8,128)(2,1)S(1)}, u32[]{:S(2)}, u32[]{:S(2)}) collective-permute-start(bf16[64,2048]{1,0:T(8,128)(2,1)S(1)} %get-tuple-element.179), channel_id=1, source_target_pairs={{0,2},{1,3},{2,0},{3,1},{4,6},{5,7},{6,4},{7,5},{8,10},{9,11},{10,... | collective-permute-start | bytes 786440 | tf_op jit(solution)/shard_map/ppermute | solution.py:47
  376.8 25.3 %collective-permute-start.52 = (bf16[64,2048]{1,0:T(8,128)(2,1)}, bf16[64,2048]{1,0:T(8,128)(2,1)}, u32[]{:S(2)}, u32[]{:S(2)}) collective-permute-start(bf16[64,2048]{1,0:T(8,128)(2,1)} %get-tuple-element.177), channel_id=1, source_target_pairs={{0,3},{1,2},{2,1},{3,0},{4,7},{5,6},{6,5},{7,4},{8,11},{9,10},{10,... | collective-permute-start | bytes 786440 | tf_op jit(solution)/shard_map/ppermute | solution.py:47
  377.9 27.1 %collective-permute-start.51 = (bf16[64,2048]{1,0:T(8,128)(2,1)}, bf16[64,2048]{1,0:T(8,128)(2,1)}, u32[]{:S(2)}, u32[]{:S(2)}) collective-permute-start(bf16[64,2048]{1,0:T(8,128)(2,1)} %get-tuple-element.177), channel_id=1, source_target_pairs={{0,2},{1,3},{2,0},{3,1},{4,6},{5,7},{6,4},{7,5},{8,10},{9,11},{10,... | collective-permute-start | bytes 786440 | tf_op jit(solution)/shard_map/ppermute | solution.py:47
  378.0 27.1 %collective-permute-start.50 = (bf16[64,2048]{1,0:T(8,128)(2,1)}, bf16[64,2048]{1,0:T(8,128)(2,1)}, u32[]{:S(2)}, u32[]{:S(2)}) collective-permute-start(bf16[64,2048]{1,0:T(8,128)(2,1)} %get-tuple-element.177), channel_id=1, source_target_pairs={{0,1},{1,0},{2,3},{3,2},{4,5},{5,4},{6,7},{7,6},{8,9},{9,8},{10,11... | collective-permute-start | bytes 786440 | tf_op jit(solution)/shard_map/ppermute | solution.py:47
  400.6 28.2 %collective-permute-start.46 = (bf16[64,2048]{1,0:T(8,128)(2,1)}, bf16[64,2048]{1,0:T(8,128)(2,1)S(1)}, u32[]{:S(2)}, u32[]{:S(2)}) collective-permute-start(bf16[64,2048]{1,0:T(8,128)(2,1)} %get-tuple-element.214), channel_id=1, source_target_pairs={{0,3},{1,2},{2,1},{3,0},{4,7},{5,6},{6,5},{7,4},{8,11},{9,10},{10,... | collective-permute-start | bytes 786440 | tf_op jit(solution)/shard_map/ppermute | solution.py:53
  401.8 30.3 %collective-permute-start.45 = (bf16[64,2048]{1,0:T(8,128)(2,1)}, bf16[64,2048]{1,0:T(8,128)(2,1)}, u32[]{:S(2)}, u32[]{:S(2)}) collective-permute-start(bf16[64,2048]{1,0:T(8,128)(2,1)} %get-tuple-element.215), channel_id=1, source_target_pairs={{0,2},{1,3},{2,0},{3,1},{4,6},{5,7},{6,4},{7,5},{8,10},{9,11},{10,... | collective-permute-start | bytes 786440 | tf_op jit(solution)/shard_map/ppermute | solution.py:53
  402.1 30.0 %collective-permute-start.44 = (bf16[64,2048]{1,0:T(8,128)(2,1)}, bf16[64,2048]{1,0:T(8,128)(2,1)}, u32[]{:S(2)}, u32[]{:S(2)}) collective-permute-start(bf16[64,2048]{1,0:T(8,128)(2,1)} %get-tuple-element.213), channel_id=1, source_target_pairs={{0,1},{1,0},{2,3},{3,2},{4,5},{5,4},{6,7},{7,6},{8,9},{9,8},{10,11... | collective-permute-start | bytes 786440 | tf_op jit(solution)/shard_map/ppermute | solution.py:53
  428.6 20.3 %collective-permute-start.54 = (bf16[64,2048]{1,0:T(8,128)(2,1)S(1)}, bf16[64,2048]{1,0:T(8,128)(2,1)S(1)}, u32[]{:S(2)}, u32[]{:S(2)}) collective-permute-start(bf16[64,2048]{1,0:T(8,128)(2,1)S(1)} %get-tuple-element.218), channel_id=1, source_target_pairs={{0,2},{1,3},{2,0},{3,1},{4,6},{5,7},{6,4},{7,5},{8,10},{9,11},{10,... | collective-permute-start | bytes 786440 | tf_op jit(solution)/shard_map/ppermute | solution.py:53
  454.0 20.3 %collective-permute-start.48 = (bf16[64,2048]{1,0:T(8,128)(2,1)S(1)}, bf16[64,2048]{1,0:T(8,128)(2,1)S(1)}, u32[]{:S(2)}, u32[]{:S(2)}) collective-permute-start(bf16[64,2048]{1,0:T(8,128)(2,1)S(1)} %get-tuple-element.188), channel_id=1, source_target_pairs={{0,2},{1,3},{2,0},{3,1},{4,6},{5,7},{6,4},{7,5},{8,10},{9,11},{10,... | collective-permute-start | bytes 786440 | tf_op jit(solution)/shard_map/ppermute | solution.py:47
  478.8 20.9 %collective-permute-start.57 = (bf16[64,2048]{1,0:T(8,128)(2,1)S(1)}, bf16[64,2048]{1,0:T(8,128)(2,1)S(1)}, u32[]{:S(2)}, u32[]{:S(2)}) collective-permute-start(bf16[64,2048]{1,0:T(8,128)(2,1)S(1)} %get-tuple-element.185), channel_id=1, source_target_pairs={{0,2},{1,3},{2,0},{3,1},{4,6},{5,7},{6,4},{7,5},{8,10},{9,11},{10,... | collective-permute-start | bytes 786440 | tf_op jit(solution)/shard_map/ppermute | solution.py:47
  537.8 172.9 %reduce-scatter.5.cloned.1.call-start = ((), (), s32[]{:S(2)}) async-start(), calls=%async_computation.8 | async-start | bytes 7077888 | tf_op jit(solution)/shard_map/reduce_scatter | solution.py:630
  580.3 143.3 %reduce-scatter.11.cloned.1.call-start = ((), (), s32[]{:S(2)}) async-start(), calls=%async_computation.11 | async-start | bytes 9437184 | tf_op jit(solution)/shard_map/reduce_scatter | solution.py:630
  593.9 249.6 %reduce-scatter.9.cloned.1.call-start = ((), (), s32[]{:S(2)}) async-start(), calls=%async_computation.10 | async-start | bytes 18874368 | tf_op jit(solution)/shard_map/reduce_scatter | solution.py:630
  657.1 26.8 %collective-permute-start.81 = (bf16[64,2048]{1,0:T(8,128)(2,1)}, bf16[64,2048]{1,0:T(8,128)(2,1)}, u32[]{:S(2)}, u32[]{:S(2)}) collective-permute-start(bf16[64,2048]{1,0:T(8,128)(2,1)} %get-tuple-element.211), channel_id=1, source_target_pairs={{0,3},{1,2},{2,1},{3,0},{4,7},{5,6},{6,5},{7,4},{8,11},{9,10},{10,... | collective-permute-start | bytes 786440 | tf_op jit(solution)/shard_map/ppermute | solution.py:53
  659.1 36.3 %collective-permute-start.80 = (bf16[64,2048]{1,0:T(8,128)(2,1)}, bf16[64,2048]{1,0:T(8,128)(2,1)}, u32[]{:S(2)}, u32[]{:S(2)}) collective-permute-start(bf16[64,2048]{1,0:T(8,128)(2,1)} %get-tuple-element.212), channel_id=1, source_target_pairs={{0,2},{1,3},{2,0},{3,1},{4,6},{5,7},{6,4},{7,5},{8,10},{9,11},{10,... | collective-permute-start | bytes 786440 | tf_op jit(solution)/shard_map/ppermute | solution.py:53
  661.0 34.3 %collective-permute-start.79 = (bf16[64,2048]{1,0:T(8,128)(2,1)S(1)}, bf16[64,2048]{1,0:T(8,128)(2,1)}, u32[]{:S(2)}, u32[]{:S(2)}) collective-permute-start(bf16[64,2048]{1,0:T(8,128)(2,1)S(1)} %get-tuple-element.210), channel_id=1, source_target_pairs={{0,1},{1,0},{2,3},{3,2},{4,5},{5,4},{6,7},{7,6},{8,9},{9,8},{10,11... | collective-permute-start | bytes 786440 | tf_op jit(solution)/shard_map/ppermute | solution.py:53
  668.2 28.4 %collective-permute-start.78 = (bf16[64,2048]{1,0:T(8,128)(2,1)}, bf16[64,2048]{1,0:T(8,128)(2,1)}, u32[]{:S(2)}, u32[]{:S(2)}) collective-permute-start(bf16[64,2048]{1,0:T(8,128)(2,1)} %get-tuple-element.208), channel_id=1, source_target_pairs={{0,3},{1,2},{2,1},{3,0},{4,7},{5,6},{6,5},{7,4},{8,11},{9,10},{10,... | collective-permute-start | bytes 786440 | tf_op jit(solution)/shard_map/ppermute | solution.py:53
  670.2 36.2 %collective-permute-start.77 = (bf16[64,2048]{1,0:T(8,128)(2,1)}, bf16[64,2048]{1,0:T(8,128)(2,1)}, u32[]{:S(2)}, u32[]{:S(2)}) collective-permute-start(bf16[64,2048]{1,0:T(8,128)(2,1)} %get-tuple-element.209), channel_id=1, source_target_pairs={{0,2},{1,3},{2,0},{3,1},{4,6},{5,7},{6,4},{7,5},{8,10},{9,11},{10,... | collective-permute-start | bytes 786440 | tf_op jit(solution)/shard_map/ppermute | solution.py:53
  683.9 22.5 %collective-permute-start.76 = (bf16[64,2048]{1,0:T(8,128)(2,1)}, bf16[64,2048]{1,0:T(8,128)(2,1)S(1)}, u32[]{:S(2)}, u32[]{:S(2)}) collective-permute-start(bf16[64,2048]{1,0:T(8,128)(2,1)} %get-tuple-element.207), channel_id=1, source_target_pairs={{0,1},{1,0},{2,3},{3,2},{4,5},{5,4},{6,7},{7,6},{8,9},{9,8},{10,11... | collective-permute-start | bytes 786440 | tf_op jit(solution)/shard_map/ppermute | solution.py:53
  (144 other events, 1646.5 us)
Sparse Core Ops, SparseCore 0:
  10.5 48.2 all-gather.5
  60.6 28.2 all-gather.7
  91.4 107.0 all-gather.9
  200.2 57.7 all-gather.11
  537.9 44.4 reduce-scatter.6
  586.0 62.5 reduce-scatter.4
  652.1 71.4 reduce-scatter.10
  727.5 115.9 reduce-scatter.8

commit v2 on v1

--- a/solution.py
+++ b/solution.py
@@ -11,6 +11,7 @@
 
 epsilon = 1e-06
 theta = 500000.0
+tile = 256
 score_scale = HD ** (-0.5)
 hidden_score = -1e30
 low = jnp.bfloat16
@@ -54,16 +55,22 @@
     ]
 
 
-def gather_rows(values):
-    return jnp.concatenate(gather_slots(values, "head"), axis=0)
-
-
-def reduce_rows(partial_rows):
-    size = lax.axis_size("head")
-    rows = partial_rows.shape[0] // size
-    slots = [partial_rows[s * rows : (s + 1) * rows] for s in range(size)]
-    arrived = exchange_slots([slot.astype(low) for slot in slots], "head")
-    return sum(slot.astype(full) for slot in arrived)
+def gather_doubling(values, axis):
+    held = values[None]
+    step = 1
+    while step < lax.axis_size(axis):
+        arrived = lax.ppermute(held, axis, xor_pairs(lax.axis_size(axis), step))
+        held = jnp.concatenate([held, arrived], axis=0)
+        step *= 2
+    return held
+
+
+def sum_doubling(values, axis):
+    step = 1
+    while step < lax.axis_size(axis):
+        values = values + lax.ppermute(values, axis, xor_pairs(lax.axis_size(axis), step))
+        step *= 2
+    return values
 
 
 def sum_heads(values):
@@ -87,14 +94,15 @@
     )
 
 
-def whole(shape):
-    return pl.BlockSpec(shape, lambda: (0,) * len(shape))
+def shape_of(shape, dtype):
+    return jax.ShapeDtypeStruct(shape, dtype)
+
+
+def sizes_of(arrays):
+    return sum(a.size * a.dtype.itemsize for a in arrays)
 
 
 def call_whole(body, outs, *args, scalars=1, scratch=(), flops=0):
-    moved = sum(a.size * a.dtype.itemsize for a in args) + sum(
-        o.size * o.dtype.itemsize for o in outs
-    )
     return pl.pallas_call(
         body,
         out_shape=outs,
@@ -103,47 +111,534 @@
         out_specs=[pl.BlockSpec(memory_space=pltpu.VMEM)] * len(outs),
         scratch_shapes=list(scratch),
         compiler_params=pltpu.CompilerParams(vmem_limit_bytes=vmem_grant),
-        cost_estimate=pl.CostEstimate(flops=flops, bytes_accessed=moved, transcendentals=0),
+        cost_estimate=pl.CostEstimate(
+            flops=flops, bytes_accessed=sizes_of(args) + sizes_of(outs), transcendentals=0
+        ),
     )(*args)
 
 
-def shape_of(shape, dtype):
-    return jax.ShapeDtypeStruct(shape, dtype)
-
-
-def send_views(me, raw, scale, gains, tables, blocks, rows, heads_local):
-    micro_count = blocks // heads_local
+def call_grid(body, steps, outs, in_specs, out_specs, *args, scratch=(), flops=0):
+    return pl.pallas_call(
+        body,
+        grid=(steps,),
+        out_shape=outs,
+        in_specs=in_specs,
+        out_specs=out_specs,
+        scratch_shapes=list(scratch),
+        compiler_params=pltpu.CompilerParams(vmem_limit_bytes=vmem_grant),
+        cost_estimate=pl.CostEstimate(
+            flops=flops, bytes_accessed=sizes_of(args) + sizes_of(outs), transcendentals=0
+        ),
+    )(*args)
+
+
+def fixed(shape):
+    return pl.BlockSpec(shape, lambda i: (0,) * len(shape))
+
+
+scalar_spec = pl.BlockSpec(memory_space=pltpu.SMEM)
+
+
+def column_tile(rows, first=0):
+    return pl.BlockSpec((rows, tile), lambda i: (0, first + i))
+
+
+def put_slots(out_refs, values):
+    rows = out_refs[0].shape[0]
+    for s, ref in enumerate(out_refs):
+        ref[...] = values[s * rows : (s + 1) * rows].astype(ref.dtype)
+
+
+def sum_slots(refs):
+    return sum(ref[...].astype(full) for ref in refs)
+
+
+def ffn_forward(slots, weights):
+    n = len(slots)
+    local_rows, width = slots[0].shape
+    rows, hidden = n * local_rows, weights.shape[1] // 3
+    steps = hidden // tile
+
+    def body(*refs):
+        wg_ref, wu_ref, wd_ref = refs[n : n + 3]
+        rows_ref, gate_ref, up_ref, middle_ref = refs[n + 3 : n + 7]
+        out_refs, total = refs[n + 7 : 2 * n + 7], refs[2 * n + 7]
+        step = pl.program_id(0)
+
+        @pl.when(step == 0)
+        def _():
+            for s in range(n):
+                rows_ref[s * local_rows : (s + 1) * local_rows, :] = refs[s][...]
+
+        values = rows_ref[...]
+        gate = dot_plain(values, wg_ref[...])
+        up = dot_plain(values, wu_ref[...])
+        gate_ref[...] = gate.astype(low)
+        up_ref[...] = up.astype(low)
+        middle = (gate * jax.nn.sigmoid(gate) * up).astype(low)
+        middle_ref[...] = middle
+        term = dot_right_t(middle, wd_ref[...])
+
+        @pl.when(step == 0)
+        def _():
+            total[...] = term
+
+        @pl.when(step > 0)
+        def _():
+            total[...] += term
+
+        @pl.when(step == steps - 1)
+        def _():
+            put_slots(out_refs, total)
+
+    results = call_grid(
+        body,
+        steps,
+        [shape_of((rows, width), low)]
+        + [shape_of((rows, hidden), low)] * 3
+        + [shape_of((local_rows, width), low)] * n,
+        [fixed((local_rows, width))] * n + [column_tile(width, k * steps) for k in range(3)],
+        [fixed((rows, width))] + [column_tile(rows)] * 3 + [fixed((local_rows, width))] * n,
+        *slots,
+        weights,
+        weights,
+        weights,
+        scratch=[pltpu.VMEM((rows, width), full)],
+        flops=6 * rows * width * hidden,
+    )
+    return results[:4], results[4:]
+
+
+def ffn_backward(slots, gate, up, weights):
+    n = len(slots)
+    local_rows, width = slots[0].shape
+    rows, hidden = gate.shape
+    steps = hidden // tile
+
+    def body(*refs):
+        gate_ref, up_ref, wg_ref, wu_ref, wd_ref = refs[n : n + 5]
+        rows_ref, gg_ref, gu_ref = refs[n + 5 : n + 8]
+        out_refs, total = refs[n + 8 : 2 * n + 8], refs[2 * n + 8]
+        step = pl.program_id(0)
+
+        @pl.when(step == 0)
+        def _():
+            for s in range(n):
+                rows_ref[s * local_rows : (s + 1) * local_rows, :] = refs[s][...]
+
+        grad_middle = dot_plain(rows_ref[...], wd_ref[...])
+        gate_values = gate_ref[...].astype(full)
+        sigmoid = jax.nn.sigmoid(gate_values)
+        silu = gate_values * sigmoid
+        grad_up = (grad_middle * silu).astype(low)
+        grad_gate = (
+            grad_middle * up_ref[...].astype(full) * (sigmoid + silu * (1.0 - sigmoid))
+        ).astype(low)
+        gg_ref[...] = grad_gate
+        gu_ref[...] = grad_up
+        term = dot_right_t(grad_gate, wg_ref[...]) + dot_right_t(grad_up, wu_ref[...])
+
+        @pl.when(step == 0)
+        def _():
+            total[...] = term
+
+        @pl.when(step > 0)
+        def _():
+            total[...] += term
+
+        @pl.when(step == steps - 1)
+        def _():
+            put_slots(out_refs, total)
+
+    results = call_grid(
+        body,
+        steps,
+        [shape_of((rows, width), low)]
+        + [shape_of((rows, hidden), low)] * 2
+        + [shape_of((local_rows, width), low)] * n,
+        [fixed((local_rows, width))] * n
+        + [column_tile(rows)] * 2
+        + [column_tile(width, k * steps) for k in range(3)],
+        [fixed((rows, width))] + [column_tile(rows)] * 2 + [fixed((local_rows, width))] * n,
+        *slots,
+        gate,
+        up,
+        weights,
+        weights,
+        weights,
+        scratch=[pltpu.VMEM((rows, width), full)],
+        flops=6 * rows * width * hidden,
+    )
+    return results[:3], results[3:]
+
+
+def ffn_weight_terms(hidden_rows, grad_rows, grad_gates, grad_ups, middles):
+    n = len(hidden_rows)
+    rows, width = hidden_rows[0].shape
+    hidden = middles[0].shape[1]
+    steps = hidden // tile
+
+    def body(*refs):
+        hidden_refs, grad_refs = refs[:n], refs[n : 2 * n]
+        groups = [refs[(2 + k) * n : (3 + k) * n] for k in range(3)]
+        out_ref, hidden_t, grad_t = refs[5 * n :]
+        step = pl.program_id(0)
+
+        @pl.when(step == 0)
+        def _():
+            for m in range(n):
+                cut = slice(m * rows, (m + 1) * rows)
+                hidden_t[:, cut] = jnp.transpose(hidden_refs[m][...])
+                grad_t[:, cut] = jnp.transpose(grad_refs[m][...])
+
+        for k, left in enumerate((hidden_t, hidden_t, grad_t)):
+
+            @pl.when(step // steps == k)
+            def _():
+                right = jnp.concatenate([ref[...] for ref in groups[k]], axis=0)
+                out_ref[...] = dot_plain(left[...], right).astype(low)
+
+    def spec(k):
+        return pl.BlockSpec((rows, tile), lambda i: (0, jnp.clip(i - k * steps, 0, steps - 1)))
+
+    return call_grid(
+        body,
+        3 * steps,
+        [shape_of((width, 3 * hidden), low)],
+        [fixed((rows, width))] * (2 * n) + [spec(k) for k in range(3) for _ in range(n)],
+        [column_tile(width)],
+        *hidden_rows,
+        *grad_rows,
+        *grad_gates,
+        *grad_ups,
+        *middles,
+        scratch=[pltpu.VMEM((width, n * rows), low)] * 2,
+        flops=6 * n * rows * width * hidden,
+    )[0]
+
+
+def after_attention(arrived, tokens, gain):
+    n = len(arrived)
+
+    def body(*refs):
+        token_ref, gain_ref, hidden_ref, low_ref, hat_ref, scale_ref = refs[n:]
+        attn = sum_slots(refs[:n])
+        scale = rms_scale(attn)
+        hat = attn * scale
+        hidden = token_ref[...].astype(full) + hat * gain_ref[...]
+        hidden_ref[...] = hidden
+        low_ref[...] = hidden.astype(low)
+        hat_ref[...] = hat
+        scale_ref[...] = scale
+
+    shape = tokens.shape
+    return call_whole(
+        body,
+        [shape_of(shape, full), shape_of(shape, low), shape_of(shape, full), shape_of((shape[0], 1), full)],
+        *arrived,
+        tokens,
+        gain,
+        scalars=0,
+    )
+
+
+def after_ffn(arrived, hidden, cotangent, gain):
+    n = len(arrived)
+
+    def body(*refs):
+        hidden_ref, grad_ref, gain_ref, out_ref, low_ref, gain_grad_ref = refs[n:]
+        down = sum_slots(refs[:n])
+        scale = rms_scale(down)
+        hat = down * scale
+        out_ref[...] = (hidden_ref[...] + hat * gain_ref[...]).astype(low)
+        grad_out = grad_ref[...].astype(full)
+        gain_grad_ref[...] = jnp.sum(grad_out * hat, axis=0, keepdims=True)
+        grad = grad_out * gain_ref[...]
+        low_ref[...] = (scale * (grad - hat * jnp.mean(grad * hat, axis=1, keepdims=True))).astype(low)
+
+    shape = hidden.shape
+    return call_whole(
+        body,
+        [shape_of(shape, low), shape_of(shape, low), shape_of((1, shape[1]), full)],
+        *arrived,
+        hidden,
+        cotangent,
+        gain,
+        scalars=0,
+    )
+
+
+def before_attention(arrived, cotangent, hat, scale, gain):
+    n = len(arrived)
+
+    def body(*refs):
+        grad_ref, hat_ref, scale_ref, gain_ref, hidden_ref, low_ref, gain_grad_ref = refs[n:]
+        grad_hidden = sum_slots(refs[:n]) + grad_ref[...].astype(full)
+        hidden_ref[...] = grad_hidden
+        hat = hat_ref[...]
+        gain_grad_ref[...] = jnp.sum(grad_hidden * hat, axis=0, keepdims=True)
+        grad = grad_hidden * gain_ref[...]
+        low_ref[...] = (
+            scale_ref[...] * (grad - hat * jnp.mean(grad * hat, axis=1, keepdims=True))
+        ).astype(low)
+
+    shape = hat.shape
+    return call_whole(
+        body,
+        [shape_of(shape, full), shape_of(shape, low), shape_of((1, shape[1]), full)],
+        *arrived,
+        cotangent,
+        hat,
+        scale,
+        gain,
+        scalars=0,
+    )
+
+
+def project_qkv(token_slots, weights):
+    count = len(token_slots)
+    local_rows, width = token_slots[0].shape
+    rows, features = count * local_rows, weights.shape[1]
+    part = features // 3
+    steps = features // tile
+    part_steps = part // tile
+
+    def body(*refs):
+        weight_ref, rows_ref, raw_ref, square_ref, totals = refs[count:]
+        step = pl.program_id(0)
+
+        @pl.when(step == 0)
+        def _():
+            for s in range(count):
+                rows_ref[s * local_rows : (s + 1) * local_rows, :] = refs[s][...]
+            totals[...] = jnp.zeros_like(totals)
+
+        raw = dot_plain(rows_ref[...], weight_ref[...])
+        raw_ref[...] = raw
+        sums = jnp.sum(raw * raw, axis=1, keepdims=True)
+        for k in range(2):
+
+            @pl.when(step // part_steps == k)
+            def _():
+                totals[:, k : k + 1] += sums
+
+        @pl.when(step == steps - 1)
+        def _():
+            square_ref[...] = jnp.transpose(totals[...])[:2, :]
+
+    return call_grid(
+        body,
+        steps,
+        [shape_of((rows, width), low), shape_of((rows, features), full), shape_of((2, rows), full)],
+        [fixed((local_rows, width))] * count + [column_tile(width)],
+        [fixed((rows, width)), column_tile(rows), fixed((2, rows))],
+        *token_slots,
+        weights,
+        scratch=[pltpu.VMEM((rows, 128), full)],
+        flops=2 * rows * width * features,
+    )
+
+
+def project_output(mixed, weights_t, micro_count, head_size):
+    rows = mixed.shape[1]
+    width = weights_t.shape[0]
+    local_rows = rows // head_size
+
+    def body(mixed_ref, weight_ref, *out_refs):
+        for m in range(micro_count):
+            values = dot_right_t(mixed_ref[m], weight_ref[...])
+            put_slots(out_refs[m * head_size : (m + 1) * head_size], values)
+
+    return call_whole(
+        body,
+        [shape_of((local_rows, width), low)] * (micro_count * head_size),
+        mixed,
+        weights_t,
+        scalars=0,
+        flops=2 * micro_count * rows * width * weights_t.shape[1],
+    )
+
+
+def project_mixed_grad(grad_slots, weights_t):
+    count = len(grad_slots)
+    local_rows, width = grad_slots[0].shape
+    rows, features = count * local_rows, weights_t.shape[1]
+
+    def body(*refs):
+        weight_ref, rows_ref, out_ref = refs[count:]
+        for s in range(count):
+            rows_ref[s * local_rows : (s + 1) * local_rows, :] = refs[s][...]
+        out_ref[...] = dot_plain(rows_ref[...], weight_ref[...]).astype(low)
+
+    return call_whole(
+        body,
+        [shape_of((rows, width), low), shape_of((rows, features), low)],
+        *grad_slots,
+        weights_t,
+        scalars=0,
+        flops=2 * rows * width * features,
+    )
+
+
+def norm_gradients(raw, scales, gains, grads):
+    rows, features = grads.shape
+    width = features // 2
+
+    def body(raw_ref, scale_ref, gain_ref, grad_ref, dot_ref, gain_grad_ref, totals):
+        totals[...] = jnp.zeros_like(totals)
+        for k in range(2):
+            cut = slice(k * width, (k + 1) * width)
+            terms = grad_ref[:, cut] * (raw_ref[:, cut] * scale_ref[:, k : k + 1])
+            gain_grad_ref[:, cut] = jnp.sum(terms, axis=0, keepdims=True)
+            totals[:, k : k + 1] = jnp.sum(terms * gain_ref[:, cut], axis=1, keepdims=True)
+        dot_ref[...] = jnp.transpose(totals[...])[:2, :]
+
+    return call_whole(
+        body,
+        [shape_of((2, rows), full), shape_of((1, features), full)],
+        raw,
+        scales,
+        gains,
+        grads,
+        scalars=0,
+        scratch=[pltpu.VMEM((rows, 128), full)],
+    )
+
+
+def project_input_grad(raw, scales, dots, gains, grads, grad_value, weights, slot_count):
+    rows, features = grad_value.shape[0], weights.shape[1]
+    width = features // 3
+    out_width = weights.shape[0]
+    local_rows = rows // slot_count
+    steps = out_width // tile
+
+    def body(raw_ref, scale_ref, dot_ref, gain_ref, grad_ref, value_ref, weight_ref, low_ref, *out_refs):
+        @pl.when(pl.program_id(0) == 0)
+        def _():
+            for k in range(2):
+                cut = slice(k * width, (k + 1) * width)
+                scale = scale_ref[:, k : k + 1]
+                hat = raw_ref[:, cut] * scale
+                grad_hat = grad_ref[:, cut] * gain_ref[:, cut]
+                low_ref[:, cut] = (scale * (grad_hat - hat * dot_ref[:, k : k + 1])).astype(low)
+            low_ref[:, 2 * width :] = value_ref[...]
+
+        put_slots(out_refs, dot_right_t(low_ref[...], weight_ref[...]))
+
+    return call_grid(
+        body,
+        steps,
+        [shape_of((rows, features), low)] + [shape_of((local_rows, out_width), low)] * slot_count,
+        [
+            fixed((rows, 2 * width)),
+            fixed((rows, 2)),
+            fixed((rows, 2)),
+            fixed((1, 2 * width)),
+            fixed((rows, 2 * width)),
+            fixed((rows, width)),
+            pl.BlockSpec((tile, features), lambda i: (i, 0)),
+        ],
+        [fixed((rows, features))]
+        + [pl.BlockSpec((local_rows, tile), lambda i: (0, i))] * slot_count,
+        raw,
+        scales,
+        dots,
+        gains,
+        grads,
+        grad_value,
+        weights,
+        flops=2 * rows * features * out_width,
+    )
+
+
+def weight_term_slots(me, left, right, blocks):
+    rows, width = left.shape
+    features = right.shape[1]
+    part = width // blocks
+    half = blocks // 2
+
+    def body(me_ref, left_ref, right_ref, odd_ref, even_ref, left_t):
+        step = pl.program_id(0)
+
+        @pl.when(step == 0)
+        def _():
+            left_t[...] = jnp.transpose(left_ref[...])
+
+        slot = jnp.where(step < half, 2 * step + 1, 2 * step - blocks)
+        place = pl.multiple_of((me_ref[0] ^ slot) * part, part)
+        term = dot_plain(left_t[pl.ds(place, part), :], right_ref[...]).astype(low)
+
+        @pl.when(step < half)
+        def _():
+            odd_ref[0] = term
+
+        @pl.when(step >= half)
+        def _():
+            even_ref[0] = term
+
+    return call_grid(
+        body,
+        blocks,
+        [shape_of((half, part, features), low)] * 2,
+        [scalar_spec, fixed((rows, width)), fixed((rows, features))],
+        [
+            pl.BlockSpec((1, part, features), lambda i: (jnp.minimum(i, half - 1), 0, 0)),
+            pl.BlockSpec((1, part, features), lambda i: (jnp.maximum(i - half, 0), 0, 0)),
+        ],
+        me,
+        left,
+        right,
+        scratch=[pltpu.VMEM((width, rows), low)],
+        flops=2 * rows * width * features,
+    )
+
+
+def to_owner(me, left, right):
+    blocks = lax.axis_size("blk")
+    odd, even = weight_term_slots(me, left, right, blocks)
+    arrived = lax.ppermute(odd, "blk", xor_pairs(blocks, 1))
+    pairs = [
+        (even[k].astype(full) + arrived[k].astype(full)) for k in range(blocks // 2)
+    ]
+    return sum(
+        [pairs[0]]
+        + [
+            lax.ppermute(pairs[k].astype(low), "blk", xor_pairs(blocks, 2 * k)).astype(full)
+            for k in range(1, blocks // 2)
+        ]
+    )
+
+
+def send_views(me, raw, scales, gains, tables, heads_local):
+    micro_count, rows = raw.shape[:2]
+    blocks = micro_count * heads_local
     width = heads_local * HD
 
     def body(me_ref, *refs):
-        raw_refs = refs[:micro_count]
-        scale_ref, gain_ref, cos_ref, sin_ref = refs[micro_count : micro_count + 4]
-        out_refs = refs[micro_count + 4 :]
+        raw_ref, scale_ref, gain_ref, cos_ref, sin_ref = refs[:5]
+        out_refs = refs[5:]
         cosine, sine = cos_ref[...], sin_ref[...]
         for s in range(blocks):
             target = me_ref[0] ^ s
             column = pl.multiple_of((target % heads_local) * HD, HD)
 
-            def piece(micro):
-                for part in range(2):
-                    values = raw_refs[micro][:, pl.ds(part * width + column, HD)]
-                    factor = scale_ref[:, 2 * micro + part : 2 * micro + part + 1]
-                    values = values * factor * gain_ref[part : part + 1, pl.ds(column, HD)]
-                    turned = values * cosine + pltpu.roll(values, HD // 2, 1) * sine
-                    out_refs[s][:, part * HD : (part + 1) * HD] = turned.astype(low)
-                out_refs[s][:, 2 * HD :] = raw_refs[micro][
-                    :, pl.ds(2 * width + column, HD)
-                ].astype(low)
-
-            for micro in range(micro_count):
-                pl.when(target // heads_local == micro)(functools.partial(piece, micro))
+            micro = target // heads_local
+            for part in range(2):
+                feature = pl.multiple_of(part * width + column, HD)
+                values = raw_ref[micro, :, pl.ds(feature, HD)]
+                values = values * scale_ref[micro, :, part : part + 1]
+                values = values * gain_ref[:, pl.ds(feature, HD)]
+                turned = values * cosine + pltpu.roll(values, HD // 2, 1) * sine
+                out_refs[s][:, part * HD : (part + 1) * HD] = turned.astype(low)
+            feature = pl.multiple_of(2 * width + column, HD)
+            out_refs[s][:, 2 * HD :] = raw_ref[micro, :, pl.ds(feature, HD)].astype(low)
 
     return call_whole(
         body,
         [shape_of((rows, 3 * HD), low)] * blocks,
         me,
-        *raw,
-        scale,
+        raw,
+        scales,
         gains,
         *tables,
     )
@@ -416,16 +911,18 @@
 
 
 class GatheredAttention:
-    def __init__(self, raw, scales, gains, tables, codes, blocks, rows, positions):
+    def __init__(self, raw, scales, gains, tables, codes, positions):
+        blocks, rows = positions.shape
         self.tables, self.rows = tables, rows
-        width = gains.shape[1]
+        width = gains.shape[1] // 2
         shape = (rows, width // HD, HD)
         self.sets = []
-        for m, values in enumerate(raw):
+        for m in range(raw.shape[0]):
+            values = raw[m]
             views = []
             for part in range(2):
                 cut = values[:, part * width : (part + 1) * width]
-                normed = cut * scales[:, 2 * m + part : 2 * m + part + 1] * gains[part]
+                normed = cut * scales[m, :, part : part + 1] * gains[:, part * width : (part + 1) * width]
                 views.append(turn(normed.reshape(shape), tables).astype(low))
             value_view = values[:, 2 * width :].astype(low).reshape(shape)
             seg_all = (codes[m] // 2).reshape(blocks, rows)
@@ -466,14 +963,14 @@
 
 
 class ExchangedAttention:
-    def __init__(self, raw, scales, gains, tables, codes, blocks, rows, positions):
-        self.blocks, self.tables = blocks, tables
-        self.heads = gains.shape[1] // HD
-        self.micro_count = len(raw)
+    def __init__(self, raw, scales, gains, tables, codes, positions):
+        self.blocks, self.tables = positions.shape[0], tables
+        self.heads = gains.shape[1] // (2 * HD)
+        self.micro_count = raw.shape[0]
         place = lax.axis_index("blk")
         self.me = place.astype(jnp.int32).reshape(1)
         self.slots = exchange_slots(
-            send_views(self.me, raw, scales, gains, tables, blocks, rows, self.heads), "blk"
+            send_views(self.me, raw, scales, gains, tables, self.heads), "blk"
         )
         codes = lax.dynamic_index_in_dim(codes, place // self.heads, 0, keepdims=False)
         seg_all = codes // 2
@@ -528,160 +1025,98 @@
     micros = range(micro_count)
     block_index = lax.axis_index("blk")
     head_index = lax.axis_index("head")
+    me = block_index.astype(jnp.int32).reshape(1)
     slot_owner = head_index ^ jnp.arange(head_size, dtype=jnp.int32)
     group_order = (
         slot_owner[:, None] * local_rows + jnp.arange(local_rows, dtype=jnp.int32)[None, :]
     ).reshape(group_rows)
     tables = rotary_tables(block_index * group_rows + group_order)
 
-    qkv_full = lax.all_gather(
-        jnp.concatenate([query_weight, key_weight, value_weight], axis=1), "blk", axis=0, tiled=True
-    )
-    output_full_t = lax.all_gather(output_weight.T, "blk", axis=0, tiled=True)
-    gate_up_full = lax.all_gather(
-        jnp.concatenate([gate_weight, up_weight], axis=1), "blk", axis=0, tiled=True
-    )
-    down_full_t = lax.all_gather(down_weight.T, "blk", axis=0, tiled=True)
-
-    codes = lax.all_gather(segments * 2 + padding, ("blk", "head"), axis=1, tiled=True)
-    token_rows = [gather_rows(tokens[m]) for m in micros]
-    raw = [dot_plain(token_rows[m], qkv_full) for m in micros]
-    squares = jnp.stack(
-        [
-            jnp.sum(jnp.square(raw[m][:, part * width : (part + 1) * width]), axis=1)
-            for m in micros
-            for part in range(2)
-        ]
-    )
-    scale_rows = lax.rsqrt(sum_heads(squares) / model_width + epsilon)
-    scales = scale_rows.T
-    gains_qk = jnp.stack([query_gain, key_gain])
-
-    codes = codes.reshape(micro_count, blocks, head_size, local_rows)[:, :, slot_owner, :]
+    def gather_weights(*parts):
+        return lax.all_gather(jnp.concatenate(parts, axis=1), "blk", axis=0, tiled=True)
+
+    qkv_full = gather_weights(query_weight, key_weight, value_weight)
+    output_full_t = gather_weights(output_weight.T)
+    ffn_full = gather_weights(gate_weight, up_weight, down_weight.T)
+
+    codes = jnp.concatenate(gather_slots(segments * 2 + padding, "head"), axis=1)
+    codes = gather_doubling(codes, "blk")
+    codes = codes[block_index ^ jnp.arange(blocks, dtype=jnp.int32)].swapaxes(0, 1)
+
+    token_slots = [slot for m in micros for slot in gather_slots(tokens[m], "head")]
+    token_rows, raw, squares = project_qkv(token_slots, qkv_full)
+
+    def by_micro(values):
+        return values.reshape(micro_count, group_rows, -1)
+
+    def sum_token_heads(values):
+        values = values.reshape(2 * micro_count, group_rows)
+        return sum_heads(values).reshape(2, micro_count * group_rows).T
+
+    scales = lax.rsqrt(sum_token_heads(squares) / model_width + epsilon)
+    gain_row = jnp.concatenate([query_gain, key_gain])[None, :]
     positions = jnp.arange(blocks, dtype=jnp.int32)[:, None] * group_rows + group_order[None, :]
     exchanged = blocks == micro_count * heads_local and blocks & (blocks - 1) == 0
     attention = (ExchangedAttention if exchanged else GatheredAttention)(
-        raw,
-        scales,
-        gains_qk,
-        tables,
-        codes.reshape(micro_count, -1),
-        blocks,
-        group_rows,
-        positions,
+        by_micro(raw), by_micro(scales), gain_row, tables, codes.reshape(micro_count, -1), positions
     )
     mixed = attention.forward()
 
-    outputs, hidden_rows_all, middle_all, grad_down_all, grad_gu_all = [], [], [], [], []
-    grad_hidden_all, grad_attn_all = [], []
-    attn_gain_grad = jnp.zeros((model_width,), full)
-    ffn_gain_grad = jnp.zeros((model_width,), full)
+    attn_slots = project_output(mixed, output_full_t, micro_count, head_size)
+    attn_gain, ffn_gain = attn_gain[None, :], ffn_gain[None, :]
+    outputs, kept = [], []
+    grad_hiddens, grad_attn_slots = [], []
+    gain_grads = []
     for m in micros:
-        attn_rows = reduce_rows(dot_right_t(mixed[m], output_full_t))
-        attn_scale = rms_scale(attn_rows)
-        attn_hat = attn_rows * attn_scale
-        hidden = tokens[m].astype(full) + attn_hat * attn_gain
-        hidden_rows = gather_rows(hidden.astype(low))
-        gate_up = dot_plain(hidden_rows, gate_up_full)
-        gate_values, up_values = gate_up[:, :hidden_width], gate_up[:, hidden_width:]
-        sigmoid_gate = jax.nn.sigmoid(gate_values)
-        silu_gate = gate_values * sigmoid_gate
-        middle = (silu_gate * up_values).astype(low)
-        down_rows = reduce_rows(dot_right_t(middle, down_full_t))
-        down_scale = rms_scale(down_rows)
-        down_hat = down_rows * down_scale
-        outputs.append((hidden + down_hat * ffn_gain).astype(low))
-        grad_out = cotangent[m].astype(full)
-        ffn_gain_grad = ffn_gain_grad + jnp.sum(grad_out * down_hat, axis=0)
-        grad_norm = grad_out * ffn_gain
-        grad_down = (
-            down_scale
-            * (grad_norm - down_hat * jnp.mean(grad_norm * down_hat, axis=1, keepdims=True))
-        ).astype(low)
-        grad_down_rows = gather_rows(grad_down)
-        grad_middle = dot_plain(grad_down_rows, down_full_t)
-        grad_gu = jnp.concatenate(
-            [
-                (
-                    grad_middle * up_values * sigmoid_gate * (1.0 + gate_values * (1.0 - sigmoid_gate))
-                ).astype(low),
-                (grad_middle * silu_gate).astype(low),
-            ],
-            axis=1,
-        )
-        grad_hidden = reduce_rows(dot_right_t(grad_gu, gate_up_full)) + grad_out
-        attn_gain_grad = attn_gain_grad + jnp.sum(grad_hidden * attn_hat, axis=0)
-        grad_norm = grad_hidden * attn_gain
-        grad_attn = (
-            attn_scale
-            * (grad_norm - attn_hat * jnp.mean(grad_norm * attn_hat, axis=1, keepdims=True))
-        ).astype(low)
-        hidden_rows_all.append(hidden_rows)
-        middle_all.append(middle)
-        grad_down_all.append(grad_down_rows)
-        grad_gu_all.append(grad_gu)
-        grad_hidden_all.append(grad_hidden)
-        grad_attn_all.append(gather_rows(grad_attn))
-
-    def joined(pieces):
-        return jnp.concatenate(pieces, axis=0)
-
-    def to_owner(values):
-        return lax.psum_scatter(
-            values.astype(low), "blk", scatter_dimension=0, tiled=True
-        ).astype(full)
-
-    grad_down_both = joined(grad_down_all)
-    grad_attn_both = joined(grad_attn_all)
-    down_grad = to_owner(dot_left_t(grad_down_both, joined(middle_all))).T
-    gate_up_grad = to_owner(dot_left_t(joined(hidden_rows_all), joined(grad_gu_all)))
-
-    grad_mixed = dot_plain(grad_attn_both, output_full_t).astype(low)
-    output_grad = to_owner(
-        dot_left_t(grad_attn_both, mixed.reshape(micro_count * group_rows, width))
-    ).T
-    grad_qk_norm, grad_value = attention.backward(
-        grad_mixed.reshape(micro_count, group_rows, width)
-    )
-
-    gain_row = jnp.concatenate([query_gain, key_gain])
-    hats, grad_hats, dots = [], [], []
-    qk_gain_grad = jnp.zeros((2 * width,), full)
-    for m in micros:
-        scale_cols = jnp.concatenate(
-            [
-                jnp.broadcast_to(scales[:, 2 * m + part : 2 * m + part + 1], (group_rows, width))
-                for part in range(2)
-            ],
-            axis=1,
-        )
-        hat = raw[m][:, : 2 * width] * scale_cols
-        grad_hat = grad_qk_norm[m] * gain_row
-        qk_gain_grad = qk_gain_grad + jnp.sum(grad_qk_norm[m] * hat, axis=0)
-        for part in range(2):
-            cut = slice(part * width, (part + 1) * width)
-            dots.append(jnp.sum(grad_hat[:, cut] * hat[:, cut], axis=1))
-        hats.append((hat, scale_cols))
-        grad_hats.append(grad_hat)
-    mean_dots = (sum_heads(jnp.stack(dots)) / model_width).T
-    input_grads, grad_qkv_all = [], []
-    for m in micros:
-        hat, scale_cols = hats[m]
-        dot_cols = jnp.concatenate(
-            [
-                jnp.broadcast_to(mean_dots[:, 2 * m + part : 2 * m + part + 1], (group_rows, width))
-                for part in range(2)
-            ],
-            axis=1,
-        )
-        grad_raw = (scale_cols * (grad_hats[m] - hat * dot_cols)).astype(low)
-        grad_qkv = jnp.concatenate([grad_raw, grad_value[m]], axis=1)
-        grad_qkv_all.append(grad_qkv)
-        input_grads.append(reduce_rows(dot_right_t(grad_qkv, qkv_full)) + grad_hidden_all[m])
-    qkv_grad = to_owner(dot_left_t(joined(token_rows), joined(grad_qkv_all)))
-
-    ffn_gain_grad, attn_gain_grad = lax.psum((ffn_gain_grad, attn_gain_grad), ("blk", "head"))
-    qk_gain_grad = lax.psum(qk_gain_grad, "blk")
+        arrived = exchange_slots(attn_slots[m * head_size : (m + 1) * head_size], "head")
+        hidden, hidden_low, attn_hat, attn_scale = after_attention(arrived, tokens[m], attn_gain)
+        (hidden_rows, gate, up, middle), slots = ffn_forward(
+            gather_slots(hidden_low, "head"), ffn_full
+        )
+        output, grad_down, ffn_gain_grad = after_ffn(
+            exchange_slots(slots, "head"), hidden, cotangent[m], ffn_gain
+        )
+        outputs.append(output)
+        (grad_rows, grad_gate, grad_up), slots = ffn_backward(
+            gather_slots(grad_down, "head"), gate, up, ffn_full
+        )
+        kept.append((hidden_rows, grad_rows, grad_gate, grad_up, middle))
+        grad_hidden, grad_attn, attn_gain_grad = before_attention(
+            exchange_slots(slots, "head"), cotangent[m], attn_hat, attn_scale, attn_gain
+        )
+        grad_hiddens.append(grad_hidden)
+        grad_attn_slots += gather_slots(grad_attn, "head")
+        gain_grads.append(jnp.concatenate([attn_gain_grad, ffn_gain_grad], axis=1))
+
+    ffn_terms = ffn_weight_terms(*zip(*kept))
+    ffn_grad = lax.psum_scatter(ffn_terms, "blk", scatter_dimension=0, tiled=True).astype(full)
+    gate_grad, up_grad, down_grad_t = jnp.split(ffn_grad, 3, axis=1)
+
+    grad_attn_rows, grad_mixed = project_mixed_grad(grad_attn_slots, output_full_t)
+    output_grad = to_owner(me, grad_attn_rows, mixed.reshape(-1, width)).T
+    grad_norm, grad_value = attention.backward(by_micro(grad_mixed))
+    grad_norm = grad_norm.reshape(-1, 2 * width)
+    grad_value = grad_value.reshape(-1, width)
+    dots, qk_gain_grad = norm_gradients(raw, scales, gain_row, grad_norm)
+    mean_dots = sum_token_heads(dots) / model_width
+    results = project_input_grad(
+        raw, scales, mean_dots, gain_row, grad_norm, grad_value, qkv_full, micro_count * head_size
+    )
+    qkv_grad = to_owner(me, token_rows, results[0])
+    input_grads = [
+        sum(
+            slot.astype(full)
+            for slot in exchange_slots(
+                results[1 + m * head_size : 1 + (m + 1) * head_size], "head"
+            )
+        )
+        + grad_hiddens[m]
+        for m in micros
+    ]
+
+    rows_grad = sum_doubling(jnp.concatenate([sum(gain_grads), qk_gain_grad], axis=1)[0], "blk")
+    qk_gain_grad = rows_grad[2 * model_width :]
+    rows_grad = sum_doubling(rows_grad[: 2 * model_width], "head")
     return (
         jnp.stack(outputs),
         jnp.stack(input_grads),
@@ -691,11 +1126,11 @@
         output_grad,
         qk_gain_grad[:width],
         qk_gain_grad[width:],
-        attn_gain_grad,
-        gate_up_grad[:, :hidden_width],
-        gate_up_grad[:, hidden_width:],
-        down_grad,
-        ffn_gain_grad,
+        rows_grad[:model_width],
+        gate_grad,
+        up_grad,
+        down_grad_t.T,
+        rows_grad[model_width:],
     )
 
 

time: 861 us -> 739 us (0.86)
  Pallas kernels: 33 us -> 203 us
  blocking collectives: 146 us -> 0 us
  matrix products: 124 us -> 0 us
  waiting for transfers between devices: 338 us -> 242 us
  starting transfers between devices: 126 us -> 218 us
    pallas_call x0 -> x9, Pallas kernels: none -> 141 us  [call_grid(): pl.pallas_call(body, grid=(steps,), out_shape=outs, in_specs=in_specs, ou...]
    reduce_scatter x4 -> x1, waiting for transfers between devices: 127 us -> 0.01 us  [on_device(): lax.psum_scatter(ffn_terms, 'blk', scatter_dimension=0, tiled=True)]
    dot_general x19 -> x0, matrix products: 124 us -> none  [the longest x8 45 us: dot_right_t(): lax.dot_general(left_side, right_side, (((1,), (1,)), ((), ())), preferre...]
    all_gather x1 -> x0, blocking collectives: 95.9 us -> none  [on_device(): lax.all_gather(segments * 2 + padding, ('blk', 'head'), axis=1, tiled=True)]
    ppermute x30 -> x33, starting transfers between devices: 59.8 us -> 126 us  [gather_slots(): lax.ppermute(values, axis, xor_pairs(size, s))]
    psum x2 -> x0, blocking collectives: 49.9 us -> none  [the longest x1 37.8 us: on_device(): lax.psum((ffn_gain_grad, attn_gain_grad), ('blk', 'head'))]
    ppermute x0 -> x16, waiting for transfers between devices: none -> 41.8 us  [the longest x6 29.2 us: to_owner(): lax.ppermute(pairs[k].astype(low), 'blk', xor_pairs(blocks, 2 * k))]
    pallas_call x6 -> x15, Pallas kernels: 33 us -> 61.7 us  [call_whole(): pl.pallas_call(body, out_shape=outs, in_specs=[pl.BlockSpec(memory_space=...]
  transfers between devices with their start and end apart: 90 -> 105, of which waited for: 40 -> 46; matrix products, arithmetic and copies ran while one was open for 20% -> 4% of each run, Pallas kernels for 2% -> 21%
where the time goes in v2:
time: 739 us; the launch traced here: 734 us
  waiting for transfers between devices  242 us (33%)
  starting transfers between devices  218 us (29%)
  Pallas kernels  203 us (27%)
  local copies, waits for them, and re-layouts  33.3 us (5%)
  other arithmetic  23.1 us (3%)
  between operations  15 us (2%)
    pallas_call x9, Pallas kernels, call_grid(): pl.pallas_call(body, grid=(steps,), out_shape=outs, in_specs=in_specs, ou...  141 us
    ppermute x52, waiting for transfers between devices, exchange_slots(): lax.ppermute(slots[s], axis, xor_pairs(size, s))  137 us
    ppermute x33, starting transfers between devices, gather_slots(): lax.ppermute(values, axis, xor_pairs(size, s))  126 us
    ppermute x52, starting transfers between devices, exchange_slots(): lax.ppermute(slots[s], axis, xor_pairs(size, s))  75.1 us
    pallas_call x15, Pallas kernels, call_whole(): pl.pallas_call(body, out_shape=outs, in_specs=[pl.BlockSpec(memory_space=...  61.7 us
    ppermute x33, waiting for transfers between devices, gather_slots(): lax.ppermute(values, axis, xor_pairs(size, s))  60.5 us
    ppermute x6, waiting for transfers between devices, to_owner(): lax.ppermute(pairs[k].astype(low), 'blk', xor_pairs(blocks, 2 * k))  29.2 us
    unnamed x220, local copies, waits for them, and re-layouts  22.3 us
  transfers between devices with their start and end apart: 105, of which 46 were waited for; matrix products, arithmetic and copies ran while one was open for 4% of the time, Pallas kernels for 21%

profile of v2, /device:TPU:0, one launch (start us, length us, event | category | flops | bytes accessed | tf_op | source)
XLA Modules:
  0.0 734.1 jit_solution(17903615029311536554)
XLA Ops:
  25.9 6.4 collective-permute-done.18
  48.4 13.3 %collective-permute-done.4.refs_6_ = bf16[64,2048]{1,0:T(8,128)(2,1)S(1)} collective-permute-done((bf16[64,2048]{1,0:T(8,128)(2,1)S(1)}, bf16[64,2048]{1,0:T(8,128)(2,1)S(1)}, u32[]{:S(2)}, u32[]{:S(2)}) %collective-permute-start.4) | collective-permute-done | bytes 262176 | tf_op jit(solution)/shard_map/ppermute | solution.py:48
  62.5 10.2 %shard_map.246 = (bf16[512,2048]{1,0:T(8,128)(2,1)}, f32[512,1536]{1,0:T(8,128)}, f32[2,512]{1,0:T(2,128)}) custom-call(bf16[64,2048]{1,0:T(8,128)(2,1)} %copy-done.5, bf16[64,2048]{1,0:T(8,128)(2,1)} %copy-done.78, bf16[64,2048]{1,0:T(8,128)(2,1)} %copy-done.79, bf16[64,2048]{1,0:T(8,128)(2,1)} %copy-done.82, bf16[64,2048]{1,0:T(8,128)(2,1)} %copy-done.6, ...), custom_call_target="tpu_custom_call" | custom-call | flops 3221225472 | bytes 13635584 | tf_op jit(solution)/shard_map/pallas_call | solution.py:121
  76.9 3.7 collective-permute-start.6
  86.0 4.9 shard_map.247
  102.7 11.6 %collective-permute-done.13.refs_5_ = bf16[256,384]{1,0:T(8,128)(2,1)S(1)} collective-permute-done((bf16[256,384]{1,0:T(8,128)(2,1)}, bf16[256,384]{1,0:T(8,128)(2,1)S(1)}, u32[]{:S(2)}, u32[]{:S(2)}) %collective-permute-start.13) | collective-permute-done | bytes 196640 | tf_op jit(solution)/shard_map/ppermute | solution.py:54
  114.3 4.8 collective-permute-done.15.refs_7_
  119.9 8.9 %shard_map.248 = (bf16[256,128]{1,0:T(8,128)(2,1)}, bf16[256,128]{1,0:T(8,128)(2,1)}, bf16[256,128]{1,0:T(8,128)(2,1)}, bf16[256,128]{1,0:T(8,128)(2,1)}, bf16[2...) custom-call(s32[1]{0:T(128)} %bitcast.me_ref, ...), custom_call_target="tpu_custom_call" | custom-call | flops 1073741824 | bytes 3186692 | tf_op jit(solution)/shard_map/pallas_call | solution.py:106
  146.7 4.0 shard_map.250
  150.9 4.2 collective-permute-start.40
  155.6 6.9 collective-permute-done.38.refs_1_
  164.9 7.3 collective-permute-done.39.refs_2_
  176.0 17.3 %collective-permute-start.41 = (bf16[64,2048]{1,0:T(8,128)(2,1)}, bf16[64,2048]{1,0:T(8,128)(2,1)S(1)}, u32[]{:S(2)}, u32[]{:S(2)}) collective-permute-start(bf16[64,2048]{1,0:T(8,128)(2,1)} %get-tuple-element.160.refs_0_), channel_id=1, source_target_pairs={{0,1},{1,0},{2,3},{3,2},{4,5},{5,4},{6,7},{7,6},{8,9},{9,8},{10,11... | collective-permute-start | bytes 786440 | tf_op jit(solution)/shard_map/ppermute | solution.py:48
  199.1 14.3 %collective-permute-start.32 = (bf16[64,2048]{1,0:T(8,128)(2,1)}, bf16[64,2048]{1,0:T(8,128)(2,1)S(1)}, u32[]{:S(2)}, u32[]{:S(2)}) collective-permute-start(bf16[64,2048]{1,0:T(8,128)(2,1)} %get-tuple-element.149.refs_0_), channel_id=1, source_target_pairs={{0,1},{1,0},{2,3},{3,2},{4,5},{5,4},{6,7},{7,6},{8,9},{9,8},{10,11... | collective-permute-start | bytes 786440 | tf_op jit(solution)/shard_map/ppermute | solution.py:48
  215.8 12.6 %collective-permute-done.42.refs_2_ = bf16[64,2048]{1,0:T(8,128)(2,1)S(1)} collective-permute-done((bf16[64,2048]{1,0:T(8,128)(2,1)}, bf16[64,2048]{1,0:T(8,128)(2,1)S(1)}, u32[]{:S(2)}, u32[]{:S(2)}) %collective-permute-start.42) | collective-permute-done | bytes 262176 | tf_op jit(solution)/shard_map/ppermute | solution.py:48
  230.5 17.0 %shard_map.255 = (bf16[256,2048]{1,0:T(8,128)(2,1)}, bf16[256,2048]{1,0:T(8,128)(2,1)}, bf16[256,2048]{1,0:T(8,128)(2,1)}, bf16[256,2048]{1,0:T(8,128)(2,1)}, bf...) custom-call(bf16[64,2048]{1,0:T(8,128)(2,1)} %get-tuple-element.160.refs, ...), custom_call_target="tpu_custom_call" | custom-call | flops 6442450944 | bytes 81788928 | tf_op jit(solution)/shard_map/pallas_call | solution.py:121
  247.5 4.9 collective-permute-start.44
  256.3 17.0 %shard_map.252 = (bf16[256,2048]{1,0:T(8,128)(2,1)}, bf16[256,2048]{1,0:T(8,128)(2,1)}, bf16[256,2048]{1,0:T(8,128)(2,1)}, bf16[256,2048]{1,0:T(8,128)(2,1)}, bf...) custom-call(bf16[64,2048]{1,0:T(8,128)(2,1)} %get-tuple-element.149.refs, ...), custom_call_target="tpu_custom_call" | custom-call | flops 6442450944 | bytes 81788928 | tf_op jit(solution)/shard_map/pallas_call | solution.py:121
  287.3 9.5 %collective-permute-done.36.refs_2_ = bf16[64,2048]{1,0:T(8,128)(2,1)S(1)} collective-permute-done((bf16[64,2048]{1,0:T(8,128)(2,1)}, bf16[64,2048]{1,0:T(8,128)(2,1)S(1)}, u32[]{:S(2)}, u32[]{:S(2)}) %collective-permute-start.36) | collective-permute-done | bytes 262176 | tf_op jit(solution)/shard_map/ppermute | solution.py:54
  300.3 16.3 %collective-permute-start.47 = (bf16[64,2048]{1,0:T(8,128)(2,1)}, bf16[64,2048]{1,0:T(8,128)(2,1)S(1)}, u32[]{:S(2)}, u32[]{:S(2)}) collective-permute-start(bf16[64,2048]{1,0:T(8,128)(2,1)} %get-tuple-element.167.refs_0_), channel_id=1, source_target_pairs={{0,1},{1,0},{2,3},{3,2},{4,5},{5,4},{6,7},{7,6},{8,9},{9,8},{10,11... | collective-permute-start | bytes 786440 | tf_op jit(solution)/shard_map/ppermute | solution.py:48
  321.7 19.6 %shard_map.259 = (bf16[256,2048]{1,0:T(8,128)(2,1)}, bf16[256,2048]{1,0:T(8,128)(2,1)}, bf16[256,2048]{1,0:T(8,128)(2,1)}, bf16[64,2048]{1,0:T(8,128)(2,1)}, bf1...) custom-call(bf16[64,2048]{1,0:T(8,128)(2,1)} %get-tuple-element.177.refs_0_, ...), custom_call_target="tpu_custom_call" | custom-call | flops 6442450944 | bytes 82837504 | tf_op jit(solution)/shard_map/pallas_call | solution.py:121
  342.2 19.6 %shard_map.257 = (bf16[256,2048]{1,0:T(8,128)(2,1)}, bf16[256,2048]{1,0:T(8,128)(2,1)}, bf16[256,2048]{1,0:T(8,128)(2,1)}, bf16[64,2048]{1,0:T(8,128)(2,1)}, bf1...) custom-call(bf16[64,2048]{1,0:T(8,128)(2,1)} %get-tuple-element.167.refs_0_, ...), custom_call_target="tpu_custom_call" | custom-call | flops 6442450944 | bytes 82837504 | tf_op jit(solution)/shard_map/pallas_call | solution.py:121
  361.9 29.3 %shard_map.269 = bf16[2048,6144]{1,0:T(8,128)(2,1)} custom-call(bf16[256,2048]{1,0:T(8,128)(2,1)} %get-tuple-element.231.refs_0_, bf16[256,2048]{1,0:T(8,128)(2,1)} %get-tuple-element.232.refs_1_, bf16[256,2048]{1,0:T(8,128)(2,1)} %get-tuple-element.233.refs_2_, bf16[256,2048]{1,0:T(8,128)(2,1)} %get-tuple-element.234.refs_3_, ...), custom_call_target="tpu_custom_call" | custom-call | flops 12884901888 | bytes 35651584 | tf_op jit(solution)/shard_map/pallas_call | solution.py:121
  392.2 14.7 %collective-permute-start.50 = (bf16[64,2048]{1,0:T(8,128)(2,1)S(1)}, bf16[64,2048]{1,0:T(8,128)(2,1)S(1)}, u32[]{:S(2)}, u32[]{:S(2)}) collective-permute-start(bf16[64,2048]{1,0:T(8,128)(2,1)S(1)} %copy-done.92), channel_id=1, source_target_pairs={{0,1},{1,0},{2,3},{3,2},{4,5},{5,4},{6,7},{7,6},{8,9},{9,8},{10,11... | collective-permute-start | bytes 786440 | tf_op jit(solution)/shard_map/ppermute | solution.py:54
  411.8 10.4 %collective-permute-done.50.refs_1_ = bf16[64,2048]{1,0:T(8,128)(2,1)S(1)} collective-permute-done((bf16[64,2048]{1,0:T(8,128)(2,1)S(1)}, bf16[64,2048]{1,0:T(8,128)(2,1)S(1)}, u32[]{:S(2)}, u32[]{:S(2)}) %collective-permute-start.50) | collective-permute-done | bytes 262176 | tf_op jit(solution)/shard_map/ppermute | solution.py:54
  422.2 6.1 collective-permute-done.51.refs_2_
  432.1 13.9 %collective-permute-start.53 = (bf16[64,2048]{1,0:T(8,128)(2,1)}, bf16[64,2048]{1,0:T(8,128)(2,1)S(1)}, u32[]{:S(2)}, u32[]{:S(2)}) collective-permute-start(bf16[64,2048]{1,0:T(8,128)(2,1)} %get-tuple-element.176.refs_0_), channel_id=1, source_target_pairs={{0,1},{1,0},{2,3},{3,2},{4,5},{5,4},{6,7},{7,6},{8,9},{9,8},{10,11... | collective-permute-start | bytes 786440 | tf_op jit(solution)/shard_map/ppermute | solution.py:48
  452.8 15.3 %collective-permute-start.62 = (bf16[64,2048]{1,0:T(8,128)(2,1)}, bf16[64,2048]{1,0:T(8,128)(2,1)S(1)}, u32[]{:S(2)}, u32[]{:S(2)}) collective-permute-start(bf16[64,2048]{1,0:T(8,128)(2,1)} %get-tuple-element.186.refs_4_), channel_id=1, source_target_pairs={{0,1},{1,0},{2,3},{3,2},{4,5},{5,4},{6,7},{7,6},{8,9},{9,8},{10,11... | collective-permute-start | bytes 786440 | tf_op jit(solution)/shard_map/ppermute | solution.py:48
  471.5 4.6 collective-permute-done.62.refs_5_
  476.1 15.9 %collective-permute-done.63.refs_6_ = bf16[64,2048]{1,0:T(8,128)(2,1)S(1)} collective-permute-done((bf16[64,2048]{1,0:T(8,128)(2,1)}, bf16[64,2048]{1,0:T(8,128)(2,1)S(1)}, u32[]{:S(2)}, u32[]{:S(2)}) %collective-permute-start.63) | collective-permute-done | bytes 262176 | tf_op jit(solution)/shard_map/ppermute | solution.py:48
  493.4 4.9 shard_map.261
  516.4 11.0 %shard_map.263 = (bf16[256,384]{1,0:T(8,128)(2,1)}, bf16[256,384]{1,0:T(8,128)(2,1)}, bf16[256,384]{1,0:T(8,128)(2,1)}, bf16[256,384]{1,0:T(8,128)(2,1)}, bf16[2...) custom-call(s32[1]{0:T(128)} %bitcast.me_ref, ...), custom_call_target="tpu_custom_call" | custom-call | flops 2684354560 | bytes 4759556 | tf_op jit(solution)/shard_map/pallas_call | solution.py:106
  533.1 6.3 collective-permute-done.73.refs_2_
  539.4 8.0 %collective-permute-done.74.refs_3_ = bf16[256,384]{1,0:T(8,128)(2,1)S(1)} collective-permute-done((bf16[256,384]{1,0:T(8,128)(2,1)}, bf16[256,384]{1,0:T(8,128)(2,1)S(1)}, u32[]{:S(2)}, u32[]{:S(2)}) %collective-permute-start.74) | collective-permute-done | bytes 196640 | tf_op jit(solution)/shard_map/ppermute | solution.py:54
  547.4 4.0 collective-permute-done.76.refs_5_
  551.4 4.4 collective-permute-done.77.refs_6_
  555.9 8.1 %collective-permute-done.78.refs_7_ = bf16[256,384]{1,0:T(8,128)(2,1)S(1)} collective-permute-done((bf16[256,384]{1,0:T(8,128)(2,1)}, bf16[256,384]{1,0:T(8,128)(2,1)S(1)}, u32[]{:S(2)}, u32[]{:S(2)}) %collective-permute-start.78) | collective-permute-done | bytes 196640 | tf_op jit(solution)/shard_map/ppermute | solution.py:54
  564.7 3.8 shard_map.264
  568.5 3.9 shard_map.265
  584.1 11.2 %shard_map.266 = (bf16[512,1536]{1,0:T(8,128)(2,1)}, bf16[64,2048]{1,0:T(8,128)(2,1)}, bf16[64,2048]{1,0:T(8,128)(2,1)}, bf16[64,2048]{1,0:T(8,128)(2,1)}, bf16[...) custom-call(f32[512,1536]{1,0:T(8,128)} %get-tuple-element.127.raw_r, ...), custom_call_target="tpu_custom_call" | custom-call | flops 3221225472 | bytes 15740928 | tf_op jit(solution)/shard_map/pallas_call | solution.py:121
  595.4 9.8 %shard_map.267 = (bf16[4,256,1536]{2,1,0:T(8,128)(2,1)}, bf16[4,256,1536]{2,1,0:T(8,128)(2,1)}) custom-call(s32[1]{0:T(128)} %bitcast.me_ref, bf16[512,2048]{1,0:T(8,128)(2,1)} %get-tuple-element.219.left_ref, bf16[512,1536]{1,0:T(8,128)(2,1)} %get-tuple-element.220.right_ref), custom_call_target="tpu_custom_call" | custom-call | flops 3221225472 | bytes 9961476 | tf_op jit(solution)/shard_map/pallas_call | solution.py:121
  605.9 4.7 collective-permute-done.96
  618.9 7.0 shard_map.268
  635.2 5.5 collective-permute-done.87
  641.7 19.3 %collective-permute-done.86 = bf16[64,2048]{1,0:T(8,128)(2,1)S(1)} collective-permute-done((bf16[64,2048]{1,0:T(8,128)(2,1)S(1)}, bf16[64,2048]{1,0:T(8,128)(2,1)S(1)}, u32[]{:S(2)}, u32[]{:S(2)}) %collective-permute-start.86) | collective-permute-done | bytes 262176 | tf_op jit(solution)/shard_map/ppermute | solution.py:54
  668.7 8.4 %collective-permute-done.83 = bf16[64,2048]{1,0:T(8,128)(2,1)S(1)} collective-permute-done((bf16[64,2048]{1,0:T(8,128)(2,1)}, bf16[64,2048]{1,0:T(8,128)(2,1)S(1)}, u32[]{:S(2)}, u32[]{:S(2)}) %collective-permute-start.83) | collective-permute-done | bytes 262176 | tf_op jit(solution)/shard_map/ppermute | solution.py:54
  684.9 14.0 %collective-permute-done.91 = bf16[256,1536]{1,0:T(8,128)(2,1)} collective-permute-done((bf16[256,1536]{1,0:T(8,128)(2,1)}, bf16[256,1536]{1,0:T(8,128)(2,1)}, u32[]{:S(2)}, u32[]{:S(2)}) %collective-permute-start.91) | collective-permute-done | bytes 786464 | tf_op jit(solution)/shard_map/ppermute | solution.py:606
  698.9 15.2 %collective-permute-done.90 = bf16[256,1536]{1,0:T(8,128)(2,1)} collective-permute-done((bf16[256,1536]{1,0:T(8,128)(2,1)}, bf16[256,1536]{1,0:T(8,128)(2,1)}, u32[]{:S(2)}, u32[]{:S(2)}) %collective-permute-start.90) | collective-permute-done | bytes 786464 | tf_op jit(solution)/shard_map/ppermute | solution.py:606
  (487 shorter events, 224.9 us)
Async XLA Ops:
  7.2 54.5 %all-gather.4.cloned.1.call-start = ((), (), s32[]{:S(2)}) async-start(), calls=%async_computation.1 | async-start | bytes 7077888 | tf_op jit(solution)/shard_map/all_gather | solution.py:1036
  9.4 137.3 %all-gather.6.cloned.1.call-start = ((), (), s32[]{:S(2)}) async-start(), calls=%async_computation.2 | async-start | bytes 2359296 | tf_op jit(solution)/shard_map/all_gather | solution.py:1036
  10.3 220.1 %all-gather.8.cloned.1.call-start = ((), (), s32[]{:S(2)}) async-start(), calls=%async_computation.3 | async-start | bytes 28311552 | tf_op jit(solution)/shard_map/all_gather | solution.py:1036
  13.9 703.6 %reduce-scatter.2.cloned.1.call-start = ((), (), s32[]{:S(2)}) async-start(), calls=%async_computation.4 | async-start | bytes 28311552 | tf_op jit(solution)/shard_map/reduce_scatter | solution.py:1092
  15.0 26.7 %collective-permute-start = (bf16[64,2048]{1,0:T(8,128)(2,1)S(1)}, bf16[64,2048]{1,0:T(8,128)(2,1)S(1)}, u32[]{:S(2)}, u32[]{:S(2)}) collective-permute-start(bf16[64,2048]{1,0:T(8,128)(2,1)S(1)} %get-tuple-element.294.refs_0_.refs_4_), channel_id=1, source_target_pairs={{0,1},{1,0},{2,3},{3,2},{4,5},{5,4},{6,7},{7,6},{8,9},{9,8},{10,11... | collective-permute-start | bytes 786440 | tf_op jit(solution)/shard_map/ppermute | solution.py:48
  18.1 27.8 %collective-permute-start.1 = (bf16[64,2048]{1,0:T(8,128)(2,1)S(1)}, bf16[64,2048]{1,0:T(8,128)(2,1)S(1)}, u32[]{:S(2)}, u32[]{:S(2)}) collective-permute-start(bf16[64,2048]{1,0:T(8,128)(2,1)S(1)} %get-tuple-element.294.refs_0_.refs_4_), channel_id=1, source_target_pairs={{0,2},{1,3},{2,0},{3,1},{4,6},{5,7},{6,4},{7,5},{8,10},{9,11},{10,... | collective-permute-start | bytes 786440 | tf_op jit(solution)/shard_map/ppermute | solution.py:48
  45.9 30.4 %collective-permute-start.21 = (s32[4,2,256]{2,1,0:T(2,128)S(1)}, s32[4,2,256]{2,1,0:T(2,128)S(1)}, u32[]{:S(2)}, u32[]{:S(2)}) collective-permute-start(s32[4,2,256]{2,1,0:T(2,128)S(1)} %pad_add_fusion.1), channel_id=1, source_target_pairs={{0,16},{4,20},{8,24},{12,28},{16,0},{20,4},{24,8},{28,12},{1,17},{... | collective-permute-start | bytes 24584 | tf_op jit(solution)/shard_map/ppermute | solution.py:62
  150.6 21.5 %collective-permute-start.39 = (bf16[64,2048]{1,0:T(8,128)(2,1)}, bf16[64,2048]{1,0:T(8,128)(2,1)S(1)}, u32[]{:S(2)}, u32[]{:S(2)}) collective-permute-start(bf16[64,2048]{1,0:T(8,128)(2,1)} %get-tuple-element.158), channel_id=1, source_target_pairs={{0,2},{1,3},{2,0},{3,1},{4,6},{5,7},{6,4},{7,5},{8,10},{9,11},{10,... | collective-permute-start | bytes 786440 | tf_op jit(solution)/shard_map/ppermute | solution.py:54
  155.0 38.3 %collective-permute-start.29 = (bf16[64,2048]{1,0:T(8,128)(2,1)}, bf16[64,2048]{1,0:T(8,128)(2,1)S(1)}, u32[]{:S(2)}, u32[]{:S(2)}) collective-permute-start(bf16[64,2048]{1,0:T(8,128)(2,1)} %get-tuple-element.146), channel_id=1, source_target_pairs={{0,1},{1,0},{2,3},{3,2},{4,5},{5,4},{6,7},{7,6},{8,9},{9,8},{10,11... | collective-permute-start | bytes 786440 | tf_op jit(solution)/shard_map/ppermute | solution.py:54
  155.0 40.7 %collective-permute-start.30 = (bf16[64,2048]{1,0:T(8,128)(2,1)}, bf16[64,2048]{1,0:T(8,128)(2,1)S(1)}, u32[]{:S(2)}, u32[]{:S(2)}) collective-permute-start(bf16[64,2048]{1,0:T(8,128)(2,1)} %get-tuple-element.147), channel_id=1, source_target_pairs={{0,2},{1,3},{2,0},{3,1},{4,6},{5,7},{6,4},{7,5},{8,10},{9,11},{10,... | collective-permute-start | bytes 786440 | tf_op jit(solution)/shard_map/ppermute | solution.py:54
  162.5 33.2 %collective-permute-start.31 = (bf16[64,2048]{1,0:T(8,128)(2,1)}, bf16[64,2048]{1,0:T(8,128)(2,1)S(1)}, u32[]{:S(2)}, u32[]{:S(2)}) collective-permute-start(bf16[64,2048]{1,0:T(8,128)(2,1)} %get-tuple-element.148), channel_id=1, source_target_pairs={{0,3},{1,2},{2,1},{3,0},{4,7},{5,6},{6,5},{7,4},{8,11},{9,10},{10,... | collective-permute-start | bytes 786440 | tf_op jit(solution)/shard_map/ppermute | solution.py:54
  176.0 37.4 %collective-permute-start.41 = (bf16[64,2048]{1,0:T(8,128)(2,1)}, bf16[64,2048]{1,0:T(8,128)(2,1)S(1)}, u32[]{:S(2)}, u32[]{:S(2)}) collective-permute-start(bf16[64,2048]{1,0:T(8,128)(2,1)} %get-tuple-element.160.refs_0_), channel_id=1, source_target_pairs={{0,1},{1,0},{2,3},{3,2},{4,5},{5,4},{6,7},{7,6},{8,9},{9,8},{10,11... | collective-permute-start | bytes 786440 | tf_op jit(solution)/shard_map/ppermute | solution.py:48
  193.3 35.1 %collective-permute-start.42 = (bf16[64,2048]{1,0:T(8,128)(2,1)}, bf16[64,2048]{1,0:T(8,128)(2,1)S(1)}, u32[]{:S(2)}, u32[]{:S(2)}) collective-permute-start(bf16[64,2048]{1,0:T(8,128)(2,1)} %get-tuple-element.160.refs_0_), channel_id=1, source_target_pairs={{0,2},{1,3},{2,0},{3,1},{4,6},{5,7},{6,4},{7,5},{8,10},{9,11},{10,... | collective-permute-start | bytes 786440 | tf_op jit(solution)/shard_map/ppermute | solution.py:48
  193.3 35.1 %collective-permute-start.43 = (bf16[64,2048]{1,0:T(8,128)(2,1)}, bf16[64,2048]{1,0:T(8,128)(2,1)S(1)}, u32[]{:S(2)}, u32[]{:S(2)}) collective-permute-start(bf16[64,2048]{1,0:T(8,128)(2,1)} %get-tuple-element.160.refs_0_), channel_id=1, source_target_pairs={{0,3},{1,2},{2,1},{3,0},{4,7},{5,6},{6,5},{7,4},{8,11},{9,10},{10,... | collective-permute-start | bytes 786440 | tf_op jit(solution)/shard_map/ppermute | solution.py:48
  199.1 53.3 %collective-permute-start.32 = (bf16[64,2048]{1,0:T(8,128)(2,1)}, bf16[64,2048]{1,0:T(8,128)(2,1)S(1)}, u32[]{:S(2)}, u32[]{:S(2)}) collective-permute-start(bf16[64,2048]{1,0:T(8,128)(2,1)} %get-tuple-element.149.refs_0_), channel_id=1, source_target_pairs={{0,1},{1,0},{2,3},{3,2},{4,5},{5,4},{6,7},{7,6},{8,9},{9,8},{10,11... | collective-permute-start | bytes 786440 | tf_op jit(solution)/shard_map/ppermute | solution.py:48
  213.4 41.4 %collective-permute-start.33 = (bf16[64,2048]{1,0:T(8,128)(2,1)}, bf16[64,2048]{1,0:T(8,128)(2,1)S(1)}, u32[]{:S(2)}, u32[]{:S(2)}) collective-permute-start(bf16[64,2048]{1,0:T(8,128)(2,1)} %get-tuple-element.149.refs_0_), channel_id=1, source_target_pairs={{0,2},{1,3},{2,0},{3,1},{4,6},{5,7},{6,4},{7,5},{8,10},{9,11},{10,... | collective-permute-start | bytes 786440 | tf_op jit(solution)/shard_map/ppermute | solution.py:48
  213.4 41.4 %collective-permute-start.34 = (bf16[64,2048]{1,0:T(8,128)(2,1)}, bf16[64,2048]{1,0:T(8,128)(2,1)S(1)}, u32[]{:S(2)}, u32[]{:S(2)}) collective-permute-start(bf16[64,2048]{1,0:T(8,128)(2,1)} %get-tuple-element.149.refs_0_), channel_id=1, source_target_pairs={{0,3},{1,2},{2,1},{3,0},{4,7},{5,6},{6,5},{7,4},{8,11},{9,10},{10,... | collective-permute-start | bytes 786440 | tf_op jit(solution)/shard_map/ppermute | solution.py:48
  247.5 28.8 %collective-permute-start.44 = (bf16[64,2048]{1,0:T(8,128)(2,1)}, bf16[64,2048]{1,0:T(8,128)(2,1)S(1)}, u32[]{:S(2)}, u32[]{:S(2)}) collective-permute-start(bf16[64,2048]{1,0:T(8,128)(2,1)} %get-tuple-element.162), channel_id=1, source_target_pairs={{0,1},{1,0},{2,3},{3,2},{4,5},{5,4},{6,7},{7,6},{8,9},{9,8},{10,11... | collective-permute-start | bytes 786440 | tf_op jit(solution)/shard_map/ppermute | solution.py:54
  252.4 26.2 %collective-permute-start.45 = (bf16[64,2048]{1,0:T(8,128)(2,1)}, bf16[64,2048]{1,0:T(8,128)(2,1)S(1)}, u32[]{:S(2)}, u32[]{:S(2)}) collective-permute-start(bf16[64,2048]{1,0:T(8,128)(2,1)} %get-tuple-element.163), channel_id=1, source_target_pairs={{0,2},{1,3},{2,0},{3,1},{4,6},{5,7},{6,4},{7,5},{8,10},{9,11},{10,... | collective-permute-start | bytes 786440 | tf_op jit(solution)/shard_map/ppermute | solution.py:54
  252.5 26.1 %collective-permute-start.46 = (bf16[64,2048]{1,0:T(8,128)(2,1)}, bf16[64,2048]{1,0:T(8,128)(2,1)S(1)}, u32[]{:S(2)}, u32[]{:S(2)}) collective-permute-start(bf16[64,2048]{1,0:T(8,128)(2,1)} %get-tuple-element.164), channel_id=1, source_target_pairs={{0,3},{1,2},{2,1},{3,0},{4,7},{5,6},{6,5},{7,4},{8,11},{9,10},{10,... | collective-permute-start | bytes 786440 | tf_op jit(solution)/shard_map/ppermute | solution.py:54
  275.3 21.6 %collective-permute-start.36 = (bf16[64,2048]{1,0:T(8,128)(2,1)}, bf16[64,2048]{1,0:T(8,128)(2,1)S(1)}, u32[]{:S(2)}, u32[]{:S(2)}) collective-permute-start(bf16[64,2048]{1,0:T(8,128)(2,1)} %get-tuple-element.152), channel_id=1, source_target_pairs={{0,2},{1,3},{2,0},{3,1},{4,6},{5,7},{6,4},{7,5},{8,10},{9,11},{10,... | collective-permute-start | bytes 786440 | tf_op jit(solution)/shard_map/ppermute | solution.py:54
  282.1 34.9 %collective-permute-start.56 = (bf16[64,2048]{1,0:T(8,128)(2,1)}, bf16[64,2048]{1,0:T(8,128)(2,1)S(1)}, u32[]{:S(2)}, u32[]{:S(2)}) collective-permute-start(bf16[64,2048]{1,0:T(8,128)(2,1)} %get-tuple-element.177.refs_0_), channel_id=1, source_target_pairs={{0,1},{1,0},{2,3},{3,2},{4,5},{5,4},{6,7},{7,6},{8,9},{9,8},{10,11... | collective-permute-start | bytes 786440 | tf_op jit(solution)/shard_map/ppermute | solution.py:48
  282.3 38.6 %collective-permute-start.57 = (bf16[64,2048]{1,0:T(8,128)(2,1)}, bf16[64,2048]{1,0:T(8,128)(2,1)S(1)}, u32[]{:S(2)}, u32[]{:S(2)}) collective-permute-start(bf16[64,2048]{1,0:T(8,128)(2,1)} %get-tuple-element.177.refs_0_), channel_id=1, source_target_pairs={{0,2},{1,3},{2,0},{3,1},{4,6},{5,7},{6,4},{7,5},{8,10},{9,11},{10,... | collective-permute-start | bytes 786440 | tf_op jit(solution)/shard_map/ppermute | solution.py:48
  284.3 36.7 %collective-permute-start.58 = (bf16[64,2048]{1,0:T(8,128)(2,1)}, bf16[64,2048]{1,0:T(8,128)(2,1)S(1)}, u32[]{:S(2)}, u32[]{:S(2)}) collective-permute-start(bf16[64,2048]{1,0:T(8,128)(2,1)} %get-tuple-element.177.refs_0_), channel_id=1, source_target_pairs={{0,3},{1,2},{2,1},{3,0},{4,7},{5,6},{6,5},{7,4},{8,11},{9,10},{10,... | collective-permute-start | bytes 786440 | tf_op jit(solution)/shard_map/ppermute | solution.py:48
  300.3 41.0 %collective-permute-start.47 = (bf16[64,2048]{1,0:T(8,128)(2,1)}, bf16[64,2048]{1,0:T(8,128)(2,1)S(1)}, u32[]{:S(2)}, u32[]{:S(2)}) collective-permute-start(bf16[64,2048]{1,0:T(8,128)(2,1)} %get-tuple-element.167.refs_0_), channel_id=1, source_target_pairs={{0,1},{1,0},{2,3},{3,2},{4,5},{5,4},{6,7},{7,6},{8,9},{9,8},{10,11... | collective-permute-start | bytes 786440 | tf_op jit(solution)/shard_map/ppermute | solution.py:48
  316.6 24.7 %collective-permute-start.48 = (bf16[64,2048]{1,0:T(8,128)(2,1)}, bf16[64,2048]{1,0:T(8,128)(2,1)S(1)}, u32[]{:S(2)}, u32[]{:S(2)}) collective-permute-start(bf16[64,2048]{1,0:T(8,128)(2,1)} %get-tuple-element.167.refs_0_), channel_id=1, source_target_pairs={{0,2},{1,3},{2,0},{3,1},{4,6},{5,7},{6,4},{7,5},{8,10},{9,11},{10,... | collective-permute-start | bytes 786440 | tf_op jit(solution)/shard_map/ppermute | solution.py:48
  317.1 24.3 %collective-permute-start.49 = (bf16[64,2048]{1,0:T(8,128)(2,1)}, bf16[64,2048]{1,0:T(8,128)(2,1)S(1)}, u32[]{:S(2)}, u32[]{:S(2)}) collective-permute-start(bf16[64,2048]{1,0:T(8,128)(2,1)} %get-tuple-element.167.refs_0_), channel_id=1, source_target_pairs={{0,3},{1,2},{2,1},{3,0},{4,7},{5,6},{6,5},{7,4},{8,11},{9,10},{10,... | collective-permute-start | bytes 786440 | tf_op jit(solution)/shard_map/ppermute | solution.py:48
  392.2 30.0 %collective-permute-start.50 = (bf16[64,2048]{1,0:T(8,128)(2,1)S(1)}, bf16[64,2048]{1,0:T(8,128)(2,1)S(1)}, u32[]{:S(2)}, u32[]{:S(2)}) collective-permute-start(bf16[64,2048]{1,0:T(8,128)(2,1)S(1)} %copy-done.92), channel_id=1, source_target_pairs={{0,1},{1,0},{2,3},{3,2},{4,5},{5,4},{6,7},{7,6},{8,9},{9,8},{10,11... | collective-permute-start | bytes 786440 | tf_op jit(solution)/shard_map/ppermute | solution.py:54
  406.9 21.5 %collective-permute-start.51 = (bf16[64,2048]{1,0:T(8,128)(2,1)S(1)}, bf16[64,2048]{1,0:T(8,128)(2,1)S(1)}, u32[]{:S(2)}, u32[]{:S(2)}) collective-permute-start(bf16[64,2048]{1,0:T(8,128)(2,1)S(1)} %copy-done.91), channel_id=1, source_target_pairs={{0,2},{1,3},{2,0},{3,1},{4,6},{5,7},{6,4},{7,5},{8,10},{9,11},{10,... | collective-permute-start | bytes 786440 | tf_op jit(solution)/shard_map/ppermute | solution.py:54
  409.3 38.6 %collective-permute-start.59 = (bf16[64,2048]{1,0:T(8,128)(2,1)S(1)}, bf16[64,2048]{1,0:T(8,128)(2,1)S(1)}, u32[]{:S(2)}, u32[]{:S(2)}) collective-permute-start(bf16[64,2048]{1,0:T(8,128)(2,1)S(1)} %copy-done.87), channel_id=1, source_target_pairs={{0,1},{1,0},{2,3},{3,2},{4,5},{5,4},{6,7},{7,6},{8,9},{9,8},{10,11... | collective-permute-start | bytes 786440 | tf_op jit(solution)/shard_map/ppermute | solution.py:54
  410.4 39.1 %collective-permute-start.60 = (bf16[64,2048]{1,0:T(8,128)(2,1)S(1)}, bf16[64,2048]{1,0:T(8,128)(2,1)S(1)}, u32[]{:S(2)}, u32[]{:S(2)}) collective-permute-start(bf16[64,2048]{1,0:T(8,128)(2,1)S(1)} %copy-done.86), channel_id=1, source_target_pairs={{0,2},{1,3},{2,0},{3,1},{4,6},{5,7},{6,4},{7,5},{8,10},{9,11},{10,... | collective-permute-start | bytes 786440 | tf_op jit(solution)/shard_map/ppermute | solution.py:54
  422.2 27.3 %collective-permute-start.61 = (bf16[64,2048]{1,0:T(8,128)(2,1)S(1)}, bf16[64,2048]{1,0:T(8,128)(2,1)S(1)}, u32[]{:S(2)}, u32[]{:S(2)}) collective-permute-start(bf16[64,2048]{1,0:T(8,128)(2,1)S(1)} %copy-done.83), channel_id=1, source_target_pairs={{0,3},{1,2},{2,1},{3,0},{4,7},{5,6},{6,5},{7,4},{8,11},{9,10},{10,... | collective-permute-start | bytes 786440 | tf_op jit(solution)/shard_map/ppermute | solution.py:54
  432.1 37.9 %collective-permute-start.53 = (bf16[64,2048]{1,0:T(8,128)(2,1)}, bf16[64,2048]{1,0:T(8,128)(2,1)S(1)}, u32[]{:S(2)}, u32[]{:S(2)}) collective-permute-start(bf16[64,2048]{1,0:T(8,128)(2,1)} %get-tuple-element.176.refs_0_), channel_id=1, source_target_pairs={{0,1},{1,0},{2,3},{3,2},{4,5},{5,4},{6,7},{7,6},{8,9},{9,8},{10,11... | collective-permute-start | bytes 786440 | tf_op jit(solution)/shard_map/ppermute | solution.py:48
  446.0 25.5 %collective-permute-start.54 = (bf16[64,2048]{1,0:T(8,128)(2,1)}, bf16[64,2048]{1,0:T(8,128)(2,1)S(1)}, u32[]{:S(2)}, u32[]{:S(2)}) collective-permute-start(bf16[64,2048]{1,0:T(8,128)(2,1)} %get-tuple-element.176.refs_0_), channel_id=1, source_target_pairs={{0,2},{1,3},{2,0},{3,1},{4,6},{5,7},{6,4},{7,5},{8,10},{9,11},{10,... | collective-permute-start | bytes 786440 | tf_op jit(solution)/shard_map/ppermute | solution.py:48
  447.9 23.6 %collective-permute-start.55 = (bf16[64,2048]{1,0:T(8,128)(2,1)}, bf16[64,2048]{1,0:T(8,128)(2,1)S(1)}, u32[]{:S(2)}, u32[]{:S(2)}) collective-permute-start(bf16[64,2048]{1,0:T(8,128)(2,1)} %get-tuple-element.176.refs_0_), channel_id=1, source_target_pairs={{0,3},{1,2},{2,1},{3,0},{4,7},{5,6},{6,5},{7,4},{8,11},{9,10},{10,... | collective-permute-start | bytes 786440 | tf_op jit(solution)/shard_map/ppermute | solution.py:48
  452.8 23.3 %collective-permute-start.62 = (bf16[64,2048]{1,0:T(8,128)(2,1)}, bf16[64,2048]{1,0:T(8,128)(2,1)S(1)}, u32[]{:S(2)}, u32[]{:S(2)}) collective-permute-start(bf16[64,2048]{1,0:T(8,128)(2,1)} %get-tuple-element.186.refs_4_), channel_id=1, source_target_pairs={{0,1},{1,0},{2,3},{3,2},{4,5},{5,4},{6,7},{7,6},{8,9},{9,8},{10,11... | collective-permute-start | bytes 786440 | tf_op jit(solution)/shard_map/ppermute | solution.py:48
  468.2 23.8 %collective-permute-start.63 = (bf16[64,2048]{1,0:T(8,128)(2,1)}, bf16[64,2048]{1,0:T(8,128)(2,1)S(1)}, u32[]{:S(2)}, u32[]{:S(2)}) collective-permute-start(bf16[64,2048]{1,0:T(8,128)(2,1)} %get-tuple-element.186.refs_4_), channel_id=1, source_target_pairs={{0,2},{1,3},{2,0},{3,1},{4,6},{5,7},{6,4},{7,5},{8,10},{9,11},{10,... | collective-permute-start | bytes 786440 | tf_op jit(solution)/shard_map/ppermute | solution.py:48
  470.0 22.0 %collective-permute-start.64 = (bf16[64,2048]{1,0:T(8,128)(2,1)}, bf16[64,2048]{1,0:T(8,128)(2,1)S(1)}, u32[]{:S(2)}, u32[]{:S(2)}) collective-permute-start(bf16[64,2048]{1,0:T(8,128)(2,1)} %get-tuple-element.186.refs_4_), channel_id=1, source_target_pairs={{0,3},{1,2},{2,1},{3,0},{4,7},{5,6},{6,5},{7,4},{8,11},{9,10},{10,... | collective-permute-start | bytes 786440 | tf_op jit(solution)/shard_map/ppermute | solution.py:48
  531.1 24.7 %collective-permute-start.77 = (bf16[256,384]{1,0:T(8,128)(2,1)}, bf16[256,384]{1,0:T(8,128)(2,1)S(1)}, u32[]{:S(2)}, u32[]{:S(2)}) collective-permute-start(bf16[256,384]{1,0:T(8,128)(2,1)} %get-tuple-element.204), channel_id=1, source_target_pairs={{0,24},{4,28},{8,16},{12,20},{16,8},{20,12},{24,0},{28,4},{1,25},{... | collective-permute-start | bytes 589832 | tf_op jit(solution)/shard_map/ppermute | solution.py:54
  539.4 24.6 %collective-permute-start.78 = (bf16[256,384]{1,0:T(8,128)(2,1)}, bf16[256,384]{1,0:T(8,128)(2,1)S(1)}, u32[]{:S(2)}, u32[]{:S(2)}) collective-permute-start(bf16[256,384]{1,0:T(8,128)(2,1)} %get-tuple-element.205), channel_id=1, source_target_pairs={{0,28},{4,24},{8,20},{12,16},{16,12},{20,8},{24,4},{28,0},{1,29},{... | collective-permute-start | bytes 589832 | tf_op jit(solution)/shard_map/ppermute | solution.py:54
  605.2 60.5 %collective-permute-start.88 = (bf16[4,256,1536]{2,1,0:T(8,128)(2,1)}, bf16[4,256,1536]{2,1,0:T(8,128)(2,1)S(1)}, u32[]{:S(2)}, u32[]{:S(2)}) collective-permute-start(bf16[4,256,1536]{2,1,0:T(8,128)(2,1)} %get-tuple-element.222), channel_id=1, source_target_pairs={{0,4},{4,0},{8,12},{12,8},{16,20},{20,16},{24,28},{28,24},{1,5},{5... | collective-permute-start | bytes 9437192 | tf_op jit(solution)/shard_map/ppermute | solution.py:599
  625.9 37.2 %collective-permute-start.92 = (bf16[4,256,512]{2,1,0:T(8,128)(2,1)}, bf16[4,256,512]{2,1,0:T(8,128)(2,1)S(1)}, u32[]{:S(2)}, u32[]{:S(2)}) collective-permute-start(bf16[4,256,512]{2,1,0:T(8,128)(2,1)} %get-tuple-element.225), channel_id=1, source_target_pairs={{0,4},{4,0},{8,12},{12,8},{16,20},{20,16},{24,28},{28,24},{1,5},{5... | collective-permute-start | bytes 3145736 | tf_op jit(solution)/shard_map/ppermute | solution.py:599
  630.6 30.4 %collective-permute-start.86 = (bf16[64,2048]{1,0:T(8,128)(2,1)S(1)}, bf16[64,2048]{1,0:T(8,128)(2,1)S(1)}, u32[]{:S(2)}, u32[]{:S(2)}) collective-permute-start(bf16[64,2048]{1,0:T(8,128)(2,1)S(1)} %copy-done.81), channel_id=1, source_target_pairs={{0,2},{1,3},{2,0},{3,1},{4,6},{5,7},{6,4},{7,5},{8,10},{9,11},{10,... | collective-permute-start | bytes 786440 | tf_op jit(solution)/shard_map/ppermute | solution.py:54
  631.4 29.6 %collective-permute-start.85 = (bf16[64,2048]{1,0:T(8,128)(2,1)S(1)}, bf16[64,2048]{1,0:T(8,128)(2,1)S(1)}, u32[]{:S(2)}, u32[]{:S(2)}) collective-permute-start(bf16[64,2048]{1,0:T(8,128)(2,1)S(1)} %copy-done.80), channel_id=1, source_target_pairs={{0,1},{1,0},{2,3},{3,2},{4,5},{5,4},{6,7},{7,6},{8,9},{9,8},{10,11... | collective-permute-start | bytes 786440 | tf_op jit(solution)/shard_map/ppermute | solution.py:54
  640.7 27.5 %collective-permute-start.84 = (bf16[64,2048]{1,0:T(8,128)(2,1)}, bf16[64,2048]{1,0:T(8,128)(2,1)S(1)}, u32[]{:S(2)}, u32[]{:S(2)}) collective-permute-start(bf16[64,2048]{1,0:T(8,128)(2,1)} %get-tuple-element.212), channel_id=1, source_target_pairs={{0,3},{1,2},{2,1},{3,0},{4,7},{5,6},{6,5},{7,4},{8,11},{9,10},{10,... | collective-permute-start | bytes 786440 | tf_op jit(solution)/shard_map/ppermute | solution.py:54
  677.1 21.7 %collective-permute-start.91 = (bf16[256,1536]{1,0:T(8,128)(2,1)}, bf16[256,1536]{1,0:T(8,128)(2,1)}, u32[]{:S(2)}, u32[]{:S(2)}) collective-permute-start(bf16[256,1536]{1,0:T(8,128)(2,1)} %get-tuple-element.281), channel_id=1, source_target_pairs={{0,24},{4,28},{8,16},{12,20},{16,8},{20,12},{24,0},{28,4},{1,25},{... | collective-permute-start | bytes 2359304 | tf_op jit(solution)/shard_map/ppermute | solution.py:606
  679.4 34.6 %collective-permute-start.90 = (bf16[256,1536]{1,0:T(8,128)(2,1)}, bf16[256,1536]{1,0:T(8,128)(2,1)}, u32[]{:S(2)}, u32[]{:S(2)}) collective-permute-start(bf16[256,1536]{1,0:T(8,128)(2,1)} %get-tuple-element.282), channel_id=1, source_target_pairs={{0,16},{4,20},{8,24},{12,28},{16,0},{20,4},{24,8},{28,12},{1,17},{... | collective-permute-start | bytes 2359304 | tf_op jit(solution)/shard_map/ppermute | solution.py:606
  680.2 33.9 %collective-permute-start.89 = (bf16[256,1536]{1,0:T(8,128)(2,1)}, bf16[256,1536]{1,0:T(8,128)(2,1)}, u32[]{:S(2)}, u32[]{:S(2)}) collective-permute-start(bf16[256,1536]{1,0:T(8,128)(2,1)} %get-tuple-element.280), channel_id=1, source_target_pairs={{0,8},{4,12},{8,0},{12,4},{16,24},{20,28},{24,16},{28,20},{1,9},{5... | collective-permute-start | bytes 2359304 | tf_op jit(solution)/shard_map/ppermute | solution.py:606
  (164 other events, 1760.9 us)
Sparse Core Ops, SparseCore 0:
  10.5 48.3 all-gather.3
  60.8 27.8 all-gather.5
  90.6 139.7 all-gather.7
  391.4 192.5 reduce-scatter.1

commit v3 on v2

--- a/solution.py
+++ b/solution.py
@@ -1,4 +1,5 @@
 import functools
+import math
 
 import jax
 import jax.numpy as jnp
@@ -11,7 +12,7 @@
 
 epsilon = 1e-06
 theta = 500000.0
-tile = 256
+widest = 512
 score_scale = HD ** (-0.5)
 hidden_score = -1e30
 low = jnp.bfloat16
@@ -73,6 +74,57 @@
     return values
 
 
+def after(values, *others):
+    return lax.optimization_barrier((values, others))[0]
+
+
+inward = [(0, 1), (3, 2)]
+outward = [(1, 0), (2, 3)]
+middle = [(1, 2), (2, 1)]
+
+
+def send_rows(values, pairs):
+    return lax.ppermute(values, "head", pairs)
+
+
+def gather_parts(values):
+    if lax.axis_size("head") != 4:
+        return gather_slots(values, "head")
+    second = send_rows(values, xor_pairs(4, 2))
+    first = send_rows(values, xor_pairs(4, 1))
+    across = send_rows(values, middle)
+    return [values, first, second, across, send_rows(second, outward)]
+
+
+def layout_of(count):
+    return [(0,), (1,), (2,), (3, 4)] if count == 5 else [(s,) for s in range(count)]
+
+
+def reduce_parts(slots):
+    if lax.axis_size("head") != 4:
+        return exchange_slots(slots, "head")
+    arrived = send_rows(slots[3], inward)
+    first = send_rows(slots[1], xor_pairs(4, 1))
+    across = send_rows(slots[3], middle)
+    passed = (slots[2].astype(full) + arrived.astype(full)).astype(low)
+    return [slots[0], first, across, send_rows(passed, xor_pairs(4, 2))]
+
+
+def exchange_chips(slots):
+    size = lax.axis_size("blk")
+    return [slots[0]] + [
+        lax.ppermute(slots[m], "blk", xor_pairs(size, 2 * m)) for m in range(1, size // 2)
+    ]
+
+
+def swap_cores(values):
+    return lax.ppermute(values, "blk", xor_pairs(lax.axis_size("blk"), 1))
+
+
+def sum_full(arrays):
+    return sum(array.astype(full) for array in arrays)
+
+
 def sum_heads(values):
     size = lax.axis_size("head")
     total = None
@@ -112,7 +164,9 @@
         scratch_shapes=list(scratch),
         compiler_params=pltpu.CompilerParams(vmem_limit_bytes=vmem_grant),
         cost_estimate=pl.CostEstimate(
-            flops=flops, bytes_accessed=sizes_of(args) + sizes_of(outs), transcendentals=0
+            flops=flops,
+            bytes_accessed=sizes_of(args) + sizes_of(outs),
+            transcendentals=0,
         ),
     )(*args)
 
@@ -139,36 +193,57 @@
 scalar_spec = pl.BlockSpec(memory_space=pltpu.SMEM)
 
 
-def column_tile(rows, first=0):
+def tile_of(size):
+    return math.gcd(size, widest)
+
+
+def column_tile(rows, tile, first=0):
     return pl.BlockSpec((rows, tile), lambda i: (0, first + i))
 
 
-def put_slots(out_refs, values):
-    rows = out_refs[0].shape[0]
-    for s, ref in enumerate(out_refs):
-        ref[...] = values[s * rows : (s + 1) * rows].astype(ref.dtype)
+def slot_cuts(micro_count, count, rows):
+    for s in range(count):
+        for m in range(micro_count):
+            first = (m * count + s) * rows
+            yield s, slice(m * rows, (m + 1) * rows), slice(first, first + rows)
+
+
+def put_slots(out_refs, values, micro_count):
+    rows = out_refs[0].shape[0] // micro_count
+    for s, inner, outer in slot_cuts(micro_count, len(out_refs), rows):
+        out_refs[s][inner, :] = values[outer].astype(out_refs[s].dtype)
+
+
+def fill_rows(rows_ref, part_refs, micro_count):
+    layout = layout_of(len(part_refs))
+    rows = part_refs[0].shape[0] // micro_count
+    for s, inner, outer in slot_cuts(micro_count, len(layout), rows):
+        rows_ref[outer, :] = functools.reduce(
+            jnp.add, [part_refs[part][inner, :] for part in layout[s]]
+        )
 
 
 def sum_slots(refs):
     return sum(ref[...].astype(full) for ref in refs)
 
 
-def ffn_forward(slots, weights):
+def ffn_forward(slots, weights, micro_count):
     n = len(slots)
     local_rows, width = slots[0].shape
-    rows, hidden = n * local_rows, weights.shape[1] // 3
+    count = len(layout_of(n))
+    rows, hidden = count * local_rows, weights.shape[1] // 3
+    tile = tile_of(hidden)
     steps = hidden // tile
 
     def body(*refs):
         wg_ref, wu_ref, wd_ref = refs[n : n + 3]
         rows_ref, gate_ref, up_ref, middle_ref = refs[n + 3 : n + 7]
-        out_refs, total = refs[n + 7 : 2 * n + 7], refs[2 * n + 7]
+        out_refs, total = refs[n + 7 : -1], refs[-1]
         step = pl.program_id(0)
 
         @pl.when(step == 0)
         def _():
-            for s in range(n):
-                rows_ref[s * local_rows : (s + 1) * local_rows, :] = refs[s][...]
+            fill_rows(rows_ref, refs[:n], micro_count)
 
         values = rows_ref[...]
         gate = dot_plain(values, wg_ref[...])
@@ -189,16 +264,16 @@
 
         @pl.when(step == steps - 1)
         def _():
-            put_slots(out_refs, total)
+            put_slots(out_refs, total[...], micro_count)
 
     results = call_grid(
         body,
         steps,
         [shape_of((rows, width), low)]
         + [shape_of((rows, hidden), low)] * 3
-        + [shape_of((local_rows, width), low)] * n,
-        [fixed((local_rows, width))] * n + [column_tile(width, k * steps) for k in range(3)],
-        [fixed((rows, width))] + [column_tile(rows)] * 3 + [fixed((local_rows, width))] * n,
+        + [shape_of((local_rows, width), low)] * count,
+        [fixed((local_rows, width))] * n + [column_tile(width, tile, k * steps) for k in range(3)],
+        [fixed((rows, width))] + [column_tile(rows, tile)] * 3 + [fixed((local_rows, width))] * count,
         *slots,
         weights,
         weights,
@@ -209,22 +284,23 @@
     return results[:4], results[4:]
 
 
-def ffn_backward(slots, gate, up, weights):
+def ffn_backward(slots, gate, up, weights, micro_count):
     n = len(slots)
     local_rows, width = slots[0].shape
     rows, hidden = gate.shape
+    count = rows // local_rows
+    tile = tile_of(hidden)
     steps = hidden // tile
 
     def body(*refs):
         gate_ref, up_ref, wg_ref, wu_ref, wd_ref = refs[n : n + 5]
         rows_ref, gg_ref, gu_ref = refs[n + 5 : n + 8]
-        out_refs, total = refs[n + 8 : 2 * n + 8], refs[2 * n + 8]
+        out_refs, total = refs[n + 8 : -1], refs[-1]
         step = pl.program_id(0)
 
         @pl.when(step == 0)
         def _():
-            for s in range(n):
-                rows_ref[s * local_rows : (s + 1) * local_rows, :] = refs[s][...]
+            fill_rows(rows_ref, refs[:n], micro_count)
 
         grad_middle = dot_plain(rows_ref[...], wd_ref[...])
         gate_values = gate_ref[...].astype(full)
@@ -248,18 +324,18 @@
 
         @pl.when(step == steps - 1)
         def _():
-            put_slots(out_refs, total)
+            put_slots(out_refs, total[...], micro_count)
 
     results = call_grid(
         body,
         steps,
         [shape_of((rows, width), low)]
         + [shape_of((rows, hidden), low)] * 2
-        + [shape_of((local_rows, width), low)] * n,
+        + [shape_of((local_rows, width), low)] * count,
         [fixed((local_rows, width))] * n
-        + [column_tile(rows)] * 2
-        + [column_tile(width, k * steps) for k in range(3)],
-        [fixed((rows, width))] + [column_tile(rows)] * 2 + [fixed((local_rows, width))] * n,
+        + [column_tile(rows, tile)] * 2
+        + [column_tile(width, tile, k * steps) for k in range(3)],
+        [fixed((rows, width))] + [column_tile(rows, tile)] * 2 + [fixed((local_rows, width))] * count,
         *slots,
         gate,
         up,
@@ -272,49 +348,58 @@
     return results[:3], results[3:]
 
 
-def ffn_weight_terms(hidden_rows, grad_rows, grad_gates, grad_ups, middles):
-    n = len(hidden_rows)
-    rows, width = hidden_rows[0].shape
-    hidden = middles[0].shape[1]
+def ffn_weight_term(held, part, lefts, rights):
+    n = len(lefts)
+    rows, width = lefts[0].shape
+    hidden = rights[0].shape[1]
+    tile = tile_of(hidden)
     steps = hidden // tile
 
     def body(*refs):
-        hidden_refs, grad_refs = refs[:n], refs[n : 2 * n]
-        groups = [refs[(2 + k) * n : (3 + k) * n] for k in range(3)]
-        out_ref, hidden_t, grad_t = refs[5 * n :]
-        step = pl.program_id(0)
-
-        @pl.when(step == 0)
+        out_ref, left_t = refs[-2:]
+
+        @pl.when(pl.program_id(0) == 0)
         def _():
             for m in range(n):
-                cut = slice(m * rows, (m + 1) * rows)
-                hidden_t[:, cut] = jnp.transpose(hidden_refs[m][...])
-                grad_t[:, cut] = jnp.transpose(grad_refs[m][...])
-
-        for k, left in enumerate((hidden_t, hidden_t, grad_t)):
-
-            @pl.when(step // steps == k)
-            def _():
-                right = jnp.concatenate([ref[...] for ref in groups[k]], axis=0)
-                out_ref[...] = dot_plain(left[...], right).astype(low)
-
-    def spec(k):
-        return pl.BlockSpec((rows, tile), lambda i: (0, jnp.clip(i - k * steps, 0, steps - 1)))
-
-    return call_grid(
-        body,
-        3 * steps,
-        [shape_of((width, 3 * hidden), low)],
-        [fixed((rows, width))] * (2 * n) + [spec(k) for k in range(3) for _ in range(n)],
-        [column_tile(width)],
-        *hidden_rows,
-        *grad_rows,
-        *grad_gates,
-        *grad_ups,
-        *middles,
-        scratch=[pltpu.VMEM((width, n * rows), low)] * 2,
-        flops=6 * n * rows * width * hidden,
-    )[0]
+                left_t[:, m * rows : (m + 1) * rows] = jnp.transpose(refs[m][...])
+
+        right = jnp.concatenate([ref[...] for ref in refs[n : 2 * n]], axis=0)
+        out_ref[...] = dot_plain(left_t[...], right).astype(low)
+
+    shape = shape_of((width, 3 * hidden), low)
+    return pl.pallas_call(
+        body,
+        grid=(steps,),
+        out_shape=shape,
+        in_specs=[fixed((rows, width))] * n
+        + [column_tile(rows, tile)] * n
+        + [pl.BlockSpec(memory_space=pl.ANY)] * len(held),
+        out_specs=column_tile(width, tile, part * steps),
+        scratch_shapes=[pltpu.VMEM((width, n * rows), low)],
+        input_output_aliases={2 * n: 0} if held else {},
+        compiler_params=pltpu.CompilerParams(vmem_limit_bytes=vmem_grant),
+        cost_estimate=pl.CostEstimate(
+            flops=2 * n * rows * width * hidden,
+            bytes_accessed=sizes_of(lefts) + width * hidden * 2,
+            transcendentals=0,
+        ),
+    )(*lefts, *rights, *held)
+
+
+def widen_ffn(grads):
+    rows, hidden = grads.shape[0], grads.shape[1] // 3
+
+    def body(grad_ref, gate_ref, up_ref, down_ref):
+        gate_ref[...] = grad_ref[:, :hidden].astype(full)
+        up_ref[...] = grad_ref[:, hidden : 2 * hidden].astype(full)
+        down_ref[...] = jnp.transpose(grad_ref[:, 2 * hidden :]).astype(full)
+
+    return call_whole(
+        body,
+        [shape_of((rows, hidden), full)] * 2 + [shape_of((hidden, rows), full)],
+        grads,
+        scalars=0,
+    )
 
 
 def after_attention(arrived, tokens, gain):
@@ -395,11 +480,12 @@
     )
 
 
-def project_qkv(token_slots, weights):
+def project_qkv(token_slots, weights, micro_count):
     count = len(token_slots)
     local_rows, width = token_slots[0].shape
-    rows, features = count * local_rows, weights.shape[1]
+    rows, features = len(layout_of(count)) * local_rows, weights.shape[1]
     part = features // 3
+    tile = tile_of(part)
     steps = features // tile
     part_steps = part // tile
 
@@ -409,8 +495,7 @@
 
         @pl.when(step == 0)
         def _():
-            for s in range(count):
-                rows_ref[s * local_rows : (s + 1) * local_rows, :] = refs[s][...]
+            fill_rows(rows_ref, refs[:count], micro_count)
             totals[...] = jnp.zeros_like(totals)
 
         raw = dot_plain(rows_ref[...], weight_ref[...])
@@ -430,8 +515,8 @@
         body,
         steps,
         [shape_of((rows, width), low), shape_of((rows, features), full), shape_of((2, rows), full)],
-        [fixed((local_rows, width))] * count + [column_tile(width)],
-        [fixed((rows, width)), column_tile(rows), fixed((2, rows))],
+        [fixed((local_rows, width))] * count + [column_tile(width, tile)],
+        [fixed((rows, width)), column_tile(rows, tile), fixed((2, rows))],
         *token_slots,
         weights,
         scratch=[pltpu.VMEM((rows, 128), full)],
@@ -439,35 +524,33 @@
     )
 
 
-def project_output(mixed, weights_t, micro_count, head_size):
-    rows = mixed.shape[1]
+def project_output(mixed, weights_t, head_size):
+    micro_count, rows, features = mixed.shape
     width = weights_t.shape[0]
-    local_rows = rows // head_size
+    local_rows = micro_count * rows // head_size
 
     def body(mixed_ref, weight_ref, *out_refs):
-        for m in range(micro_count):
-            values = dot_right_t(mixed_ref[m], weight_ref[...])
-            put_slots(out_refs[m * head_size : (m + 1) * head_size], values)
+        values = dot_right_t(mixed_ref[...].reshape(micro_count * rows, features), weight_ref[...])
+        put_slots(out_refs, values, micro_count)
 
     return call_whole(
         body,
-        [shape_of((local_rows, width), low)] * (micro_count * head_size),
+        [shape_of((local_rows, width), low)] * head_size,
         mixed,
         weights_t,
         scalars=0,
-        flops=2 * micro_count * rows * width * weights_t.shape[1],
-    )
-
-
-def project_mixed_grad(grad_slots, weights_t):
+        flops=2 * micro_count * rows * width * features,
+    )
+
+
+def project_mixed_grad(grad_slots, weights_t, micro_count):
     count = len(grad_slots)
     local_rows, width = grad_slots[0].shape
-    rows, features = count * local_rows, weights_t.shape[1]
+    rows, features = len(layout_of(count)) * local_rows, weights_t.shape[1]
 
     def body(*refs):
         weight_ref, rows_ref, out_ref = refs[count:]
-        for s in range(count):
-            rows_ref[s * local_rows : (s + 1) * local_rows, :] = refs[s][...]
+        fill_rows(rows_ref, refs[:count], micro_count)
         out_ref[...] = dot_plain(rows_ref[...], weight_ref[...]).astype(low)
 
     return call_whole(
@@ -505,11 +588,12 @@
     )
 
 
-def project_input_grad(raw, scales, dots, gains, grads, grad_value, weights, slot_count):
+def project_input_grad(raw, scales, dots, gains, grads, grad_value, weights, slot_count, micro_count):
     rows, features = grad_value.shape[0], weights.shape[1]
     width = features // 3
     out_width = weights.shape[0]
     local_rows = rows // slot_count
+    tile = tile_of(out_width)
     steps = out_width // tile
 
     def body(raw_ref, scale_ref, dot_ref, gain_ref, grad_ref, value_ref, weight_ref, low_ref, *out_refs):
@@ -521,14 +605,16 @@
                 hat = raw_ref[:, cut] * scale
                 grad_hat = grad_ref[:, cut] * gain_ref[:, cut]
                 low_ref[:, cut] = (scale * (grad_hat - hat * dot_ref[:, k : k + 1])).astype(low)
-            low_ref[:, 2 * width :] = value_ref[...]
-
-        put_slots(out_refs, dot_right_t(low_ref[...], weight_ref[...]))
+
+        terms = dot_right_t(low_ref[...], weight_ref[:, : 2 * width])
+        terms += dot_right_t(value_ref[...], weight_ref[:, 2 * width :])
+        put_slots(out_refs, terms, micro_count)
 
     return call_grid(
         body,
         steps,
-        [shape_of((rows, features), low)] + [shape_of((local_rows, out_width), low)] * slot_count,
+        [shape_of((rows, 2 * width), low)]
+        + [shape_of((local_rows, out_width), low)] * slot_count,
         [
             fixed((rows, 2 * width)),
             fixed((rows, 2)),
@@ -538,7 +624,7 @@
             fixed((rows, width)),
             pl.BlockSpec((tile, features), lambda i: (i, 0)),
         ],
-        [fixed((rows, features))]
+        [fixed((rows, 2 * width))]
         + [pl.BlockSpec((local_rows, tile), lambda i: (0, i))] * slot_count,
         raw,
         scales,
@@ -551,22 +637,27 @@
     )
 
 
-def weight_term_slots(me, left, right, blocks):
-    rows, width = left.shape
-    features = right.shape[1]
+def weight_term_slots(me, lefts, rights, blocks):
+    n = len(lefts)
+    rows, width = lefts[0].shape
+    features = rights[0].shape[1]
     part = width // blocks
     half = blocks // 2
 
-    def body(me_ref, left_ref, right_ref, odd_ref, even_ref, left_t):
+    def body(me_ref, *refs):
+        odd_ref, even_ref, left_t, right_all = refs[2 * n :]
         step = pl.program_id(0)
 
         @pl.when(step == 0)
         def _():
-            left_t[...] = jnp.transpose(left_ref[...])
+            for m in range(n):
+                cut = slice(m * rows, (m + 1) * rows)
+                left_t[:, cut] = jnp.transpose(refs[m][...])
+                right_all[cut, :] = refs[n + m][...]
 
         slot = jnp.where(step < half, 2 * step + 1, 2 * step - blocks)
         place = pl.multiple_of((me_ref[0] ^ slot) * part, part)
-        term = dot_plain(left_t[pl.ds(place, part), :], right_ref[...]).astype(low)
+        term = dot_plain(left_t[pl.ds(place, part), :], right_all[...]).astype(low)
 
         @pl.when(step < half)
         def _():
@@ -580,33 +671,27 @@
         body,
         blocks,
         [shape_of((half, part, features), low)] * 2,
-        [scalar_spec, fixed((rows, width)), fixed((rows, features))],
+        [scalar_spec] + [fixed((rows, width))] * n + [fixed((rows, features))] * n,
         [
             pl.BlockSpec((1, part, features), lambda i: (jnp.minimum(i, half - 1), 0, 0)),
             pl.BlockSpec((1, part, features), lambda i: (jnp.maximum(i - half, 0), 0, 0)),
         ],
         me,
-        left,
-        right,
-        scratch=[pltpu.VMEM((width, rows), low)],
-        flops=2 * rows * width * features,
-    )
-
-
-def to_owner(me, left, right):
-    blocks = lax.axis_size("blk")
-    odd, even = weight_term_slots(me, left, right, blocks)
-    arrived = lax.ppermute(odd, "blk", xor_pairs(blocks, 1))
-    pairs = [
-        (even[k].astype(full) + arrived[k].astype(full)) for k in range(blocks // 2)
-    ]
-    return sum(
-        [pairs[0]]
-        + [
-            lax.ppermute(pairs[k].astype(low), "blk", xor_pairs(blocks, 2 * k)).astype(full)
-            for k in range(1, blocks // 2)
-        ]
-    )
+        *lefts,
+        *rights,
+        scratch=[pltpu.VMEM((width, n * rows), low), pltpu.VMEM((n * rows, features), low)],
+        flops=2 * n * rows * width * features,
+    )
+
+
+def to_owner(terms, *others):
+    odd, even = terms
+    blocks = 2 * even.shape[0]
+    arrived = swap_cores(odd)
+    even = after(even, *others)
+    pairs = [even[k].astype(full) + arrived[k].astype(full) for k in range(blocks // 2)]
+    slots = exchange_chips([pairs[0]] + [pair.astype(low) for pair in pairs[1:]])
+    return sum(slot.astype(full) for slot in slots)
 
 
 def send_views(me, raw, scales, gains, tables, heads_local):
@@ -947,7 +1032,7 @@
             [mixed.reshape(self.rows, -1).astype(low) for mixed, norm in results]
         )
 
-    def backward(self, grad_mixed):
+    def backward(self, grad_mixed, *others):
         norms, values = [], []
         for m, (view, mark, stacked) in enumerate(self.sets):
             grad_query, terms = gathered_backward(
@@ -988,10 +1073,11 @@
             self.heads,
         )
 
-    def backward(self, grad_mixed):
+    def backward(self, grad_mixed, *others):
         grad_slots = exchange_slots(
             split_mixed(self.me, grad_mixed, self.blocks, self.heads), "blk"
         )
+        grad_slots = [after(grad_slots[0], *others)] + grad_slots[1:]
         back_slots = exchange_slots(
             attention_backward(self.me, self.slots, grad_slots, *self.kept, *self.marks), "blk"
         )
@@ -1021,8 +1107,6 @@
     group_rows = local_rows * head_size
     width = query_weight.shape[1]
     heads_local = width // HD
-    hidden_width = gate_weight.shape[1]
-    micros = range(micro_count)
     block_index = lax.axis_index("blk")
     head_index = lax.axis_index("head")
     me = block_index.astype(jnp.int32).reshape(1)
@@ -1039,19 +1123,20 @@
     output_full_t = gather_weights(output_weight.T)
     ffn_full = gather_weights(gate_weight, up_weight, down_weight.T)
 
+    def by_micro(values):
+        return values.reshape(micro_count, -1, values.shape[-1])
+
+    def all_rows(values):
+        return values.reshape(-1, values.shape[-1])
+
+    def sum_token_heads(values):
+        values = values.reshape(2 * micro_count, group_rows)
+        return sum_heads(values).reshape(2, micro_count * group_rows).T
+
+    token_rows, raw, squares = project_qkv(gather_parts(all_rows(tokens)), qkv_full, micro_count)
     codes = jnp.concatenate(gather_slots(segments * 2 + padding, "head"), axis=1)
     codes = gather_doubling(codes, "blk")
     codes = codes[block_index ^ jnp.arange(blocks, dtype=jnp.int32)].swapaxes(0, 1)
-
-    token_slots = [slot for m in micros for slot in gather_slots(tokens[m], "head")]
-    token_rows, raw, squares = project_qkv(token_slots, qkv_full)
-
-    def by_micro(values):
-        return values.reshape(micro_count, group_rows, -1)
-
-    def sum_token_heads(values):
-        values = values.reshape(2 * micro_count, group_rows)
-        return sum_heads(values).reshape(2, micro_count * group_rows).T
 
     scales = lax.rsqrt(sum_token_heads(squares) / model_width + epsilon)
     gain_row = jnp.concatenate([query_gain, key_gain])[None, :]
@@ -1062,75 +1147,63 @@
     )
     mixed = attention.forward()
 
-    attn_slots = project_output(mixed, output_full_t, micro_count, head_size)
     attn_gain, ffn_gain = attn_gain[None, :], ffn_gain[None, :]
-    outputs, kept = [], []
-    grad_hiddens, grad_attn_slots = [], []
-    gain_grads = []
-    for m in micros:
-        arrived = exchange_slots(attn_slots[m * head_size : (m + 1) * head_size], "head")
-        hidden, hidden_low, attn_hat, attn_scale = after_attention(arrived, tokens[m], attn_gain)
-        (hidden_rows, gate, up, middle), slots = ffn_forward(
-            gather_slots(hidden_low, "head"), ffn_full
-        )
-        output, grad_down, ffn_gain_grad = after_ffn(
-            exchange_slots(slots, "head"), hidden, cotangent[m], ffn_gain
-        )
-        outputs.append(output)
-        (grad_rows, grad_gate, grad_up), slots = ffn_backward(
-            gather_slots(grad_down, "head"), gate, up, ffn_full
-        )
-        kept.append((hidden_rows, grad_rows, grad_gate, grad_up, middle))
-        grad_hidden, grad_attn, attn_gain_grad = before_attention(
-            exchange_slots(slots, "head"), cotangent[m], attn_hat, attn_scale, attn_gain
-        )
-        grad_hiddens.append(grad_hidden)
-        grad_attn_slots += gather_slots(grad_attn, "head")
-        gain_grads.append(jnp.concatenate([attn_gain_grad, ffn_gain_grad], axis=1))
-
-    ffn_terms = ffn_weight_terms(*zip(*kept))
-    ffn_grad = lax.psum_scatter(ffn_terms, "blk", scatter_dimension=0, tiled=True).astype(full)
-    gate_grad, up_grad, down_grad_t = jnp.split(ffn_grad, 3, axis=1)
-
-    grad_attn_rows, grad_mixed = project_mixed_grad(grad_attn_slots, output_full_t)
-    output_grad = to_owner(me, grad_attn_rows, mixed.reshape(-1, width)).T
-    grad_norm, grad_value = attention.backward(by_micro(grad_mixed))
-    grad_norm = grad_norm.reshape(-1, 2 * width)
-    grad_value = grad_value.reshape(-1, width)
+    token_own, grad_own = all_rows(tokens), all_rows(cotangent)
+    arrived = reduce_parts(project_output(mixed, output_full_t, head_size))
+    hidden, hidden_low, attn_hat, attn_scale = after_attention(arrived, token_own, attn_gain)
+    (hidden_rows, gate, up, middle_rows), slots = ffn_forward(
+        gather_parts(hidden_low), ffn_full, micro_count
+    )
+    output, grad_down, ffn_gain_grad = after_ffn(reduce_parts(slots), hidden, grad_own, ffn_gain)
+    (grad_rows, grad_gate, grad_up), slots = ffn_backward(
+        gather_parts(grad_down), gate, up, ffn_full, micro_count
+    )
+    arrived = reduce_parts(slots)
+    grad_hidden, grad_attn, attn_gain_grad = before_attention(
+        arrived, grad_own, attn_hat, attn_scale, attn_gain
+    )
+    ffn_terms = ffn_weight_term([], 2, [grad_rows], [middle_rows])
+    ffn_terms = ffn_weight_term([ffn_terms], 0, [hidden_rows], [grad_gate])
+    ffn_terms = ffn_weight_term([ffn_terms], 1, [hidden_rows], [grad_up])
+    ffn_terms = after(ffn_terms, *arrived)
+    ffn_grads = widen_ffn(
+        lax.psum_scatter(ffn_terms, "blk", scatter_dimension=0, tiled=True)
+    )
+    norm_gain_grads = sum_doubling(
+        jnp.concatenate([attn_gain_grad, ffn_gain_grad], axis=1)[0], "blk"
+    )
+    norm_gain_grads = sum_doubling(norm_gain_grads, "head")
+
+    grad_attn_rows, grad_mixed = project_mixed_grad(
+        gather_parts(grad_attn), output_full_t, micro_count
+    )
+    output_terms = weight_term_slots(me, [grad_attn_rows], [all_rows(mixed)], blocks)
+    grad_norm, grad_value = attention.backward(by_micro(grad_mixed), *output_terms)
+    grad_norm, grad_value = all_rows(grad_norm), all_rows(grad_value)
     dots, qk_gain_grad = norm_gradients(raw, scales, gain_row, grad_norm)
-    mean_dots = sum_token_heads(dots) / model_width
+    mean_dots = sum_token_heads(after(dots, norm_gain_grads)) / model_width
+    value_terms = weight_term_slots(me, [token_rows], [grad_value], blocks)
     results = project_input_grad(
-        raw, scales, mean_dots, gain_row, grad_norm, grad_value, qkv_full, micro_count * head_size
-    )
-    qkv_grad = to_owner(me, token_rows, results[0])
-    input_grads = [
-        sum(
-            slot.astype(full)
-            for slot in exchange_slots(
-                results[1 + m * head_size : 1 + (m + 1) * head_size], "head"
-            )
-        )
-        + grad_hiddens[m]
-        for m in micros
-    ]
-
-    rows_grad = sum_doubling(jnp.concatenate([sum(gain_grads), qk_gain_grad], axis=1)[0], "blk")
-    qk_gain_grad = rows_grad[2 * model_width :]
-    rows_grad = sum_doubling(rows_grad[: 2 * model_width], "head")
+        raw, scales, mean_dots, gain_row, grad_norm, grad_value, qkv_full, head_size, micro_count
+    )
+    input_grad = sum_full(reduce_parts(results[1:])) + grad_hidden
+    output_grad = to_owner(output_terms).T
+    value_grad = to_owner(value_terms)
+    qk_grad = to_owner(weight_term_slots(me, [token_rows], [results[0]], blocks), *ffn_grads)
+
+    qk_gain_grad = sum_doubling(qk_gain_grad[0], "blk")
     return (
-        jnp.stack(outputs),
-        jnp.stack(input_grads),
-        qkv_grad[:, :width],
-        qkv_grad[:, width : 2 * width],
-        qkv_grad[:, 2 * width :],
+        by_micro(output),
+        by_micro(input_grad),
+        qk_grad[:, :width],
+        qk_grad[:, width:],
+        value_grad,
         output_grad,
         qk_gain_grad[:width],
         qk_gain_grad[width:],
-        rows_grad[:model_width],
-        gate_grad,
-        up_grad,
-        down_grad_t.T,
-        rows_grad[model_width:],
+        norm_gain_grads[:model_width],
+        *ffn_grads,
+        norm_gain_grads[model_width:],
     )
 
 

time: 739 us -> 676 us (0.915)
  starting transfers between devices: 218 us -> 124 us
  waiting for transfers between devices: 242 us -> 310 us
  Pallas kernels: 203 us -> 177 us
  local copies, waits for them, and re-layouts: 33.3 us -> 18 us
    ppermute x8 -> x44, waiting for transfers between devices: 29.2 us -> 225 us  [the longest x32 199 us: send_rows(): return lax.ppermute(values, 'head', pairs)]
    ppermute x33 -> x9, starting transfers between devices: 126 us -> 14 us  [gather_slots(): lax.ppermute(values, axis, xor_pairs(size, s))]
    ppermute x52 -> x28, waiting for transfers between devices: 137 us -> 54.2 us  [exchange_slots(): lax.ppermute(slots[s], axis, xor_pairs(size, s))]
    ppermute x8 -> x44, starting transfers between devices: 7.05 us -> 69.3 us  [the longest x32 56.5 us: send_rows(): return lax.ppermute(values, 'head', pairs)]
    ppermute x33 -> x9, waiting for transfers between devices: 60.5 us -> 6.04 us  [gather_slots(): lax.ppermute(values, axis, xor_pairs(size, s))]
    pallas_call x9 -> x7, Pallas kernels: 141 us -> 87.5 us  [call_grid(): pl.pallas_call(body, grid=(steps,), out_shape=outs, in_specs=in_specs, ou...]
    ppermute x52 -> x28, starting transfers between devices: 75.1 us -> 31 us  [exchange_slots(): lax.ppermute(slots[s], axis, xor_pairs(size, s))]
    pallas_call x0 -> x3, Pallas kernels: none -> 27.4 us  [ffn_weight_term(): pl.pallas_call(body, grid=(steps,), out_shape=shape, in_specs=[fixed((row...]
  transfers between devices with their start and end apart: 105 -> 96, of which waited for: 46 -> 51; matrix products, arithmetic and copies ran while one was open for 4% -> 5% of each run, Pallas kernels for 21% -> 19%
where the time goes in v3:
time: 676 us; the launch traced here: 671 us
  waiting for transfers between devices  310 us (46%)
  Pallas kernels  177 us (26%)
  starting transfers between devices  124 us (18%)
  other arithmetic  27 us (4%)
  local copies, waits for them, and re-layouts  18 us (3%)
  between operations  14.9 us (2%)
    ppermute x32, waiting for transfers between devices, send_rows(): return lax.ppermute(values, 'head', pairs)  199 us
    pallas_call x7, Pallas kernels, call_grid(): pl.pallas_call(body, grid=(steps,), out_shape=outs, in_specs=in_specs, ou...  87.5 us
    pallas_call x13, Pallas kernels, call_whole(): pl.pallas_call(body, out_shape=outs, in_specs=[pl.BlockSpec(memory_space=...  62.2 us
    ppermute x32, starting transfers between devices, send_rows(): return lax.ppermute(values, 'head', pairs)  56.5 us
    ppermute x28, waiting for transfers between devices, exchange_slots(): lax.ppermute(slots[s], axis, xor_pairs(size, s))  54.2 us
    ppermute x28, starting transfers between devices, exchange_slots(): lax.ppermute(slots[s], axis, xor_pairs(size, s))  31 us
    pallas_call x3, Pallas kernels, ffn_weight_term(): pl.pallas_call(body, grid=(steps,), out_shape=shape, in_specs=[fixed((row...  27.4 us
    ppermute x9, waiting for transfers between devices, exchange_chips(): lax.ppermute(slots[m], 'blk', xor_pairs(size, 2 * m))  26.1 us
  transfers between devices with their start and end apart: 96, of which 51 were waited for; matrix products, arithmetic and copies ran while one was open for 5% of the time, Pallas kernels for 19%

profile of v3, /device:TPU:0, one launch (start us, length us, event | category | flops | bytes accessed | tf_op | source)
XLA Modules:
  0.0 671.0 jit_solution(11157703143403473291)
XLA Ops:
  14.6 5.0 collective-permute-start.16
  20.9 4.1 collective-permute-start.1
  27.1 31.5 %collective-permute-done.1.refs_2_ = bf16[128,2048]{1,0:T(8,128)(2,1)S(1)} collective-permute-done((bf16[128,2048]{1,0:T(8,128)(2,1)S(1)}, bf16[128,2048]{1,0:T(8,128)(2,1)S(1)}, u32[]{:S(2)}, u32[]{:S(2)}) %collective-permute-start.1) | collective-permute-done | bytes 524320 | tf_op jit(solution)/shard_map/ppermute | solution.py:87
  66.3 6.5 collective-permute-done.3.refs_4_
  72.7 9.2 %shard_map.246 = (bf16[512,2048]{1,0:T(8,128)(2,1)}, f32[512,1536]{1,0:T(8,128)}, f32[2,512]{1,0:T(2,128)}) custom-call(bf16[128,2048]{1,0:T(8,128)(2,1)} %bitcast.92, bf16[128,2048]{1,0:T(8,128)(2,1)} %copy-done.59, bf16[128,2048]{1,0:T(8,128)(2,1)} %copy-done.58, bf16[128,2048]{1,0:T(8,128)(2,1)} %copy-done.57, ...), custom_call_target="tpu_custom_call" | custom-call | flops 3221225472 | bytes 14159872 | tf_op jit(solution)/shard_map/pallas_call | solution.py:175
  91.8 4.9 shard_map.247
  108.5 5.2 collective-permute-done.9.refs_3_
  113.7 11.1 %collective-permute-done.11.refs_5_ = bf16[256,384]{1,0:T(8,128)(2,1)S(1)} collective-permute-done((bf16[256,384]{1,0:T(8,128)(2,1)}, bf16[256,384]{1,0:T(8,128)(2,1)S(1)}, u32[]{:S(2)}, u32[]{:S(2)}) %collective-permute-start.11) | collective-permute-done | bytes 196640 | tf_op jit(solution)/shard_map/ppermute | solution.py:55
  124.8 5.3 collective-permute-done.13.refs_7_
  130.8 8.8 %shard_map.248 = (bf16[256,128]{1,0:T(8,128)(2,1)}, bf16[256,128]{1,0:T(8,128)(2,1)}, bf16[256,128]{1,0:T(8,128)(2,1)}, bf16[256,128]{1,0:T(8,128)(2,1)}, bf16[2...) custom-call(s32[1]{0:T(128)} %bitcast.me_ref, ...), custom_call_target="tpu_custom_call" | custom-call | flops 1073741824 | bytes 3186692 | tf_op jit(solution)/shard_map/pallas_call | solution.py:158
  157.6 4.3 shard_map.250
  167.9 8.6 %collective-permute-done.29 = bf16[128,2048]{1,0:T(8,128)(2,1)S(1)} collective-permute-done((bf16[128,2048]{1,0:T(8,128)(2,1)}, bf16[128,2048]{1,0:T(8,128)(2,1)S(1)}, u32[]{:S(2)}, u32[]{:S(2)}) %collective-permute-start.29) | collective-permute-done | bytes 524320 | tf_op jit(solution)/shard_map/ppermute | solution.py:87
  177.6 4.0 collective-permute-start.30
  181.6 6.1 collective-permute-done.27.refs_1_
  187.7 16.0 %collective-permute-done.30.refs_3_ = bf16[128,2048]{1,0:T(8,128)(2,1)S(1)} collective-permute-done((bf16[128,2048]{1,0:T(8,128)(2,1)S(1)}, bf16[128,2048]{1,0:T(8,128)(2,1)S(1)}, u32[]{:S(2)}, u32[]{:S(2)}) %collective-permute-start.30) | collective-permute-done | bytes 524320 | tf_op jit(solution)/shard_map/ppermute | solution.py:87
  209.1 4.8 collective-permute-start.31
  213.8 18.1 %collective-permute-done.32.refs_2_ = bf16[128,2048]{1,0:T(8,128)(2,1)S(1)} collective-permute-done((bf16[128,2048]{1,0:T(8,128)(2,1)}, bf16[128,2048]{1,0:T(8,128)(2,1)S(1)}, u32[]{:S(2)}, u32[]{:S(2)}) %collective-permute-start.32) | collective-permute-done | bytes 524320 | tf_op jit(solution)/shard_map/ppermute | solution.py:87
  234.9 12.7 %collective-permute-done.34.refs_4_ = bf16[128,2048]{1,0:T(8,128)(2,1)S(1)} collective-permute-done((bf16[128,2048]{1,0:T(8,128)(2,1)S(1)}, bf16[128,2048]{1,0:T(8,128)(2,1)S(1)}, u32[]{:S(2)}, u32[]{:S(2)}) %collective-permute-start.34) | collective-permute-done | bytes 524320 | tf_op jit(solution)/shard_map/ppermute | solution.py:87
  248.4 22.5 %shard_map.252 = (bf16[512,2048]{1,0:T(8,128)(2,1)}, bf16[512,2048]{1,0:T(8,128)(2,1)}, bf16[512,2048]{1,0:T(8,128)(2,1)}, bf16[512,2048]{1,0:T(8,128)(2,1)}, bf...) custom-call(bf16[128,2048]{1,0:T(8,128)(2,1)} %get-tuple-element.125, ...), custom_call_target="tpu_custom_call" | custom-call | flops 12884901888 | bytes 88604672 | tf_op jit(solution)/shard_map/pallas_call | solution.py:175
  274.9 10.1 %collective-permute-done.37 = bf16[128,2048]{1,0:T(8,128)(2,1)S(1)} collective-permute-done((bf16[128,2048]{1,0:T(8,128)(2,1)}, bf16[128,2048]{1,0:T(8,128)(2,1)S(1)}, u32[]{:S(2)}, u32[]{:S(2)}) %collective-permute-start.37) | collective-permute-done | bytes 524320 | tf_op jit(solution)/shard_map/ppermute | solution.py:87
  289.2 7.0 %collective-permute-done.35.refs_1_ = bf16[128,2048]{1,0:T(8,128)(2,1)S(1)} collective-permute-done((bf16[128,2048]{1,0:T(8,128)(2,1)}, bf16[128,2048]{1,0:T(8,128)(2,1)S(1)}, u32[]{:S(2)}, u32[]{:S(2)}) %collective-permute-start.35) | collective-permute-done | bytes 524320 | tf_op jit(solution)/shard_map/ppermute | solution.py:87
  296.3 12.7 %collective-permute-done.38.refs_3_ = bf16[128,2048]{1,0:T(8,128)(2,1)S(1)} collective-permute-done((bf16[128,2048]{1,0:T(8,128)(2,1)S(1)}, bf16[128,2048]{1,0:T(8,128)(2,1)S(1)}, u32[]{:S(2)}, u32[]{:S(2)}) %collective-permute-start.38) | collective-permute-done | bytes 524320 | tf_op jit(solution)/shard_map/ppermute | solution.py:87
  314.3 4.7 collective-permute-start.39
  319.0 18.3 %collective-permute-done.40.refs_2_ = bf16[128,2048]{1,0:T(8,128)(2,1)S(1)} collective-permute-done((bf16[128,2048]{1,0:T(8,128)(2,1)}, bf16[128,2048]{1,0:T(8,128)(2,1)S(1)}, u32[]{:S(2)}, u32[]{:S(2)}) %collective-permute-start.40) | collective-permute-done | bytes 524320 | tf_op jit(solution)/shard_map/ppermute | solution.py:87
  338.6 10.6 %collective-permute-done.42.refs_4_ = bf16[128,2048]{1,0:T(8,128)(2,1)S(1)} collective-permute-done((bf16[128,2048]{1,0:T(8,128)(2,1)S(1)}, bf16[128,2048]{1,0:T(8,128)(2,1)S(1)}, u32[]{:S(2)}, u32[]{:S(2)}) %collective-permute-start.42) | collective-permute-done | bytes 524320 | tf_op jit(solution)/shard_map/ppermute | solution.py:87
  350.0 24.0 %shard_map.254 = (bf16[512,2048]{1,0:T(8,128)(2,1)}, bf16[512,2048]{1,0:T(8,128)(2,1)}, bf16[512,2048]{1,0:T(8,128)(2,1)}, bf16[128,2048]{1,0:T(8,128)(2,1)}, bf...) custom-call(bf16[128,2048]{1,0:T(8,128)(2,1)} %get-tuple-element.132.refs_0_, ...), custom_call_target="tpu_custom_call" | custom-call | flops 12884901888 | bytes 90701824 | tf_op jit(solution)/shard_map/pallas_call | solution.py:175
  378.5 9.2 %shard_map.264.refs_2_ = bf16[2048,6144]{1,0:T(8,128)(2,1)} custom-call(bf16[512,2048]{1,0:T(8,128)(2,1)} %get-tuple-element.182.refs_0_, bf16[512,2048]{1,0:T(8,128)(2,1)} %get-tuple-element.183.refs_1_), custom_call_target="tpu_custom_call" | custom-call | flops 4294967296 | bytes 10485760 | tf_op jit(solution)/shard_map/pallas_call | solution.py:370
  391.7 9.1 %shard_map.265.refs_2_ = bf16[2048,6144]{1,0:T(8,128)(2,1)} custom-call(bf16[512,2048]{1,0:T(8,128)(2,1)} %get-tuple-element.179.refs_0_, bf16[512,2048]{1,0:T(8,128)(2,1)} %get-tuple-element.181.refs_1_, bf16[2048,6144]{1,0:T(8,128)(2,1)} %shard_map.264.refs_2_), custom_call_target="tpu_custom_call", output_to_operand_aliasing={{}: (2, {})} | custom-call | flops 4294967296 | bytes 10485760 | tf_op jit(solution)/shard_map/pallas_call | solution.py:370
  400.8 9.1 %shard_map.266 = bf16[2048,6144]{1,0:T(8,128)(2,1)} custom-call(bf16[512,2048]{1,0:T(8,128)(2,1)} %get-tuple-element.179.refs_0_, bf16[512,2048]{1,0:T(8,128)(2,1)} %get-tuple-element.180.refs_1_, bf16[2048,6144]{1,0:T(8,128)(2,1)} %shard_map.265.refs_2_), custom_call_target="tpu_custom_call", output_to_operand_aliasing={{}: (2, {})} | custom-call | flops 4294967296 | bytes 10485760 | tf_op jit(solution)/shard_map/pallas_call | solution.py:370
  415.7 4.7 collective-permute-start.47
  420.5 15.9 %collective-permute-done.48.refs_2_ = bf16[128,2048]{1,0:T(8,128)(2,1)S(1)} collective-permute-done((bf16[128,2048]{1,0:T(8,128)(2,1)}, bf16[128,2048]{1,0:T(8,128)(2,1)S(1)}, u32[]{:S(2)}, u32[]{:S(2)}) %collective-permute-start.48) | collective-permute-done | bytes 524320 | tf_op jit(solution)/shard_map/ppermute | solution.py:87
  437.7 10.6 %collective-permute-done.50.refs_4_ = bf16[128,2048]{1,0:T(8,128)(2,1)S(1)} collective-permute-done((bf16[128,2048]{1,0:T(8,128)(2,1)S(1)}, bf16[128,2048]{1,0:T(8,128)(2,1)S(1)}, u32[]{:S(2)}, u32[]{:S(2)}) %collective-permute-start.50) | collective-permute-done | bytes 524320 | tf_op jit(solution)/shard_map/ppermute | solution.py:87
  449.0 5.0 shard_map.256
  466.5 7.1 %shard_map.258 = (bf16[4,256,512]{2,1,0:T(8,128)(2,1)}, bf16[4,256,512]{2,1,0:T(8,128)(2,1)}) custom-call(s32[1]{0:T(128)} %bitcast.me_ref, bf16[512,2048]{1,0:T(8,128)(2,1)} %get-tuple-element.144.refs_0_, bf16[512,512]{1,0:T(8,128)(2,1)} %bitcast.100), custom_call_target="tpu_custom_call" | custom-call | flops 1073741824 | bytes 4718596 | tf_op jit(solution)/shard_map/pallas_call | solution.py:175
  474.3 11.0 %shard_map.259 = (bf16[256,384]{1,0:T(8,128)(2,1)}, bf16[256,384]{1,0:T(8,128)(2,1)}, bf16[256,384]{1,0:T(8,128)(2,1)}, bf16[256,384]{1,0:T(8,128)(2,1)}, bf16[2...) custom-call(s32[1]{0:T(128)} %bitcast.me_ref, ...), custom_call_target="tpu_custom_call" | custom-call | flops 2684354560 | bytes 4759556 | tf_op jit(solution)/shard_map/pallas_call | solution.py:158
  489.9 9.3 %collective-permute-done.66 = f32[4096]{0:T(1024)S(1)} collective-permute-done((f32[4096]{0:T(1024)S(1)}, f32[4096]{0:T(1024)S(1)}, u32[]{:S(2)}, u32[]{:S(2)}) %collective-permute-start.66) | collective-permute-done | bytes 16416 | tf_op jit(solution)/shard_map/ppermute | solution.py:72
  514.5 5.7 collective-permute-done.60.refs_3_
  521.4 16.1 %collective-permute-done.62.refs_5_ = bf16[256,384]{1,0:T(8,128)(2,1)S(1)} collective-permute-done((bf16[256,384]{1,0:T(8,128)(2,1)}, bf16[256,384]{1,0:T(8,128)(2,1)S(1)}, u32[]{:S(2)}, u32[]{:S(2)}) %collective-permute-start.62) | collective-permute-done | bytes 196640 | tf_op jit(solution)/shard_map/ppermute | solution.py:55
  541.8 4.0 shard_map.261
  557.0 9.3 %shard_map.262 = (bf16[512,1024]{1,0:T(8,128)(2,1)}, bf16[128,2048]{1,0:T(8,128)(2,1)}, bf16[128,2048]{1,0:T(8,128)(2,1)}, bf16[128,2048]{1,0:T(8,128)(2,1)}, bf16[128,2048]{1,0:T(8,128)(2,1)}) custom-call(f32[512,1536]{1,0:T(8,128)} %get-tuple-element.103.raw_ref, f32[512,2]{1,0:T(8,128)} %bitcast.84, f32[512,2]{1,0:T(8,128)} %multiply_bitcast_fusion.dot_ref, ...), custom_call_target="tpu_custom_call" | custom-call | flops 3221225472 | bytes 15216640 | tf_op jit(solution)/shard_map/pallas_call | solution.py:175
  566.3 8.6 %shard_map.263 = (bf16[4,256,1024]{2,1,0:T(8,128)(2,1)}, bf16[4,256,1024]{2,1,0:T(8,128)(2,1)}) custom-call(s32[1]{0:T(128)} %bitcast.me_ref, bf16[512,2048]{1,0:T(8,128)(2,1)} %get-tuple-element.176.refs_0_, bf16[512,1024]{1,0:T(8,128)(2,1)} %get-tuple-element.177.refs_1_), custom_call_target="tpu_custom_call" | custom-call | flops 2147483648 | bytes 7340036 | tf_op jit(solution)/shard_map/pallas_call | solution.py:175
  583.8 6.8 %shard_map.268 = (bf16[4,256,512]{2,1,0:T(8,128)(2,1)}, bf16[4,256,512]{2,1,0:T(8,128)(2,1)}) custom-call(s32[1]{0:T(128)} %bitcast.me_ref, bf16[512,2048]{1,0:T(8,128)(2,1)} %get-tuple-element.176.refs_0_, bf16[512,512]{1,0:T(8,128)(2,1)} %bitcast.98), custom_call_target="tpu_custom_call" | custom-call | flops 1073741824 | bytes 4718596 | tf_op jit(solution)/shard_map/pallas_call | solution.py:175
  596.3 4.3 collective-permute-done.86
  602.1 3.9 collective-permute-done.88
  614.3 5.1 shard_map.267
  627.6 9.7 %collective-permute-done.76 = bf16[128,2048]{1,0:T(8,128)(2,1)} collective-permute-done((bf16[128,2048]{1,0:T(8,128)(2,1)}, bf16[128,2048]{1,0:T(8,128)(2,1)}, u32[]{:S(2)}, u32[]{:S(2)}) %collective-permute-start.76) | collective-permute-done | bytes 524320 | tf_op jit(solution)/shard_map/ppermute | solution.py:87
  645.1 5.4 collective-permute-done.80
  650.6 11.1 %collective-permute-done.79 = bf16[256,1024]{1,0:T(8,128)(2,1)S(1)} collective-permute-done((bf16[256,1024]{1,0:T(8,128)(2,1)S(1)}, bf16[256,1024]{1,0:T(8,128)(2,1)S(1)}, u32[]{:S(2)}, u32[]{:S(2)}) %collective-permute-start.79) | collective-permute-done | bytes 524320 | tf_op jit(solution)/shard_map/ppermute | solution.py:116
  (400 shorter events, 198.9 us)
Async XLA Ops:
  7.2 65.5 %all-gather.4.cloned.1.call-start = ((), (), s32[]{:S(2)}) async-start(), calls=%async_computation.1 | async-start | bytes 7077888 | tf_op jit(solution)/shard_map/all_gather | solution.py:1120
  9.4 148.2 %all-gather.6.cloned.1.call-start = ((), (), s32[]{:S(2)}) async-start(), calls=%async_computation.2 | async-start | bytes 2359296 | tf_op jit(solution)/shard_map/all_gather | solution.py:1120
  10.3 237.3 %all-gather.8.cloned.1.call-start = ((), (), s32[]{:S(2)}) async-start(), calls=%async_computation.3 | async-start | bytes 28311552 | tf_op jit(solution)/shard_map/all_gather | solution.py:1120
  13.9 600.4 %reduce-scatter.2.cloned.1.call-start = ((), (), s32[]{:S(2)}) async-start(), calls=%async_computation.4 | async-start | bytes 28311552 | tf_op jit(solution)/shard_map/reduce_scatter | solution.py:1170
  19.6 40.2 %collective-permute-start.15 = (s32[2,64]{1,0:T(2,128)S(1)}, s32[2,64]{1,0:T(2,128)S(1)}, u32[]{:S(2)}, u32[]{:S(2)}) collective-permute-start(s32[2,64]{1,0:T(2,128)S(1)} %multiply_add_fusion), channel_id=1, source_target_pairs={{0,2},{1,3},{2,0},{3,1},{4,6},{5,7},{6,4},{7,5},{8,10},{9,11},{10,... | collective-permute-start | bytes 1544 | tf_op jit(solution)/shard_map/ppermute | solution.py:49
  19.6 40.2 %collective-permute-start.14 = (s32[2,64]{1,0:T(2,128)S(1)}, s32[2,64]{1,0:T(2,128)S(1)}, u32[]{:S(2)}, u32[]{:S(2)}) collective-permute-start(s32[2,64]{1,0:T(2,128)S(1)} %multiply_add_fusion), channel_id=1, source_target_pairs={{0,1},{1,0},{2,3},{3,2},{4,5},{5,4},{6,7},{7,6},{8,9},{9,8},{10,11... | collective-permute-start | bytes 1544 | tf_op jit(solution)/shard_map/ppermute | solution.py:49
  20.2 46.0 %collective-permute-start.2 = (bf16[128,2048]{1,0:T(8,128)(2,1)S(1)}, bf16[128,2048]{1,0:T(8,128)(2,1)S(1)}, u32[]{:S(2)}, u32[]{:S(2)}) collective-permute-start(bf16[128,2048]{1,0:T(8,128)(2,1)S(1)} %bitcast.94), channel_id=1, source_target_pairs={{1,2},{2,1},{5,6},{6,5},{9,10},{10,9},{13,14},{14,13},{17,18},{18,... | collective-permute-start | bytes 1572872 | tf_op jit(solution)/shard_map/ppermute | solution.py:87
  20.9 37.6 %collective-permute-start.1 = (bf16[128,2048]{1,0:T(8,128)(2,1)S(1)}, bf16[128,2048]{1,0:T(8,128)(2,1)S(1)}, u32[]{:S(2)}, u32[]{:S(2)}) collective-permute-start(bf16[128,2048]{1,0:T(8,128)(2,1)S(1)} %bitcast.95), channel_id=1, source_target_pairs={{0,2},{1,3},{2,0},{3,1},{4,6},{5,7},{6,4},{7,5},{8,10},{9,11},{10,... | collective-permute-start | bytes 1572872 | tf_op jit(solution)/shard_map/ppermute | solution.py:87
  26.8 39.5 %collective-permute-start = (bf16[128,2048]{1,0:T(8,128)(2,1)S(1)}, bf16[128,2048]{1,0:T(8,128)(2,1)S(1)}, u32[]{:S(2)}, u32[]{:S(2)}) collective-permute-start(bf16[128,2048]{1,0:T(8,128)(2,1)S(1)} %bitcast.96), channel_id=1, source_target_pairs={{0,1},{1,0},{2,3},{3,2},{4,5},{5,4},{6,7},{7,6},{8,9},{9,8},{10,11... | collective-permute-start | bytes 1572872 | tf_op jit(solution)/shard_map/ppermute | solution.py:87
  64.7 18.6 %collective-permute-start.19 = (s32[4,2,256]{2,1,0:T(2,128)S(1)}, s32[4,2,256]{2,1,0:T(2,128)S(1)}, u32[]{:S(2)}, u32[]{:S(2)}) collective-permute-start(s32[4,2,256]{2,1,0:T(2,128)S(1)} %pad_add_fusion.1), channel_id=1, source_target_pairs={{0,16},{4,20},{8,24},{12,28},{16,0},{20,4},{24,8},{28,12},{1,17},{... | collective-permute-start | bytes 24584 | tf_op jit(solution)/shard_map/ppermute | solution.py:63
  101.1 23.7 %collective-permute-start.11 = (bf16[256,384]{1,0:T(8,128)(2,1)}, bf16[256,384]{1,0:T(8,128)(2,1)S(1)}, u32[]{:S(2)}, u32[]{:S(2)}) collective-permute-start(bf16[256,384]{1,0:T(8,128)(2,1)} %get-tuple-element.110), channel_id=1, source_target_pairs={{0,20},{4,16},{8,28},{12,24},{16,4},{20,0},{24,12},{28,8},{1,21},{... | collective-permute-start | bytes 589832 | tf_op jit(solution)/shard_map/ppermute | solution.py:55
  101.2 23.6 %collective-permute-start.12 = (bf16[256,384]{1,0:T(8,128)(2,1)}, bf16[256,384]{1,0:T(8,128)(2,1)S(1)}, u32[]{:S(2)}, u32[]{:S(2)}) collective-permute-start(bf16[256,384]{1,0:T(8,128)(2,1)} %get-tuple-element.111), channel_id=1, source_target_pairs={{0,24},{4,28},{8,16},{12,20},{16,8},{20,12},{24,0},{28,4},{1,25},{... | collective-permute-start | bytes 589832 | tf_op jit(solution)/shard_map/ppermute | solution.py:55
  105.3 24.9 %collective-permute-start.13 = (bf16[256,384]{1,0:T(8,128)(2,1)}, bf16[256,384]{1,0:T(8,128)(2,1)S(1)}, u32[]{:S(2)}, u32[]{:S(2)}) collective-permute-start(bf16[256,384]{1,0:T(8,128)(2,1)} %get-tuple-element.112), channel_id=1, source_target_pairs={{0,28},{4,24},{8,20},{12,16},{16,12},{20,8},{24,4},{28,0},{1,29},{... | collective-permute-start | bytes 589832 | tf_op jit(solution)/shard_map/ppermute | solution.py:55
  163.9 23.8 %collective-permute-start.28 = (bf16[128,2048]{1,0:T(8,128)(2,1)}, bf16[128,2048]{1,0:T(8,128)(2,1)S(1)}, u32[]{:S(2)}, u32[]{:S(2)}) collective-permute-start(bf16[128,2048]{1,0:T(8,128)(2,1)} %get-tuple-element.123), channel_id=1, source_target_pairs={{1,2},{2,1},{5,6},{6,5},{9,10},{10,9},{13,14},{14,13},{17,18},{18,... | collective-permute-start | bytes 1572872 | tf_op jit(solution)/shard_map/ppermute | solution.py:87
  165.2 22.6 %collective-permute-start.27 = (bf16[128,2048]{1,0:T(8,128)(2,1)}, bf16[128,2048]{1,0:T(8,128)(2,1)S(1)}, u32[]{:S(2)}, u32[]{:S(2)}) collective-permute-start(bf16[128,2048]{1,0:T(8,128)(2,1)} %get-tuple-element.122), channel_id=1, source_target_pairs={{0,1},{1,0},{2,3},{3,2},{4,5},{5,4},{6,7},{7,6},{8,9},{9,8},{10,11... | collective-permute-start | bytes 1572872 | tf_op jit(solution)/shard_map/ppermute | solution.py:87
  177.6 26.1 %collective-permute-start.30 = (bf16[128,2048]{1,0:T(8,128)(2,1)S(1)}, bf16[128,2048]{1,0:T(8,128)(2,1)S(1)}, u32[]{:S(2)}, u32[]{:S(2)}) collective-permute-start(bf16[128,2048]{1,0:T(8,128)(2,1)S(1)} %add_convert_fusion.6), channel_id=1, source_target_pairs={{0,2},{1,3},{2,0},{3,1},{4,6},{5,7},{6,4},{7,5},{8,10},{9,11},{10,... | collective-permute-start | bytes 1572872 | tf_op jit(solution)/shard_map/ppermute | solution.py:87
  208.4 23.6 %collective-permute-start.32 = (bf16[128,2048]{1,0:T(8,128)(2,1)}, bf16[128,2048]{1,0:T(8,128)(2,1)S(1)}, u32[]{:S(2)}, u32[]{:S(2)}) collective-permute-start(bf16[128,2048]{1,0:T(8,128)(2,1)} %get-tuple-element.125.refs_0_), channel_id=1, source_target_pairs={{0,2},{1,3},{2,0},{3,1},{4,6},{5,7},{6,4},{7,5},{8,10},{9,11},{10,... | collective-permute-start | bytes 1572872 | tf_op jit(solution)/shard_map/ppermute | solution.py:87
  208.4 24.9 %collective-permute-start.33 = (bf16[128,2048]{1,0:T(8,128)(2,1)}, bf16[128,2048]{1,0:T(8,128)(2,1)S(1)}, u32[]{:S(2)}, u32[]{:S(2)}) collective-permute-start(bf16[128,2048]{1,0:T(8,128)(2,1)} %get-tuple-element.125.refs_0_), channel_id=1, source_target_pairs={{1,2},{2,1},{5,6},{6,5},{9,10},{10,9},{13,14},{14,13},{17,18},{18,... | collective-permute-start | bytes 1572872 | tf_op jit(solution)/shard_map/ppermute | solution.py:87
  209.1 25.8 %collective-permute-start.31 = (bf16[128,2048]{1,0:T(8,128)(2,1)}, bf16[128,2048]{1,0:T(8,128)(2,1)S(1)}, u32[]{:S(2)}, u32[]{:S(2)}) collective-permute-start(bf16[128,2048]{1,0:T(8,128)(2,1)} %get-tuple-element.125.refs_0_), channel_id=1, source_target_pairs={{0,1},{1,0},{2,3},{3,2},{4,5},{5,4},{6,7},{7,6},{8,9},{9,8},{10,11... | collective-permute-start | bytes 1572872 | tf_op jit(solution)/shard_map/ppermute | solution.py:87
  232.0 15.6 %collective-permute-start.34 = (bf16[128,2048]{1,0:T(8,128)(2,1)S(1)}, bf16[128,2048]{1,0:T(8,128)(2,1)S(1)}, u32[]{:S(2)}, u32[]{:S(2)}) collective-permute-start(bf16[128,2048]{1,0:T(8,128)(2,1)S(1)} %collective-permute-done.32.refs_2_), channel_id=1, source_target_pairs={{1,0},{2,3},{5,4},{6,7},{9,8},{10,11},{13,12},{14,15},{17,16},{18,... | collective-permute-start | bytes 1572872 | tf_op jit(solution)/shard_map/ppermute | solution.py:87
  272.4 23.9 %collective-permute-start.36 = (bf16[128,2048]{1,0:T(8,128)(2,1)}, bf16[128,2048]{1,0:T(8,128)(2,1)S(1)}, u32[]{:S(2)}, u32[]{:S(2)}) collective-permute-start(bf16[128,2048]{1,0:T(8,128)(2,1)} %get-tuple-element.128), channel_id=1, source_target_pairs={{1,2},{2,1},{5,6},{6,5},{9,10},{10,9},{13,14},{14,13},{17,18},{18,... | collective-permute-start | bytes 1572872 | tf_op jit(solution)/shard_map/ppermute | solution.py:87
  273.1 23.2 %collective-permute-start.35 = (bf16[128,2048]{1,0:T(8,128)(2,1)}, bf16[128,2048]{1,0:T(8,128)(2,1)S(1)}, u32[]{:S(2)}, u32[]{:S(2)}) collective-permute-start(bf16[128,2048]{1,0:T(8,128)(2,1)} %get-tuple-element.127), channel_id=1, source_target_pairs={{0,1},{1,0},{2,3},{3,2},{4,5},{5,4},{6,7},{7,6},{8,9},{9,8},{10,11... | collective-permute-start | bytes 1572872 | tf_op jit(solution)/shard_map/ppermute | solution.py:87
  286.2 22.8 %collective-permute-start.38 = (bf16[128,2048]{1,0:T(8,128)(2,1)S(1)}, bf16[128,2048]{1,0:T(8,128)(2,1)S(1)}, u32[]{:S(2)}, u32[]{:S(2)}) collective-permute-start(bf16[128,2048]{1,0:T(8,128)(2,1)S(1)} %add_convert_fusion.5), channel_id=1, source_target_pairs={{0,2},{1,3},{2,0},{3,1},{4,6},{5,7},{6,4},{7,5},{8,10},{9,11},{10,... | collective-permute-start | bytes 1572872 | tf_op jit(solution)/shard_map/ppermute | solution.py:87
  313.5 23.8 %collective-permute-start.40 = (bf16[128,2048]{1,0:T(8,128)(2,1)}, bf16[128,2048]{1,0:T(8,128)(2,1)S(1)}, u32[]{:S(2)}, u32[]{:S(2)}) collective-permute-start(bf16[128,2048]{1,0:T(8,128)(2,1)} %get-tuple-element.132.refs_0_), channel_id=1, source_target_pairs={{0,2},{1,3},{2,0},{3,1},{4,6},{5,7},{6,4},{7,5},{8,10},{9,11},{10,... | collective-permute-start | bytes 1572872 | tf_op jit(solution)/shard_map/ppermute | solution.py:87
  313.6 25.0 %collective-permute-start.41 = (bf16[128,2048]{1,0:T(8,128)(2,1)}, bf16[128,2048]{1,0:T(8,128)(2,1)S(1)}, u32[]{:S(2)}, u32[]{:S(2)}) collective-permute-start(bf16[128,2048]{1,0:T(8,128)(2,1)} %get-tuple-element.132.refs_0_), channel_id=1, source_target_pairs={{1,2},{2,1},{5,6},{6,5},{9,10},{10,9},{13,14},{14,13},{17,18},{18,... | collective-permute-start | bytes 1572872 | tf_op jit(solution)/shard_map/ppermute | solution.py:87
  314.3 24.3 %collective-permute-start.39 = (bf16[128,2048]{1,0:T(8,128)(2,1)}, bf16[128,2048]{1,0:T(8,128)(2,1)S(1)}, u32[]{:S(2)}, u32[]{:S(2)}) collective-permute-start(bf16[128,2048]{1,0:T(8,128)(2,1)} %get-tuple-element.132.refs_0_), channel_id=1, source_target_pairs={{0,1},{1,0},{2,3},{3,2},{4,5},{5,4},{6,7},{7,6},{8,9},{9,8},{10,11... | collective-permute-start | bytes 1572872 | tf_op jit(solution)/shard_map/ppermute | solution.py:87
  375.5 34.4 %collective-permute-start.44 = (bf16[128,2048]{1,0:T(8,128)(2,1)}, bf16[128,2048]{1,0:T(8,128)(2,1)S(1)}, u32[]{:S(2)}, u32[]{:S(2)}) collective-permute-start(bf16[128,2048]{1,0:T(8,128)(2,1)} %get-tuple-element.137), channel_id=1, source_target_pairs={{1,2},{2,1},{5,6},{6,5},{9,10},{10,9},{13,14},{14,13},{17,18},{18,... | collective-permute-start | bytes 1572872 | tf_op jit(solution)/shard_map/ppermute | solution.py:87
  376.4 33.5 %collective-permute-start.43 = (bf16[128,2048]{1,0:T(8,128)(2,1)}, bf16[128,2048]{1,0:T(8,128)(2,1)S(1)}, u32[]{:S(2)}, u32[]{:S(2)}) collective-permute-start(bf16[128,2048]{1,0:T(8,128)(2,1)} %get-tuple-element.136), channel_id=1, source_target_pairs={{0,1},{1,0},{2,3},{3,2},{4,5},{5,4},{6,7},{7,6},{8,9},{9,8},{10,11... | collective-permute-start | bytes 1572872 | tf_op jit(solution)/shard_map/ppermute | solution.py:87
  388.3 21.9 %collective-permute-start.46 = (bf16[128,2048]{1,0:T(8,128)(2,1)S(1)}, bf16[128,2048]{1,0:T(8,128)(2,1)S(1)}, u32[]{:S(2)}, u32[]{:S(2)}) collective-permute-start(bf16[128,2048]{1,0:T(8,128)(2,1)S(1)} %add_convert_fusion.4), channel_id=1, source_target_pairs={{0,2},{1,3},{2,0},{3,1},{4,6},{5,7},{6,4},{7,5},{8,10},{9,11},{10,... | collective-permute-start | bytes 1572872 | tf_op jit(solution)/shard_map/ppermute | solution.py:87
  415.0 21.3 %collective-permute-start.48 = (bf16[128,2048]{1,0:T(8,128)(2,1)}, bf16[128,2048]{1,0:T(8,128)(2,1)S(1)}, u32[]{:S(2)}, u32[]{:S(2)}) collective-permute-start(bf16[128,2048]{1,0:T(8,128)(2,1)} %get-tuple-element.141.refs_0_), channel_id=1, source_target_pairs={{0,2},{1,3},{2,0},{3,1},{4,6},{5,7},{6,4},{7,5},{8,10},{9,11},{10,... | collective-permute-start | bytes 1572872 | tf_op jit(solution)/shard_map/ppermute | solution.py:87
  415.0 22.6 %collective-permute-start.49 = (bf16[128,2048]{1,0:T(8,128)(2,1)}, bf16[128,2048]{1,0:T(8,128)(2,1)S(1)}, u32[]{:S(2)}, u32[]{:S(2)}) collective-permute-start(bf16[128,2048]{1,0:T(8,128)(2,1)} %get-tuple-element.141.refs_0_), channel_id=1, source_target_pairs={{1,2},{2,1},{5,6},{6,5},{9,10},{10,9},{13,14},{14,13},{17,18},{18,... | collective-permute-start | bytes 1572872 | tf_op jit(solution)/shard_map/ppermute | solution.py:87
  415.7 21.9 %collective-permute-start.47 = (bf16[128,2048]{1,0:T(8,128)(2,1)}, bf16[128,2048]{1,0:T(8,128)(2,1)S(1)}, u32[]{:S(2)}, u32[]{:S(2)}) collective-permute-start(bf16[128,2048]{1,0:T(8,128)(2,1)} %get-tuple-element.141.refs_0_), channel_id=1, source_target_pairs={{0,1},{1,0},{2,3},{3,2},{4,5},{5,4},{6,7},{7,6},{8,9},{9,8},{10,11... | collective-permute-start | bytes 1572872 | tf_op jit(solution)/shard_map/ppermute | solution.py:87
  485.3 26.4 %collective-permute-start.58 = (bf16[256,384]{1,0:T(8,128)(2,1)}, bf16[256,384]{1,0:T(8,128)(2,1)S(1)}, u32[]{:S(2)}, u32[]{:S(2)}) collective-permute-start(bf16[256,384]{1,0:T(8,128)(2,1)} %get-tuple-element.158), channel_id=1, source_target_pairs={{0,4},{4,0},{8,12},{12,8},{16,20},{20,16},{24,28},{28,24},{1,5},{5... | collective-permute-start | bytes 589832 | tf_op jit(solution)/shard_map/ppermute | solution.py:55
  486.6 26.0 %collective-permute-start.59 = (bf16[256,384]{1,0:T(8,128)(2,1)}, bf16[256,384]{1,0:T(8,128)(2,1)S(1)}, u32[]{:S(2)}, u32[]{:S(2)}) collective-permute-start(bf16[256,384]{1,0:T(8,128)(2,1)} %get-tuple-element.159), channel_id=1, source_target_pairs={{0,8},{4,12},{8,0},{12,4},{16,24},{20,28},{24,16},{28,20},{1,9},{5... | collective-permute-start | bytes 589832 | tf_op jit(solution)/shard_map/ppermute | solution.py:55
  511.7 25.8 %collective-permute-start.62 = (bf16[256,384]{1,0:T(8,128)(2,1)}, bf16[256,384]{1,0:T(8,128)(2,1)S(1)}, u32[]{:S(2)}, u32[]{:S(2)}) collective-permute-start(bf16[256,384]{1,0:T(8,128)(2,1)} %get-tuple-element.162), channel_id=1, source_target_pairs={{0,20},{4,16},{8,28},{12,24},{16,4},{20,0},{24,12},{28,8},{1,21},{... | collective-permute-start | bytes 589832 | tf_op jit(solution)/shard_map/ppermute | solution.py:55
  511.7 25.7 %collective-permute-start.63 = (bf16[256,384]{1,0:T(8,128)(2,1)}, bf16[256,384]{1,0:T(8,128)(2,1)S(1)}, u32[]{:S(2)}, u32[]{:S(2)}) collective-permute-start(bf16[256,384]{1,0:T(8,128)(2,1)} %get-tuple-element.163), channel_id=1, source_target_pairs={{0,24},{4,28},{8,16},{12,20},{16,8},{20,12},{24,0},{28,4},{1,25},{... | collective-permute-start | bytes 589832 | tf_op jit(solution)/shard_map/ppermute | solution.py:55
  512.6 24.8 %collective-permute-start.64 = (bf16[256,384]{1,0:T(8,128)(2,1)}, bf16[256,384]{1,0:T(8,128)(2,1)S(1)}, u32[]{:S(2)}, u32[]{:S(2)}) collective-permute-start(bf16[256,384]{1,0:T(8,128)(2,1)} %get-tuple-element.164), channel_id=1, source_target_pairs={{0,28},{4,24},{8,20},{12,16},{16,12},{20,8},{24,4},{28,0},{1,29},{... | collective-permute-start | bytes 589832 | tf_op jit(solution)/shard_map/ppermute | solution.py:55
  548.0 43.2 %collective-permute-start.85 = (bf16[4,256,512]{2,1,0:T(8,128)(2,1)S(1)}, bf16[4,256,512]{2,1,0:T(8,128)(2,1)S(1)}, u32[]{:S(2)}, u32[]{:S(2)}) collective-permute-start(bf16[4,256,512]{2,1,0:T(8,128)(2,1)S(1)} %copy-done.56), channel_id=1, source_target_pairs={{0,4},{4,0},{8,12},{12,8},{16,20},{20,16},{24,28},{28,24},{1,5},{5... | collective-permute-start | bytes 3145736 | tf_op jit(solution)/shard_map/ppermute | solution.py:121
  574.9 44.5 %collective-permute-start.77 = (bf16[4,256,1024]{2,1,0:T(8,128)(2,1)}, bf16[4,256,1024]{2,1,0:T(8,128)(2,1)}, u32[]{:S(2)}, u32[]{:S(2)}) collective-permute-start(bf16[4,256,1024]{2,1,0:T(8,128)(2,1)} %get-tuple-element.189), channel_id=1, source_target_pairs={{0,4},{4,0},{8,12},{12,8},{16,20},{20,16},{24,28},{28,24},{1,5},{5... | collective-permute-start | bytes 6291464 | tf_op jit(solution)/shard_map/ppermute | solution.py:121
  590.6 20.0 %collective-permute-start.81 = (bf16[4,256,512]{2,1,0:T(8,128)(2,1)}, bf16[4,256,512]{2,1,0:T(8,128)(2,1)}, u32[]{:S(2)}, u32[]{:S(2)}) collective-permute-start(bf16[4,256,512]{2,1,0:T(8,128)(2,1)} %get-tuple-element.191), channel_id=1, source_target_pairs={{0,4},{4,0},{8,12},{12,8},{16,20},{20,16},{24,28},{28,24},{1,5},{5... | collective-permute-start | bytes 3145736 | tf_op jit(solution)/shard_map/ppermute | solution.py:121
  600.6 25.3 %collective-permute-start.74 = (bf16[128,2048]{1,0:T(8,128)(2,1)}, bf16[128,2048]{1,0:T(8,128)(2,1)}, u32[]{:S(2)}, u32[]{:S(2)}) collective-permute-start(bf16[128,2048]{1,0:T(8,128)(2,1)} %get-tuple-element.173), channel_id=1, source_target_pairs={{1,2},{2,1},{5,6},{6,5},{9,10},{10,9},{13,14},{14,13},{17,18},{18,... | collective-permute-start | bytes 1572872 | tf_op jit(solution)/shard_map/ppermute | solution.py:87
  606.0 19.2 %collective-permute-start.73 = (bf16[128,2048]{1,0:T(8,128)(2,1)}, bf16[128,2048]{1,0:T(8,128)(2,1)}, u32[]{:S(2)}, u32[]{:S(2)}) collective-permute-start(bf16[128,2048]{1,0:T(8,128)(2,1)} %get-tuple-element.172), channel_id=1, source_target_pairs={{0,1},{1,0},{2,3},{3,2},{4,5},{5,4},{6,7},{7,6},{8,9},{9,8},{10,11... | collective-permute-start | bytes 1572872 | tf_op jit(solution)/shard_map/ppermute | solution.py:87
  607.4 29.9 %collective-permute-start.76 = (bf16[128,2048]{1,0:T(8,128)(2,1)}, bf16[128,2048]{1,0:T(8,128)(2,1)}, u32[]{:S(2)}, u32[]{:S(2)}) collective-permute-start(bf16[128,2048]{1,0:T(8,128)(2,1)} %add_convert_fusion.3), channel_id=1, source_target_pairs={{0,2},{1,3},{2,0},{3,1},{4,6},{5,7},{6,4},{7,5},{8,10},{9,11},{10,... | collective-permute-start | bytes 1572872 | tf_op jit(solution)/shard_map/ppermute | solution.py:87
  612.8 25.9 %collective-permute-start.82 = (bf16[256,512]{1,0:T(8,128)(2,1)}, bf16[256,512]{1,0:T(8,128)(2,1)S(1)}, u32[]{:S(2)}, u32[]{:S(2)}) collective-permute-start(bf16[256,512]{1,0:T(8,128)(2,1)} %get-tuple-element.238), channel_id=1, source_target_pairs={{0,8},{4,12},{8,0},{12,4},{16,24},{20,28},{24,16},{28,20},{1,9},{5... | collective-permute-start | bytes 786440 | tf_op jit(solution)/shard_map/ppermute | solution.py:116
  619.4 23.8 %collective-permute-start.84 = (bf16[256,512]{1,0:T(8,128)(2,1)S(1)}, bf16[256,512]{1,0:T(8,128)(2,1)S(1)}, u32[]{:S(2)}, u32[]{:S(2)}) collective-permute-start(bf16[256,512]{1,0:T(8,128)(2,1)S(1)} %copy-done.32), channel_id=1, source_target_pairs={{0,24},{4,28},{8,16},{12,20},{16,8},{20,12},{24,0},{28,4},{1,25},{... | collective-permute-start | bytes 786440 | tf_op jit(solution)/shard_map/ppermute | solution.py:116
  625.3 17.9 %collective-permute-start.83 = (bf16[256,512]{1,0:T(8,128)(2,1)S(1)}, bf16[256,512]{1,0:T(8,128)(2,1)S(1)}, u32[]{:S(2)}, u32[]{:S(2)}) collective-permute-start(bf16[256,512]{1,0:T(8,128)(2,1)S(1)} %copy-done.31), channel_id=1, source_target_pairs={{0,16},{4,20},{8,24},{12,28},{16,0},{20,4},{24,8},{28,12},{1,17},{... | collective-permute-start | bytes 786440 | tf_op jit(solution)/shard_map/ppermute | solution.py:116
  626.0 19.2 %collective-permute-start.78 = (bf16[256,1024]{1,0:T(8,128)(2,1)S(1)}, bf16[256,1024]{1,0:T(8,128)(2,1)S(1)}, u32[]{:S(2)}, u32[]{:S(2)}) collective-permute-start(bf16[256,1024]{1,0:T(8,128)(2,1)S(1)} %get-tuple-element.232), channel_id=1, source_target_pairs={{0,8},{4,12},{8,0},{12,4},{16,24},{20,28},{24,16},{28,20},{1,9},{5... | collective-permute-start | bytes 1572872 | tf_op jit(solution)/shard_map/ppermute | solution.py:116
  638.7 23.0 %collective-permute-start.79 = (bf16[256,1024]{1,0:T(8,128)(2,1)S(1)}, bf16[256,1024]{1,0:T(8,128)(2,1)S(1)}, u32[]{:S(2)}, u32[]{:S(2)}) collective-permute-start(bf16[256,1024]{1,0:T(8,128)(2,1)S(1)} %get-tuple-element.234), channel_id=1, source_target_pairs={{0,16},{4,20},{8,24},{12,28},{16,0},{20,4},{24,8},{28,12},{1,17},{... | collective-permute-start | bytes 1572872 | tf_op jit(solution)/shard_map/ppermute | solution.py:116
  (122 other events, 1143.5 us)
Sparse Core Ops, SparseCore 0:
  10.5 48.2 all-gather.3
  61.2 27.8 all-gather.5
  91.0 145.6 all-gather.7
  410.3 181.5 reduce-scatter.1

commit v4 on v3

--- a/solution.py
+++ b/solution.py
@@ -125,14 +125,18 @@
     return sum(array.astype(full) for array in arrays)
 
 
-def sum_heads(values):
+def sum_heads(values, others=None):
     size = lax.axis_size("head")
-    total = None
-    for s, arrived in enumerate(gather_slots(values, "head")):
-        slots = jnp.split(arrived, size, axis=1)
+    count = values.size
+    sent = values.reshape(-1)
+    if others is not None:
+        sent = jnp.concatenate([sent, others])
+    total = 0.0
+    for s, arrived in enumerate(gather_slots(sent, "head")):
+        slots = jnp.split(arrived[:count].reshape(values.shape), size, axis=1)
         ordered = jnp.concatenate([slots[t ^ s] for t in range(size)], axis=1)
-        total = ordered if total is None else total + ordered
-    return total
+        total = total + jnp.concatenate([ordered.reshape(-1), arrived[count:]])
+    return total[:count].reshape(values.shape), total[count:]
 
 
 def rotary_tables(positions):
@@ -348,7 +352,7 @@
     return results[:3], results[3:]
 
 
-def ffn_weight_term(held, part, lefts, rights):
+def ffn_weight_term(held, part, parts, lefts, rights):
     n = len(lefts)
     rows, width = lefts[0].shape
     hidden = rights[0].shape[1]
@@ -366,7 +370,7 @@
         right = jnp.concatenate([ref[...] for ref in refs[n : 2 * n]], axis=0)
         out_ref[...] = dot_plain(left_t[...], right).astype(low)
 
-    shape = shape_of((width, 3 * hidden), low)
+    shape = shape_of((width, parts * hidden), low)
     return pl.pallas_call(
         body,
         grid=(steps,),
@@ -386,18 +390,19 @@
     )(*lefts, *rights, *held)
 
 
-def widen_ffn(grads):
-    rows, hidden = grads.shape[0], grads.shape[1] // 3
-
-    def body(grad_ref, gate_ref, up_ref, down_ref):
+def widen_ffn(grads, down_grads):
+    rows, hidden = down_grads.shape
+
+    def body(grad_ref, turned_ref, gate_ref, up_ref, down_ref):
         gate_ref[...] = grad_ref[:, :hidden].astype(full)
-        up_ref[...] = grad_ref[:, hidden : 2 * hidden].astype(full)
-        down_ref[...] = jnp.transpose(grad_ref[:, 2 * hidden :]).astype(full)
+        up_ref[...] = grad_ref[:, hidden:].astype(full)
+        down_ref[...] = jnp.transpose(turned_ref[...]).astype(full)
 
     return call_whole(
         body,
         [shape_of((rows, hidden), full)] * 2 + [shape_of((hidden, rows), full)],
         grads,
+        down_grads,
         scalars=0,
     )
 
@@ -543,24 +548,40 @@
     )
 
 
-def project_mixed_grad(grad_slots, weights_t, micro_count):
-    count = len(grad_slots)
-    local_rows, width = grad_slots[0].shape
-    rows, features = len(layout_of(count)) * local_rows, weights_t.shape[1]
+def project_mixed_grad(grad_rows, weights_t, head_size):
+    rows, width = grad_rows.shape
+    features = weights_t.shape[1] // head_size
+
+    def body(grad_ref, weight_ref, *out_refs):
+        term = dot_plain(grad_ref[...], weight_ref[...]).astype(low)
+        for s in range(head_size):
+
+            @pl.when(pl.program_id(0) == s)
+            def _():
+                out_refs[s][...] = term
+
+    return call_grid(
+        body,
+        head_size,
+        [shape_of((rows, features), low)] * head_size,
+        [fixed((rows, width)), column_tile(width, features)],
+        [fixed((rows, features))] * head_size,
+        grad_rows,
+        weights_t,
+        flops=2 * rows * width * weights_t.shape[1],
+    )
+
+
+def join_rows(parts, micro_count):
+    rows, width = parts[0].shape
+    count = len(parts)
 
     def body(*refs):
-        weight_ref, rows_ref, out_ref = refs[count:]
-        fill_rows(rows_ref, refs[:count], micro_count)
-        out_ref[...] = dot_plain(rows_ref[...], weight_ref[...]).astype(low)
+        fill_rows(refs[count], refs[:count], micro_count)
 
     return call_whole(
-        body,
-        [shape_of((rows, width), low), shape_of((rows, features), low)],
-        *grad_slots,
-        weights_t,
-        scalars=0,
-        flops=2 * rows * width * features,
-    )
+        body, [shape_of((len(layout_of(count)) * rows, width), low)], *parts, scalars=0
+    )[0]
 
 
 def norm_gradients(raw, scales, gains, grads):
@@ -637,61 +658,67 @@
     )
 
 
-def weight_term_slots(me, lefts, rights, blocks):
-    n = len(lefts)
-    rows, width = lefts[0].shape
-    features = rights[0].shape[1]
+def weight_term_slots(me, pairs, blocks):
+    n = len(pairs)
+    rows, width = pairs[0][0].shape
+    sizes = [right.shape[1] for _, right in pairs]
+    features = sum(sizes)
     part = width // blocks
     half = blocks // 2
 
     def body(me_ref, *refs):
-        odd_ref, even_ref, left_t, right_all = refs[2 * n :]
+        odd_ref, even_ref = refs[2 * n : 2 * n + 2]
+        lefts = refs[2 * n + 2 :]
         step = pl.program_id(0)
 
         @pl.when(step == 0)
         def _():
-            for m in range(n):
-                cut = slice(m * rows, (m + 1) * rows)
-                left_t[:, cut] = jnp.transpose(refs[m][...])
-                right_all[cut, :] = refs[n + m][...]
+            for left_t, left in zip(lefts, refs[:n]):
+                left_t[...] = jnp.transpose(left[...])
 
         slot = jnp.where(step < half, 2 * step + 1, 2 * step - blocks)
         place = pl.multiple_of((me_ref[0] ^ slot) * part, part)
-        term = dot_plain(left_t[pl.ds(place, part), :], right_all[...]).astype(low)
-
-        @pl.when(step < half)
-        def _():
-            odd_ref[0] = term
-
-        @pl.when(step >= half)
-        def _():
-            even_ref[0] = term
+        first = 0
+        for left_t, right, size in zip(lefts, refs[n : 2 * n], sizes):
+            term = dot_plain(left_t[pl.ds(place, part), :], right[...]).astype(low)
+            cut = slice(first, first + size)
+            first += size
+
+            @pl.when(step < half)
+            def _():
+                odd_ref[0, :, cut] = term
+
+            @pl.when(step >= half)
+            def _():
+                even_ref[0, :, cut] = term
 
     return call_grid(
         body,
         blocks,
         [shape_of((half, part, features), low)] * 2,
-        [scalar_spec] + [fixed((rows, width))] * n + [fixed((rows, features))] * n,
+        [scalar_spec]
+        + [fixed((rows, width))] * n
+        + [fixed((rows, size)) for size in sizes],
         [
             pl.BlockSpec((1, part, features), lambda i: (jnp.minimum(i, half - 1), 0, 0)),
             pl.BlockSpec((1, part, features), lambda i: (jnp.maximum(i - half, 0), 0, 0)),
         ],
         me,
-        *lefts,
-        *rights,
-        scratch=[pltpu.VMEM((width, n * rows), low), pltpu.VMEM((n * rows, features), low)],
-        flops=2 * n * rows * width * features,
-    )
-
-
-def to_owner(terms, *others):
+        *[left for left, _ in pairs],
+        *[right for _, right in pairs],
+        scratch=[pltpu.VMEM((width, rows), low)] * n,
+        flops=2 * rows * width * features,
+    )
+
+
+def add_cores(terms):
     odd, even = terms
-    blocks = 2 * even.shape[0]
     arrived = swap_cores(odd)
-    even = after(even, *others)
-    pairs = [even[k].astype(full) + arrived[k].astype(full) for k in range(blocks // 2)]
-    slots = exchange_chips([pairs[0]] + [pair.astype(low) for pair in pairs[1:]])
-    return sum(slot.astype(full) for slot in slots)
+    return [even[k].astype(full) + arrived[k].astype(full) for k in range(even.shape[0])]
+
+
+def add_chips(pairs):
+    return sum_full(exchange_chips([pairs[0]] + [pair.astype(low) for pair in pairs[1:]]))
 
 
 def send_views(me, raw, scales, gains, tables, heads_local):
@@ -884,16 +911,22 @@
     )[0]
 
 
-def split_mixed(me, mixed, blocks, heads_local):
-    micro_count, rows = mixed.shape[:2]
-
-    def body(me_ref, mixed_ref, *out_refs):
-        for s in range(blocks):
-            target = me_ref[0] ^ s
+def split_mixed(me, slots, micro_count, heads_local):
+    count = len(slots)
+    rows = slots[0].shape[0] // micro_count
+    blocks = micro_count * heads_local
+
+    def body(me_ref, *refs):
+        for t in range(blocks):
+            target = me_ref[0] ^ t
             column = pl.multiple_of((target % heads_local) * HD, HD)
-            out_refs[s][...] = mixed_ref[target // heads_local, :, pl.ds(column, HD)]
-
-    return call_whole(body, [shape_of((rows, HD), low)] * blocks, me, mixed)
+            first = pl.multiple_of((target // heads_local) * rows, rows)
+            for s in range(count):
+                refs[count + t][s * rows : (s + 1) * rows, :] = refs[s][
+                    pl.ds(first, rows), pl.ds(column, HD)
+                ]
+
+    return call_whole(body, [shape_of((count * rows, HD), low)] * blocks, me, *slots)
 
 
 def receive_grads(me, slots, tables, micro_count, heads_local):
@@ -1024,6 +1057,7 @@
                 positions,
             )
             self.sets.append((views[0], mark, stacked))
+        self.slots = [one[2][0] for one in self.sets]
 
     def forward(self):
         results = [gathered_forward(*one) for one in self.sets]
@@ -1032,7 +1066,9 @@
             [mixed.reshape(self.rows, -1).astype(low) for mixed, norm in results]
         )
 
-    def backward(self, grad_mixed, *others):
+    def backward(self, grad_parts, *others):
+        grad_mixed = jnp.stack(grad_parts).reshape(len(grad_parts), len(self.sets), -1, grad_parts[0].shape[1])
+        grad_mixed = grad_mixed.swapaxes(0, 1).reshape(len(self.sets), self.rows, -1)
         norms, values = [], []
         for m, (view, mark, stacked) in enumerate(self.sets):
             grad_query, terms = gathered_backward(
@@ -1073,14 +1109,15 @@
             self.heads,
         )
 
-    def backward(self, grad_mixed, *others):
+    def backward(self, grad_parts, *others):
         grad_slots = exchange_slots(
-            split_mixed(self.me, grad_mixed, self.blocks, self.heads), "blk"
+            split_mixed(self.me, grad_parts, self.micro_count, self.heads), "blk"
         )
-        grad_slots = [after(grad_slots[0], *others)] + grad_slots[1:]
+        self.arrived = grad_slots[1:]
         back_slots = exchange_slots(
             attention_backward(self.me, self.slots, grad_slots, *self.kept, *self.marks), "blk"
         )
+        back_slots = after(back_slots, *others)
         return receive_grads(self.me, back_slots, self.tables, self.micro_count, self.heads)
 
 
@@ -1129,22 +1166,23 @@
     def all_rows(values):
         return values.reshape(-1, values.shape[-1])
 
-    def sum_token_heads(values):
-        values = values.reshape(2 * micro_count, group_rows)
-        return sum_heads(values).reshape(2, micro_count * group_rows).T
+    def sum_token_heads(values, others=None):
+        sums, others = sum_heads(values.reshape(2 * micro_count, group_rows), others)
+        return sums.reshape(2, micro_count * group_rows).T, others
 
     token_rows, raw, squares = project_qkv(gather_parts(all_rows(tokens)), qkv_full, micro_count)
     codes = jnp.concatenate(gather_slots(segments * 2 + padding, "head"), axis=1)
     codes = gather_doubling(codes, "blk")
     codes = codes[block_index ^ jnp.arange(blocks, dtype=jnp.int32)].swapaxes(0, 1)
 
-    scales = lax.rsqrt(sum_token_heads(squares) / model_width + epsilon)
+    scales = lax.rsqrt(sum_token_heads(squares)[0] / model_width + epsilon)
     gain_row = jnp.concatenate([query_gain, key_gain])[None, :]
     positions = jnp.arange(blocks, dtype=jnp.int32)[:, None] * group_rows + group_order[None, :]
     exchanged = blocks == micro_count * heads_local and blocks & (blocks - 1) == 0
     attention = (ExchangedAttention if exchanged else GatheredAttention)(
         by_micro(raw), by_micro(scales), gain_row, tables, codes.reshape(micro_count, -1), positions
     )
+    output_parts = gather_slots(after(output_weight.T, attention.slots[1]), "head")
     mixed = attention.forward()
 
     attn_gain, ffn_gain = attn_gain[None, :], ffn_gain[None, :]
@@ -1154,50 +1192,61 @@
     (hidden_rows, gate, up, middle_rows), slots = ffn_forward(
         gather_parts(hidden_low), ffn_full, micro_count
     )
+    output_all_t = gather_weights(*after(output_parts, gate))
     output, grad_down, ffn_gain_grad = after_ffn(reduce_parts(slots), hidden, grad_own, ffn_gain)
-    (grad_rows, grad_gate, grad_up), slots = ffn_backward(
-        gather_parts(grad_down), gate, up, ffn_full, micro_count
+    grad_parts = gather_parts(grad_down)
+    grad_rows = join_rows(grad_parts, micro_count)
+    down_terms = ffn_weight_term([], 0, 1, [grad_rows], [middle_rows])
+    (_, grad_gate, grad_up), slots = ffn_backward(
+        grad_parts, after(gate, down_terms), up, ffn_full, micro_count
     )
     arrived = reduce_parts(slots)
     grad_hidden, grad_attn, attn_gain_grad = before_attention(
         arrived, grad_own, attn_hat, attn_scale, attn_gain
     )
-    ffn_terms = ffn_weight_term([], 2, [grad_rows], [middle_rows])
-    ffn_terms = ffn_weight_term([ffn_terms], 0, [hidden_rows], [grad_gate])
-    ffn_terms = ffn_weight_term([ffn_terms], 1, [hidden_rows], [grad_up])
+    ffn_terms = ffn_weight_term([], 0, 2, [hidden_rows], [grad_gate])
+    ffn_terms = ffn_weight_term([ffn_terms], 1, 2, [hidden_rows], [grad_up])
     ffn_terms = after(ffn_terms, *arrived)
+    down_grads = lax.psum_scatter(down_terms, "blk", scatter_dimension=0, tiled=True)
     ffn_grads = widen_ffn(
-        lax.psum_scatter(ffn_terms, "blk", scatter_dimension=0, tiled=True)
-    )
-    norm_gain_grads = sum_doubling(
-        jnp.concatenate([attn_gain_grad, ffn_gain_grad], axis=1)[0], "blk"
-    )
-    norm_gain_grads = sum_doubling(norm_gain_grads, "head")
-
-    grad_attn_rows, grad_mixed = project_mixed_grad(
-        gather_parts(grad_attn), output_full_t, micro_count
-    )
-    output_terms = weight_term_slots(me, [grad_attn_rows], [all_rows(mixed)], blocks)
-    grad_norm, grad_value = attention.backward(by_micro(grad_mixed), *output_terms)
+        lax.psum_scatter(ffn_terms, "blk", scatter_dimension=0, tiled=True), down_grads
+    )
+
+    grad_parts = exchange_slots(project_mixed_grad(grad_attn, output_all_t, head_size), "head")
+    grad_attn_parts = gather_parts(after(grad_attn, *grad_parts[1:]))
+    grad_norm, grad_value = attention.backward(grad_parts, *grad_attn_parts[1:])
+    grad_attn_rows = join_rows(grad_attn_parts, micro_count)
     grad_norm, grad_value = all_rows(grad_norm), all_rows(grad_value)
     dots, qk_gain_grad = norm_gradients(raw, scales, gain_row, grad_norm)
-    mean_dots = sum_token_heads(after(dots, norm_gain_grads)) / model_width
-    value_terms = weight_term_slots(me, [token_rows], [grad_value], blocks)
+    dots, gain_grads = sum_token_heads(
+        dots, jnp.concatenate([attn_gain_grad, ffn_gain_grad], axis=1)[0]
+    )
+    mean_dots = dots / model_width
+    gain_grads = jnp.concatenate([gain_grads, qk_gain_grad[0]])
+    early_terms = weight_term_slots(
+        me, [(grad_attn_rows, all_rows(mixed)), (token_rows, grad_value)], blocks
+    )
+    mean_dots = after(mean_dots, *early_terms)
     results = project_input_grad(
         raw, scales, mean_dots, gain_row, grad_norm, grad_value, qkv_full, head_size, micro_count
     )
-    input_grad = sum_full(reduce_parts(results[1:])) + grad_hidden
-    output_grad = to_owner(output_terms).T
-    value_grad = to_owner(value_terms)
-    qk_grad = to_owner(weight_term_slots(me, [token_rows], [results[0]], blocks), *ffn_grads)
-
-    qk_gain_grad = sum_doubling(qk_gain_grad[0], "blk")
+    input_parts = exchange_slots(results[1:], "head")
+    early_grads = add_chips(add_cores(early_terms))
+    output_grad = early_grads[:, :width].T
+    qk_terms = weight_term_slots(me, [(token_rows, results[0])], blocks)
+    qk_pairs = add_cores(qk_terms)
+    gain_grads = sum_doubling(after(gain_grads, *qk_terms), "blk")
+    norm_gain_grads = gain_grads[: 2 * model_width]
+    qk_gain_grad = gain_grads[2 * model_width :]
+    qk_slots = exchange_chips([qk_pairs[0]] + [pair.astype(low) for pair in qk_pairs[1:]])
+    input_grad = sum_full(after(input_parts, *qk_slots[1:])) + grad_hidden
+    qk_grad = sum_full(after(qk_slots, ffn_grads, output_grad))
     return (
         by_micro(output),
         by_micro(input_grad),
         qk_grad[:, :width],
         qk_grad[:, width:],
-        value_grad,
+        early_grads[:, width:],
         output_grad,
         qk_gain_grad[:width],
         qk_gain_grad[width:],

time: 676 us -> 628 us (0.929)
  waiting for transfers between devices: 310 us -> 264 us
  starting transfers between devices: 124 us -> 116 us
  Pallas kernels: 177 us -> 184 us
    ppermute x32 -> x28, waiting for transfers between devices: 199 us -> 142 us  [send_rows(): return lax.ppermute(values, 'head', pairs)]
    ppermute x28 -> x34, waiting for transfers between devices: 54.2 us -> 80.7 us  [exchange_slots(): lax.ppermute(slots[s], axis, xor_pairs(size, s))]
    ppermute x8 -> x3, waiting for transfers between devices: 23.6 us -> 6.83 us  [sum_doubling(): lax.ppermute(values, axis, xor_pairs(lax.axis_size(axis), step))]
    ppermute x9 -> x12, waiting for transfers between devices: 6.04 us -> 18.4 us  [gather_slots(): lax.ppermute(values, axis, xor_pairs(size, s))]
    ppermute x9 -> x6, waiting for transfers between devices: 26.1 us -> 14.5 us  [exchange_chips(): lax.ppermute(slots[m], 'blk', xor_pairs(size, 2 * m))]
    ppermute x32 -> x28, starting transfers between devices: 56.5 us -> 48 us  [send_rows(): return lax.ppermute(values, 'head', pairs)]
    ppermute x9 -> x12, starting transfers between devices: 14 us -> 20.3 us  [gather_slots(): lax.ppermute(values, axis, xor_pairs(size, s))]
    pallas_call x13 -> x14, Pallas kernels: 62.2 us -> 65.7 us  [call_whole(): pl.pallas_call(body, out_shape=outs, in_specs=[pl.BlockSpec(memory_space=...]
  transfers between devices with their start and end apart: 96 -> 94, of which waited for: 51 -> 44; matrix products, arithmetic and copies ran while one was open for 5% -> 4% of each run, Pallas kernels for 19% -> 29%
where the time goes in v4:
time: 628 us; the launch traced here: 622 us
  waiting for transfers between devices  264 us (42%)
  Pallas kernels  184 us (29%)
  starting transfers between devices  116 us (18%)
  other arithmetic  22.7 us (4%)
  local copies, waits for them, and re-layouts  20 us (3%)
  between operations  15.4 us (2%)
    ppermute x28, waiting for transfers between devices, send_rows(): return lax.ppermute(values, 'head', pairs)  142 us
    pallas_call x7, Pallas kernels, call_grid(): pl.pallas_call(body, grid=(steps,), out_shape=outs, in_specs=in_specs, ou...  91.2 us
    ppermute x34, waiting for transfers between devices, exchange_slots(): lax.ppermute(slots[s], axis, xor_pairs(size, s))  80.7 us
    pallas_call x14, Pallas kernels, call_whole(): pl.pallas_call(body, out_shape=outs, in_specs=[pl.BlockSpec(memory_space=...  65.7 us
    ppermute x28, starting transfers between devices, send_rows(): return lax.ppermute(values, 'head', pairs)  48 us
    ppermute x34, starting transfers between devices, exchange_slots(): lax.ppermute(slots[s], axis, xor_pairs(size, s))  33 us
    pallas_call x3, Pallas kernels, ffn_weight_term(): pl.pallas_call(body, grid=(steps,), out_shape=shape, in_specs=[fixed((row...  27.5 us
    ppermute x12, starting transfers between devices, gather_slots(): lax.ppermute(values, axis, xor_pairs(size, s))  20.3 us
  transfers between devices with their start and end apart: 94, of which 44 were waited for; matrix products, arithmetic and copies ran while one was open for 4% of the time, Pallas kernels for 29%

profile of v4, /device:TPU:0, one launch (start us, length us, event | category | flops | bytes accessed | tf_op | source)
XLA Modules:
  0.0 622.5 jit_solution(3462153043734617836)
XLA Ops:
  26.8 16.8 %collective-permute-done.16 = s32[2,64]{1,0:T(2,128)S(1)} collective-permute-done((s32[2,64]{1,0:T(2,128)S(1)}, s32[2,64]{1,0:T(2,128)S(1)}, u32[]{:S(2)}, u32[]{:S(2)}) %collective-permute-start.16) | collective-permute-done | bytes 544 | tf_op jit(solution)/shard_map/ppermute | solution.py:49
  52.0 6.6 %collective-permute-done.3.refs_4_ = bf16[128,2048]{1,0:T(8,128)(2,1)S(1)} collective-permute-done((bf16[128,2048]{1,0:T(8,128)(2,1)S(1)}, bf16[128,2048]{1,0:T(8,128)(2,1)S(1)}, u32[]{:S(2)}, u32[]{:S(2)}) %collective-permute-start.3) | collective-permute-done | bytes 524320 | tf_op jit(solution)/shard_map/ppermute | solution.py:87
  59.4 9.3 %shard_map.246 = (bf16[512,2048]{1,0:T(8,128)(2,1)}, f32[512,1536]{1,0:T(8,128)}, f32[2,512]{1,0:T(2,128)}) custom-call(bf16[128,2048]{1,0:T(8,128)(2,1)} %bitcast.90, bf16[128,2048]{1,0:T(8,128)(2,1)} %copy-done.58, bf16[128,2048]{1,0:T(8,128)(2,1)} %copy-done.59, bf16[128,2048]{1,0:T(8,128)(2,1)} %copy-done.60, bf16[128,2048]{1,0:T(8,128)(2,1)} %copy-done.61, ...), custom_call_target="tpu_custom_call" | custom-call | flops 3221225472 | bytes 14159872 | tf_op jit(solution)/shard_map/pallas_call | solution.py:179
  78.4 5.2 shard_map.247
  96.0 9.9 %collective-permute-done.11.refs_5_ = bf16[256,384]{1,0:T(8,128)(2,1)S(1)} collective-permute-done((bf16[256,384]{1,0:T(8,128)(2,1)}, bf16[256,384]{1,0:T(8,128)(2,1)S(1)}, u32[]{:S(2)}, u32[]{:S(2)}) %collective-permute-start.11) | collective-permute-done | bytes 196640 | tf_op jit(solution)/shard_map/ppermute | solution.py:55
  106.7 9.4 %shard_map.248 = (bf16[256,128]{1,0:T(8,128)(2,1)}, bf16[256,128]{1,0:T(8,128)(2,1)}, bf16[256,128]{1,0:T(8,128)(2,1)}, bf16[256,128]{1,0:T(8,128)(2,1)}, bf16[2...) custom-call(s32[1]{0:T(128)} %bitcast.me_ref, ...), custom_call_target="tpu_custom_call" | custom-call | flops 1073741824 | bytes 3186692 | tf_op jit(solution)/shard_map/pallas_call | solution.py:162
  133.6 4.3 shard_map.250
  137.9 4.0 collective-permute-start.29
  143.9 10.5 %collective-permute-done.29 = bf16[128,2048]{1,0:T(8,128)(2,1)S(1)} collective-permute-done((bf16[128,2048]{1,0:T(8,128)(2,1)}, bf16[128,2048]{1,0:T(8,128)(2,1)S(1)}, u32[]{:S(2)}, u32[]{:S(2)}) %collective-permute-start.29) | collective-permute-done | bytes 524320 | tf_op jit(solution)/shard_map/ppermute | solution.py:87
  157.9 7.8 %collective-permute-done.27.refs_1_ = bf16[128,2048]{1,0:T(8,128)(2,1)S(1)} collective-permute-done((bf16[128,2048]{1,0:T(8,128)(2,1)}, bf16[128,2048]{1,0:T(8,128)(2,1)S(1)}, u32[]{:S(2)}, u32[]{:S(2)}) %collective-permute-start.27) | collective-permute-done | bytes 524320 | tf_op jit(solution)/shard_map/ppermute | solution.py:87
  165.7 15.6 %collective-permute-done.30.refs_3_ = bf16[128,2048]{1,0:T(8,128)(2,1)S(1)} collective-permute-done((bf16[128,2048]{1,0:T(8,128)(2,1)S(1)}, bf16[128,2048]{1,0:T(8,128)(2,1)S(1)}, u32[]{:S(2)}, u32[]{:S(2)}) %collective-permute-start.30) | collective-permute-done | bytes 524320 | tf_op jit(solution)/shard_map/ppermute | solution.py:87
  182.1 3.8 shard_map.251
  189.3 21.1 %collective-permute-done.32.refs_2_ = bf16[128,2048]{1,0:T(8,128)(2,1)S(1)} collective-permute-done((bf16[128,2048]{1,0:T(8,128)(2,1)}, bf16[128,2048]{1,0:T(8,128)(2,1)S(1)}, u32[]{:S(2)}, u32[]{:S(2)}) %collective-permute-start.32) | collective-permute-done | bytes 524320 | tf_op jit(solution)/shard_map/ppermute | solution.py:87
  217.0 11.8 %collective-permute-done.34.refs_4_ = bf16[128,2048]{1,0:T(8,128)(2,1)S(1)} collective-permute-done((bf16[128,2048]{1,0:T(8,128)(2,1)S(1)}, bf16[128,2048]{1,0:T(8,128)(2,1)S(1)}, u32[]{:S(2)}, u32[]{:S(2)}) %collective-permute-start.34) | collective-permute-done | bytes 524320 | tf_op jit(solution)/shard_map/ppermute | solution.py:87
  229.5 22.5 %shard_map.252 = (bf16[512,2048]{1,0:T(8,128)(2,1)}, bf16[512,2048]{1,0:T(8,128)(2,1)}, bf16[512,2048]{1,0:T(8,128)(2,1)}, bf16[512,2048]{1,0:T(8,128)(2,1)}, bf...) custom-call(bf16[128,2048]{1,0:T(8,128)(2,1)} %get-tuple-element.146, ...), custom_call_target="tpu_custom_call" | custom-call | flops 12884901888 | bytes 88604672 | tf_op jit(solution)/shard_map/pallas_call | solution.py:179
  257.1 9.9 %collective-permute-done.37 = bf16[128,2048]{1,0:T(8,128)(2,1)S(1)} collective-permute-done((bf16[128,2048]{1,0:T(8,128)(2,1)S(1)}, bf16[128,2048]{1,0:T(8,128)(2,1)S(1)}, u32[]{:S(2)}, u32[]{:S(2)}) %collective-permute-start.37) | collective-permute-done | bytes 524320 | tf_op jit(solution)/shard_map/ppermute | solution.py:87
  267.1 3.4 collective-permute-start.38
  270.6 7.7 %collective-permute-done.35.refs_1_ = bf16[128,2048]{1,0:T(8,128)(2,1)S(1)} collective-permute-done((bf16[128,2048]{1,0:T(8,128)(2,1)S(1)}, bf16[128,2048]{1,0:T(8,128)(2,1)S(1)}, u32[]{:S(2)}, u32[]{:S(2)}) %collective-permute-start.35) | collective-permute-done | bytes 524320 | tf_op jit(solution)/shard_map/ppermute | solution.py:87
  278.2 11.7 %collective-permute-done.38.refs_3_ = bf16[128,2048]{1,0:T(8,128)(2,1)S(1)} collective-permute-done((bf16[128,2048]{1,0:T(8,128)(2,1)S(1)}, bf16[128,2048]{1,0:T(8,128)(2,1)S(1)}, u32[]{:S(2)}, u32[]{:S(2)}) %collective-permute-start.38) | collective-permute-done | bytes 524320 | tf_op jit(solution)/shard_map/ppermute | solution.py:87
  290.8 3.8 shard_map.253
  298.1 19.7 %collective-permute-done.40.refs_2_ = bf16[128,2048]{1,0:T(8,128)(2,1)S(1)} collective-permute-done((bf16[128,2048]{1,0:T(8,128)(2,1)}, bf16[128,2048]{1,0:T(8,128)(2,1)S(1)}, u32[]{:S(2)}, u32[]{:S(2)}) %collective-permute-start.40) | collective-permute-done | bytes 524320 | tf_op jit(solution)/shard_map/ppermute | solution.py:87
  319.2 10.1 %collective-permute-done.42.refs_4_ = bf16[128,2048]{1,0:T(8,128)(2,1)S(1)} collective-permute-done((bf16[128,2048]{1,0:T(8,128)(2,1)S(1)}, bf16[128,2048]{1,0:T(8,128)(2,1)S(1)}, u32[]{:S(2)}, u32[]{:S(2)}) %collective-permute-start.42) | collective-permute-done | bytes 524320 | tf_op jit(solution)/shard_map/ppermute | solution.py:87
  330.1 3.2 shard_map.254.refs_0_
  333.3 9.3 %shard_map.255 = bf16[2048,2048]{1,0:T(8,128)(2,1)} custom-call(bf16[512,2048]{1,0:T(8,128)(2,1)} %shard_map.254.refs_0_, bf16[512,2048]{1,0:T(8,128)(2,1)} %get-tuple-element.155.refs_1_), custom_call_target="tpu_custom_call" | custom-call | flops 4294967296 | bytes 10485760 | tf_op jit(solution)/shard_map/pallas_call | solution.py:374
  342.8 24.7 %shard_map.256 = (bf16[512,2048]{1,0:T(8,128)(2,1)}, bf16[512,2048]{1,0:T(8,128)(2,1)}, bf16[512,2048]{1,0:T(8,128)(2,1)}, bf16[128,2048]{1,0:T(8,128)(2,1)}, bf...) custom-call(bf16[128,2048]{1,0:T(8,128)(2,1)} %get-tuple-element.153.refs_0_, ...), custom_call_target="tpu_custom_call" | custom-call | flops 12884901888 | bytes 90701824 | tf_op jit(solution)/shard_map/pallas_call | solution.py:179
  372.7 9.1 %collective-permute-done.45 = bf16[128,2048]{1,0:T(8,128)(2,1)S(1)} collective-permute-done((bf16[128,2048]{1,0:T(8,128)(2,1)}, bf16[128,2048]{1,0:T(8,128)(2,1)S(1)}, u32[]{:S(2)}, u32[]{:S(2)}) %collective-permute-start.45) | collective-permute-done | bytes 524320 | tf_op jit(solution)/shard_map/ppermute | solution.py:87
  382.9 4.1 collective-permute-start.46
  387.0 9.1 %shard_map.267.refs_2_ = bf16[2048,4096]{1,0:T(8,128)(2,1)} custom-call(bf16[512,2048]{1,0:T(8,128)(2,1)} %get-tuple-element.222.refs_0_, bf16[512,2048]{1,0:T(8,128)(2,1)} %get-tuple-element.224.refs_1_), custom_call_target="tpu_custom_call" | custom-call | flops 4294967296 | bytes 10485760 | tf_op jit(solution)/shard_map/pallas_call | solution.py:374
  396.2 9.1 %shard_map.268 = bf16[2048,4096]{1,0:T(8,128)(2,1)} custom-call(bf16[512,2048]{1,0:T(8,128)(2,1)} %get-tuple-element.222.refs_0_, bf16[512,2048]{1,0:T(8,128)(2,1)} %get-tuple-element.223.refs_1_, bf16[2048,4096]{1,0:T(8,128)(2,1)} %shard_map.267.refs_2_), custom_call_target="tpu_custom_call", output_to_operand_aliasing={{}: (2, {})} | custom-call | flops 4294967296 | bytes 10485760 | tf_op jit(solution)/shard_map/pallas_call | solution.py:374
  406.4 3.8 shard_map.257
  410.2 6.3 %shard_map.258 = (bf16[128,512]{1,0:T(8,128)(2,1)}, bf16[128,512]{1,0:T(8,128)(2,1)}, bf16[128,512]{1,0:T(8,128)(2,1)}, bf16[128,512]{1,0:T(8,128)(2,1)}) custom-call(bf16[128,2048]{1,0:T(8,128)(2,1)} %get-tuple-element.192.grad_ref.refs_0_, bf16[2048,2048]{1,0:T(8,128)(2,1)} %all-gather.11.cloned.1.call-done.weight_ref), custom_call_target="tpu_custom_call" | custom-call | flops 1073741824 | bytes 9437184 | tf_op jit(solution)/shard_map/pallas_call | solution.py:179
  439.7 12.0 %shard_map.260 = (bf16[256,384]{1,0:T(8,128)(2,1)}, bf16[256,384]{1,0:T(8,128)(2,1)}, bf16[256,384]{1,0:T(8,128)(2,1)}, bf16[256,384]{1,0:T(8,128)(2,1)}, bf16[2...) custom-call(s32[1]{0:T(128)} %bitcast.me_ref, ...), custom_call_target="tpu_custom_call" | custom-call | flops 2684354560 | bytes 4759556 | tf_op jit(solution)/shard_map/pallas_call | solution.py:162
  455.4 8.2 %collective-permute-done.61.refs_2_ = bf16[256,384]{1,0:T(8,128)(2,1)S(1)} collective-permute-done((bf16[256,384]{1,0:T(8,128)(2,1)}, bf16[256,384]{1,0:T(8,128)(2,1)S(1)}, u32[]{:S(2)}, u32[]{:S(2)}) %collective-permute-start.61) | collective-permute-done | bytes 196640 | tf_op jit(solution)/shard_map/ppermute | solution.py:55
  465.8 5.4 collective-permute-done.62.refs_3_
  476.1 10.3 %collective-permute-done.65.refs_6_ = bf16[256,384]{1,0:T(8,128)(2,1)S(1)} collective-permute-done((bf16[256,384]{1,0:T(8,128)(2,1)}, bf16[256,384]{1,0:T(8,128)(2,1)S(1)}, u32[]{:S(2)}, u32[]{:S(2)}) %collective-permute-start.65) | collective-permute-done | bytes 196640 | tf_op jit(solution)/shard_map/ppermute | solution.py:55
  486.4 7.8 %collective-permute-done.66.refs_7_ = bf16[256,384]{1,0:T(8,128)(2,1)S(1)} collective-permute-done((bf16[256,384]{1,0:T(8,128)(2,1)}, bf16[256,384]{1,0:T(8,128)(2,1)S(1)}, u32[]{:S(2)}, u32[]{:S(2)}) %collective-permute-start.66) | collective-permute-done | bytes 196640 | tf_op jit(solution)/shard_map/ppermute | solution.py:55
  494.9 3.6 shard_map.261
  498.5 4.2 shard_map.262
  503.4 3.3 collective-permute-start.71
  512.8 10.7 %shard_map.264 = (bf16[4,256,1024]{2,1,0:T(8,128)(2,1)}, bf16[4,256,1024]{2,1,0:T(8,128)(2,1)}) custom-call(s32[1]{0:T(128)} %bitcast.me_ref, bf16[512,2048]{1,0:T(8,128)(2,1)} %shard_map.263.refs_0_, bf16[512,2048]{1,0:T(8,128)(2,1)} %get-tuple-element.205.refs_1_.refs_0_, bf16[512,512]{1,0:T(8,128)(2,1)} %bitcast.97, bf16[512,512]{1,0:T(8,128)(2,1)} %bitcast.95), custom_call_target="tpu_custom_call" | custom-call | flops 2147483648 | bytes 9437188 | tf_op jit(solution)/shard_map/pallas_call | solution.py:179
  524.9 9.2 %shard_map.265 = (bf16[512,1024]{1,0:T(8,128)(2,1)}, bf16[128,2048]{1,0:T(8,128)(2,1)}, bf16[128,2048]{1,0:T(8,128)(2,1)}, bf16[128,2048]{1,0:T(8,128)(2,1)}, bf16[128,2048]{1,0:T(8,128)(2,1)}) custom-call(f32[512,1536]{1,0:T(8,128)} %get-tuple-element.124.raw_ref, f32[512,2]{1,0:T(8,128)} %bitcast.77, f32[512,2]{1,0:T(8,128)} %bitcast.86, ...), custom_call_target="tpu_custom_call" | custom-call | flops 3221225472 | bytes 15216640 | tf_op jit(solution)/shard_map/pallas_call | solution.py:179
  534.1 8.5 %shard_map.266 = (bf16[4,256,1024]{2,1,0:T(8,128)(2,1)}, bf16[4,256,1024]{2,1,0:T(8,128)(2,1)}) custom-call(s32[1]{0:T(128)} %bitcast.me_ref, bf16[512,2048]{1,0:T(8,128)(2,1)} %get-tuple-element.205.refs_1_.refs_0_, bf16[512,1024]{1,0:T(8,128)(2,1)} %get-tuple-element.214.refs_1_), custom_call_target="tpu_custom_call" | custom-call | flops 2147483648 | bytes 7340036 | tf_op jit(solution)/shard_map/pallas_call | solution.py:179
  543.1 3.6 collective-permute-done.85
  563.7 7.2 %collective-permute-done.74 = bf16[128,2048]{1,0:T(8,128)(2,1)S(1)} collective-permute-done((bf16[128,2048]{1,0:T(8,128)(2,1)}, bf16[128,2048]{1,0:T(8,128)(2,1)S(1)}, u32[]{:S(2)}, u32[]{:S(2)}) %collective-permute-start.74) | collective-permute-done | bytes 524320 | tf_op jit(solution)/shard_map/ppermute | solution.py:55
  573.2 6.3 %collective-permute-done.83 = bf16[256,1024]{1,0:T(8,128)(2,1)S(1)} collective-permute-done((bf16[256,1024]{1,0:T(8,128)(2,1)S(1)}, bf16[256,1024]{1,0:T(8,128)(2,1)S(1)}, u32[]{:S(2)}, u32[]{:S(2)}) %collective-permute-start.83) | collective-permute-done | bytes 524320 | tf_op jit(solution)/shard_map/ppermute | solution.py:116
  586.8 11.5 %collective-permute-done.75 = bf16[128,2048]{1,0:T(8,128)(2,1)} collective-permute-done((bf16[128,2048]{1,0:T(8,128)(2,1)}, bf16[128,2048]{1,0:T(8,128)(2,1)}, u32[]{:S(2)}, u32[]{:S(2)}) %collective-permute-start.75) | collective-permute-done | bytes 524320 | tf_op jit(solution)/shard_map/ppermute | solution.py:55
  598.3 6.7 %collective-permute-done.79 = bf16[256,1024]{1,0:T(8,128)(2,1)} collective-permute-done((bf16[256,1024]{1,0:T(8,128)(2,1)}, bf16[256,1024]{1,0:T(8,128)(2,1)}, u32[]{:S(2)}, u32[]{:S(2)}) %collective-permute-start.79) | collective-permute-done | bytes 524320 | tf_op jit(solution)/shard_map/ppermute | solution.py:116
  607.7 5.0 shard_map.269
  (415 shorter events, 180.1 us)
Async XLA Ops:
  7.2 51.7 %all-gather.5.cloned.1.call-start = ((), (), s32[]{:S(2)}) async-start(), calls=%async_computation.2 | async-start | bytes 7077888 | tf_op jit(solution)/shard_map/all_gather | solution.py:1157
  9.4 124.2 %all-gather.7.cloned.1.call-start = ((), (), s32[]{:S(2)}) async-start(), calls=%async_computation.3 | async-start | bytes 2359296 | tf_op jit(solution)/shard_map/all_gather | solution.py:1157
  10.3 218.4 %all-gather.9.cloned.1.call-start = ((), (), s32[]{:S(2)}) async-start(), calls=%async_computation.4 | async-start | bytes 28311552 | tf_op jit(solution)/shard_map/all_gather | solution.py:1157
  14.0 396.2 %all-gather.11.cloned.1.call-start = ((), (), s32[]{:S(2)}) async-start(), calls=%async_computation.5 | async-start | bytes 9437184 | tf_op jit(solution)/shard_map/all_gather | solution.py:1157
  15.0 37.0 %collective-permute-start = (bf16[128,2048]{1,0:T(8,128)(2,1)S(1)}, bf16[128,2048]{1,0:T(8,128)(2,1)S(1)}, u32[]{:S(2)}, u32[]{:S(2)}) collective-permute-start(bf16[128,2048]{1,0:T(8,128)(2,1)S(1)} %bitcast.92), channel_id=1, source_target_pairs={{0,1},{1,0},{2,3},{3,2},{4,5},{5,4},{6,7},{7,6},{8,9},{9,8},{10,11... | collective-permute-start | bytes 1572872 | tf_op jit(solution)/shard_map/ppermute | solution.py:87
  18.1 26.2 %collective-permute-start.1 = (bf16[128,2048]{1,0:T(8,128)(2,1)S(1)}, bf16[128,2048]{1,0:T(8,128)(2,1)S(1)}, u32[]{:S(2)}, u32[]{:S(2)}) collective-permute-start(bf16[128,2048]{1,0:T(8,128)(2,1)S(1)} %bitcast.93), channel_id=1, source_target_pairs={{0,2},{1,3},{2,0},{3,1},{4,6},{5,7},{6,4},{7,5},{8,10},{9,11},{10,... | collective-permute-start | bytes 1572872 | tf_op jit(solution)/shard_map/ppermute | solution.py:87
  20.7 22.9 %collective-permute-start.16 = (s32[2,64]{1,0:T(2,128)S(1)}, s32[2,64]{1,0:T(2,128)S(1)}, u32[]{:S(2)}, u32[]{:S(2)}) collective-permute-start(s32[2,64]{1,0:T(2,128)S(1)} %multiply_add_fusion), channel_id=1, source_target_pairs={{0,3},{1,2},{2,1},{3,0},{4,7},{5,6},{6,5},{7,4},{8,11},{9,10},{10,... | collective-permute-start | bytes 1544 | tf_op jit(solution)/shard_map/ppermute | solution.py:49
  20.7 24.8 %collective-permute-start.15 = (s32[2,64]{1,0:T(2,128)S(1)}, s32[2,64]{1,0:T(2,128)S(1)}, u32[]{:S(2)}, u32[]{:S(2)}) collective-permute-start(s32[2,64]{1,0:T(2,128)S(1)} %multiply_add_fusion), channel_id=1, source_target_pairs={{0,2},{1,3},{2,0},{3,1},{4,6},{5,7},{6,4},{7,5},{8,10},{9,11},{10,... | collective-permute-start | bytes 1544 | tf_op jit(solution)/shard_map/ppermute | solution.py:49
  22.6 22.9 %collective-permute-start.14 = (s32[2,64]{1,0:T(2,128)S(1)}, s32[2,64]{1,0:T(2,128)S(1)}, u32[]{:S(2)}, u32[]{:S(2)}) collective-permute-start(s32[2,64]{1,0:T(2,128)S(1)} %multiply_add_fusion), channel_id=1, source_target_pairs={{0,1},{1,0},{2,3},{3,2},{4,5},{5,4},{6,7},{7,6},{8,9},{9,8},{10,11... | collective-permute-start | bytes 1544 | tf_op jit(solution)/shard_map/ppermute | solution.py:49
  50.5 21.9 %collective-permute-start.19 = (s32[4,2,256]{2,1,0:T(2,128)S(1)}, s32[4,2,256]{2,1,0:T(2,128)S(1)}, u32[]{:S(2)}, u32[]{:S(2)}) collective-permute-start(s32[4,2,256]{2,1,0:T(2,128)S(1)} %pad_add_fusion.1), channel_id=1, source_target_pairs={{0,16},{4,20},{8,24},{12,28},{16,0},{20,4},{24,8},{28,12},{1,17},{... | collective-permute-start | bytes 24584 | tf_op jit(solution)/shard_map/ppermute | solution.py:63
  87.4 18.5 %collective-permute-start.11 = (bf16[256,384]{1,0:T(8,128)(2,1)}, bf16[256,384]{1,0:T(8,128)(2,1)S(1)}, u32[]{:S(2)}, u32[]{:S(2)}) collective-permute-start(bf16[256,384]{1,0:T(8,128)(2,1)} %get-tuple-element.131), channel_id=1, source_target_pairs={{0,20},{4,16},{8,28},{12,24},{16,4},{20,0},{24,12},{28,8},{1,21},{... | collective-permute-start | bytes 589832 | tf_op jit(solution)/shard_map/ppermute | solution.py:55
  141.9 23.8 %collective-permute-start.28 = (bf16[128,2048]{1,0:T(8,128)(2,1)}, bf16[128,2048]{1,0:T(8,128)(2,1)S(1)}, u32[]{:S(2)}, u32[]{:S(2)}) collective-permute-start(bf16[128,2048]{1,0:T(8,128)(2,1)} %get-tuple-element.144), channel_id=1, source_target_pairs={{1,2},{2,1},{5,6},{6,5},{9,10},{10,9},{13,14},{14,13},{17,18},{18,... | collective-permute-start | bytes 1572872 | tf_op jit(solution)/shard_map/ppermute | solution.py:87
  143.1 22.6 %collective-permute-start.27 = (bf16[128,2048]{1,0:T(8,128)(2,1)}, bf16[128,2048]{1,0:T(8,128)(2,1)S(1)}, u32[]{:S(2)}, u32[]{:S(2)}) collective-permute-start(bf16[128,2048]{1,0:T(8,128)(2,1)} %get-tuple-element.143), channel_id=1, source_target_pairs={{0,1},{1,0},{2,3},{3,2},{4,5},{5,4},{6,7},{7,6},{8,9},{9,8},{10,11... | collective-permute-start | bytes 1572872 | tf_op jit(solution)/shard_map/ppermute | solution.py:87
  155.8 25.5 %collective-permute-start.30 = (bf16[128,2048]{1,0:T(8,128)(2,1)S(1)}, bf16[128,2048]{1,0:T(8,128)(2,1)S(1)}, u32[]{:S(2)}, u32[]{:S(2)}) collective-permute-start(bf16[128,2048]{1,0:T(8,128)(2,1)S(1)} %add_convert_fusion.8), channel_id=1, source_target_pairs={{0,2},{1,3},{2,0},{3,1},{4,6},{5,7},{6,4},{7,5},{8,10},{9,11},{10,... | collective-permute-start | bytes 1572872 | tf_op jit(solution)/shard_map/ppermute | solution.py:87
  185.9 24.6 %collective-permute-start.32 = (bf16[128,2048]{1,0:T(8,128)(2,1)}, bf16[128,2048]{1,0:T(8,128)(2,1)S(1)}, u32[]{:S(2)}, u32[]{:S(2)}) collective-permute-start(bf16[128,2048]{1,0:T(8,128)(2,1)} %get-tuple-element.146.refs_0_), channel_id=1, source_target_pairs={{0,2},{1,3},{2,0},{3,1},{4,6},{5,7},{6,4},{7,5},{8,10},{9,11},{10,... | collective-permute-start | bytes 1572872 | tf_op jit(solution)/shard_map/ppermute | solution.py:87
  185.9 28.7 %collective-permute-start.31 = (bf16[128,2048]{1,0:T(8,128)(2,1)}, bf16[128,2048]{1,0:T(8,128)(2,1)S(1)}, u32[]{:S(2)}, u32[]{:S(2)}) collective-permute-start(bf16[128,2048]{1,0:T(8,128)(2,1)} %get-tuple-element.146.refs_0_), channel_id=1, source_target_pairs={{0,1},{1,0},{2,3},{3,2},{4,5},{5,4},{6,7},{7,6},{8,9},{9,8},{10,11... | collective-permute-start | bytes 1572872 | tf_op jit(solution)/shard_map/ppermute | solution.py:87
  188.6 28.3 %collective-permute-start.33 = (bf16[128,2048]{1,0:T(8,128)(2,1)}, bf16[128,2048]{1,0:T(8,128)(2,1)S(1)}, u32[]{:S(2)}, u32[]{:S(2)}) collective-permute-start(bf16[128,2048]{1,0:T(8,128)(2,1)} %get-tuple-element.146.refs_0_), channel_id=1, source_target_pairs={{1,2},{2,1},{5,6},{6,5},{9,10},{10,9},{13,14},{14,13},{17,18},{18,... | collective-permute-start | bytes 1572872 | tf_op jit(solution)/shard_map/ppermute | solution.py:87
  211.8 40.3 %collective-permute-start.47 = (bf16[256,512]{1,0:T(8,128)(2,1)S(1)}, bf16[256,512]{1,0:T(8,128)(2,1)S(1)}, u32[]{:S(2)}, u32[]{:S(2)}) collective-permute-start(bf16[256,512]{1,0:T(8,128)(2,1)S(1)} %bitcast.80), channel_id=1, source_target_pairs={{0,1},{1,0},{2,3},{3,2},{4,5},{5,4},{6,7},{7,6},{8,9},{9,8},{10,11... | collective-permute-start | bytes 786440 | tf_op jit(solution)/shard_map/ppermute | solution.py:49
  214.5 37.6 %collective-permute-start.48 = (bf16[256,512]{1,0:T(8,128)(2,1)S(1)}, bf16[256,512]{1,0:T(8,128)(2,1)S(1)}, u32[]{:S(2)}, u32[]{:S(2)}) collective-permute-start(bf16[256,512]{1,0:T(8,128)(2,1)S(1)} %bitcast.81), channel_id=1, source_target_pairs={{0,2},{1,3},{2,0},{3,1},{4,6},{5,7},{6,4},{7,5},{8,10},{9,11},{10,... | collective-permute-start | bytes 786440 | tf_op jit(solution)/shard_map/ppermute | solution.py:49
  214.6 37.5 %collective-permute-start.49 = (bf16[256,512]{1,0:T(8,128)(2,1)S(1)}, bf16[256,512]{1,0:T(8,128)(2,1)S(1)}, u32[]{:S(2)}, u32[]{:S(2)}) collective-permute-start(bf16[256,512]{1,0:T(8,128)(2,1)S(1)} %bitcast.82), channel_id=1, source_target_pairs={{0,3},{1,2},{2,1},{3,0},{4,7},{5,6},{6,5},{7,4},{8,11},{9,10},{10,... | collective-permute-start | bytes 786440 | tf_op jit(solution)/shard_map/ppermute | solution.py:49
  253.3 354.4 %reduce-scatter.5.cloned.1.call-start = ((), (), s32[]{:S(2)}) async-start(), calls=%async_computation.7 | async-start | bytes 9437184 | tf_op jit(solution)/shard_map/reduce_scatter | solution.py:1210
  254.7 23.6 %collective-permute-start.36 = (bf16[128,2048]{1,0:T(8,128)(2,1)S(1)}, bf16[128,2048]{1,0:T(8,128)(2,1)S(1)}, u32[]{:S(2)}, u32[]{:S(2)}) collective-permute-start(bf16[128,2048]{1,0:T(8,128)(2,1)S(1)} %copy-done.62), channel_id=1, source_target_pairs={{1,2},{2,1},{5,6},{6,5},{9,10},{10,9},{13,14},{14,13},{17,18},{18,... | collective-permute-start | bytes 1572872 | tf_op jit(solution)/shard_map/ppermute | solution.py:87
  255.4 22.9 %collective-permute-start.35 = (bf16[128,2048]{1,0:T(8,128)(2,1)S(1)}, bf16[128,2048]{1,0:T(8,128)(2,1)S(1)}, u32[]{:S(2)}, u32[]{:S(2)}) collective-permute-start(bf16[128,2048]{1,0:T(8,128)(2,1)S(1)} %copy-done.63), channel_id=1, source_target_pairs={{0,1},{1,0},{2,3},{3,2},{4,5},{5,4},{6,7},{7,6},{8,9},{9,8},{10,11... | collective-permute-start | bytes 1572872 | tf_op jit(solution)/shard_map/ppermute | solution.py:87
  267.1 22.8 %collective-permute-start.38 = (bf16[128,2048]{1,0:T(8,128)(2,1)S(1)}, bf16[128,2048]{1,0:T(8,128)(2,1)S(1)}, u32[]{:S(2)}, u32[]{:S(2)}) collective-permute-start(bf16[128,2048]{1,0:T(8,128)(2,1)S(1)} %add_convert_fusion.7), channel_id=1, source_target_pairs={{0,2},{1,3},{2,0},{3,1},{4,6},{5,7},{6,4},{7,5},{8,10},{9,11},{10,... | collective-permute-start | bytes 1572872 | tf_op jit(solution)/shard_map/ppermute | solution.py:87
  294.5 23.3 %collective-permute-start.40 = (bf16[128,2048]{1,0:T(8,128)(2,1)}, bf16[128,2048]{1,0:T(8,128)(2,1)S(1)}, u32[]{:S(2)}, u32[]{:S(2)}) collective-permute-start(bf16[128,2048]{1,0:T(8,128)(2,1)} %get-tuple-element.153.refs_0_), channel_id=1, source_target_pairs={{0,2},{1,3},{2,0},{3,1},{4,6},{5,7},{6,4},{7,5},{8,10},{9,11},{10,... | collective-permute-start | bytes 1572872 | tf_op jit(solution)/shard_map/ppermute | solution.py:87
  294.9 24.3 %collective-permute-start.39 = (bf16[128,2048]{1,0:T(8,128)(2,1)}, bf16[128,2048]{1,0:T(8,128)(2,1)S(1)}, u32[]{:S(2)}, u32[]{:S(2)}) collective-permute-start(bf16[128,2048]{1,0:T(8,128)(2,1)} %get-tuple-element.153.refs_0_), channel_id=1, source_target_pairs={{0,1},{1,0},{2,3},{3,2},{4,5},{5,4},{6,7},{7,6},{8,9},{9,8},{10,11... | collective-permute-start | bytes 1572872 | tf_op jit(solution)/shard_map/ppermute | solution.py:87
  297.4 21.7 %collective-permute-start.41 = (bf16[128,2048]{1,0:T(8,128)(2,1)}, bf16[128,2048]{1,0:T(8,128)(2,1)S(1)}, u32[]{:S(2)}, u32[]{:S(2)}) collective-permute-start(bf16[128,2048]{1,0:T(8,128)(2,1)} %get-tuple-element.153.refs_0_), channel_id=1, source_target_pairs={{1,2},{2,1},{5,6},{6,5},{9,10},{10,9},{13,14},{14,13},{17,18},{18,... | collective-permute-start | bytes 1572872 | tf_op jit(solution)/shard_map/ppermute | solution.py:87
  342.6 265.1 %reduce-scatter.3.cloned.1.call-start = ((), (), s32[]{:S(2)}) async-start(), calls=%async_computation.6 | async-start | bytes 18874368 | tf_op jit(solution)/shard_map/reduce_scatter | solution.py:1212
  369.1 36.1 %collective-permute-start.44 = (bf16[128,2048]{1,0:T(8,128)(2,1)}, bf16[128,2048]{1,0:T(8,128)(2,1)S(1)}, u32[]{:S(2)}, u32[]{:S(2)}) collective-permute-start(bf16[128,2048]{1,0:T(8,128)(2,1)} %get-tuple-element.160), channel_id=1, source_target_pairs={{1,2},{2,1},{5,6},{6,5},{9,10},{10,9},{13,14},{14,13},{17,18},{18,... | collective-permute-start | bytes 1572872 | tf_op jit(solution)/shard_map/ppermute | solution.py:87
  369.8 35.4 %collective-permute-start.43 = (bf16[128,2048]{1,0:T(8,128)(2,1)}, bf16[128,2048]{1,0:T(8,128)(2,1)S(1)}, u32[]{:S(2)}, u32[]{:S(2)}) collective-permute-start(bf16[128,2048]{1,0:T(8,128)(2,1)} %get-tuple-element.159), channel_id=1, source_target_pairs={{0,1},{1,0},{2,3},{3,2},{4,5},{5,4},{6,7},{7,6},{8,9},{9,8},{10,11... | collective-permute-start | bytes 1572872 | tf_op jit(solution)/shard_map/ppermute | solution.py:87
  382.9 22.5 %collective-permute-start.46 = (bf16[128,2048]{1,0:T(8,128)(2,1)S(1)}, bf16[128,2048]{1,0:T(8,128)(2,1)S(1)}, u32[]{:S(2)}, u32[]{:S(2)}) collective-permute-start(bf16[128,2048]{1,0:T(8,128)(2,1)S(1)} %add_convert_fusion.6), channel_id=1, source_target_pairs={{0,2},{1,3},{2,0},{3,1},{4,6},{5,7},{6,4},{7,5},{8,10},{9,11},{10,... | collective-permute-start | bytes 1572872 | tf_op jit(solution)/shard_map/ppermute | solution.py:87
  434.8 37.1 %collective-permute-start.68 = (bf16[128,2048]{1,0:T(8,128)(2,1)S(1)}, bf16[128,2048]{1,0:T(8,128)(2,1)S(1)}, u32[]{:S(2)}, u32[]{:S(2)}) collective-permute-start(bf16[128,2048]{1,0:T(8,128)(2,1)S(1)} %copy-done.5), channel_id=1, source_target_pairs={{0,2},{1,3},{2,0},{3,1},{4,6},{5,7},{6,4},{7,5},{8,10},{9,11},{10,... | collective-permute-start | bytes 1572872 | tf_op jit(solution)/shard_map/ppermute | solution.py:87
  453.7 19.6 %collective-permute-start.63 = (bf16[256,384]{1,0:T(8,128)(2,1)}, bf16[256,384]{1,0:T(8,128)(2,1)S(1)}, u32[]{:S(2)}, u32[]{:S(2)}) collective-permute-start(bf16[256,384]{1,0:T(8,128)(2,1)} %get-tuple-element.188), channel_id=1, source_target_pairs={{0,16},{4,20},{8,24},{12,28},{16,0},{20,4},{24,8},{28,12},{1,17},{... | collective-permute-start | bytes 589832 | tf_op jit(solution)/shard_map/ppermute | solution.py:55
  455.0 19.1 %collective-permute-start.64 = (bf16[256,384]{1,0:T(8,128)(2,1)}, bf16[256,384]{1,0:T(8,128)(2,1)S(1)}, u32[]{:S(2)}, u32[]{:S(2)}) collective-permute-start(bf16[256,384]{1,0:T(8,128)(2,1)} %get-tuple-element.189), channel_id=1, source_target_pairs={{0,20},{4,16},{8,28},{12,24},{16,4},{20,0},{24,12},{28,8},{1,21},{... | collective-permute-start | bytes 589832 | tf_op jit(solution)/shard_map/ppermute | solution.py:55
  463.6 30.7 %collective-permute-start.67 = (bf16[128,2048]{1,0:T(8,128)(2,1)S(1)}, bf16[128,2048]{1,0:T(8,128)(2,1)S(1)}, u32[]{:S(2)}, u32[]{:S(2)}) collective-permute-start(bf16[128,2048]{1,0:T(8,128)(2,1)S(1)} %copy-done.5), channel_id=1, source_target_pairs={{0,1},{1,0},{2,3},{3,2},{4,5},{5,4},{6,7},{7,6},{8,9},{9,8},{10,11... | collective-permute-start | bytes 1572872 | tf_op jit(solution)/shard_map/ppermute | solution.py:87
  471.2 23.0 %collective-permute-start.69 = (bf16[128,2048]{1,0:T(8,128)(2,1)S(1)}, bf16[128,2048]{1,0:T(8,128)(2,1)S(1)}, u32[]{:S(2)}, u32[]{:S(2)}) collective-permute-start(bf16[128,2048]{1,0:T(8,128)(2,1)S(1)} %copy-done.5), channel_id=1, source_target_pairs={{1,2},{2,1},{5,6},{6,5},{9,10},{10,9},{13,14},{14,13},{17,18},{18,... | collective-permute-start | bytes 1572872 | tf_op jit(solution)/shard_map/ppermute | solution.py:87
  471.9 22.3 %collective-permute-start.70 = (bf16[128,2048]{1,0:T(8,128)(2,1)S(1)}, bf16[128,2048]{1,0:T(8,128)(2,1)S(1)}, u32[]{:S(2)}, u32[]{:S(2)}) collective-permute-start(bf16[128,2048]{1,0:T(8,128)(2,1)S(1)} %collective-permute-done.68.refs_2_), channel_id=1, source_target_pairs={{1,0},{2,3},{5,4},{6,7},{9,8},{10,11},{13,12},{14,15},{17,16},{18,... | collective-permute-start | bytes 1572872 | tf_op jit(solution)/shard_map/ppermute | solution.py:87
  474.1 20.1 %collective-permute-start.66 = (bf16[256,384]{1,0:T(8,128)(2,1)}, bf16[256,384]{1,0:T(8,128)(2,1)S(1)}, u32[]{:S(2)}, u32[]{:S(2)}) collective-permute-start(bf16[256,384]{1,0:T(8,128)(2,1)} %get-tuple-element.191), channel_id=1, source_target_pairs={{0,28},{4,24},{8,20},{12,16},{16,12},{20,8},{24,4},{28,0},{1,29},{... | collective-permute-start | bytes 589832 | tf_op jit(solution)/shard_map/ppermute | solution.py:55
  503.4 20.1 %collective-permute-start.71 = (f32[5120]{0:T(1024)S(1)}, f32[5120]{0:T(1024)S(1)}, u32[]{:S(2)}, u32[]{:S(2)}) collective-permute-start(f32[5120]{0:T(1024)S(1)} %pad_maximum_fusion.5), channel_id=1, source_target_pairs={{0,1},{1,0},{2,3},{3,2},{4,5},{5,4},{6,7},{7,6},{8,9},{9,8},{10,11... | collective-permute-start | bytes 61448 | tf_op jit(solution)/shard_map/ppermute | solution.py:49
  523.5 31.4 %collective-permute-start.81 = (bf16[4,256,1024]{2,1,0:T(8,128)(2,1)}, bf16[4,256,1024]{2,1,0:T(8,128)(2,1)S(1)}, u32[]{:S(2)}, u32[]{:S(2)}) collective-permute-start(bf16[4,256,1024]{2,1,0:T(8,128)(2,1)} %get-tuple-element.207), channel_id=1, source_target_pairs={{0,4},{4,0},{8,12},{12,8},{16,20},{20,16},{24,28},{28,24},{1,5},{5... | collective-permute-start | bytes 6291464 | tf_op jit(solution)/shard_map/ppermute | solution.py:121
  551.8 19.1 %collective-permute-start.74 = (bf16[128,2048]{1,0:T(8,128)(2,1)}, bf16[128,2048]{1,0:T(8,128)(2,1)S(1)}, u32[]{:S(2)}, u32[]{:S(2)}) collective-permute-start(bf16[128,2048]{1,0:T(8,128)(2,1)} %get-tuple-element.211), channel_id=1, source_target_pairs={{0,1},{1,0},{2,3},{3,2},{4,5},{5,4},{6,7},{7,6},{8,9},{9,8},{10,11... | collective-permute-start | bytes 1572872 | tf_op jit(solution)/shard_map/ppermute | solution.py:55
  557.8 21.7 %collective-permute-start.83 = (bf16[256,1024]{1,0:T(8,128)(2,1)S(1)}, bf16[256,1024]{1,0:T(8,128)(2,1)S(1)}, u32[]{:S(2)}, u32[]{:S(2)}) collective-permute-start(bf16[256,1024]{1,0:T(8,128)(2,1)S(1)} %get-tuple-element.276), channel_id=1, source_target_pairs={{0,16},{4,20},{8,24},{12,28},{16,0},{20,4},{24,8},{28,12},{1,17},{... | collective-permute-start | bytes 1572872 | tf_op jit(solution)/shard_map/ppermute | solution.py:116
  558.9 23.6 %collective-permute-start.82 = (bf16[256,1024]{1,0:T(8,128)(2,1)S(1)}, bf16[256,1024]{1,0:T(8,128)(2,1)S(1)}, u32[]{:S(2)}, u32[]{:S(2)}) collective-permute-start(bf16[256,1024]{1,0:T(8,128)(2,1)S(1)} %get-tuple-element.274), channel_id=1, source_target_pairs={{0,8},{4,12},{8,0},{12,4},{16,24},{20,28},{24,16},{28,20},{1,9},{5... | collective-permute-start | bytes 1572872 | tf_op jit(solution)/shard_map/ppermute | solution.py:116
  559.7 38.5 %collective-permute-start.75 = (bf16[128,2048]{1,0:T(8,128)(2,1)}, bf16[128,2048]{1,0:T(8,128)(2,1)}, u32[]{:S(2)}, u32[]{:S(2)}) collective-permute-start(bf16[128,2048]{1,0:T(8,128)(2,1)} %get-tuple-element.212), channel_id=1, source_target_pairs={{0,2},{1,3},{2,0},{3,1},{4,6},{5,7},{6,4},{7,5},{8,10},{9,11},{10,... | collective-permute-start | bytes 1572872 | tf_op jit(solution)/shard_map/ppermute | solution.py:55
  570.9 27.4 %collective-permute-start.76 = (bf16[128,2048]{1,0:T(8,128)(2,1)}, bf16[128,2048]{1,0:T(8,128)(2,1)}, u32[]{:S(2)}, u32[]{:S(2)}) collective-permute-start(bf16[128,2048]{1,0:T(8,128)(2,1)} %get-tuple-element.213), channel_id=1, source_target_pairs={{0,3},{1,2},{2,1},{3,0},{4,7},{5,6},{6,5},{7,4},{8,11},{9,10},{10,... | collective-permute-start | bytes 1572872 | tf_op jit(solution)/shard_map/ppermute | solution.py:55
  572.4 25.9 %collective-permute-start.78 = (bf16[256,1024]{1,0:T(8,128)(2,1)}, bf16[256,1024]{1,0:T(8,128)(2,1)}, u32[]{:S(2)}, u32[]{:S(2)}) collective-permute-start(bf16[256,1024]{1,0:T(8,128)(2,1)} %get-tuple-element.280), channel_id=1, source_target_pairs={{0,8},{4,12},{8,0},{12,4},{16,24},{20,28},{24,16},{28,20},{1,9},{5... | collective-permute-start | bytes 1572872 | tf_op jit(solution)/shard_map/ppermute | solution.py:116
  579.5 25.5 %collective-permute-start.79 = (bf16[256,1024]{1,0:T(8,128)(2,1)}, bf16[256,1024]{1,0:T(8,128)(2,1)}, u32[]{:S(2)}, u32[]{:S(2)}) collective-permute-start(bf16[256,1024]{1,0:T(8,128)(2,1)} %get-tuple-element.279), channel_id=1, source_target_pairs={{0,16},{4,20},{8,24},{12,28},{16,0},{20,4},{24,8},{28,12},{1,17},{... | collective-permute-start | bytes 1572872 | tf_op jit(solution)/shard_map/ppermute | solution.py:116
  582.5 22.5 %collective-permute-start.80 = (bf16[256,1024]{1,0:T(8,128)(2,1)}, bf16[256,1024]{1,0:T(8,128)(2,1)}, u32[]{:S(2)}, u32[]{:S(2)}) collective-permute-start(bf16[256,1024]{1,0:T(8,128)(2,1)} %get-tuple-element.278), channel_id=1, source_target_pairs={{0,24},{4,28},{8,16},{12,20},{16,8},{20,12},{24,0},{28,4},{1,25},{... | collective-permute-start | bytes 1572872 | tf_op jit(solution)/shard_map/ppermute | solution.py:116
  (124 other events, 1270.6 us)
Sparse Core Ops, SparseCore 0:
  10.5 48.3 all-gather.4
  61.4 28.7 all-gather.6
  92.1 133.2 all-gather.8
  253.4 54.3 all-gather.10
  342.7 71.3 reduce-scatter.4
  417.9 132.7 reduce-scatter.2

commit v5 on v4

--- a/solution.py
+++ b/solution.py
@@ -115,6 +115,16 @@
     return [slots[0]] + [
         lax.ppermute(slots[m], "blk", xor_pairs(size, 2 * m)) for m in range(1, size // 2)
     ]
+
+
+def exchange_blocks(slots):
+    size = len(slots)
+    if size != 8:
+        return exchange_slots(slots, "blk")
+    arrived = {s: lax.ppermute(slots[s], "blk", xor_pairs(size, s)) for s in range(2, size - 1)}
+    for s in (size - 1, 1):
+        arrived[s] = lax.ppermute(after(slots[s], arrived[2]), "blk", xor_pairs(size, s))
+    return [slots[0]] + [arrived[s] for s in range(1, size)]
 
 
 def swap_cores(values):
@@ -609,7 +619,24 @@
     )
 
 
-def project_input_grad(raw, scales, dots, gains, grads, grad_value, weights, slot_count, micro_count):
+def norm_backward(raw, scales, dots, gains, grads):
+    rows, features = grads.shape
+    width = features // 2
+
+    def body(raw_ref, scale_ref, dot_ref, gain_ref, grad_ref, low_ref):
+        for k in range(2):
+            cut = slice(k * width, (k + 1) * width)
+            scale = scale_ref[:, k : k + 1]
+            hat = raw_ref[:, cut] * scale
+            grad_hat = grad_ref[:, cut] * gain_ref[:, cut]
+            low_ref[:, cut] = (scale * (grad_hat - hat * dot_ref[:, k : k + 1])).astype(low)
+
+    return call_whole(
+        body, [shape_of((rows, features), low)], raw, scales, dots, gains, grads, scalars=0
+    )[0]
+
+
+def project_input_grad(grad_qk, grad_value, weights, slot_count, micro_count):
     rows, features = grad_value.shape[0], weights.shape[1]
     width = features // 3
     out_width = weights.shape[0]
@@ -617,48 +644,29 @@
     tile = tile_of(out_width)
     steps = out_width // tile
 
-    def body(raw_ref, scale_ref, dot_ref, gain_ref, grad_ref, value_ref, weight_ref, low_ref, *out_refs):
-        @pl.when(pl.program_id(0) == 0)
-        def _():
-            for k in range(2):
-                cut = slice(k * width, (k + 1) * width)
-                scale = scale_ref[:, k : k + 1]
-                hat = raw_ref[:, cut] * scale
-                grad_hat = grad_ref[:, cut] * gain_ref[:, cut]
-                low_ref[:, cut] = (scale * (grad_hat - hat * dot_ref[:, k : k + 1])).astype(low)
-
-        terms = dot_right_t(low_ref[...], weight_ref[:, : 2 * width])
+    def body(qk_ref, value_ref, weight_ref, *out_refs):
+        terms = dot_right_t(qk_ref[...], weight_ref[:, : 2 * width])
         terms += dot_right_t(value_ref[...], weight_ref[:, 2 * width :])
         put_slots(out_refs, terms, micro_count)
 
     return call_grid(
         body,
         steps,
-        [shape_of((rows, 2 * width), low)]
-        + [shape_of((local_rows, out_width), low)] * slot_count,
+        [shape_of((local_rows, out_width), low)] * slot_count,
         [
-            fixed((rows, 2 * width)),
-            fixed((rows, 2)),
-            fixed((rows, 2)),
-            fixed((1, 2 * width)),
             fixed((rows, 2 * width)),
             fixed((rows, width)),
             pl.BlockSpec((tile, features), lambda i: (i, 0)),
         ],
-        [fixed((rows, 2 * width))]
-        + [pl.BlockSpec((local_rows, tile), lambda i: (0, i))] * slot_count,
-        raw,
-        scales,
-        dots,
-        gains,
-        grads,
+        [column_tile(local_rows, tile)] * slot_count,
+        grad_qk,
         grad_value,
         weights,
         flops=2 * rows * features * out_width,
     )
 
 
-def weight_term_slots(me, pairs, blocks):
+def weight_term_slots(me, pairs, blocks, place, places, held=()):
     n = len(pairs)
     rows, width = pairs[0][0].shape
     sizes = [right.shape[1] for _, right in pairs]
@@ -667,8 +675,8 @@
     half = blocks // 2
 
     def body(me_ref, *refs):
-        odd_ref, even_ref = refs[2 * n : 2 * n + 2]
-        lefts = refs[2 * n + 2 :]
+        odd_ref, even_ref = refs[-2 - n : -n]
+        lefts = refs[-n:]
         step = pl.program_id(0)
 
         @pl.when(step == 0)
@@ -677,10 +685,10 @@
                 left_t[...] = jnp.transpose(left[...])
 
         slot = jnp.where(step < half, 2 * step + 1, 2 * step - blocks)
-        place = pl.multiple_of((me_ref[0] ^ slot) * part, part)
+        rows_at = pl.multiple_of((me_ref[0] ^ slot) * part, part)
         first = 0
         for left_t, right, size in zip(lefts, refs[n : 2 * n], sizes):
-            term = dot_plain(left_t[pl.ds(place, part), :], right[...]).astype(low)
+            term = dot_plain(left_t[pl.ds(rows_at, part), :], right[...]).astype(low)
             cut = slice(first, first + size)
             first += size
 
@@ -692,33 +700,60 @@
             def _():
                 even_ref[0, :, cut] = term
 
-    return call_grid(
-        body,
-        blocks,
-        [shape_of((half, part, features), low)] * 2,
-        [scalar_spec]
+    outs = [shape_of((half, part, places * features), low)] * 2
+    return pl.pallas_call(
+        body,
+        grid=(blocks,),
+        out_shape=outs,
+        in_specs=[scalar_spec]
         + [fixed((rows, width))] * n
-        + [fixed((rows, size)) for size in sizes],
-        [
-            pl.BlockSpec((1, part, features), lambda i: (jnp.minimum(i, half - 1), 0, 0)),
-            pl.BlockSpec((1, part, features), lambda i: (jnp.maximum(i - half, 0), 0, 0)),
+        + [fixed((rows, size)) for size in sizes]
+        + [pl.BlockSpec(memory_space=pl.ANY)] * len(held),
+        out_specs=[
+            pl.BlockSpec((1, part, features), lambda i: (jnp.minimum(i, half - 1), 0, place)),
+            pl.BlockSpec((1, part, features), lambda i: (jnp.maximum(i - half, 0), 0, place)),
         ],
-        me,
-        *[left for left, _ in pairs],
-        *[right for _, right in pairs],
-        scratch=[pltpu.VMEM((width, rows), low)] * n,
-        flops=2 * rows * width * features,
-    )
-
-
-def add_cores(terms):
+        scratch_shapes=[pltpu.VMEM((width, rows), low)] * n,
+        input_output_aliases={1 + 2 * n + k: k for k in range(len(held))},
+        compiler_params=pltpu.CompilerParams(vmem_limit_bytes=vmem_grant),
+        cost_estimate=pl.CostEstimate(
+            flops=2 * rows * width * features,
+            bytes_accessed=n * rows * width * 2 + rows * features * 2 + width * features * 2,
+            transcendentals=0,
+        ),
+    )(me, *[left for left, _ in pairs], *[right for _, right in pairs], *held)
+
+
+def add_cores(terms, *others):
     odd, even = terms
     arrived = swap_cores(odd)
+    even = after(even, *others) if others else even
     return [even[k].astype(full) + arrived[k].astype(full) for k in range(even.shape[0])]
 
 
-def add_chips(pairs):
-    return sum_full(exchange_chips([pairs[0]] + [pair.astype(low) for pair in pairs[1:]]))
+def add_chips(pairs, *others):
+    half = pairs[0].shape[1] // 2
+    one, other = slice(0, half), slice(half, 2 * half)
+    if len(pairs) != 4:
+        slots = exchange_chips([pairs[0]] + [pair.astype(low) for pair in pairs[1:]])
+        total = sum_full(slots)
+        return total[:, one], total[:, other]
+    along = [xor_pairs(8, 2), xor_pairs(8, 4)]
+    sent = [
+        jnp.stack([pairs[1][:, one], pairs[3][:, one]]).astype(low),
+        jnp.stack([pairs[2][:, other], pairs[3][:, other]]).astype(low),
+    ]
+    arrived = [lax.ppermute(sent[k], "blk", along[k]).astype(full) for k in range(2)]
+    sent = [
+        (pairs[2][:, one] + arrived[0][1]).astype(low),
+        (pairs[1][:, other] + arrived[1][1]).astype(low),
+    ]
+    sent = after(sent, *others)
+    final = [lax.ppermute(sent[k], "blk", along[1 - k]).astype(full) for k in range(2)]
+    return (
+        pairs[0][:, one] + arrived[0][0] + final[0],
+        pairs[0][:, other] + arrived[1][0] + final[1],
+    )
 
 
 def send_views(me, raw, scales, gains, tables, heads_local):
@@ -1090,8 +1125,8 @@
         self.micro_count = raw.shape[0]
         place = lax.axis_index("blk")
         self.me = place.astype(jnp.int32).reshape(1)
-        self.slots = exchange_slots(
-            send_views(self.me, raw, scales, gains, tables, self.heads), "blk"
+        self.slots = exchange_blocks(
+            send_views(self.me, raw, scales, gains, tables, self.heads)
         )
         codes = lax.dynamic_index_in_dim(codes, place // self.heads, 0, keepdims=False)
         seg_all = codes // 2
@@ -1223,24 +1258,26 @@
     )
     mean_dots = dots / model_width
     gain_grads = jnp.concatenate([gain_grads, qk_gain_grad[0]])
+    grad_qk = norm_backward(raw, scales, mean_dots, gain_row, grad_norm)
     early_terms = weight_term_slots(
-        me, [(grad_attn_rows, all_rows(mixed)), (token_rows, grad_value)], blocks
-    )
-    mean_dots = after(mean_dots, *early_terms)
-    results = project_input_grad(
-        raw, scales, mean_dots, gain_row, grad_norm, grad_value, qkv_full, head_size, micro_count
-    )
-    input_parts = exchange_slots(results[1:], "head")
-    early_grads = add_chips(add_cores(early_terms))
+        me, [(grad_attn_rows, all_rows(mixed)), (token_rows, grad_value)], blocks, 0, 2
+    )
+    hops = [gain_grads]
+    for k in range(blocks.bit_length() - 1):
+        hops.append(hops[-1] + lax.ppermute(hops[-1], "blk", xor_pairs(blocks, 1 << k)))
+    norm_gain_grads = hops[-1][: 2 * model_width]
+    qk_gain_grad = hops[-1][2 * model_width :]
+    terms = weight_term_slots(
+        me, [(token_rows, after(grad_qk, hops[1]))], blocks, 1, 2, early_terms
+    )
+    slots = project_input_grad(
+        after(grad_qk, *terms), grad_value, qkv_full, head_size, micro_count
+    )
+    pairs = add_cores(terms, hops[-1], *slots)
+    input_parts = reduce_parts(slots)
+    early_grads, qk_grad = add_chips(pairs, *ffn_grads, input_parts[1])
     output_grad = early_grads[:, :width].T
-    qk_terms = weight_term_slots(me, [(token_rows, results[0])], blocks)
-    qk_pairs = add_cores(qk_terms)
-    gain_grads = sum_doubling(after(gain_grads, *qk_terms), "blk")
-    norm_gain_grads = gain_grads[: 2 * model_width]
-    qk_gain_grad = gain_grads[2 * model_width :]
-    qk_slots = exchange_chips([qk_pairs[0]] + [pair.astype(low) for pair in qk_pairs[1:]])
-    input_grad = sum_full(after(input_parts, *qk_slots[1:])) + grad_hidden
-    qk_grad = sum_full(after(qk_slots, ffn_grads, output_grad))
+    input_grad = sum_full(input_parts) + grad_hidden
     return (
         by_micro(output),
         by_micro(input_grad),

time: 628 us -> 622 us (level)
  waiting for transfers between devices: 264 us -> 252 us
    ppermute x34 -> x24, waiting for transfers between devices: 80.7 us -> 48.5 us  [exchange_slots(): lax.ppermute(slots[s], axis, xor_pairs(size, s))]
    ppermute x28 -> x32, waiting for transfers between devices: 142 us -> 166 us  [send_rows(): return lax.ppermute(values, 'head', pairs)]
    pallas_call x7 -> x5, Pallas kernels: 91.2 us -> 70 us  [call_grid(): pl.pallas_call(body, grid=(steps,), out_shape=outs, in_specs=in_specs, ou...]
    pallas_call x0 -> x2, Pallas kernels: none -> 19.5 us  [weight_term_slots(): pl.pallas_call(body, grid=(blocks,), out_shape=outs, in_specs=[scalar_spe...]
    ppermute x28 -> x32, starting transfers between devices: 48 us -> 57.4 us  [send_rows(): return lax.ppermute(values, 'head', pairs)]
    ppermute x34 -> x24, starting transfers between devices: 33 us -> 23.9 us  [exchange_slots(): lax.ppermute(slots[s], axis, xor_pairs(size, s))]
    pallas_call x14 -> x15, Pallas kernels: 65.7 us -> 69.7 us  [call_whole(): pl.pallas_call(body, out_shape=outs, in_specs=[pl.BlockSpec(memory_space=...]
    ppermute x9 -> x14, waiting for transfers between devices: 21.3 us -> 17.4 us  [the longest x5 8.05 us: exchange_blocks(): lax.ppermute(slots[s], 'blk', xor_pairs(size, s))]
  transfers between devices with their start and end apart: 94 -> 92, of which waited for: 44 -> 40; matrix products, arithmetic and copies ran while one was open for 4% -> 5% of each run, Pallas kernels for 29% -> 30%
where the time goes in v5:
time: 622 us; the launch traced here: 618 us
  waiting for transfers between devices  252 us (41%)
  Pallas kernels  187 us (30%)
  starting transfers between devices  116 us (19%)
  other arithmetic  26.5 us (4%)
  local copies, waits for them, and re-layouts  20.6 us (3%)
  between operations  15.5 us (2%)
    ppermute x32, waiting for transfers between devices, send_rows(): return lax.ppermute(values, 'head', pairs)  166 us
    pallas_call x5, Pallas kernels, call_grid(): pl.pallas_call(body, grid=(steps,), out_shape=outs, in_specs=in_specs, ou...  70 us
    pallas_call x15, Pallas kernels, call_whole(): pl.pallas_call(body, out_shape=outs, in_specs=[pl.BlockSpec(memory_space=...  69.7 us
    ppermute x32, starting transfers between devices, send_rows(): return lax.ppermute(values, 'head', pairs)  57.4 us
    ppermute x24, waiting for transfers between devices, exchange_slots(): lax.ppermute(slots[s], axis, xor_pairs(size, s))  48.5 us
    pallas_call x3, Pallas kernels, ffn_weight_term(): pl.pallas_call(body, grid=(steps,), out_shape=shape, in_specs=[fixed((row...  27.5 us
    ppermute x24, starting transfers between devices, exchange_slots(): lax.ppermute(slots[s], axis, xor_pairs(size, s))  23.9 us
    pallas_call x2, Pallas kernels, weight_term_slots(): pl.pallas_call(body, grid=(blocks,), out_shape=outs, in_specs=[scalar_spe...  19.5 us
  transfers between devices with their start and end apart: 92, of which 40 were waited for; matrix products, arithmetic and copies ran while one was open for 5% of the time, Pallas kernels for 30%

profile of v5, /device:TPU:0, one launch (start us, length us, event | category | flops | bytes accessed | tf_op | source)
XLA Modules:
  0.0 617.8 jit_solution(10384341300954342446)
XLA Ops:
  15.0 4.0 collective-permute-start.1
  21.2 3.9 collective-permute-start.16
  26.8 15.9 %collective-permute-done.14 = s32[2,64]{1,0:T(2,128)S(1)} collective-permute-done((s32[2,64]{1,0:T(2,128)S(1)}, s32[2,64]{1,0:T(2,128)S(1)}, u32[]{:S(2)}, u32[]{:S(2)}) %collective-permute-start.14) | collective-permute-done | bytes 544 | tf_op jit(solution)/shard_map/ppermute | solution.py:49
  51.2 7.3 %collective-permute-done.3.refs_4_ = bf16[128,2048]{1,0:T(8,128)(2,1)S(1)} collective-permute-done((bf16[128,2048]{1,0:T(8,128)(2,1)S(1)}, bf16[128,2048]{1,0:T(8,128)(2,1)S(1)}, u32[]{:S(2)}, u32[]{:S(2)}) %collective-permute-start.3) | collective-permute-done | bytes 524320 | tf_op jit(solution)/shard_map/ppermute | solution.py:87
  59.3 9.1 %shard_map.246 = (bf16[512,2048]{1,0:T(8,128)(2,1)}, f32[512,1536]{1,0:T(8,128)}, f32[2,512]{1,0:T(2,128)}) custom-call(bf16[128,2048]{1,0:T(8,128)(2,1)} %bitcast.110, bf16[128,2048]{1,0:T(8,128)(2,1)} %copy-done.64, bf16[128,2048]{1,0:T(8,128)(2,1)} %copy-done.63, bf16[128,2048]{1,0:T(8,128)(2,1)} %copy-done.65, bf16[128,2048]{1,0:T(8,128)(2,1)} %copy-done.66, ...), custom_call_target="tpu_custom_call" | custom-call | flops 3221225472 | bytes 14159872 | tf_op jit(solution)/shard_map/pallas_call | solution.py:189
  78.8 5.2 shard_map.247
  92.4 4.9 collective-permute-done.10.refs_4_
  100.1 4.8 collective-permute-done.13.refs_7_
  105.7 9.3 %shard_map.248 = (bf16[256,128]{1,0:T(8,128)(2,1)}, bf16[256,128]{1,0:T(8,128)(2,1)}, bf16[256,128]{1,0:T(8,128)(2,1)}, bf16[256,128]{1,0:T(8,128)(2,1)}, bf16[2...) custom-call(s32[1]{0:T(128)} %bitcast.me_ref, ...), custom_call_target="tpu_custom_call" | custom-call | flops 1073741824 | bytes 3186692 | tf_op jit(solution)/shard_map/pallas_call | solution.py:172
  123.7 3.7 collective-permute-done.24.refs_5_
  132.3 4.3 shard_map.250
  142.7 9.5 %collective-permute-done.29 = bf16[128,2048]{1,0:T(8,128)(2,1)S(1)} collective-permute-done((bf16[128,2048]{1,0:T(8,128)(2,1)}, bf16[128,2048]{1,0:T(8,128)(2,1)S(1)}, u32[]{:S(2)}, u32[]{:S(2)}) %collective-permute-start.29) | collective-permute-done | bytes 524320 | tf_op jit(solution)/shard_map/ppermute | solution.py:87
  156.8 6.7 %collective-permute-done.27.refs_1_ = bf16[128,2048]{1,0:T(8,128)(2,1)S(1)} collective-permute-done((bf16[128,2048]{1,0:T(8,128)(2,1)}, bf16[128,2048]{1,0:T(8,128)(2,1)S(1)}, u32[]{:S(2)}, u32[]{:S(2)}) %collective-permute-start.27) | collective-permute-done | bytes 524320 | tf_op jit(solution)/shard_map/ppermute | solution.py:87
  163.5 16.3 %collective-permute-done.30.refs_3_ = bf16[128,2048]{1,0:T(8,128)(2,1)S(1)} collective-permute-done((bf16[128,2048]{1,0:T(8,128)(2,1)S(1)}, bf16[128,2048]{1,0:T(8,128)(2,1)S(1)}, u32[]{:S(2)}, u32[]{:S(2)}) %collective-permute-start.30) | collective-permute-done | bytes 524320 | tf_op jit(solution)/shard_map/ppermute | solution.py:87
  180.6 3.8 shard_map.251
  187.4 21.2 %collective-permute-done.32.refs_2_ = bf16[128,2048]{1,0:T(8,128)(2,1)S(1)} collective-permute-done((bf16[128,2048]{1,0:T(8,128)(2,1)}, bf16[128,2048]{1,0:T(8,128)(2,1)S(1)}, u32[]{:S(2)}, u32[]{:S(2)}) %collective-permute-start.32) | collective-permute-done | bytes 524320 | tf_op jit(solution)/shard_map/ppermute | solution.py:87
  215.2 12.7 %collective-permute-done.34.refs_4_ = bf16[128,2048]{1,0:T(8,128)(2,1)S(1)} collective-permute-done((bf16[128,2048]{1,0:T(8,128)(2,1)S(1)}, bf16[128,2048]{1,0:T(8,128)(2,1)S(1)}, u32[]{:S(2)}, u32[]{:S(2)}) %collective-permute-start.34) | collective-permute-done | bytes 524320 | tf_op jit(solution)/shard_map/ppermute | solution.py:87
  228.6 22.5 %shard_map.252 = (bf16[512,2048]{1,0:T(8,128)(2,1)}, bf16[512,2048]{1,0:T(8,128)(2,1)}, bf16[512,2048]{1,0:T(8,128)(2,1)}, bf16[512,2048]{1,0:T(8,128)(2,1)}, bf...) custom-call(bf16[128,2048]{1,0:T(8,128)(2,1)} %get-tuple-element.144, ...), custom_call_target="tpu_custom_call" | custom-call | flops 12884901888 | bytes 88604672 | tf_op jit(solution)/shard_map/pallas_call | solution.py:189
  256.6 9.4 %collective-permute-done.37 = bf16[128,2048]{1,0:T(8,128)(2,1)S(1)} collective-permute-done((bf16[128,2048]{1,0:T(8,128)(2,1)S(1)}, bf16[128,2048]{1,0:T(8,128)(2,1)S(1)}, u32[]{:S(2)}, u32[]{:S(2)}) %collective-permute-start.37) | collective-permute-done | bytes 524320 | tf_op jit(solution)/shard_map/ppermute | solution.py:87
  269.6 7.6 %collective-permute-done.35.refs_1_ = bf16[128,2048]{1,0:T(8,128)(2,1)S(1)} collective-permute-done((bf16[128,2048]{1,0:T(8,128)(2,1)S(1)}, bf16[128,2048]{1,0:T(8,128)(2,1)S(1)}, u32[]{:S(2)}, u32[]{:S(2)}) %collective-permute-start.35) | collective-permute-done | bytes 524320 | tf_op jit(solution)/shard_map/ppermute | solution.py:87
  277.2 14.6 %collective-permute-done.38.refs_3_ = bf16[128,2048]{1,0:T(8,128)(2,1)S(1)} collective-permute-done((bf16[128,2048]{1,0:T(8,128)(2,1)S(1)}, bf16[128,2048]{1,0:T(8,128)(2,1)S(1)}, u32[]{:S(2)}, u32[]{:S(2)}) %collective-permute-start.38) | collective-permute-done | bytes 524320 | tf_op jit(solution)/shard_map/ppermute | solution.py:87
  292.6 3.8 shard_map.253
  299.2 21.8 %collective-permute-done.40.refs_2_ = bf16[128,2048]{1,0:T(8,128)(2,1)S(1)} collective-permute-done((bf16[128,2048]{1,0:T(8,128)(2,1)}, bf16[128,2048]{1,0:T(8,128)(2,1)S(1)}, u32[]{:S(2)}, u32[]{:S(2)}) %collective-permute-start.40) | collective-permute-done | bytes 524320 | tf_op jit(solution)/shard_map/ppermute | solution.py:87
  322.4 10.1 %collective-permute-done.42.refs_4_ = bf16[128,2048]{1,0:T(8,128)(2,1)S(1)} collective-permute-done((bf16[128,2048]{1,0:T(8,128)(2,1)S(1)}, bf16[128,2048]{1,0:T(8,128)(2,1)S(1)}, u32[]{:S(2)}, u32[]{:S(2)}) %collective-permute-start.42) | collective-permute-done | bytes 524320 | tf_op jit(solution)/shard_map/ppermute | solution.py:87
  336.5 9.3 %shard_map.255 = bf16[2048,2048]{1,0:T(8,128)(2,1)} custom-call(bf16[512,2048]{1,0:T(8,128)(2,1)} %shard_map.254.refs_0_, bf16[512,2048]{1,0:T(8,128)(2,1)} %get-tuple-element.153.refs_1_), custom_call_target="tpu_custom_call" | custom-call | flops 4294967296 | bytes 10485760 | tf_op jit(solution)/shard_map/pallas_call | solution.py:384
  346.2 24.7 %shard_map.256 = (bf16[512,2048]{1,0:T(8,128)(2,1)}, bf16[512,2048]{1,0:T(8,128)(2,1)}, bf16[512,2048]{1,0:T(8,128)(2,1)}, bf16[128,2048]{1,0:T(8,128)(2,1)}, bf...) custom-call(bf16[128,2048]{1,0:T(8,128)(2,1)} %get-tuple-element.151.refs_0_, ...), custom_call_target="tpu_custom_call" | custom-call | flops 12884901888 | bytes 90701824 | tf_op jit(solution)/shard_map/pallas_call | solution.py:189
  376.0 9.2 %collective-permute-done.45 = bf16[128,2048]{1,0:T(8,128)(2,1)S(1)} collective-permute-done((bf16[128,2048]{1,0:T(8,128)(2,1)}, bf16[128,2048]{1,0:T(8,128)(2,1)S(1)}, u32[]{:S(2)}, u32[]{:S(2)}) %collective-permute-start.45) | collective-permute-done | bytes 524320 | tf_op jit(solution)/shard_map/ppermute | solution.py:87
  386.4 3.9 collective-permute-start.46
  390.4 9.2 %shard_map.268.refs_2_ = bf16[2048,4096]{1,0:T(8,128)(2,1)} custom-call(bf16[512,2048]{1,0:T(8,128)(2,1)} %get-tuple-element.218.refs_0_, bf16[512,2048]{1,0:T(8,128)(2,1)} %get-tuple-element.220.refs_1_), custom_call_target="tpu_custom_call" | custom-call | flops 4294967296 | bytes 10485760 | tf_op jit(solution)/shard_map/pallas_call | solution.py:384
  399.6 9.1 %shard_map.269 = bf16[2048,4096]{1,0:T(8,128)(2,1)} custom-call(bf16[512,2048]{1,0:T(8,128)(2,1)} %get-tuple-element.218.refs_0_, bf16[512,2048]{1,0:T(8,128)(2,1)} %get-tuple-element.219.refs_1_, bf16[2048,4096]{1,0:T(8,128)(2,1)} %shard_map.268.refs_2_), custom_call_target="tpu_custom_call", output_to_operand_aliasing={{}: (2, {})} | custom-call | flops 4294967296 | bytes 10485760 | tf_op jit(solution)/shard_map/pallas_call | solution.py:384
  409.8 3.9 shard_map.257
  413.7 6.2 %shard_map.258 = (bf16[128,512]{1,0:T(8,128)(2,1)}, bf16[128,512]{1,0:T(8,128)(2,1)}, bf16[128,512]{1,0:T(8,128)(2,1)}, bf16[128,512]{1,0:T(8,128)(2,1)}) custom-call(bf16[128,2048]{1,0:T(8,128)(2,1)} %get-tuple-element.190.grad_ref.refs_0_, bf16[2048,2048]{1,0:T(8,128)(2,1)} %all-gather.11.cloned.1.call-done.weight_ref), custom_call_target="tpu_custom_call" | custom-call | flops 1073741824 | bytes 9437184 | tf_op jit(solution)/shard_map/pallas_call | solution.py:189
  444.4 11.9 %shard_map.260 = (bf16[256,384]{1,0:T(8,128)(2,1)}, bf16[256,384]{1,0:T(8,128)(2,1)}, bf16[256,384]{1,0:T(8,128)(2,1)}, bf16[256,384]{1,0:T(8,128)(2,1)}, bf16[2...) custom-call(s32[1]{0:T(128)} %bitcast.me_ref, ...), custom_call_target="tpu_custom_call" | custom-call | flops 2684354560 | bytes 4759556 | tf_op jit(solution)/shard_map/pallas_call | solution.py:172
  460.2 8.4 %collective-permute-done.61.refs_2_ = bf16[256,384]{1,0:T(8,128)(2,1)S(1)} collective-permute-done((bf16[256,384]{1,0:T(8,128)(2,1)}, bf16[256,384]{1,0:T(8,128)(2,1)S(1)}, u32[]{:S(2)}, u32[]{:S(2)}) %collective-permute-start.61) | collective-permute-done | bytes 196640 | tf_op jit(solution)/shard_map/ppermute | solution.py:55
  471.0 5.0 collective-permute-done.62.refs_3_
  481.4 9.8 %collective-permute-done.65.refs_6_ = bf16[256,384]{1,0:T(8,128)(2,1)S(1)} collective-permute-done((bf16[256,384]{1,0:T(8,128)(2,1)}, bf16[256,384]{1,0:T(8,128)(2,1)S(1)}, u32[]{:S(2)}, u32[]{:S(2)}) %collective-permute-start.65) | collective-permute-done | bytes 196640 | tf_op jit(solution)/shard_map/ppermute | solution.py:55
  491.1 8.4 %collective-permute-done.66.refs_7_ = bf16[256,384]{1,0:T(8,128)(2,1)S(1)} collective-permute-done((bf16[256,384]{1,0:T(8,128)(2,1)}, bf16[256,384]{1,0:T(8,128)(2,1)S(1)}, u32[]{:S(2)}, u32[]{:S(2)}) %collective-permute-start.66) | collective-permute-done | bytes 196640 | tf_op jit(solution)/shard_map/ppermute | solution.py:55
  503.9 4.2 shard_map.262
  510.3 3.6 collective-permute-start.72
  517.2 10.7 %shard_map.265 = (bf16[4,256,2048]{2,1,0:T(8,128)(2,1)}, bf16[4,256,2048]{2,1,0:T(8,128)(2,1)}) custom-call(s32[1]{0:T(128)} %bitcast.me_ref, bf16[512,2048]{1,0:T(8,128)(2,1)} %shard_map.264.refs_0_, bf16[512,2048]{1,0:T(8,128)(2,1)} %get-tuple-element.203.refs_1_.refs_0_, bf16[512,512]{1,0:T(8,128)(2,1)} %bitcast.115, bf16[512,512]{1,0:T(8,128)(2,1)} %bitcast.141), custom_call_target="tpu_custom_call" | custom-call | flops 2147483648 | bytes 9437184 | tf_op jit(solution)/shard_map/pallas_call | solution.py:704
  529.4 4.2 shard_map.263.refs_1_.qk_ref
  533.6 8.7 %shard_map.266 = (bf16[4,256,2048]{2,1,0:T(8,128)(2,1)}, bf16[4,256,2048]{2,1,0:T(8,128)(2,1)}) custom-call(s32[1]{0:T(128)} %bitcast.me_ref, bf16[512,2048]{1,0:T(8,128)(2,1)} %get-tuple-element.203.refs_1_.refs_0_, bf16[512,1024]{1,0:T(8,128)(2,1)} %shard_map.263.refs_1_.qk_ref, ...), custom_call_target="tpu_custom_call", output_to_operand_aliasing={{0}: (3, {}), {1}: (4, {})} | custom-call | flops 2147483648 | bytes 7340032 | tf_op jit(solution)/shard_map/pallas_call | solution.py:704
  548.0 7.5 %shard_map.267 = (bf16[128,2048]{1,0:T(8,128)(2,1)}, bf16[128,2048]{1,0:T(8,128)(2,1)}, bf16[128,2048]{1,0:T(8,128)(2,1)}, bf16[128,2048]{1,0:T(8,128)(2,1)}) custom-call(bf16[512,1024]{1,0:T(8,128)(2,1)} %shard_map.263.refs_1_.qk_ref, bf16[512,512]{1,0:T(8,128)(2,1)} %bitcast.142, bf16[2048,1536]{1,0:T(8,128)(2,1)} %all-gather.5.cloned.1.call-done.refs_5_.weight_ref), custom_call_target="tpu_custom_call" | custom-call | flops 3221225472 | bytes 9961472 | tf_op jit(solution)/shard_map/pallas_call | solution.py:189
  555.6 4.0 add_bitcast_fusion
  562.4 4.0 collective-permute-start.77
  569.2 9.9 %collective-permute-done.77 = bf16[128,2048]{1,0:T(8,128)(2,1)S(1)} collective-permute-done((bf16[128,2048]{1,0:T(8,128)(2,1)}, bf16[128,2048]{1,0:T(8,128)(2,1)S(1)}, u32[]{:S(2)}, u32[]{:S(2)}) %collective-permute-start.77) | collective-permute-done | bytes 524320 | tf_op jit(solution)/shard_map/ppermute | solution.py:87
  587.8 5.1 shard_map.270
  595.0 9.3 %collective-permute-done.78 = bf16[128,2048]{1,0:T(8,128)(2,1)} collective-permute-done((bf16[128,2048]{1,0:T(8,128)(2,1)}, bf16[128,2048]{1,0:T(8,128)(2,1)}, u32[]{:S(2)}, u32[]{:S(2)}) %collective-permute-start.78) | collective-permute-done | bytes 524320 | tf_op jit(solution)/shard_map/ppermute | solution.py:87
  (430 shorter events, 179.4 us)
Async XLA Ops:
  7.2 51.7 %all-gather.5.cloned.1.call-start = ((), (), s32[]{:S(2)}) async-start(), calls=%async_computation.2 | async-start | bytes 7077888 | tf_op jit(solution)/shard_map/all_gather | solution.py:1192
  9.4 122.9 %all-gather.7.cloned.1.call-start = ((), (), s32[]{:S(2)}) async-start(), calls=%async_computation.3 | async-start | bytes 2359296 | tf_op jit(solution)/shard_map/all_gather | solution.py:1192
  10.3 217.5 %all-gather.9.cloned.1.call-start = ((), (), s32[]{:S(2)}) async-start(), calls=%async_computation.4 | async-start | bytes 28311552 | tf_op jit(solution)/shard_map/all_gather | solution.py:1192
  14.0 399.6 %all-gather.11.cloned.1.call-start = ((), (), s32[]{:S(2)}) async-start(), calls=%async_computation.5 | async-start | bytes 9437184 | tf_op jit(solution)/shard_map/all_gather | solution.py:1192
  15.0 28.3 %collective-permute-start.1 = (bf16[128,2048]{1,0:T(8,128)(2,1)S(1)}, bf16[128,2048]{1,0:T(8,128)(2,1)S(1)}, u32[]{:S(2)}, u32[]{:S(2)}) collective-permute-start(bf16[128,2048]{1,0:T(8,128)(2,1)S(1)} %bitcast.112), channel_id=1, source_target_pairs={{0,2},{1,3},{2,0},{3,1},{4,6},{5,7},{6,4},{7,5},{8,10},{9,11},{10,... | collective-permute-start | bytes 1572872 | tf_op jit(solution)/shard_map/ppermute | solution.py:87
  19.1 32.1 %collective-permute-start = (bf16[128,2048]{1,0:T(8,128)(2,1)S(1)}, bf16[128,2048]{1,0:T(8,128)(2,1)S(1)}, u32[]{:S(2)}, u32[]{:S(2)}) collective-permute-start(bf16[128,2048]{1,0:T(8,128)(2,1)S(1)} %bitcast.113), channel_id=1, source_target_pairs={{0,1},{1,0},{2,3},{3,2},{4,5},{5,4},{6,7},{7,6},{8,9},{9,8},{10,11... | collective-permute-start | bytes 1572872 | tf_op jit(solution)/shard_map/ppermute | solution.py:87
  20.7 22.0 %collective-permute-start.14 = (s32[2,64]{1,0:T(2,128)S(1)}, s32[2,64]{1,0:T(2,128)S(1)}, u32[]{:S(2)}, u32[]{:S(2)}) collective-permute-start(s32[2,64]{1,0:T(2,128)S(1)} %multiply_add_fusion), channel_id=1, source_target_pairs={{0,1},{1,0},{2,3},{3,2},{4,5},{5,4},{6,7},{7,6},{8,9},{9,8},{10,11... | collective-permute-start | bytes 1544 | tf_op jit(solution)/shard_map/ppermute | solution.py:49
  21.2 23.5 %collective-permute-start.15 = (s32[2,64]{1,0:T(2,128)S(1)}, s32[2,64]{1,0:T(2,128)S(1)}, u32[]{:S(2)}, u32[]{:S(2)}) collective-permute-start(s32[2,64]{1,0:T(2,128)S(1)} %multiply_add_fusion), channel_id=1, source_target_pairs={{0,2},{1,3},{2,0},{3,1},{4,6},{5,7},{6,4},{7,5},{8,10},{9,11},{10,... | collective-permute-start | bytes 1544 | tf_op jit(solution)/shard_map/ppermute | solution.py:49
  21.2 23.5 %collective-permute-start.16 = (s32[2,64]{1,0:T(2,128)S(1)}, s32[2,64]{1,0:T(2,128)S(1)}, u32[]{:S(2)}, u32[]{:S(2)}) collective-permute-start(s32[2,64]{1,0:T(2,128)S(1)} %multiply_add_fusion), channel_id=1, source_target_pairs={{0,3},{1,2},{2,1},{3,0},{4,7},{5,6},{6,5},{7,4},{8,11},{9,10},{10,... | collective-permute-start | bytes 1544 | tf_op jit(solution)/shard_map/ppermute | solution.py:49
  49.6 23.1 %collective-permute-start.19 = (s32[4,2,256]{2,1,0:T(2,128)S(1)}, s32[4,2,256]{2,1,0:T(2,128)S(1)}, u32[]{:S(2)}, u32[]{:S(2)}) collective-permute-start(s32[4,2,256]{2,1,0:T(2,128)S(1)} %pad_add_fusion.1), channel_id=1, source_target_pairs={{0,16},{4,20},{8,24},{12,28},{16,0},{20,4},{24,8},{28,12},{1,17},{... | collective-permute-start | bytes 24584 | tf_op jit(solution)/shard_map/ppermute | solution.py:63
  136.6 15.7 %collective-permute-start.29 = (bf16[128,2048]{1,0:T(8,128)(2,1)}, bf16[128,2048]{1,0:T(8,128)(2,1)S(1)}, u32[]{:S(2)}, u32[]{:S(2)}) collective-permute-start(bf16[128,2048]{1,0:T(8,128)(2,1)} %get-tuple-element.142), channel_id=1, source_target_pairs={{0,1},{3,2},{4,5},{7,6},{8,9},{11,10},{12,13},{15,14},{16,17},{19,... | collective-permute-start | bytes 1572872 | tf_op jit(solution)/shard_map/ppermute | solution.py:87
  139.7 23.8 %collective-permute-start.28 = (bf16[128,2048]{1,0:T(8,128)(2,1)}, bf16[128,2048]{1,0:T(8,128)(2,1)S(1)}, u32[]{:S(2)}, u32[]{:S(2)}) collective-permute-start(bf16[128,2048]{1,0:T(8,128)(2,1)} %get-tuple-element.142), channel_id=1, source_target_pairs={{1,2},{2,1},{5,6},{6,5},{9,10},{10,9},{13,14},{14,13},{17,18},{18,... | collective-permute-start | bytes 1572872 | tf_op jit(solution)/shard_map/ppermute | solution.py:87
  140.6 22.9 %collective-permute-start.27 = (bf16[128,2048]{1,0:T(8,128)(2,1)}, bf16[128,2048]{1,0:T(8,128)(2,1)S(1)}, u32[]{:S(2)}, u32[]{:S(2)}) collective-permute-start(bf16[128,2048]{1,0:T(8,128)(2,1)} %get-tuple-element.141), channel_id=1, source_target_pairs={{0,1},{1,0},{2,3},{3,2},{4,5},{5,4},{6,7},{7,6},{8,9},{9,8},{10,11... | collective-permute-start | bytes 1572872 | tf_op jit(solution)/shard_map/ppermute | solution.py:87
  153.5 26.3 %collective-permute-start.30 = (bf16[128,2048]{1,0:T(8,128)(2,1)S(1)}, bf16[128,2048]{1,0:T(8,128)(2,1)S(1)}, u32[]{:S(2)}, u32[]{:S(2)}) collective-permute-start(bf16[128,2048]{1,0:T(8,128)(2,1)S(1)} %add_convert_fusion.4), channel_id=1, source_target_pairs={{0,2},{1,3},{2,0},{3,1},{4,6},{5,7},{6,4},{7,5},{8,10},{9,11},{10,... | collective-permute-start | bytes 1572872 | tf_op jit(solution)/shard_map/ppermute | solution.py:87
  184.5 24.2 %collective-permute-start.32 = (bf16[128,2048]{1,0:T(8,128)(2,1)}, bf16[128,2048]{1,0:T(8,128)(2,1)S(1)}, u32[]{:S(2)}, u32[]{:S(2)}) collective-permute-start(bf16[128,2048]{1,0:T(8,128)(2,1)} %get-tuple-element.144.refs_0_), channel_id=1, source_target_pairs={{0,2},{1,3},{2,0},{3,1},{4,6},{5,7},{6,4},{7,5},{8,10},{9,11},{10,... | collective-permute-start | bytes 1572872 | tf_op jit(solution)/shard_map/ppermute | solution.py:87
  184.5 29.2 %collective-permute-start.31 = (bf16[128,2048]{1,0:T(8,128)(2,1)}, bf16[128,2048]{1,0:T(8,128)(2,1)S(1)}, u32[]{:S(2)}, u32[]{:S(2)}) collective-permute-start(bf16[128,2048]{1,0:T(8,128)(2,1)} %get-tuple-element.144.refs_0_), channel_id=1, source_target_pairs={{0,1},{1,0},{2,3},{3,2},{4,5},{5,4},{6,7},{7,6},{8,9},{9,8},{10,11... | collective-permute-start | bytes 1572872 | tf_op jit(solution)/shard_map/ppermute | solution.py:87
  186.8 28.4 %collective-permute-start.33 = (bf16[128,2048]{1,0:T(8,128)(2,1)}, bf16[128,2048]{1,0:T(8,128)(2,1)S(1)}, u32[]{:S(2)}, u32[]{:S(2)}) collective-permute-start(bf16[128,2048]{1,0:T(8,128)(2,1)} %get-tuple-element.144.refs_0_), channel_id=1, source_target_pairs={{1,2},{2,1},{5,6},{6,5},{9,10},{10,9},{13,14},{14,13},{17,18},{18,... | collective-permute-start | bytes 1572872 | tf_op jit(solution)/shard_map/ppermute | solution.py:87
  208.6 19.2 %collective-permute-start.34 = (bf16[128,2048]{1,0:T(8,128)(2,1)S(1)}, bf16[128,2048]{1,0:T(8,128)(2,1)S(1)}, u32[]{:S(2)}, u32[]{:S(2)}) collective-permute-start(bf16[128,2048]{1,0:T(8,128)(2,1)S(1)} %collective-permute-done.32.refs_2_), channel_id=1, source_target_pairs={{1,0},{2,3},{5,4},{6,7},{9,8},{10,11},{13,12},{14,15},{17,16},{18,... | collective-permute-start | bytes 1572872 | tf_op jit(solution)/shard_map/ppermute | solution.py:87
  209.9 41.3 %collective-permute-start.47 = (bf16[256,512]{1,0:T(8,128)(2,1)S(1)}, bf16[256,512]{1,0:T(8,128)(2,1)S(1)}, u32[]{:S(2)}, u32[]{:S(2)}) collective-permute-start(bf16[256,512]{1,0:T(8,128)(2,1)S(1)} %bitcast.100), channel_id=1, source_target_pairs={{0,1},{1,0},{2,3},{3,2},{4,5},{5,4},{6,7},{7,6},{8,9},{9,8},{10,11... | collective-permute-start | bytes 786440 | tf_op jit(solution)/shard_map/ppermute | solution.py:49
  212.7 38.6 %collective-permute-start.48 = (bf16[256,512]{1,0:T(8,128)(2,1)S(1)}, bf16[256,512]{1,0:T(8,128)(2,1)S(1)}, u32[]{:S(2)}, u32[]{:S(2)}) collective-permute-start(bf16[256,512]{1,0:T(8,128)(2,1)S(1)} %bitcast.101), channel_id=1, source_target_pairs={{0,2},{1,3},{2,0},{3,1},{4,6},{5,7},{6,4},{7,5},{8,10},{9,11},{10,... | collective-permute-start | bytes 786440 | tf_op jit(solution)/shard_map/ppermute | solution.py:49
  213.7 37.5 %collective-permute-start.49 = (bf16[256,512]{1,0:T(8,128)(2,1)S(1)}, bf16[256,512]{1,0:T(8,128)(2,1)S(1)}, u32[]{:S(2)}, u32[]{:S(2)}) collective-permute-start(bf16[256,512]{1,0:T(8,128)(2,1)S(1)} %bitcast.102), channel_id=1, source_target_pairs={{0,3},{1,2},{2,1},{3,0},{4,7},{5,6},{6,5},{7,4},{8,11},{9,10},{10,... | collective-permute-start | bytes 786440 | tf_op jit(solution)/shard_map/ppermute | solution.py:49
  252.4 335.3 %reduce-scatter.5.cloned.1.call-start = ((), (), s32[]{:S(2)}) async-start(), calls=%async_computation.7 | async-start | bytes 9437184 | tf_op jit(solution)/shard_map/reduce_scatter | solution.py:1245
  253.8 23.5 %collective-permute-start.36 = (bf16[128,2048]{1,0:T(8,128)(2,1)S(1)}, bf16[128,2048]{1,0:T(8,128)(2,1)S(1)}, u32[]{:S(2)}, u32[]{:S(2)}) collective-permute-start(bf16[128,2048]{1,0:T(8,128)(2,1)S(1)} %copy-done.67), channel_id=1, source_target_pairs={{1,2},{2,1},{5,6},{6,5},{9,10},{10,9},{13,14},{14,13},{17,18},{18,... | collective-permute-start | bytes 1572872 | tf_op jit(solution)/shard_map/ppermute | solution.py:87
  254.5 22.7 %collective-permute-start.35 = (bf16[128,2048]{1,0:T(8,128)(2,1)S(1)}, bf16[128,2048]{1,0:T(8,128)(2,1)S(1)}, u32[]{:S(2)}, u32[]{:S(2)}) collective-permute-start(bf16[128,2048]{1,0:T(8,128)(2,1)S(1)} %copy-done.68), channel_id=1, source_target_pairs={{0,1},{1,0},{2,3},{3,2},{4,5},{5,4},{6,7},{7,6},{8,9},{9,8},{10,11... | collective-permute-start | bytes 1572872 | tf_op jit(solution)/shard_map/ppermute | solution.py:87
  266.1 25.7 %collective-permute-start.38 = (bf16[128,2048]{1,0:T(8,128)(2,1)S(1)}, bf16[128,2048]{1,0:T(8,128)(2,1)S(1)}, u32[]{:S(2)}, u32[]{:S(2)}) collective-permute-start(bf16[128,2048]{1,0:T(8,128)(2,1)S(1)} %add_convert_fusion.3), channel_id=1, source_target_pairs={{0,2},{1,3},{2,0},{3,1},{4,6},{5,7},{6,4},{7,5},{8,10},{9,11},{10,... | collective-permute-start | bytes 1572872 | tf_op jit(solution)/shard_map/ppermute | solution.py:87
  296.4 24.6 %collective-permute-start.40 = (bf16[128,2048]{1,0:T(8,128)(2,1)}, bf16[128,2048]{1,0:T(8,128)(2,1)S(1)}, u32[]{:S(2)}, u32[]{:S(2)}) collective-permute-start(bf16[128,2048]{1,0:T(8,128)(2,1)} %get-tuple-element.151.refs_0_), channel_id=1, source_target_pairs={{0,2},{1,3},{2,0},{3,1},{4,6},{5,7},{6,4},{7,5},{8,10},{9,11},{10,... | collective-permute-start | bytes 1572872 | tf_op jit(solution)/shard_map/ppermute | solution.py:87
  296.4 25.9 %collective-permute-start.39 = (bf16[128,2048]{1,0:T(8,128)(2,1)}, bf16[128,2048]{1,0:T(8,128)(2,1)S(1)}, u32[]{:S(2)}, u32[]{:S(2)}) collective-permute-start(bf16[128,2048]{1,0:T(8,128)(2,1)} %get-tuple-element.151.refs_0_), channel_id=1, source_target_pairs={{0,1},{1,0},{2,3},{3,2},{4,5},{5,4},{6,7},{7,6},{8,9},{9,8},{10,11... | collective-permute-start | bytes 1572872 | tf_op jit(solution)/shard_map/ppermute | solution.py:87
  298.5 23.8 %collective-permute-start.41 = (bf16[128,2048]{1,0:T(8,128)(2,1)}, bf16[128,2048]{1,0:T(8,128)(2,1)S(1)}, u32[]{:S(2)}, u32[]{:S(2)}) collective-permute-start(bf16[128,2048]{1,0:T(8,128)(2,1)} %get-tuple-element.151.refs_0_), channel_id=1, source_target_pairs={{1,2},{2,1},{5,6},{6,5},{9,10},{10,9},{13,14},{14,13},{17,18},{18,... | collective-permute-start | bytes 1572872 | tf_op jit(solution)/shard_map/ppermute | solution.py:87
  345.8 241.9 %reduce-scatter.3.cloned.1.call-start = ((), (), s32[]{:S(2)}) async-start(), calls=%async_computation.6 | async-start | bytes 18874368 | tf_op jit(solution)/shard_map/reduce_scatter | solution.py:1247
  372.6 36.1 %collective-permute-start.44 = (bf16[128,2048]{1,0:T(8,128)(2,1)}, bf16[128,2048]{1,0:T(8,128)(2,1)S(1)}, u32[]{:S(2)}, u32[]{:S(2)}) collective-permute-start(bf16[128,2048]{1,0:T(8,128)(2,1)} %get-tuple-element.158), channel_id=1, source_target_pairs={{1,2},{2,1},{5,6},{6,5},{9,10},{10,9},{13,14},{14,13},{17,18},{18,... | collective-permute-start | bytes 1572872 | tf_op jit(solution)/shard_map/ppermute | solution.py:87
  373.3 35.4 %collective-permute-start.43 = (bf16[128,2048]{1,0:T(8,128)(2,1)}, bf16[128,2048]{1,0:T(8,128)(2,1)S(1)}, u32[]{:S(2)}, u32[]{:S(2)}) collective-permute-start(bf16[128,2048]{1,0:T(8,128)(2,1)} %get-tuple-element.157), channel_id=1, source_target_pairs={{0,1},{1,0},{2,3},{3,2},{4,5},{5,4},{6,7},{7,6},{8,9},{9,8},{10,11... | collective-permute-start | bytes 1572872 | tf_op jit(solution)/shard_map/ppermute | solution.py:87
  386.4 22.3 %collective-permute-start.46 = (bf16[128,2048]{1,0:T(8,128)(2,1)S(1)}, bf16[128,2048]{1,0:T(8,128)(2,1)S(1)}, u32[]{:S(2)}, u32[]{:S(2)}) collective-permute-start(bf16[128,2048]{1,0:T(8,128)(2,1)S(1)} %add_convert_fusion.2), channel_id=1, source_target_pairs={{0,2},{1,3},{2,0},{3,1},{4,6},{5,7},{6,4},{7,5},{8,10},{9,11},{10,... | collective-permute-start | bytes 1572872 | tf_op jit(solution)/shard_map/ppermute | solution.py:87
  439.0 37.7 %collective-permute-start.68 = (bf16[128,2048]{1,0:T(8,128)(2,1)S(1)}, bf16[128,2048]{1,0:T(8,128)(2,1)S(1)}, u32[]{:S(2)}, u32[]{:S(2)}) collective-permute-start(bf16[128,2048]{1,0:T(8,128)(2,1)S(1)} %copy-done.10), channel_id=1, source_target_pairs={{0,2},{1,3},{2,0},{3,1},{4,6},{5,7},{6,4},{7,5},{8,10},{9,11},{10,... | collective-permute-start | bytes 1572872 | tf_op jit(solution)/shard_map/ppermute | solution.py:87
  458.1 17.9 %collective-permute-start.62 = (bf16[256,384]{1,0:T(8,128)(2,1)}, bf16[256,384]{1,0:T(8,128)(2,1)S(1)}, u32[]{:S(2)}, u32[]{:S(2)}) collective-permute-start(bf16[256,384]{1,0:T(8,128)(2,1)} %get-tuple-element.185), channel_id=1, source_target_pairs={{0,12},{4,8},{8,4},{12,0},{16,28},{20,24},{24,20},{28,16},{1,13},{... | collective-permute-start | bytes 589832 | tf_op jit(solution)/shard_map/ppermute | solution.py:55
  458.3 19.7 %collective-permute-start.63 = (bf16[256,384]{1,0:T(8,128)(2,1)}, bf16[256,384]{1,0:T(8,128)(2,1)S(1)}, u32[]{:S(2)}, u32[]{:S(2)}) collective-permute-start(bf16[256,384]{1,0:T(8,128)(2,1)} %get-tuple-element.186), channel_id=1, source_target_pairs={{0,16},{4,20},{8,24},{12,28},{16,0},{20,4},{24,8},{28,12},{1,17},{... | collective-permute-start | bytes 589832 | tf_op jit(solution)/shard_map/ppermute | solution.py:55
  459.9 19.6 %collective-permute-start.64 = (bf16[256,384]{1,0:T(8,128)(2,1)}, bf16[256,384]{1,0:T(8,128)(2,1)S(1)}, u32[]{:S(2)}, u32[]{:S(2)}) collective-permute-start(bf16[256,384]{1,0:T(8,128)(2,1)} %get-tuple-element.187), channel_id=1, source_target_pairs={{0,20},{4,16},{8,28},{12,24},{16,4},{20,0},{24,12},{28,8},{1,21},{... | collective-permute-start | bytes 589832 | tf_op jit(solution)/shard_map/ppermute | solution.py:55
  468.6 31.0 %collective-permute-start.67 = (bf16[128,2048]{1,0:T(8,128)(2,1)S(1)}, bf16[128,2048]{1,0:T(8,128)(2,1)S(1)}, u32[]{:S(2)}, u32[]{:S(2)}) collective-permute-start(bf16[128,2048]{1,0:T(8,128)(2,1)S(1)} %copy-done.10), channel_id=1, source_target_pairs={{0,1},{1,0},{2,3},{3,2},{4,5},{5,4},{6,7},{7,6},{8,9},{9,8},{10,11... | collective-permute-start | bytes 1572872 | tf_op jit(solution)/shard_map/ppermute | solution.py:87
  476.0 23.6 %collective-permute-start.69 = (bf16[128,2048]{1,0:T(8,128)(2,1)S(1)}, bf16[128,2048]{1,0:T(8,128)(2,1)S(1)}, u32[]{:S(2)}, u32[]{:S(2)}) collective-permute-start(bf16[128,2048]{1,0:T(8,128)(2,1)S(1)} %copy-done.10), channel_id=1, source_target_pairs={{1,2},{2,1},{5,6},{6,5},{9,10},{10,9},{13,14},{14,13},{17,18},{18,... | collective-permute-start | bytes 1572872 | tf_op jit(solution)/shard_map/ppermute | solution.py:87
  476.7 22.9 %collective-permute-start.70 = (bf16[128,2048]{1,0:T(8,128)(2,1)S(1)}, bf16[128,2048]{1,0:T(8,128)(2,1)S(1)}, u32[]{:S(2)}, u32[]{:S(2)}) collective-permute-start(bf16[128,2048]{1,0:T(8,128)(2,1)S(1)} %collective-permute-done.68.refs_2_), channel_id=1, source_target_pairs={{1,0},{2,3},{5,4},{6,7},{9,8},{10,11},{13,12},{14,15},{17,16},{18,... | collective-permute-start | bytes 1572872 | tf_op jit(solution)/shard_map/ppermute | solution.py:87
  479.5 20.1 %collective-permute-start.66 = (bf16[256,384]{1,0:T(8,128)(2,1)}, bf16[256,384]{1,0:T(8,128)(2,1)S(1)}, u32[]{:S(2)}, u32[]{:S(2)}) collective-permute-start(bf16[256,384]{1,0:T(8,128)(2,1)} %get-tuple-element.189), channel_id=1, source_target_pairs={{0,28},{4,24},{8,20},{12,16},{16,12},{20,8},{24,4},{28,0},{1,29},{... | collective-permute-start | bytes 589832 | tf_op jit(solution)/shard_map/ppermute | solution.py:55
  508.8 19.1 %collective-permute-start.73 = (f32[5120]{0:T(1024)S(1)}, f32[5120]{0:T(1024)S(1)}, u32[]{:S(2)}, u32[]{:S(2)}) collective-permute-start(f32[5120]{0:T(1024)S(1)} %pad_maximum_fusion.7), channel_id=1, source_target_pairs={{0,3},{1,2},{2,1},{3,0},{4,7},{5,6},{6,5},{7,4},{8,11},{9,10},{10,... | collective-permute-start | bytes 61448 | tf_op jit(solution)/shard_map/ppermute | solution.py:49
  510.3 17.6 %collective-permute-start.72 = (f32[5120]{0:T(1024)S(1)}, f32[5120]{0:T(1024)S(1)}, u32[]{:S(2)}, u32[]{:S(2)}) collective-permute-start(f32[5120]{0:T(1024)S(1)} %pad_maximum_fusion.7), channel_id=1, source_target_pairs={{0,2},{1,3},{2,0},{3,1},{4,6},{5,7},{6,4},{7,5},{8,10},{9,11},{10,... | collective-permute-start | bytes 61448 | tf_op jit(solution)/shard_map/ppermute | solution.py:49
  559.9 24.4 %collective-permute-start.82 = (bf16[2,256,1024]{2,1,0:T(8,128)(2,1)S(1)}, bf16[2,256,1024]{2,1,0:T(8,128)(2,1)S(1)}, u32[]{:S(2)}, u32[]{:S(2)}) collective-permute-start(bf16[2,256,1024]{2,1,0:T(8,128)(2,1)S(1)} %pad_maximum_fusion.2), channel_id=1, source_target_pairs={{0,16},{4,20},{8,24},{12,28},{16,0},{20,4},{24,8},{28,12},{1,17},{... | collective-permute-start | bytes 3145736 | tf_op jit(solution)/shard_map/ppermute | solution.py:746
  561.0 24.0 %collective-permute-start.83 = (bf16[2,256,1024]{2,1,0:T(8,128)(2,1)S(1)}, bf16[2,256,1024]{2,1,0:T(8,128)(2,1)S(1)}, u32[]{:S(2)}, u32[]{:S(2)}) collective-permute-start(bf16[2,256,1024]{2,1,0:T(8,128)(2,1)S(1)} %pad_maximum_fusion.3), channel_id=1, source_target_pairs={{0,8},{4,12},{8,0},{12,4},{16,24},{20,28},{24,16},{28,20},{1,9},{5... | collective-permute-start | bytes 3145736 | tf_op jit(solution)/shard_map/ppermute | solution.py:746
  562.4 16.7 %collective-permute-start.77 = (bf16[128,2048]{1,0:T(8,128)(2,1)}, bf16[128,2048]{1,0:T(8,128)(2,1)S(1)}, u32[]{:S(2)}, u32[]{:S(2)}) collective-permute-start(bf16[128,2048]{1,0:T(8,128)(2,1)} %get-tuple-element.214), channel_id=1, source_target_pairs={{0,1},{3,2},{4,5},{7,6},{8,9},{11,10},{12,13},{15,14},{16,17},{19,... | collective-permute-start | bytes 1572872 | tf_op jit(solution)/shard_map/ppermute | solution.py:87
  566.4 26.5 %collective-permute-start.75 = (bf16[128,2048]{1,0:T(8,128)(2,1)}, bf16[128,2048]{1,0:T(8,128)(2,1)}, u32[]{:S(2)}, u32[]{:S(2)}) collective-permute-start(bf16[128,2048]{1,0:T(8,128)(2,1)} %get-tuple-element.213), channel_id=1, source_target_pairs={{0,1},{1,0},{2,3},{3,2},{4,5},{5,4},{6,7},{7,6},{8,9},{9,8},{10,11... | collective-permute-start | bytes 1572872 | tf_op jit(solution)/shard_map/ppermute | solution.py:87
  566.5 28.5 %collective-permute-start.76 = (bf16[128,2048]{1,0:T(8,128)(2,1)}, bf16[128,2048]{1,0:T(8,128)(2,1)}, u32[]{:S(2)}, u32[]{:S(2)}) collective-permute-start(bf16[128,2048]{1,0:T(8,128)(2,1)} %get-tuple-element.214), channel_id=1, source_target_pairs={{1,2},{2,1},{5,6},{6,5},{9,10},{10,9},{13,14},{14,13},{17,18},{18,... | collective-permute-start | bytes 1572872 | tf_op jit(solution)/shard_map/ppermute | solution.py:87
  580.0 24.3 %collective-permute-start.78 = (bf16[128,2048]{1,0:T(8,128)(2,1)}, bf16[128,2048]{1,0:T(8,128)(2,1)}, u32[]{:S(2)}, u32[]{:S(2)}) collective-permute-start(bf16[128,2048]{1,0:T(8,128)(2,1)} %add_convert_fusion.1), channel_id=1, source_target_pairs={{0,2},{1,3},{2,0},{3,1},{4,6},{5,7},{6,4},{7,5},{8,10},{9,11},{10,... | collective-permute-start | bytes 1572872 | tf_op jit(solution)/shard_map/ppermute | solution.py:87
  (127 other events, 1233.4 us)
Sparse Core Ops, SparseCore 0:
  10.5 48.3 all-gather.4
  61.4 29.9 all-gather.6
  93.3 133.1 all-gather.8
  252.5 52.4 all-gather.10
  345.9 71.1 reduce-scatter.4
  421.0 133.1 reduce-scatter.2

commit v6 on v5

--- a/solution.py
+++ b/solution.py
@@ -398,6 +398,35 @@
             transcendentals=0,
         ),
     )(*lefts, *rights, *held)
+
+
+def down_weight_term(parts, right, micro_count):
+    n = len(parts)
+    width = parts[0].shape[1]
+    rows, hidden = right.shape
+    tile = tile_of(hidden)
+
+    def body(*refs):
+        right_ref, out_ref, left, left_t = refs[n:]
+
+        @pl.when(pl.program_id(0) == 0)
+        def _():
+            fill_rows(left, refs[:n], micro_count)
+            left_t[...] = jnp.transpose(left[...])
+
+        out_ref[...] = dot_plain(left_t[...], right_ref[...]).astype(low)
+
+    return call_grid(
+        body,
+        hidden // tile,
+        [shape_of((width, hidden), low)],
+        [fixed(part.shape) for part in parts] + [column_tile(rows, tile)],
+        [column_tile(width, tile)],
+        *parts,
+        right,
+        scratch=[pltpu.VMEM((rows, width), low), pltpu.VMEM((width, rows), low)],
+        flops=2 * rows * width * hidden,
+    )[0]
 
 
 def widen_ffn(grads, down_grads):
@@ -1149,8 +1178,8 @@
             split_mixed(self.me, grad_parts, self.micro_count, self.heads), "blk"
         )
         self.arrived = grad_slots[1:]
-        back_slots = exchange_slots(
-            attention_backward(self.me, self.slots, grad_slots, *self.kept, *self.marks), "blk"
+        back_slots = exchange_blocks(
+            attention_backward(self.me, self.slots, grad_slots, *self.kept, *self.marks)
         )
         back_slots = after(back_slots, *others)
         return receive_grads(self.me, back_slots, self.tables, self.micro_count, self.heads)
@@ -1230,8 +1259,7 @@
     output_all_t = gather_weights(*after(output_parts, gate))
     output, grad_down, ffn_gain_grad = after_ffn(reduce_parts(slots), hidden, grad_own, ffn_gain)
     grad_parts = gather_parts(grad_down)
-    grad_rows = join_rows(grad_parts, micro_count)
-    down_terms = ffn_weight_term([], 0, 1, [grad_rows], [middle_rows])
+    down_terms = down_weight_term(grad_parts, middle_rows, micro_count)
     (_, grad_gate, grad_up), slots = ffn_backward(
         grad_parts, after(gate, down_terms), up, ffn_full, micro_count
     )

time: 622 us -> 618 us (level)
    ppermute x24 -> x17, waiting for transfers between devices: 48.5 us -> 16.9 us  [exchange_slots(): lax.ppermute(slots[s], axis, xor_pairs(size, s))]
    ppermute x5 -> x10, waiting for transfers between devices: 8.05 us -> 27 us  [exchange_blocks(): lax.ppermute(slots[s], 'blk', xor_pairs(size, s))]
    pallas_call x5 -> x6, Pallas kernels: 70 us -> 79.3 us  [call_grid(): pl.pallas_call(body, grid=(steps,), out_shape=outs, in_specs=in_specs, ou...]
    pallas_call x3 -> x2, Pallas kernels: 27.5 us -> 18.3 us  [ffn_weight_term(): pl.pallas_call(body, grid=(steps,), out_shape=shape, in_specs=[fixed((row...]
    ppermute x2 -> x4, waiting for transfers between devices: 4.85 us -> 12.1 us  [exchange_blocks(): lax.ppermute(after(slots[s], arrived[2]), 'blk', xor_pairs(size, s))]
    ppermute x24 -> x17, starting transfers between devices: 23.9 us -> 16.7 us  [exchange_slots(): lax.ppermute(slots[s], axis, xor_pairs(size, s))]
    pallas_call x15 -> x14, Pallas kernels: 69.7 us -> 66.6 us  [call_whole(): pl.pallas_call(body, out_shape=outs, in_specs=[pl.BlockSpec(memory_space=...]
  transfers between devices with their start and end apart: 92 -> 92, of which waited for: 40 -> 41; matrix products, arithmetic and copies ran while one was open for 5% -> 5% of each run, Pallas kernels for 30% -> 30%
where the time goes in v6:
time: 618 us; the launch traced here: 614 us
  waiting for transfers between devices  255 us (41%)
  Pallas kernels  183 us (30%)
  starting transfers between devices  113 us (18%)
  other arithmetic  26.5 us (4%)
  local copies, waits for them, and re-layouts  20.1 us (3%)
  between operations  15.5 us (3%)
    ppermute x32, waiting for transfers between devices, send_rows(): return lax.ppermute(values, 'head', pairs)  172 us
    pallas_call x6, Pallas kernels, call_grid(): pl.pallas_call(body, grid=(steps,), out_shape=outs, in_specs=in_specs, ou...  79.3 us
    pallas_call x14, Pallas kernels, call_whole(): pl.pallas_call(body, out_shape=outs, in_specs=[pl.BlockSpec(memory_space=...  66.6 us
    ppermute x32, starting transfers between devices, send_rows(): return lax.ppermute(values, 'head', pairs)  54.4 us
    ppermute x10, waiting for transfers between devices, exchange_blocks(): lax.ppermute(slots[s], 'blk', xor_pairs(size, s))  27 us
    pallas_call x2, Pallas kernels, weight_term_slots(): pl.pallas_call(body, grid=(blocks,), out_shape=outs, in_specs=[scalar_spe...  19.4 us
    ppermute x12, waiting for transfers between devices, gather_slots(): lax.ppermute(values, axis, xor_pairs(size, s))  19 us
    pallas_call x2, Pallas kernels, ffn_weight_term(): pl.pallas_call(body, grid=(steps,), out_shape=shape, in_specs=[fixed((row...  18.3 us
  transfers between devices with their start and end apart: 92, of which 41 were waited for; matrix products, arithmetic and copies ran while one was open for 5% of the time, Pallas kernels for 30%

profile of v6, /device:TPU:0, one launch (start us, length us, event | category | flops | bytes accessed | tf_op | source)
XLA Modules:
  0.0 613.8 jit_solution(11402375260740909737)
XLA Ops:
  15.0 4.0 collective-permute-start.1
  21.2 3.9 collective-permute-start.16
  26.8 15.9 %collective-permute-done.14 = s32[2,64]{1,0:T(2,128)S(1)} collective-permute-done((s32[2,64]{1,0:T(2,128)S(1)}, s32[2,64]{1,0:T(2,128)S(1)}, u32[]{:S(2)}, u32[]{:S(2)}) %collective-permute-start.14) | collective-permute-done | bytes 544 | tf_op jit(solution)/shard_map/ppermute | solution.py:49
  51.2 7.3 %collective-permute-done.3.refs_4_ = bf16[128,2048]{1,0:T(8,128)(2,1)S(1)} collective-permute-done((bf16[128,2048]{1,0:T(8,128)(2,1)S(1)}, bf16[128,2048]{1,0:T(8,128)(2,1)S(1)}, u32[]{:S(2)}, u32[]{:S(2)}) %collective-permute-start.3) | collective-permute-done | bytes 524320 | tf_op jit(solution)/shard_map/ppermute | solution.py:87
  59.3 9.1 %shard_map.246 = (bf16[512,2048]{1,0:T(8,128)(2,1)}, f32[512,1536]{1,0:T(8,128)}, f32[2,512]{1,0:T(2,128)}) custom-call(bf16[128,2048]{1,0:T(8,128)(2,1)} %bitcast.110, bf16[128,2048]{1,0:T(8,128)(2,1)} %copy-done.64, bf16[128,2048]{1,0:T(8,128)(2,1)} %copy-done.63, bf16[128,2048]{1,0:T(8,128)(2,1)} %copy-done.65, bf16[128,2048]{1,0:T(8,128)(2,1)} %copy-done.66, ...), custom_call_target="tpu_custom_call" | custom-call | flops 3221225472 | bytes 14159872 | tf_op jit(solution)/shard_map/pallas_call | solution.py:189
  78.8 5.2 shard_map.247
  92.4 4.9 collective-permute-done.10.refs_4_
  100.1 4.8 collective-permute-done.13.refs_7_
  105.7 9.3 %shard_map.248 = (bf16[256,128]{1,0:T(8,128)(2,1)}, bf16[256,128]{1,0:T(8,128)(2,1)}, bf16[256,128]{1,0:T(8,128)(2,1)}, bf16[256,128]{1,0:T(8,128)(2,1)}, bf16[2...) custom-call(s32[1]{0:T(128)} %bitcast.me_ref, ...), custom_call_target="tpu_custom_call" | custom-call | flops 1073741824 | bytes 3186692 | tf_op jit(solution)/shard_map/pallas_call | solution.py:172
  123.7 3.7 collective-permute-done.24.refs_5_
  132.3 4.3 shard_map.250
  142.7 9.5 %collective-permute-done.29 = bf16[128,2048]{1,0:T(8,128)(2,1)S(1)} collective-permute-done((bf16[128,2048]{1,0:T(8,128)(2,1)}, bf16[128,2048]{1,0:T(8,128)(2,1)S(1)}, u32[]{:S(2)}, u32[]{:S(2)}) %collective-permute-start.29) | collective-permute-done | bytes 524320 | tf_op jit(solution)/shard_map/ppermute | solution.py:87
  156.8 6.7 %collective-permute-done.27.refs_1_ = bf16[128,2048]{1,0:T(8,128)(2,1)S(1)} collective-permute-done((bf16[128,2048]{1,0:T(8,128)(2,1)}, bf16[128,2048]{1,0:T(8,128)(2,1)S(1)}, u32[]{:S(2)}, u32[]{:S(2)}) %collective-permute-start.27) | collective-permute-done | bytes 524320 | tf_op jit(solution)/shard_map/ppermute | solution.py:87
  163.5 16.3 %collective-permute-done.30.refs_3_ = bf16[128,2048]{1,0:T(8,128)(2,1)S(1)} collective-permute-done((bf16[128,2048]{1,0:T(8,128)(2,1)S(1)}, bf16[128,2048]{1,0:T(8,128)(2,1)S(1)}, u32[]{:S(2)}, u32[]{:S(2)}) %collective-permute-start.30) | collective-permute-done | bytes 524320 | tf_op jit(solution)/shard_map/ppermute | solution.py:87
  180.6 3.8 shard_map.251
  187.4 21.2 %collective-permute-done.32.refs_2_ = bf16[128,2048]{1,0:T(8,128)(2,1)S(1)} collective-permute-done((bf16[128,2048]{1,0:T(8,128)(2,1)}, bf16[128,2048]{1,0:T(8,128)(2,1)S(1)}, u32[]{:S(2)}, u32[]{:S(2)}) %collective-permute-start.32) | collective-permute-done | bytes 524320 | tf_op jit(solution)/shard_map/ppermute | solution.py:87
  215.2 12.7 %collective-permute-done.34.refs_4_ = bf16[128,2048]{1,0:T(8,128)(2,1)S(1)} collective-permute-done((bf16[128,2048]{1,0:T(8,128)(2,1)S(1)}, bf16[128,2048]{1,0:T(8,128)(2,1)S(1)}, u32[]{:S(2)}, u32[]{:S(2)}) %collective-permute-start.34) | collective-permute-done | bytes 524320 | tf_op jit(solution)/shard_map/ppermute | solution.py:87
  228.6 22.5 %shard_map.252 = (bf16[512,2048]{1,0:T(8,128)(2,1)}, bf16[512,2048]{1,0:T(8,128)(2,1)}, bf16[512,2048]{1,0:T(8,128)(2,1)}, bf16[512,2048]{1,0:T(8,128)(2,1)}, bf...) custom-call(bf16[128,2048]{1,0:T(8,128)(2,1)} %get-tuple-element.146, ...), custom_call_target="tpu_custom_call" | custom-call | flops 12884901888 | bytes 88604672 | tf_op jit(solution)/shard_map/pallas_call | solution.py:189
  256.6 9.4 %collective-permute-done.37 = bf16[128,2048]{1,0:T(8,128)(2,1)S(1)} collective-permute-done((bf16[128,2048]{1,0:T(8,128)(2,1)S(1)}, bf16[128,2048]{1,0:T(8,128)(2,1)S(1)}, u32[]{:S(2)}, u32[]{:S(2)}) %collective-permute-start.37) | collective-permute-done | bytes 524320 | tf_op jit(solution)/shard_map/ppermute | solution.py:87
  269.6 7.6 %collective-permute-done.35.refs_1_ = bf16[128,2048]{1,0:T(8,128)(2,1)S(1)} collective-permute-done((bf16[128,2048]{1,0:T(8,128)(2,1)S(1)}, bf16[128,2048]{1,0:T(8,128)(2,1)S(1)}, u32[]{:S(2)}, u32[]{:S(2)}) %collective-permute-start.35) | collective-permute-done | bytes 524320 | tf_op jit(solution)/shard_map/ppermute | solution.py:87
  277.2 14.6 %collective-permute-done.38.refs_3_ = bf16[128,2048]{1,0:T(8,128)(2,1)S(1)} collective-permute-done((bf16[128,2048]{1,0:T(8,128)(2,1)S(1)}, bf16[128,2048]{1,0:T(8,128)(2,1)S(1)}, u32[]{:S(2)}, u32[]{:S(2)}) %collective-permute-start.38) | collective-permute-done | bytes 524320 | tf_op jit(solution)/shard_map/ppermute | solution.py:87
  292.6 3.8 shard_map.253
  299.2 21.8 %collective-permute-done.40.refs_2_ = bf16[128,2048]{1,0:T(8,128)(2,1)S(1)} collective-permute-done((bf16[128,2048]{1,0:T(8,128)(2,1)}, bf16[128,2048]{1,0:T(8,128)(2,1)S(1)}, u32[]{:S(2)}, u32[]{:S(2)}) %collective-permute-start.40) | collective-permute-done | bytes 524320 | tf_op jit(solution)/shard_map/ppermute | solution.py:87
  322.4 10.1 %collective-permute-done.42.refs_4_ = bf16[128,2048]{1,0:T(8,128)(2,1)S(1)} collective-permute-done((bf16[128,2048]{1,0:T(8,128)(2,1)S(1)}, bf16[128,2048]{1,0:T(8,128)(2,1)S(1)}, u32[]{:S(2)}, u32[]{:S(2)}) %collective-permute-start.42) | collective-permute-done | bytes 524320 | tf_op jit(solution)/shard_map/ppermute | solution.py:87
  333.3 9.3 %shard_map.254 = bf16[2048,2048]{1,0:T(8,128)(2,1)} custom-call(bf16[128,2048]{1,0:T(8,128)(2,1)} %get-tuple-element.153.refs_0_, bf16[128,2048]{1,0:T(8,128)(2,1)} %copy-done.13, bf16[128,2048]{1,0:T(8,128)(2,1)} %copy-done.11, bf16[128,2048]{1,0:T(8,128)(2,1)} %copy-done.15, bf16[128,2048]{1,0:T(8,128)(2,1)} %copy-done.17, ...), custom_call_target="tpu_custom_call" | custom-call | flops 4294967296 | bytes 13107200 | tf_op jit(solution)/shard_map/pallas_call | solution.py:189
  343.1 24.7 %shard_map.255 = (bf16[512,2048]{1,0:T(8,128)(2,1)}, bf16[512,2048]{1,0:T(8,128)(2,1)}, bf16[512,2048]{1,0:T(8,128)(2,1)}, bf16[128,2048]{1,0:T(8,128)(2,1)}, bf...) custom-call(bf16[128,2048]{1,0:T(8,128)(2,1)} %get-tuple-element.153.refs_0_, ...), custom_call_target="tpu_custom_call" | custom-call | flops 12884901888 | bytes 90701824 | tf_op jit(solution)/shard_map/pallas_call | solution.py:189
  372.9 9.2 %collective-permute-done.45 = bf16[128,2048]{1,0:T(8,128)(2,1)S(1)} collective-permute-done((bf16[128,2048]{1,0:T(8,128)(2,1)}, bf16[128,2048]{1,0:T(8,128)(2,1)S(1)}, u32[]{:S(2)}, u32[]{:S(2)}) %collective-permute-start.45) | collective-permute-done | bytes 524320 | tf_op jit(solution)/shard_map/ppermute | solution.py:87
  383.3 3.9 collective-permute-start.46
  387.2 9.2 %shard_map.267.refs_2_ = bf16[2048,4096]{1,0:T(8,128)(2,1)} custom-call(bf16[512,2048]{1,0:T(8,128)(2,1)} %get-tuple-element.222.refs_0_, bf16[512,2048]{1,0:T(8,128)(2,1)} %get-tuple-element.224.refs_1_), custom_call_target="tpu_custom_call" | custom-call | flops 4294967296 | bytes 10485760 | tf_op jit(solution)/shard_map/pallas_call | solution.py:384
  396.4 9.1 %shard_map.268 = bf16[2048,4096]{1,0:T(8,128)(2,1)} custom-call(bf16[512,2048]{1,0:T(8,128)(2,1)} %get-tuple-element.222.refs_0_, bf16[512,2048]{1,0:T(8,128)(2,1)} %get-tuple-element.223.refs_1_, bf16[2048,4096]{1,0:T(8,128)(2,1)} %shard_map.267.refs_2_), custom_call_target="tpu_custom_call", output_to_operand_aliasing={{}: (2, {})} | custom-call | flops 4294967296 | bytes 10485760 | tf_op jit(solution)/shard_map/pallas_call | solution.py:384
  406.6 3.9 shard_map.256
  410.5 6.2 %shard_map.257 = (bf16[128,512]{1,0:T(8,128)(2,1)}, bf16[128,512]{1,0:T(8,128)(2,1)}, bf16[128,512]{1,0:T(8,128)(2,1)}, bf16[128,512]{1,0:T(8,128)(2,1)}) custom-call(bf16[128,2048]{1,0:T(8,128)(2,1)} %get-tuple-element.194.grad_ref.refs_0_, bf16[2048,2048]{1,0:T(8,128)(2,1)} %all-gather.11.cloned.1.call-done.weight_ref), custom_call_target="tpu_custom_call" | custom-call | flops 1073741824 | bytes 9437184 | tf_op jit(solution)/shard_map/pallas_call | solution.py:189
  441.3 11.9 %shard_map.259 = (bf16[256,384]{1,0:T(8,128)(2,1)}, bf16[256,384]{1,0:T(8,128)(2,1)}, bf16[256,384]{1,0:T(8,128)(2,1)}, bf16[256,384]{1,0:T(8,128)(2,1)}, bf16[2...) custom-call(s32[1]{0:T(128)} %bitcast.me_ref, ...), custom_call_target="tpu_custom_call" | custom-call | flops 2684354560 | bytes 4759556 | tf_op jit(solution)/shard_map/pallas_call | solution.py:172
  456.7 8.3 %collective-permute-done.60.refs_2_ = bf16[256,384]{1,0:T(8,128)(2,1)S(1)} collective-permute-done((bf16[256,384]{1,0:T(8,128)(2,1)}, bf16[256,384]{1,0:T(8,128)(2,1)S(1)}, u32[]{:S(2)}, u32[]{:S(2)}) %collective-permute-start.60) | collective-permute-done | bytes 196640 | tf_op jit(solution)/shard_map/ppermute | solution.py:124
  466.3 6.4 %collective-permute-done.62.refs_3_ = bf16[256,384]{1,0:T(8,128)(2,1)S(1)} collective-permute-done((bf16[256,384]{1,0:T(8,128)(2,1)}, bf16[256,384]{1,0:T(8,128)(2,1)S(1)}, u32[]{:S(2)}, u32[]{:S(2)}) %collective-permute-start.62) | collective-permute-done | bytes 196640 | tf_op jit(solution)/shard_map/ppermute | solution.py:124
  478.8 4.2 collective-permute-done.65.refs_6_
  483.1 7.3 %collective-permute-done.66.refs_7_ = bf16[256,384]{1,0:T(8,128)(2,1)S(1)} collective-permute-done((bf16[256,384]{1,0:T(8,128)(2,1)}, bf16[256,384]{1,0:T(8,128)(2,1)S(1)}, u32[]{:S(2)}, u32[]{:S(2)}) %collective-permute-start.66) | collective-permute-done | bytes 196640 | tf_op jit(solution)/shard_map/ppermute | solution.py:126
  490.4 8.0 %collective-permute-done.70.refs_4_ = bf16[128,2048]{1,0:T(8,128)(2,1)S(1)} collective-permute-done((bf16[128,2048]{1,0:T(8,128)(2,1)S(1)}, bf16[128,2048]{1,0:T(8,128)(2,1)S(1)}, u32[]{:S(2)}, u32[]{:S(2)}) %collective-permute-start.70) | collective-permute-done | bytes 524320 | tf_op jit(solution)/shard_map/ppermute | solution.py:87
  498.4 3.9 shard_map.260
  502.3 4.0 shard_map.261
  514.6 10.8 %shard_map.264 = (bf16[4,256,2048]{2,1,0:T(8,128)(2,1)}, bf16[4,256,2048]{2,1,0:T(8,128)(2,1)}) custom-call(s32[1]{0:T(128)} %bitcast.me_ref, bf16[512,2048]{1,0:T(8,128)(2,1)} %shard_map.263.refs_0_, bf16[512,2048]{1,0:T(8,128)(2,1)} %get-tuple-element.207.refs_1_.refs_0_, bf16[512,512]{1,0:T(8,128)(2,1)} %bitcast.115, bf16[512,512]{1,0:T(8,128)(2,1)} %bitcast.141), custom_call_target="tpu_custom_call" | custom-call | flops 2147483648 | bytes 9437184 | tf_op jit(solution)/shard_map/pallas_call | solution.py:733
  526.9 4.2 shard_map.262.refs_1_.qk_ref
  531.1 8.5 %shard_map.265 = (bf16[4,256,2048]{2,1,0:T(8,128)(2,1)}, bf16[4,256,2048]{2,1,0:T(8,128)(2,1)}) custom-call(s32[1]{0:T(128)} %bitcast.me_ref, bf16[512,2048]{1,0:T(8,128)(2,1)} %get-tuple-element.207.refs_1_.refs_0_, bf16[512,1024]{1,0:T(8,128)(2,1)} %shard_map.262.refs_1_.qk_ref, ...), custom_call_target="tpu_custom_call", output_to_operand_aliasing={{0}: (3, {}), {1}: (4, {})} | custom-call | flops 2147483648 | bytes 7340032 | tf_op jit(solution)/shard_map/pallas_call | solution.py:733
  545.2 7.5 %shard_map.266 = (bf16[128,2048]{1,0:T(8,128)(2,1)}, bf16[128,2048]{1,0:T(8,128)(2,1)}, bf16[128,2048]{1,0:T(8,128)(2,1)}, bf16[128,2048]{1,0:T(8,128)(2,1)}) custom-call(bf16[512,1024]{1,0:T(8,128)(2,1)} %shard_map.262.refs_1_.qk_ref, bf16[512,512]{1,0:T(8,128)(2,1)} %bitcast.142, bf16[2048,1536]{1,0:T(8,128)(2,1)} %all-gather.5.cloned.1.call-done.refs_5_.weight_ref), custom_call_target="tpu_custom_call" | custom-call | flops 3221225472 | bytes 9961472 | tf_op jit(solution)/shard_map/pallas_call | solution.py:189
  552.7 4.0 add_bitcast_fusion
  564.9 9.9 %collective-permute-done.77 = bf16[128,2048]{1,0:T(8,128)(2,1)S(1)} collective-permute-done((bf16[128,2048]{1,0:T(8,128)(2,1)}, bf16[128,2048]{1,0:T(8,128)(2,1)S(1)}, u32[]{:S(2)}, u32[]{:S(2)}) %collective-permute-start.77) | collective-permute-done | bytes 524320 | tf_op jit(solution)/shard_map/ppermute | solution.py:87
  585.1 5.1 shard_map.269
  592.6 7.6 %collective-permute-done.78 = bf16[128,2048]{1,0:T(8,128)(2,1)} collective-permute-done((bf16[128,2048]{1,0:T(8,128)(2,1)}, bf16[128,2048]{1,0:T(8,128)(2,1)}, u32[]{:S(2)}, u32[]{:S(2)}) %collective-permute-start.78) | collective-permute-done | bytes 524320 | tf_op jit(solution)/shard_map/ppermute | solution.py:87
  (429 shorter events, 178.6 us)
Async XLA Ops:
  7.2 51.7 %all-gather.5.cloned.1.call-start = ((), (), s32[]{:S(2)}) async-start(), calls=%async_computation.2 | async-start | bytes 7077888 | tf_op jit(solution)/shard_map/all_gather | solution.py:1221
  9.4 122.9 %all-gather.7.cloned.1.call-start = ((), (), s32[]{:S(2)}) async-start(), calls=%async_computation.3 | async-start | bytes 2359296 | tf_op jit(solution)/shard_map/all_gather | solution.py:1221
  10.3 217.5 %all-gather.9.cloned.1.call-start = ((), (), s32[]{:S(2)}) async-start(), calls=%async_computation.4 | async-start | bytes 28311552 | tf_op jit(solution)/shard_map/all_gather | solution.py:1221
  14.0 396.5 %all-gather.11.cloned.1.call-start = ((), (), s32[]{:S(2)}) async-start(), calls=%async_computation.5 | async-start | bytes 9437184 | tf_op jit(solution)/shard_map/all_gather | solution.py:1221
  15.0 28.3 %collective-permute-start.1 = (bf16[128,2048]{1,0:T(8,128)(2,1)S(1)}, bf16[128,2048]{1,0:T(8,128)(2,1)S(1)}, u32[]{:S(2)}, u32[]{:S(2)}) collective-permute-start(bf16[128,2048]{1,0:T(8,128)(2,1)S(1)} %bitcast.112), channel_id=1, source_target_pairs={{0,2},{1,3},{2,0},{3,1},{4,6},{5,7},{6,4},{7,5},{8,10},{9,11},{10,... | collective-permute-start | bytes 1572872 | tf_op jit(solution)/shard_map/ppermute | solution.py:87
  19.1 32.1 %collective-permute-start = (bf16[128,2048]{1,0:T(8,128)(2,1)S(1)}, bf16[128,2048]{1,0:T(8,128)(2,1)S(1)}, u32[]{:S(2)}, u32[]{:S(2)}) collective-permute-start(bf16[128,2048]{1,0:T(8,128)(2,1)S(1)} %bitcast.113), channel_id=1, source_target_pairs={{0,1},{1,0},{2,3},{3,2},{4,5},{5,4},{6,7},{7,6},{8,9},{9,8},{10,11... | collective-permute-start | bytes 1572872 | tf_op jit(solution)/shard_map/ppermute | solution.py:87
  20.7 22.0 %collective-permute-start.14 = (s32[2,64]{1,0:T(2,128)S(1)}, s32[2,64]{1,0:T(2,128)S(1)}, u32[]{:S(2)}, u32[]{:S(2)}) collective-permute-start(s32[2,64]{1,0:T(2,128)S(1)} %multiply_add_fusion), channel_id=1, source_target_pairs={{0,1},{1,0},{2,3},{3,2},{4,5},{5,4},{6,7},{7,6},{8,9},{9,8},{10,11... | collective-permute-start | bytes 1544 | tf_op jit(solution)/shard_map/ppermute | solution.py:49
  21.2 23.5 %collective-permute-start.15 = (s32[2,64]{1,0:T(2,128)S(1)}, s32[2,64]{1,0:T(2,128)S(1)}, u32[]{:S(2)}, u32[]{:S(2)}) collective-permute-start(s32[2,64]{1,0:T(2,128)S(1)} %multiply_add_fusion), channel_id=1, source_target_pairs={{0,2},{1,3},{2,0},{3,1},{4,6},{5,7},{6,4},{7,5},{8,10},{9,11},{10,... | collective-permute-start | bytes 1544 | tf_op jit(solution)/shard_map/ppermute | solution.py:49
  21.2 23.5 %collective-permute-start.16 = (s32[2,64]{1,0:T(2,128)S(1)}, s32[2,64]{1,0:T(2,128)S(1)}, u32[]{:S(2)}, u32[]{:S(2)}) collective-permute-start(s32[2,64]{1,0:T(2,128)S(1)} %multiply_add_fusion), channel_id=1, source_target_pairs={{0,3},{1,2},{2,1},{3,0},{4,7},{5,6},{6,5},{7,4},{8,11},{9,10},{10,... | collective-permute-start | bytes 1544 | tf_op jit(solution)/shard_map/ppermute | solution.py:49
  49.6 23.1 %collective-permute-start.19 = (s32[4,2,256]{2,1,0:T(2,128)S(1)}, s32[4,2,256]{2,1,0:T(2,128)S(1)}, u32[]{:S(2)}, u32[]{:S(2)}) collective-permute-start(s32[4,2,256]{2,1,0:T(2,128)S(1)} %pad_add_fusion.1), channel_id=1, source_target_pairs={{0,16},{4,20},{8,24},{12,28},{16,0},{20,4},{24,8},{28,12},{1,17},{... | collective-permute-start | bytes 24584 | tf_op jit(solution)/shard_map/ppermute | solution.py:63
  136.6 15.7 %collective-permute-start.29 = (bf16[128,2048]{1,0:T(8,128)(2,1)}, bf16[128,2048]{1,0:T(8,128)(2,1)S(1)}, u32[]{:S(2)}, u32[]{:S(2)}) collective-permute-start(bf16[128,2048]{1,0:T(8,128)(2,1)} %get-tuple-element.144), channel_id=1, source_target_pairs={{0,1},{3,2},{4,5},{7,6},{8,9},{11,10},{12,13},{15,14},{16,17},{19,... | collective-permute-start | bytes 1572872 | tf_op jit(solution)/shard_map/ppermute | solution.py:87
  139.7 23.8 %collective-permute-start.28 = (bf16[128,2048]{1,0:T(8,128)(2,1)}, bf16[128,2048]{1,0:T(8,128)(2,1)S(1)}, u32[]{:S(2)}, u32[]{:S(2)}) collective-permute-start(bf16[128,2048]{1,0:T(8,128)(2,1)} %get-tuple-element.144), channel_id=1, source_target_pairs={{1,2},{2,1},{5,6},{6,5},{9,10},{10,9},{13,14},{14,13},{17,18},{18,... | collective-permute-start | bytes 1572872 | tf_op jit(solution)/shard_map/ppermute | solution.py:87
  140.6 22.9 %collective-permute-start.27 = (bf16[128,2048]{1,0:T(8,128)(2,1)}, bf16[128,2048]{1,0:T(8,128)(2,1)S(1)}, u32[]{:S(2)}, u32[]{:S(2)}) collective-permute-start(bf16[128,2048]{1,0:T(8,128)(2,1)} %get-tuple-element.143), channel_id=1, source_target_pairs={{0,1},{1,0},{2,3},{3,2},{4,5},{5,4},{6,7},{7,6},{8,9},{9,8},{10,11... | collective-permute-start | bytes 1572872 | tf_op jit(solution)/shard_map/ppermute | solution.py:87
  153.5 26.3 %collective-permute-start.30 = (bf16[128,2048]{1,0:T(8,128)(2,1)S(1)}, bf16[128,2048]{1,0:T(8,128)(2,1)S(1)}, u32[]{:S(2)}, u32[]{:S(2)}) collective-permute-start(bf16[128,2048]{1,0:T(8,128)(2,1)S(1)} %add_convert_fusion.4), channel_id=1, source_target_pairs={{0,2},{1,3},{2,0},{3,1},{4,6},{5,7},{6,4},{7,5},{8,10},{9,11},{10,... | collective-permute-start | bytes 1572872 | tf_op jit(solution)/shard_map/ppermute | solution.py:87
  184.5 24.2 %collective-permute-start.32 = (bf16[128,2048]{1,0:T(8,128)(2,1)}, bf16[128,2048]{1,0:T(8,128)(2,1)S(1)}, u32[]{:S(2)}, u32[]{:S(2)}) collective-permute-start(bf16[128,2048]{1,0:T(8,128)(2,1)} %get-tuple-element.146.refs_0_), channel_id=1, source_target_pairs={{0,2},{1,3},{2,0},{3,1},{4,6},{5,7},{6,4},{7,5},{8,10},{9,11},{10,... | collective-permute-start | bytes 1572872 | tf_op jit(solution)/shard_map/ppermute | solution.py:87
  184.5 29.2 %collective-permute-start.31 = (bf16[128,2048]{1,0:T(8,128)(2,1)}, bf16[128,2048]{1,0:T(8,128)(2,1)S(1)}, u32[]{:S(2)}, u32[]{:S(2)}) collective-permute-start(bf16[128,2048]{1,0:T(8,128)(2,1)} %get-tuple-element.146.refs_0_), channel_id=1, source_target_pairs={{0,1},{1,0},{2,3},{3,2},{4,5},{5,4},{6,7},{7,6},{8,9},{9,8},{10,11... | collective-permute-start | bytes 1572872 | tf_op jit(solution)/shard_map/ppermute | solution.py:87
  186.8 28.4 %collective-permute-start.33 = (bf16[128,2048]{1,0:T(8,128)(2,1)}, bf16[128,2048]{1,0:T(8,128)(2,1)S(1)}, u32[]{:S(2)}, u32[]{:S(2)}) collective-permute-start(bf16[128,2048]{1,0:T(8,128)(2,1)} %get-tuple-element.146.refs_0_), channel_id=1, source_target_pairs={{1,2},{2,1},{5,6},{6,5},{9,10},{10,9},{13,14},{14,13},{17,18},{18,... | collective-permute-start | bytes 1572872 | tf_op jit(solution)/shard_map/ppermute | solution.py:87
  208.6 19.2 %collective-permute-start.34 = (bf16[128,2048]{1,0:T(8,128)(2,1)S(1)}, bf16[128,2048]{1,0:T(8,128)(2,1)S(1)}, u32[]{:S(2)}, u32[]{:S(2)}) collective-permute-start(bf16[128,2048]{1,0:T(8,128)(2,1)S(1)} %collective-permute-done.32.refs_2_), channel_id=1, source_target_pairs={{1,0},{2,3},{5,4},{6,7},{9,8},{10,11},{13,12},{14,15},{17,16},{18,... | collective-permute-start | bytes 1572872 | tf_op jit(solution)/shard_map/ppermute | solution.py:87
  209.9 41.3 %collective-permute-start.47 = (bf16[256,512]{1,0:T(8,128)(2,1)S(1)}, bf16[256,512]{1,0:T(8,128)(2,1)S(1)}, u32[]{:S(2)}, u32[]{:S(2)}) collective-permute-start(bf16[256,512]{1,0:T(8,128)(2,1)S(1)} %bitcast.100), channel_id=1, source_target_pairs={{0,1},{1,0},{2,3},{3,2},{4,5},{5,4},{6,7},{7,6},{8,9},{9,8},{10,11... | collective-permute-start | bytes 786440 | tf_op jit(solution)/shard_map/ppermute | solution.py:49
  212.7 38.6 %collective-permute-start.48 = (bf16[256,512]{1,0:T(8,128)(2,1)S(1)}, bf16[256,512]{1,0:T(8,128)(2,1)S(1)}, u32[]{:S(2)}, u32[]{:S(2)}) collective-permute-start(bf16[256,512]{1,0:T(8,128)(2,1)S(1)} %bitcast.101), channel_id=1, source_target_pairs={{0,2},{1,3},{2,0},{3,1},{4,6},{5,7},{6,4},{7,5},{8,10},{9,11},{10,... | collective-permute-start | bytes 786440 | tf_op jit(solution)/shard_map/ppermute | solution.py:49
  213.7 37.5 %collective-permute-start.49 = (bf16[256,512]{1,0:T(8,128)(2,1)S(1)}, bf16[256,512]{1,0:T(8,128)(2,1)S(1)}, u32[]{:S(2)}, u32[]{:S(2)}) collective-permute-start(bf16[256,512]{1,0:T(8,128)(2,1)S(1)} %bitcast.102), channel_id=1, source_target_pairs={{0,3},{1,2},{2,1},{3,0},{4,7},{5,6},{6,5},{7,4},{8,11},{9,10},{10,... | collective-permute-start | bytes 786440 | tf_op jit(solution)/shard_map/ppermute | solution.py:49
  252.4 332.7 %reduce-scatter.5.cloned.1.call-start = ((), (), s32[]{:S(2)}) async-start(), calls=%async_computation.7 | async-start | bytes 9437184 | tf_op jit(solution)/shard_map/reduce_scatter | solution.py:1273
  253.8 23.5 %collective-permute-start.36 = (bf16[128,2048]{1,0:T(8,128)(2,1)S(1)}, bf16[128,2048]{1,0:T(8,128)(2,1)S(1)}, u32[]{:S(2)}, u32[]{:S(2)}) collective-permute-start(bf16[128,2048]{1,0:T(8,128)(2,1)S(1)} %copy-done.67), channel_id=1, source_target_pairs={{1,2},{2,1},{5,6},{6,5},{9,10},{10,9},{13,14},{14,13},{17,18},{18,... | collective-permute-start | bytes 1572872 | tf_op jit(solution)/shard_map/ppermute | solution.py:87
  254.5 22.7 %collective-permute-start.35 = (bf16[128,2048]{1,0:T(8,128)(2,1)S(1)}, bf16[128,2048]{1,0:T(8,128)(2,1)S(1)}, u32[]{:S(2)}, u32[]{:S(2)}) collective-permute-start(bf16[128,2048]{1,0:T(8,128)(2,1)S(1)} %copy-done.68), channel_id=1, source_target_pairs={{0,1},{1,0},{2,3},{3,2},{4,5},{5,4},{6,7},{7,6},{8,9},{9,8},{10,11... | collective-permute-start | bytes 1572872 | tf_op jit(solution)/shard_map/ppermute | solution.py:87
  266.1 25.7 %collective-permute-start.38 = (bf16[128,2048]{1,0:T(8,128)(2,1)S(1)}, bf16[128,2048]{1,0:T(8,128)(2,1)S(1)}, u32[]{:S(2)}, u32[]{:S(2)}) collective-permute-start(bf16[128,2048]{1,0:T(8,128)(2,1)S(1)} %add_convert_fusion.3), channel_id=1, source_target_pairs={{0,2},{1,3},{2,0},{3,1},{4,6},{5,7},{6,4},{7,5},{8,10},{9,11},{10,... | collective-permute-start | bytes 1572872 | tf_op jit(solution)/shard_map/ppermute | solution.py:87
  296.4 24.6 %collective-permute-start.40 = (bf16[128,2048]{1,0:T(8,128)(2,1)}, bf16[128,2048]{1,0:T(8,128)(2,1)S(1)}, u32[]{:S(2)}, u32[]{:S(2)}) collective-permute-start(bf16[128,2048]{1,0:T(8,128)(2,1)} %get-tuple-element.153.refs_0_), channel_id=1, source_target_pairs={{0,2},{1,3},{2,0},{3,1},{4,6},{5,7},{6,4},{7,5},{8,10},{9,11},{10,... | collective-permute-start | bytes 1572872 | tf_op jit(solution)/shard_map/ppermute | solution.py:87
  296.4 25.9 %collective-permute-start.39 = (bf16[128,2048]{1,0:T(8,128)(2,1)}, bf16[128,2048]{1,0:T(8,128)(2,1)S(1)}, u32[]{:S(2)}, u32[]{:S(2)}) collective-permute-start(bf16[128,2048]{1,0:T(8,128)(2,1)} %get-tuple-element.153.refs_0_), channel_id=1, source_target_pairs={{0,1},{1,0},{2,3},{3,2},{4,5},{5,4},{6,7},{7,6},{8,9},{9,8},{10,11... | collective-permute-start | bytes 1572872 | tf_op jit(solution)/shard_map/ppermute | solution.py:87
  298.5 23.8 %collective-permute-start.41 = (bf16[128,2048]{1,0:T(8,128)(2,1)}, bf16[128,2048]{1,0:T(8,128)(2,1)S(1)}, u32[]{:S(2)}, u32[]{:S(2)}) collective-permute-start(bf16[128,2048]{1,0:T(8,128)(2,1)} %get-tuple-element.153.refs_0_), channel_id=1, source_target_pairs={{1,2},{2,1},{5,6},{6,5},{9,10},{10,9},{13,14},{14,13},{17,18},{18,... | collective-permute-start | bytes 1572872 | tf_op jit(solution)/shard_map/ppermute | solution.py:87
  342.6 242.4 %reduce-scatter.3.cloned.1.call-start = ((), (), s32[]{:S(2)}) async-start(), calls=%async_computation.6 | async-start | bytes 18874368 | tf_op jit(solution)/shard_map/reduce_scatter | solution.py:1275
  369.4 36.1 %collective-permute-start.44 = (bf16[128,2048]{1,0:T(8,128)(2,1)}, bf16[128,2048]{1,0:T(8,128)(2,1)S(1)}, u32[]{:S(2)}, u32[]{:S(2)}) collective-permute-start(bf16[128,2048]{1,0:T(8,128)(2,1)} %get-tuple-element.160), channel_id=1, source_target_pairs={{1,2},{2,1},{5,6},{6,5},{9,10},{10,9},{13,14},{14,13},{17,18},{18,... | collective-permute-start | bytes 1572872 | tf_op jit(solution)/shard_map/ppermute | solution.py:87
  370.1 35.4 %collective-permute-start.43 = (bf16[128,2048]{1,0:T(8,128)(2,1)}, bf16[128,2048]{1,0:T(8,128)(2,1)S(1)}, u32[]{:S(2)}, u32[]{:S(2)}) collective-permute-start(bf16[128,2048]{1,0:T(8,128)(2,1)} %get-tuple-element.159), channel_id=1, source_target_pairs={{0,1},{1,0},{2,3},{3,2},{4,5},{5,4},{6,7},{7,6},{8,9},{9,8},{10,11... | collective-permute-start | bytes 1572872 | tf_op jit(solution)/shard_map/ppermute | solution.py:87
  383.3 22.2 %collective-permute-start.46 = (bf16[128,2048]{1,0:T(8,128)(2,1)S(1)}, bf16[128,2048]{1,0:T(8,128)(2,1)S(1)}, u32[]{:S(2)}, u32[]{:S(2)}) collective-permute-start(bf16[128,2048]{1,0:T(8,128)(2,1)S(1)} %add_convert_fusion.2), channel_id=1, source_target_pairs={{0,2},{1,3},{2,0},{3,1},{4,6},{5,7},{6,4},{7,5},{8,10},{9,11},{10,... | collective-permute-start | bytes 1572872 | tf_op jit(solution)/shard_map/ppermute | solution.py:87
  435.8 39.6 %collective-permute-start.68 = (bf16[128,2048]{1,0:T(8,128)(2,1)S(1)}, bf16[128,2048]{1,0:T(8,128)(2,1)S(1)}, u32[]{:S(2)}, u32[]{:S(2)}) collective-permute-start(bf16[128,2048]{1,0:T(8,128)(2,1)S(1)} %copy-done.6), channel_id=1, source_target_pairs={{0,2},{1,3},{2,0},{3,1},{4,6},{5,7},{6,4},{7,5},{8,10},{9,11},{10,... | collective-permute-start | bytes 1572872 | tf_op jit(solution)/shard_map/ppermute | solution.py:87
  454.6 18.2 %collective-permute-start.62 = (bf16[256,384]{1,0:T(8,128)(2,1)}, bf16[256,384]{1,0:T(8,128)(2,1)S(1)}, u32[]{:S(2)}, u32[]{:S(2)}) collective-permute-start(bf16[256,384]{1,0:T(8,128)(2,1)} %get-tuple-element.188), channel_id=1, source_target_pairs={{0,12},{4,8},{8,4},{12,0},{16,28},{20,24},{24,20},{28,16},{1,13},{... | collective-permute-start | bytes 589832 | tf_op jit(solution)/shard_map/ppermute | solution.py:124
  454.9 19.8 %collective-permute-start.63 = (bf16[256,384]{1,0:T(8,128)(2,1)}, bf16[256,384]{1,0:T(8,128)(2,1)S(1)}, u32[]{:S(2)}, u32[]{:S(2)}) collective-permute-start(bf16[256,384]{1,0:T(8,128)(2,1)} %get-tuple-element.189), channel_id=1, source_target_pairs={{0,16},{4,20},{8,24},{12,28},{16,0},{20,4},{24,8},{28,12},{1,17},{... | collective-permute-start | bytes 589832 | tf_op jit(solution)/shard_map/ppermute | solution.py:124
  456.2 20.6 %collective-permute-start.64 = (bf16[256,384]{1,0:T(8,128)(2,1)}, bf16[256,384]{1,0:T(8,128)(2,1)S(1)}, u32[]{:S(2)}, u32[]{:S(2)}) collective-permute-start(bf16[256,384]{1,0:T(8,128)(2,1)} %get-tuple-element.190), channel_id=1, source_target_pairs={{0,20},{4,16},{8,28},{12,24},{16,4},{20,0},{24,12},{28,8},{1,21},{... | collective-permute-start | bytes 589832 | tf_op jit(solution)/shard_map/ppermute | solution.py:124
  465.0 18.0 %collective-permute-start.65 = (bf16[256,384]{1,0:T(8,128)(2,1)}, bf16[256,384]{1,0:T(8,128)(2,1)S(1)}, u32[]{:S(2)}, u32[]{:S(2)}) collective-permute-start(bf16[256,384]{1,0:T(8,128)(2,1)} %get-tuple-element.191), channel_id=1, source_target_pairs={{0,24},{4,28},{8,16},{12,20},{16,8},{20,12},{24,0},{28,4},{1,25},{... | collective-permute-start | bytes 589832 | tf_op jit(solution)/shard_map/ppermute | solution.py:124
  472.8 17.6 %collective-permute-start.67 = (bf16[128,2048]{1,0:T(8,128)(2,1)S(1)}, bf16[128,2048]{1,0:T(8,128)(2,1)S(1)}, u32[]{:S(2)}, u32[]{:S(2)}) collective-permute-start(bf16[128,2048]{1,0:T(8,128)(2,1)S(1)} %copy-done.6), channel_id=1, source_target_pairs={{0,1},{1,0},{2,3},{3,2},{4,5},{5,4},{6,7},{7,6},{8,9},{9,8},{10,11... | collective-permute-start | bytes 1572872 | tf_op jit(solution)/shard_map/ppermute | solution.py:87
  474.8 15.6 %collective-permute-start.69 = (bf16[128,2048]{1,0:T(8,128)(2,1)S(1)}, bf16[128,2048]{1,0:T(8,128)(2,1)S(1)}, u32[]{:S(2)}, u32[]{:S(2)}) collective-permute-start(bf16[128,2048]{1,0:T(8,128)(2,1)S(1)} %copy-done.6), channel_id=1, source_target_pairs={{1,2},{2,1},{5,6},{6,5},{9,10},{10,9},{13,14},{14,13},{17,18},{18,... | collective-permute-start | bytes 1572872 | tf_op jit(solution)/shard_map/ppermute | solution.py:87
  475.5 22.9 %collective-permute-start.70 = (bf16[128,2048]{1,0:T(8,128)(2,1)S(1)}, bf16[128,2048]{1,0:T(8,128)(2,1)S(1)}, u32[]{:S(2)}, u32[]{:S(2)}) collective-permute-start(bf16[128,2048]{1,0:T(8,128)(2,1)S(1)} %collective-permute-done.68.refs_2_), channel_id=1, source_target_pairs={{1,0},{2,3},{5,4},{6,7},{9,8},{10,11},{13,12},{14,15},{17,16},{18,... | collective-permute-start | bytes 1572872 | tf_op jit(solution)/shard_map/ppermute | solution.py:87
  507.0 18.4 %collective-permute-start.73 = (f32[5120]{0:T(1024)S(1)}, f32[5120]{0:T(1024)S(1)}, u32[]{:S(2)}, u32[]{:S(2)}) collective-permute-start(f32[5120]{0:T(1024)S(1)} %pad_maximum_fusion.7), channel_id=1, source_target_pairs={{0,3},{1,2},{2,1},{3,0},{4,7},{5,6},{6,5},{7,4},{8,11},{9,10},{10,... | collective-permute-start | bytes 61448 | tf_op jit(solution)/shard_map/ppermute | solution.py:49
  509.4 16.0 %collective-permute-start.72 = (f32[5120]{0:T(1024)S(1)}, f32[5120]{0:T(1024)S(1)}, u32[]{:S(2)}, u32[]{:S(2)}) collective-permute-start(f32[5120]{0:T(1024)S(1)} %pad_maximum_fusion.7), channel_id=1, source_target_pairs={{0,2},{1,3},{2,0},{3,1},{4,6},{5,7},{6,4},{7,5},{8,10},{9,11},{10,... | collective-permute-start | bytes 61448 | tf_op jit(solution)/shard_map/ppermute | solution.py:49
  509.4 16.3 %collective-permute-start.71 = (f32[5120]{0:T(1024)S(1)}, f32[5120]{0:T(1024)S(1)}, u32[]{:S(2)}, u32[]{:S(2)}) collective-permute-start(f32[5120]{0:T(1024)S(1)} %pad_maximum_fusion.7), channel_id=1, source_target_pairs={{0,1},{1,0},{2,3},{3,2},{4,5},{5,4},{6,7},{7,6},{8,9},{9,8},{10,11... | collective-permute-start | bytes 61448 | tf_op jit(solution)/shard_map/ppermute | solution.py:49
  557.1 24.3 %collective-permute-start.82 = (bf16[2,256,1024]{2,1,0:T(8,128)(2,1)S(1)}, bf16[2,256,1024]{2,1,0:T(8,128)(2,1)S(1)}, u32[]{:S(2)}, u32[]{:S(2)}) collective-permute-start(bf16[2,256,1024]{2,1,0:T(8,128)(2,1)S(1)} %pad_maximum_fusion.2), channel_id=1, source_target_pairs={{0,16},{4,20},{8,24},{12,28},{16,0},{20,4},{24,8},{28,12},{1,17},{... | collective-permute-start | bytes 3145736 | tf_op jit(solution)/shard_map/ppermute | solution.py:775
  558.5 23.9 %collective-permute-start.83 = (bf16[2,256,1024]{2,1,0:T(8,128)(2,1)S(1)}, bf16[2,256,1024]{2,1,0:T(8,128)(2,1)S(1)}, u32[]{:S(2)}, u32[]{:S(2)}) collective-permute-start(bf16[2,256,1024]{2,1,0:T(8,128)(2,1)S(1)} %pad_maximum_fusion.3), channel_id=1, source_target_pairs={{0,8},{4,12},{8,0},{12,4},{16,24},{20,28},{24,16},{28,20},{1,9},{5... | collective-permute-start | bytes 3145736 | tf_op jit(solution)/shard_map/ppermute | solution.py:775
  562.1 28.1 %collective-permute-start.75 = (bf16[128,2048]{1,0:T(8,128)(2,1)}, bf16[128,2048]{1,0:T(8,128)(2,1)}, u32[]{:S(2)}, u32[]{:S(2)}) collective-permute-start(bf16[128,2048]{1,0:T(8,128)(2,1)} %get-tuple-element.217), channel_id=1, source_target_pairs={{0,1},{1,0},{2,3},{3,2},{4,5},{5,4},{6,7},{7,6},{8,9},{9,8},{10,11... | collective-permute-start | bytes 1572872 | tf_op jit(solution)/shard_map/ppermute | solution.py:87
  562.2 30.4 %collective-permute-start.76 = (bf16[128,2048]{1,0:T(8,128)(2,1)}, bf16[128,2048]{1,0:T(8,128)(2,1)}, u32[]{:S(2)}, u32[]{:S(2)}) collective-permute-start(bf16[128,2048]{1,0:T(8,128)(2,1)} %get-tuple-element.218), channel_id=1, source_target_pairs={{1,2},{2,1},{5,6},{6,5},{9,10},{10,9},{13,14},{14,13},{17,18},{18,... | collective-permute-start | bytes 1572872 | tf_op jit(solution)/shard_map/ppermute | solution.py:87
  575.7 24.5 %collective-permute-start.78 = (bf16[128,2048]{1,0:T(8,128)(2,1)}, bf16[128,2048]{1,0:T(8,128)(2,1)}, u32[]{:S(2)}, u32[]{:S(2)}) collective-permute-start(bf16[128,2048]{1,0:T(8,128)(2,1)} %add_convert_fusion.1), channel_id=1, source_target_pairs={{0,2},{1,3},{2,0},{3,1},{4,6},{5,7},{6,4},{7,5},{8,10},{9,11},{10,... | collective-permute-start | bytes 1572872 | tf_op jit(solution)/shard_map/ppermute | solution.py:87
  (127 other events, 1245.2 us)
Sparse Core Ops, SparseCore 0:
  10.5 48.3 all-gather.4
  61.4 29.9 all-gather.6
  93.3 133.1 all-gather.8
  252.5 52.4 all-gather.10
  342.8 71.1 reduce-scatter.4
  417.8 133.1 reduce-scatter.2

commit v7 on v6

--- a/solution.py
+++ b/solution.py
@@ -1174,8 +1174,8 @@
         )
 
     def backward(self, grad_parts, *others):
-        grad_slots = exchange_slots(
-            split_mixed(self.me, grad_parts, self.micro_count, self.heads), "blk"
+        grad_slots = exchange_blocks(
+            split_mixed(self.me, grad_parts, self.micro_count, self.heads)
         )
         self.arrived = grad_slots[1:]
         back_slots = exchange_blocks(

time: 618 us -> 618 us (level)
    ppermute x17 -> x10, starting transfers between devices: 16.7 us -> 9.46 us  [exchange_slots(): lax.ppermute(slots[s], axis, xor_pairs(size, s))]
    ppermute x10 -> x15, starting transfers between devices: 9.95 us -> 16.6 us  [exchange_blocks(): lax.ppermute(slots[s], 'blk', xor_pairs(size, s))]
    ppermute x17 -> x10, waiting for transfers between devices: 16.9 us -> 14.4 us  [exchange_slots(): lax.ppermute(slots[s], axis, xor_pairs(size, s))]
    ppermute x10 -> x15, waiting for transfers between devices: 27 us -> 26.1 us  [exchange_blocks(): lax.ppermute(slots[s], 'blk', xor_pairs(size, s))]
  transfers between devices with their start and end apart: 92 -> 92, of which waited for: 41 -> 44; matrix products, arithmetic and copies ran while one was open for 5% -> 5% of each run, Pallas kernels for 30% -> 30%
where the time goes in v7:
time: 618 us; the launch traced here: 613 us
  waiting for transfers between devices  256 us (41%)
  Pallas kernels  184 us (30%)
  starting transfers between devices  111 us (18%)
  other arithmetic  26.5 us (4%)
  local copies, waits for them, and re-layouts  20 us (3%)
  between operations  15.5 us (3%)
    ppermute x32, waiting for transfers between devices, send_rows(): return lax.ppermute(values, 'head', pairs)  176 us
    pallas_call x6, Pallas kernels, call_grid(): pl.pallas_call(body, grid=(steps,), out_shape=outs, in_specs=in_specs, ou...  79.3 us
    pallas_call x14, Pallas kernels, call_whole(): pl.pallas_call(body, out_shape=outs, in_specs=[pl.BlockSpec(memory_space=...  66.8 us
    ppermute x32, starting transfers between devices, send_rows(): return lax.ppermute(values, 'head', pairs)  55.1 us
    ppermute x15, waiting for transfers between devices, exchange_blocks(): lax.ppermute(slots[s], 'blk', xor_pairs(size, s))  26.1 us
    pallas_call x2, Pallas kernels, weight_term_slots(): pl.pallas_call(body, grid=(blocks,), out_shape=outs, in_specs=[scalar_spe...  19.4 us
    ppermute x12, waiting for transfers between devices, gather_slots(): lax.ppermute(values, axis, xor_pairs(size, s))  19 us
    pallas_call x2, Pallas kernels, ffn_weight_term(): pl.pallas_call(body, grid=(steps,), out_shape=shape, in_specs=[fixed((row...  18.3 us
  transfers between devices with their start and end apart: 92, of which 44 were waited for; matrix products, arithmetic and copies ran while one was open for 5% of the time, Pallas kernels for 30%

profile of v7, /device:TPU:0, one launch (start us, length us, event | category | flops | bytes accessed | tf_op | source)
XLA Modules:
  0.0 613.1 jit_solution(4786584138218248268)
XLA Ops:
  15.0 4.0 collective-permute-start.1
  21.2 3.9 collective-permute-start.16
  26.8 15.9 %collective-permute-done.14 = s32[2,64]{1,0:T(2,128)S(1)} collective-permute-done((s32[2,64]{1,0:T(2,128)S(1)}, s32[2,64]{1,0:T(2,128)S(1)}, u32[]{:S(2)}, u32[]{:S(2)}) %collective-permute-start.14) | collective-permute-done | bytes 544 | tf_op jit(solution)/shard_map/ppermute | solution.py:49
  51.2 7.3 %collective-permute-done.3.refs_4_ = bf16[128,2048]{1,0:T(8,128)(2,1)S(1)} collective-permute-done((bf16[128,2048]{1,0:T(8,128)(2,1)S(1)}, bf16[128,2048]{1,0:T(8,128)(2,1)S(1)}, u32[]{:S(2)}, u32[]{:S(2)}) %collective-permute-start.3) | collective-permute-done | bytes 524320 | tf_op jit(solution)/shard_map/ppermute | solution.py:87
  59.3 9.1 %shard_map.246 = (bf16[512,2048]{1,0:T(8,128)(2,1)}, f32[512,1536]{1,0:T(8,128)}, f32[2,512]{1,0:T(2,128)}) custom-call(bf16[128,2048]{1,0:T(8,128)(2,1)} %bitcast.110, bf16[128,2048]{1,0:T(8,128)(2,1)} %copy-done.64, bf16[128,2048]{1,0:T(8,128)(2,1)} %copy-done.63, bf16[128,2048]{1,0:T(8,128)(2,1)} %copy-done.65, bf16[128,2048]{1,0:T(8,128)(2,1)} %copy-done.66, ...), custom_call_target="tpu_custom_call" | custom-call | flops 3221225472 | bytes 14159872 | tf_op jit(solution)/shard_map/pallas_call | solution.py:189
  78.8 5.2 shard_map.247
  92.4 4.9 collective-permute-done.10.refs_4_
  100.1 4.8 collective-permute-done.13.refs_7_
  105.7 9.3 %shard_map.248 = (bf16[256,128]{1,0:T(8,128)(2,1)}, bf16[256,128]{1,0:T(8,128)(2,1)}, bf16[256,128]{1,0:T(8,128)(2,1)}, bf16[256,128]{1,0:T(8,128)(2,1)}, bf16[2...) custom-call(s32[1]{0:T(128)} %bitcast.me_ref, ...), custom_call_target="tpu_custom_call" | custom-call | flops 1073741824 | bytes 3186692 | tf_op jit(solution)/shard_map/pallas_call | solution.py:172
  132.3 4.3 shard_map.250
  142.7 9.5 %collective-permute-done.29 = bf16[128,2048]{1,0:T(8,128)(2,1)S(1)} collective-permute-done((bf16[128,2048]{1,0:T(8,128)(2,1)}, bf16[128,2048]{1,0:T(8,128)(2,1)S(1)}, u32[]{:S(2)}, u32[]{:S(2)}) %collective-permute-start.29) | collective-permute-done | bytes 524320 | tf_op jit(solution)/shard_map/ppermute | solution.py:87
  156.8 6.7 %collective-permute-done.27.refs_1_ = bf16[128,2048]{1,0:T(8,128)(2,1)S(1)} collective-permute-done((bf16[128,2048]{1,0:T(8,128)(2,1)}, bf16[128,2048]{1,0:T(8,128)(2,1)S(1)}, u32[]{:S(2)}, u32[]{:S(2)}) %collective-permute-start.27) | collective-permute-done | bytes 524320 | tf_op jit(solution)/shard_map/ppermute | solution.py:87
  163.5 16.3 %collective-permute-done.30.refs_3_ = bf16[128,2048]{1,0:T(8,128)(2,1)S(1)} collective-permute-done((bf16[128,2048]{1,0:T(8,128)(2,1)S(1)}, bf16[128,2048]{1,0:T(8,128)(2,1)S(1)}, u32[]{:S(2)}, u32[]{:S(2)}) %collective-permute-start.30) | collective-permute-done | bytes 524320 | tf_op jit(solution)/shard_map/ppermute | solution.py:87
  180.6 3.8 shard_map.251
  187.4 21.2 %collective-permute-done.32.refs_2_ = bf16[128,2048]{1,0:T(8,128)(2,1)S(1)} collective-permute-done((bf16[128,2048]{1,0:T(8,128)(2,1)}, bf16[128,2048]{1,0:T(8,128)(2,1)S(1)}, u32[]{:S(2)}, u32[]{:S(2)}) %collective-permute-start.32) | collective-permute-done | bytes 524320 | tf_op jit(solution)/shard_map/ppermute | solution.py:87
  215.2 12.7 %collective-permute-done.34.refs_4_ = bf16[128,2048]{1,0:T(8,128)(2,1)S(1)} collective-permute-done((bf16[128,2048]{1,0:T(8,128)(2,1)S(1)}, bf16[128,2048]{1,0:T(8,128)(2,1)S(1)}, u32[]{:S(2)}, u32[]{:S(2)}) %collective-permute-start.34) | collective-permute-done | bytes 524320 | tf_op jit(solution)/shard_map/ppermute | solution.py:87
  228.6 22.5 %shard_map.252 = (bf16[512,2048]{1,0:T(8,128)(2,1)}, bf16[512,2048]{1,0:T(8,128)(2,1)}, bf16[512,2048]{1,0:T(8,128)(2,1)}, bf16[512,2048]{1,0:T(8,128)(2,1)}, bf...) custom-call(bf16[128,2048]{1,0:T(8,128)(2,1)} %get-tuple-element.148, ...), custom_call_target="tpu_custom_call" | custom-call | flops 12884901888 | bytes 88604672 | tf_op jit(solution)/shard_map/pallas_call | solution.py:189
  256.6 9.4 %collective-permute-done.37 = bf16[128,2048]{1,0:T(8,128)(2,1)S(1)} collective-permute-done((bf16[128,2048]{1,0:T(8,128)(2,1)S(1)}, bf16[128,2048]{1,0:T(8,128)(2,1)S(1)}, u32[]{:S(2)}, u32[]{:S(2)}) %collective-permute-start.37) | collective-permute-done | bytes 524320 | tf_op jit(solution)/shard_map/ppermute | solution.py:87
  269.6 7.6 %collective-permute-done.35.refs_1_ = bf16[128,2048]{1,0:T(8,128)(2,1)S(1)} collective-permute-done((bf16[128,2048]{1,0:T(8,128)(2,1)S(1)}, bf16[128,2048]{1,0:T(8,128)(2,1)S(1)}, u32[]{:S(2)}, u32[]{:S(2)}) %collective-permute-start.35) | collective-permute-done | bytes 524320 | tf_op jit(solution)/shard_map/ppermute | solution.py:87
  277.2 14.6 %collective-permute-done.38.refs_3_ = bf16[128,2048]{1,0:T(8,128)(2,1)S(1)} collective-permute-done((bf16[128,2048]{1,0:T(8,128)(2,1)S(1)}, bf16[128,2048]{1,0:T(8,128)(2,1)S(1)}, u32[]{:S(2)}, u32[]{:S(2)}) %collective-permute-start.38) | collective-permute-done | bytes 524320 | tf_op jit(solution)/shard_map/ppermute | solution.py:87
  292.6 3.8 shard_map.253
  299.2 21.8 %collective-permute-done.40.refs_2_ = bf16[128,2048]{1,0:T(8,128)(2,1)S(1)} collective-permute-done((bf16[128,2048]{1,0:T(8,128)(2,1)}, bf16[128,2048]{1,0:T(8,128)(2,1)S(1)}, u32[]{:S(2)}, u32[]{:S(2)}) %collective-permute-start.40) | collective-permute-done | bytes 524320 | tf_op jit(solution)/shard_map/ppermute | solution.py:87
  322.4 10.1 %collective-permute-done.42.refs_4_ = bf16[128,2048]{1,0:T(8,128)(2,1)S(1)} collective-permute-done((bf16[128,2048]{1,0:T(8,128)(2,1)S(1)}, bf16[128,2048]{1,0:T(8,128)(2,1)S(1)}, u32[]{:S(2)}, u32[]{:S(2)}) %collective-permute-start.42) | collective-permute-done | bytes 524320 | tf_op jit(solution)/shard_map/ppermute | solution.py:87
  333.3 9.3 %shard_map.254 = bf16[2048,2048]{1,0:T(8,128)(2,1)} custom-call(bf16[128,2048]{1,0:T(8,128)(2,1)} %get-tuple-element.155.refs_0_, bf16[128,2048]{1,0:T(8,128)(2,1)} %copy-done.13, bf16[128,2048]{1,0:T(8,128)(2,1)} %copy-done.11, bf16[128,2048]{1,0:T(8,128)(2,1)} %copy-done.15, bf16[128,2048]{1,0:T(8,128)(2,1)} %copy-done.17, ...), custom_call_target="tpu_custom_call" | custom-call | flops 4294967296 | bytes 13107200 | tf_op jit(solution)/shard_map/pallas_call | solution.py:189
  343.1 24.7 %shard_map.255 = (bf16[512,2048]{1,0:T(8,128)(2,1)}, bf16[512,2048]{1,0:T(8,128)(2,1)}, bf16[512,2048]{1,0:T(8,128)(2,1)}, bf16[128,2048]{1,0:T(8,128)(2,1)}, bf...) custom-call(bf16[128,2048]{1,0:T(8,128)(2,1)} %get-tuple-element.155.refs_0_, ...), custom_call_target="tpu_custom_call" | custom-call | flops 12884901888 | bytes 90701824 | tf_op jit(solution)/shard_map/pallas_call | solution.py:189
  372.9 9.2 %collective-permute-done.45 = bf16[128,2048]{1,0:T(8,128)(2,1)S(1)} collective-permute-done((bf16[128,2048]{1,0:T(8,128)(2,1)}, bf16[128,2048]{1,0:T(8,128)(2,1)S(1)}, u32[]{:S(2)}, u32[]{:S(2)}) %collective-permute-start.45) | collective-permute-done | bytes 524320 | tf_op jit(solution)/shard_map/ppermute | solution.py:87
  383.3 3.9 collective-permute-start.46
  387.2 9.2 %shard_map.267.refs_2_ = bf16[2048,4096]{1,0:T(8,128)(2,1)} custom-call(bf16[512,2048]{1,0:T(8,128)(2,1)} %get-tuple-element.226.refs_0_, bf16[512,2048]{1,0:T(8,128)(2,1)} %get-tuple-element.228.refs_1_), custom_call_target="tpu_custom_call" | custom-call | flops 4294967296 | bytes 10485760 | tf_op jit(solution)/shard_map/pallas_call | solution.py:384
  396.4 9.1 %shard_map.268 = bf16[2048,4096]{1,0:T(8,128)(2,1)} custom-call(bf16[512,2048]{1,0:T(8,128)(2,1)} %get-tuple-element.226.refs_0_, bf16[512,2048]{1,0:T(8,128)(2,1)} %get-tuple-element.227.refs_1_, bf16[2048,4096]{1,0:T(8,128)(2,1)} %shard_map.267.refs_2_), custom_call_target="tpu_custom_call", output_to_operand_aliasing={{}: (2, {})} | custom-call | flops 4294967296 | bytes 10485760 | tf_op jit(solution)/shard_map/pallas_call | solution.py:384
  406.6 3.9 shard_map.256
  410.5 6.2 %shard_map.257 = (bf16[128,512]{1,0:T(8,128)(2,1)}, bf16[128,512]{1,0:T(8,128)(2,1)}, bf16[128,512]{1,0:T(8,128)(2,1)}, bf16[128,512]{1,0:T(8,128)(2,1)}) custom-call(bf16[128,2048]{1,0:T(8,128)(2,1)} %get-tuple-element.198.grad_ref.refs_0_, bf16[2048,2048]{1,0:T(8,128)(2,1)} %all-gather.11.cloned.1.call-done.weight_ref), custom_call_target="tpu_custom_call" | custom-call | flops 1073741824 | bytes 9437184 | tf_op jit(solution)/shard_map/pallas_call | solution.py:189
  440.4 12.0 %shard_map.259 = (bf16[256,384]{1,0:T(8,128)(2,1)}, bf16[256,384]{1,0:T(8,128)(2,1)}, bf16[256,384]{1,0:T(8,128)(2,1)}, bf16[256,384]{1,0:T(8,128)(2,1)}, bf16[2...) custom-call(s32[1]{0:T(128)} %bitcast.me_ref, ...), custom_call_target="tpu_custom_call" | custom-call | flops 2684354560 | bytes 4759556 | tf_op jit(solution)/shard_map/pallas_call | solution.py:172
  456.2 8.2 %collective-permute-done.60.refs_2_ = bf16[256,384]{1,0:T(8,128)(2,1)S(1)} collective-permute-done((bf16[256,384]{1,0:T(8,128)(2,1)}, bf16[256,384]{1,0:T(8,128)(2,1)S(1)}, u32[]{:S(2)}, u32[]{:S(2)}) %collective-permute-start.60) | collective-permute-done | bytes 196640 | tf_op jit(solution)/shard_map/ppermute | solution.py:124
  466.2 6.0 collective-permute-done.62.refs_3_
  482.4 4.8 collective-permute-done.67.refs_1_
  490.3 8.1 %collective-permute-done.70.refs_4_ = bf16[128,2048]{1,0:T(8,128)(2,1)S(1)} collective-permute-done((bf16[128,2048]{1,0:T(8,128)(2,1)S(1)}, bf16[128,2048]{1,0:T(8,128)(2,1)S(1)}, u32[]{:S(2)}, u32[]{:S(2)}) %collective-permute-start.70) | collective-permute-done | bytes 524320 | tf_op jit(solution)/shard_map/ppermute | solution.py:87
  498.4 3.9 shard_map.260
  502.4 4.0 shard_map.261
  514.6 10.8 %shard_map.264 = (bf16[4,256,2048]{2,1,0:T(8,128)(2,1)}, bf16[4,256,2048]{2,1,0:T(8,128)(2,1)}) custom-call(s32[1]{0:T(128)} %bitcast.me_ref, bf16[512,2048]{1,0:T(8,128)(2,1)} %shard_map.263.refs_0_, bf16[512,2048]{1,0:T(8,128)(2,1)} %get-tuple-element.211.refs_1_.refs_0_, bf16[512,512]{1,0:T(8,128)(2,1)} %bitcast.115, bf16[512,512]{1,0:T(8,128)(2,1)} %bitcast.141), custom_call_target="tpu_custom_call" | custom-call | flops 2147483648 | bytes 9437184 | tf_op jit(solution)/shard_map/pallas_call | solution.py:733
  526.9 4.2 shard_map.262.refs_1_.qk_ref
  531.1 8.5 %shard_map.265 = (bf16[4,256,2048]{2,1,0:T(8,128)(2,1)}, bf16[4,256,2048]{2,1,0:T(8,128)(2,1)}) custom-call(s32[1]{0:T(128)} %bitcast.me_ref, bf16[512,2048]{1,0:T(8,128)(2,1)} %get-tuple-element.211.refs_1_.refs_0_, bf16[512,1024]{1,0:T(8,128)(2,1)} %shard_map.262.refs_1_.qk_ref, ...), custom_call_target="tpu_custom_call", output_to_operand_aliasing={{0}: (3, {}), {1}: (4, {})} | custom-call | flops 2147483648 | bytes 7340032 | tf_op jit(solution)/shard_map/pallas_call | solution.py:733
  540.1 4.2 collective-permute-done.79
  545.8 7.5 %shard_map.266 = (bf16[128,2048]{1,0:T(8,128)(2,1)}, bf16[128,2048]{1,0:T(8,128)(2,1)}, bf16[128,2048]{1,0:T(8,128)(2,1)}, bf16[128,2048]{1,0:T(8,128)(2,1)}) custom-call(bf16[512,1024]{1,0:T(8,128)(2,1)} %shard_map.262.refs_1_.qk_ref, bf16[512,512]{1,0:T(8,128)(2,1)} %bitcast.142, bf16[2048,1536]{1,0:T(8,128)(2,1)} %all-gather.5.cloned.1.call-done.refs_5_.weight_ref), custom_call_target="tpu_custom_call" | custom-call | flops 3221225472 | bytes 9961472 | tf_op jit(solution)/shard_map/pallas_call | solution.py:189
  553.4 4.0 add_bitcast_fusion
  563.5 9.9 %collective-permute-done.77 = bf16[128,2048]{1,0:T(8,128)(2,1)S(1)} collective-permute-done((bf16[128,2048]{1,0:T(8,128)(2,1)}, bf16[128,2048]{1,0:T(8,128)(2,1)S(1)}, u32[]{:S(2)}, u32[]{:S(2)}) %collective-permute-start.77) | collective-permute-done | bytes 524320 | tf_op jit(solution)/shard_map/ppermute | solution.py:87
  577.2 4.5 collective-permute-done.82
  585.1 5.1 shard_map.269
  592.1 7.2 %collective-permute-done.78 = bf16[128,2048]{1,0:T(8,128)(2,1)} collective-permute-done((bf16[128,2048]{1,0:T(8,128)(2,1)}, bf16[128,2048]{1,0:T(8,128)(2,1)}, u32[]{:S(2)}, u32[]{:S(2)}) %collective-permute-start.78) | collective-permute-done | bytes 524320 | tf_op jit(solution)/shard_map/ppermute | solution.py:87
  (429 shorter events, 180.3 us)
Async XLA Ops:
  7.2 51.7 %all-gather.5.cloned.1.call-start = ((), (), s32[]{:S(2)}) async-start(), calls=%async_computation.2 | async-start | bytes 7077888 | tf_op jit(solution)/shard_map/all_gather | solution.py:1221
  9.4 122.9 %all-gather.7.cloned.1.call-start = ((), (), s32[]{:S(2)}) async-start(), calls=%async_computation.3 | async-start | bytes 2359296 | tf_op jit(solution)/shard_map/all_gather | solution.py:1221
  10.3 217.5 %all-gather.9.cloned.1.call-start = ((), (), s32[]{:S(2)}) async-start(), calls=%async_computation.4 | async-start | bytes 28311552 | tf_op jit(solution)/shard_map/all_gather | solution.py:1221
  14.0 396.5 %all-gather.11.cloned.1.call-start = ((), (), s32[]{:S(2)}) async-start(), calls=%async_computation.5 | async-start | bytes 9437184 | tf_op jit(solution)/shard_map/all_gather | solution.py:1221
  15.0 28.3 %collective-permute-start.1 = (bf16[128,2048]{1,0:T(8,128)(2,1)S(1)}, bf16[128,2048]{1,0:T(8,128)(2,1)S(1)}, u32[]{:S(2)}, u32[]{:S(2)}) collective-permute-start(bf16[128,2048]{1,0:T(8,128)(2,1)S(1)} %bitcast.112), channel_id=1, source_target_pairs={{0,2},{1,3},{2,0},{3,1},{4,6},{5,7},{6,4},{7,5},{8,10},{9,11},{10,... | collective-permute-start | bytes 1572872 | tf_op jit(solution)/shard_map/ppermute | solution.py:87
  19.1 32.1 %collective-permute-start = (bf16[128,2048]{1,0:T(8,128)(2,1)S(1)}, bf16[128,2048]{1,0:T(8,128)(2,1)S(1)}, u32[]{:S(2)}, u32[]{:S(2)}) collective-permute-start(bf16[128,2048]{1,0:T(8,128)(2,1)S(1)} %bitcast.113), channel_id=1, source_target_pairs={{0,1},{1,0},{2,3},{3,2},{4,5},{5,4},{6,7},{7,6},{8,9},{9,8},{10,11... | collective-permute-start | bytes 1572872 | tf_op jit(solution)/shard_map/ppermute | solution.py:87
  20.7 22.0 %collective-permute-start.14 = (s32[2,64]{1,0:T(2,128)S(1)}, s32[2,64]{1,0:T(2,128)S(1)}, u32[]{:S(2)}, u32[]{:S(2)}) collective-permute-start(s32[2,64]{1,0:T(2,128)S(1)} %multiply_add_fusion), channel_id=1, source_target_pairs={{0,1},{1,0},{2,3},{3,2},{4,5},{5,4},{6,7},{7,6},{8,9},{9,8},{10,11... | collective-permute-start | bytes 1544 | tf_op jit(solution)/shard_map/ppermute | solution.py:49
  21.2 23.5 %collective-permute-start.15 = (s32[2,64]{1,0:T(2,128)S(1)}, s32[2,64]{1,0:T(2,128)S(1)}, u32[]{:S(2)}, u32[]{:S(2)}) collective-permute-start(s32[2,64]{1,0:T(2,128)S(1)} %multiply_add_fusion), channel_id=1, source_target_pairs={{0,2},{1,3},{2,0},{3,1},{4,6},{5,7},{6,4},{7,5},{8,10},{9,11},{10,... | collective-permute-start | bytes 1544 | tf_op jit(solution)/shard_map/ppermute | solution.py:49
  21.2 23.5 %collective-permute-start.16 = (s32[2,64]{1,0:T(2,128)S(1)}, s32[2,64]{1,0:T(2,128)S(1)}, u32[]{:S(2)}, u32[]{:S(2)}) collective-permute-start(s32[2,64]{1,0:T(2,128)S(1)} %multiply_add_fusion), channel_id=1, source_target_pairs={{0,3},{1,2},{2,1},{3,0},{4,7},{5,6},{6,5},{7,4},{8,11},{9,10},{10,... | collective-permute-start | bytes 1544 | tf_op jit(solution)/shard_map/ppermute | solution.py:49
  43.3 15.2 %collective-permute-start.3 = (bf16[128,2048]{1,0:T(8,128)(2,1)S(1)}, bf16[128,2048]{1,0:T(8,128)(2,1)S(1)}, u32[]{:S(2)}, u32[]{:S(2)}) collective-permute-start(bf16[128,2048]{1,0:T(8,128)(2,1)S(1)} %collective-permute-done.1.refs_2_), channel_id=1, source_target_pairs={{1,0},{2,3},{5,4},{6,7},{9,8},{10,11},{13,12},{14,15},{17,16},{18,... | collective-permute-start | bytes 1572872 | tf_op jit(solution)/shard_map/ppermute | solution.py:87
  49.6 23.1 %collective-permute-start.19 = (s32[4,2,256]{2,1,0:T(2,128)S(1)}, s32[4,2,256]{2,1,0:T(2,128)S(1)}, u32[]{:S(2)}, u32[]{:S(2)}) collective-permute-start(s32[4,2,256]{2,1,0:T(2,128)S(1)} %pad_add_fusion.1), channel_id=1, source_target_pairs={{0,16},{4,20},{8,24},{12,28},{16,0},{20,4},{24,8},{28,12},{1,17},{... | collective-permute-start | bytes 24584 | tf_op jit(solution)/shard_map/ppermute | solution.py:63
  136.6 15.7 %collective-permute-start.29 = (bf16[128,2048]{1,0:T(8,128)(2,1)}, bf16[128,2048]{1,0:T(8,128)(2,1)S(1)}, u32[]{:S(2)}, u32[]{:S(2)}) collective-permute-start(bf16[128,2048]{1,0:T(8,128)(2,1)} %get-tuple-element.146), channel_id=1, source_target_pairs={{0,1},{3,2},{4,5},{7,6},{8,9},{11,10},{12,13},{15,14},{16,17},{19,... | collective-permute-start | bytes 1572872 | tf_op jit(solution)/shard_map/ppermute | solution.py:87
  139.7 23.8 %collective-permute-start.28 = (bf16[128,2048]{1,0:T(8,128)(2,1)}, bf16[128,2048]{1,0:T(8,128)(2,1)S(1)}, u32[]{:S(2)}, u32[]{:S(2)}) collective-permute-start(bf16[128,2048]{1,0:T(8,128)(2,1)} %get-tuple-element.146), channel_id=1, source_target_pairs={{1,2},{2,1},{5,6},{6,5},{9,10},{10,9},{13,14},{14,13},{17,18},{18,... | collective-permute-start | bytes 1572872 | tf_op jit(solution)/shard_map/ppermute | solution.py:87
  140.6 22.9 %collective-permute-start.27 = (bf16[128,2048]{1,0:T(8,128)(2,1)}, bf16[128,2048]{1,0:T(8,128)(2,1)S(1)}, u32[]{:S(2)}, u32[]{:S(2)}) collective-permute-start(bf16[128,2048]{1,0:T(8,128)(2,1)} %get-tuple-element.145), channel_id=1, source_target_pairs={{0,1},{1,0},{2,3},{3,2},{4,5},{5,4},{6,7},{7,6},{8,9},{9,8},{10,11... | collective-permute-start | bytes 1572872 | tf_op jit(solution)/shard_map/ppermute | solution.py:87
  153.5 26.3 %collective-permute-start.30 = (bf16[128,2048]{1,0:T(8,128)(2,1)S(1)}, bf16[128,2048]{1,0:T(8,128)(2,1)S(1)}, u32[]{:S(2)}, u32[]{:S(2)}) collective-permute-start(bf16[128,2048]{1,0:T(8,128)(2,1)S(1)} %add_convert_fusion.4), channel_id=1, source_target_pairs={{0,2},{1,3},{2,0},{3,1},{4,6},{5,7},{6,4},{7,5},{8,10},{9,11},{10,... | collective-permute-start | bytes 1572872 | tf_op jit(solution)/shard_map/ppermute | solution.py:87
  184.5 24.2 %collective-permute-start.32 = (bf16[128,2048]{1,0:T(8,128)(2,1)}, bf16[128,2048]{1,0:T(8,128)(2,1)S(1)}, u32[]{:S(2)}, u32[]{:S(2)}) collective-permute-start(bf16[128,2048]{1,0:T(8,128)(2,1)} %get-tuple-element.148.refs_0_), channel_id=1, source_target_pairs={{0,2},{1,3},{2,0},{3,1},{4,6},{5,7},{6,4},{7,5},{8,10},{9,11},{10,... | collective-permute-start | bytes 1572872 | tf_op jit(solution)/shard_map/ppermute | solution.py:87
  184.5 29.2 %collective-permute-start.31 = (bf16[128,2048]{1,0:T(8,128)(2,1)}, bf16[128,2048]{1,0:T(8,128)(2,1)S(1)}, u32[]{:S(2)}, u32[]{:S(2)}) collective-permute-start(bf16[128,2048]{1,0:T(8,128)(2,1)} %get-tuple-element.148.refs_0_), channel_id=1, source_target_pairs={{0,1},{1,0},{2,3},{3,2},{4,5},{5,4},{6,7},{7,6},{8,9},{9,8},{10,11... | collective-permute-start | bytes 1572872 | tf_op jit(solution)/shard_map/ppermute | solution.py:87
  186.8 28.4 %collective-permute-start.33 = (bf16[128,2048]{1,0:T(8,128)(2,1)}, bf16[128,2048]{1,0:T(8,128)(2,1)S(1)}, u32[]{:S(2)}, u32[]{:S(2)}) collective-permute-start(bf16[128,2048]{1,0:T(8,128)(2,1)} %get-tuple-element.148.refs_0_), channel_id=1, source_target_pairs={{1,2},{2,1},{5,6},{6,5},{9,10},{10,9},{13,14},{14,13},{17,18},{18,... | collective-permute-start | bytes 1572872 | tf_op jit(solution)/shard_map/ppermute | solution.py:87
  208.6 19.2 %collective-permute-start.34 = (bf16[128,2048]{1,0:T(8,128)(2,1)S(1)}, bf16[128,2048]{1,0:T(8,128)(2,1)S(1)}, u32[]{:S(2)}, u32[]{:S(2)}) collective-permute-start(bf16[128,2048]{1,0:T(8,128)(2,1)S(1)} %collective-permute-done.32.refs_2_), channel_id=1, source_target_pairs={{1,0},{2,3},{5,4},{6,7},{9,8},{10,11},{13,12},{14,15},{17,16},{18,... | collective-permute-start | bytes 1572872 | tf_op jit(solution)/shard_map/ppermute | solution.py:87
  209.9 41.3 %collective-permute-start.47 = (bf16[256,512]{1,0:T(8,128)(2,1)S(1)}, bf16[256,512]{1,0:T(8,128)(2,1)S(1)}, u32[]{:S(2)}, u32[]{:S(2)}) collective-permute-start(bf16[256,512]{1,0:T(8,128)(2,1)S(1)} %bitcast.100), channel_id=1, source_target_pairs={{0,1},{1,0},{2,3},{3,2},{4,5},{5,4},{6,7},{7,6},{8,9},{9,8},{10,11... | collective-permute-start | bytes 786440 | tf_op jit(solution)/shard_map/ppermute | solution.py:49
  212.7 38.6 %collective-permute-start.48 = (bf16[256,512]{1,0:T(8,128)(2,1)S(1)}, bf16[256,512]{1,0:T(8,128)(2,1)S(1)}, u32[]{:S(2)}, u32[]{:S(2)}) collective-permute-start(bf16[256,512]{1,0:T(8,128)(2,1)S(1)} %bitcast.101), channel_id=1, source_target_pairs={{0,2},{1,3},{2,0},{3,1},{4,6},{5,7},{6,4},{7,5},{8,10},{9,11},{10,... | collective-permute-start | bytes 786440 | tf_op jit(solution)/shard_map/ppermute | solution.py:49
  213.7 37.5 %collective-permute-start.49 = (bf16[256,512]{1,0:T(8,128)(2,1)S(1)}, bf16[256,512]{1,0:T(8,128)(2,1)S(1)}, u32[]{:S(2)}, u32[]{:S(2)}) collective-permute-start(bf16[256,512]{1,0:T(8,128)(2,1)S(1)} %bitcast.102), channel_id=1, source_target_pairs={{0,3},{1,2},{2,1},{3,0},{4,7},{5,6},{6,5},{7,4},{8,11},{9,10},{10,... | collective-permute-start | bytes 786440 | tf_op jit(solution)/shard_map/ppermute | solution.py:49
  252.4 332.7 %reduce-scatter.5.cloned.1.call-start = ((), (), s32[]{:S(2)}) async-start(), calls=%async_computation.7 | async-start | bytes 9437184 | tf_op jit(solution)/shard_map/reduce_scatter | solution.py:1273
  253.8 23.5 %collective-permute-start.36 = (bf16[128,2048]{1,0:T(8,128)(2,1)S(1)}, bf16[128,2048]{1,0:T(8,128)(2,1)S(1)}, u32[]{:S(2)}, u32[]{:S(2)}) collective-permute-start(bf16[128,2048]{1,0:T(8,128)(2,1)S(1)} %copy-done.67), channel_id=1, source_target_pairs={{1,2},{2,1},{5,6},{6,5},{9,10},{10,9},{13,14},{14,13},{17,18},{18,... | collective-permute-start | bytes 1572872 | tf_op jit(solution)/shard_map/ppermute | solution.py:87
  254.5 22.7 %collective-permute-start.35 = (bf16[128,2048]{1,0:T(8,128)(2,1)S(1)}, bf16[128,2048]{1,0:T(8,128)(2,1)S(1)}, u32[]{:S(2)}, u32[]{:S(2)}) collective-permute-start(bf16[128,2048]{1,0:T(8,128)(2,1)S(1)} %copy-done.68), channel_id=1, source_target_pairs={{0,1},{1,0},{2,3},{3,2},{4,5},{5,4},{6,7},{7,6},{8,9},{9,8},{10,11... | collective-permute-start | bytes 1572872 | tf_op jit(solution)/shard_map/ppermute | solution.py:87
  266.1 25.7 %collective-permute-start.38 = (bf16[128,2048]{1,0:T(8,128)(2,1)S(1)}, bf16[128,2048]{1,0:T(8,128)(2,1)S(1)}, u32[]{:S(2)}, u32[]{:S(2)}) collective-permute-start(bf16[128,2048]{1,0:T(8,128)(2,1)S(1)} %add_convert_fusion.3), channel_id=1, source_target_pairs={{0,2},{1,3},{2,0},{3,1},{4,6},{5,7},{6,4},{7,5},{8,10},{9,11},{10,... | collective-permute-start | bytes 1572872 | tf_op jit(solution)/shard_map/ppermute | solution.py:87
  296.4 24.6 %collective-permute-start.40 = (bf16[128,2048]{1,0:T(8,128)(2,1)}, bf16[128,2048]{1,0:T(8,128)(2,1)S(1)}, u32[]{:S(2)}, u32[]{:S(2)}) collective-permute-start(bf16[128,2048]{1,0:T(8,128)(2,1)} %get-tuple-element.155.refs_0_), channel_id=1, source_target_pairs={{0,2},{1,3},{2,0},{3,1},{4,6},{5,7},{6,4},{7,5},{8,10},{9,11},{10,... | collective-permute-start | bytes 1572872 | tf_op jit(solution)/shard_map/ppermute | solution.py:87
  296.4 25.9 %collective-permute-start.39 = (bf16[128,2048]{1,0:T(8,128)(2,1)}, bf16[128,2048]{1,0:T(8,128)(2,1)S(1)}, u32[]{:S(2)}, u32[]{:S(2)}) collective-permute-start(bf16[128,2048]{1,0:T(8,128)(2,1)} %get-tuple-element.155.refs_0_), channel_id=1, source_target_pairs={{0,1},{1,0},{2,3},{3,2},{4,5},{5,4},{6,7},{7,6},{8,9},{9,8},{10,11... | collective-permute-start | bytes 1572872 | tf_op jit(solution)/shard_map/ppermute | solution.py:87
  298.5 23.8 %collective-permute-start.41 = (bf16[128,2048]{1,0:T(8,128)(2,1)}, bf16[128,2048]{1,0:T(8,128)(2,1)S(1)}, u32[]{:S(2)}, u32[]{:S(2)}) collective-permute-start(bf16[128,2048]{1,0:T(8,128)(2,1)} %get-tuple-element.155.refs_0_), channel_id=1, source_target_pairs={{1,2},{2,1},{5,6},{6,5},{9,10},{10,9},{13,14},{14,13},{17,18},{18,... | collective-permute-start | bytes 1572872 | tf_op jit(solution)/shard_map/ppermute | solution.py:87
  342.6 242.5 %reduce-scatter.3.cloned.1.call-start = ((), (), s32[]{:S(2)}) async-start(), calls=%async_computation.6 | async-start | bytes 18874368 | tf_op jit(solution)/shard_map/reduce_scatter | solution.py:1275
  369.4 36.1 %collective-permute-start.44 = (bf16[128,2048]{1,0:T(8,128)(2,1)}, bf16[128,2048]{1,0:T(8,128)(2,1)S(1)}, u32[]{:S(2)}, u32[]{:S(2)}) collective-permute-start(bf16[128,2048]{1,0:T(8,128)(2,1)} %get-tuple-element.162), channel_id=1, source_target_pairs={{1,2},{2,1},{5,6},{6,5},{9,10},{10,9},{13,14},{14,13},{17,18},{18,... | collective-permute-start | bytes 1572872 | tf_op jit(solution)/shard_map/ppermute | solution.py:87
  370.1 35.4 %collective-permute-start.43 = (bf16[128,2048]{1,0:T(8,128)(2,1)}, bf16[128,2048]{1,0:T(8,128)(2,1)S(1)}, u32[]{:S(2)}, u32[]{:S(2)}) collective-permute-start(bf16[128,2048]{1,0:T(8,128)(2,1)} %get-tuple-element.161), channel_id=1, source_target_pairs={{0,1},{1,0},{2,3},{3,2},{4,5},{5,4},{6,7},{7,6},{8,9},{9,8},{10,11... | collective-permute-start | bytes 1572872 | tf_op jit(solution)/shard_map/ppermute | solution.py:87
  383.3 22.2 %collective-permute-start.46 = (bf16[128,2048]{1,0:T(8,128)(2,1)S(1)}, bf16[128,2048]{1,0:T(8,128)(2,1)S(1)}, u32[]{:S(2)}, u32[]{:S(2)}) collective-permute-start(bf16[128,2048]{1,0:T(8,128)(2,1)S(1)} %add_convert_fusion.2), channel_id=1, source_target_pairs={{0,2},{1,3},{2,0},{3,1},{4,6},{5,7},{6,4},{7,5},{8,10},{9,11},{10,... | collective-permute-start | bytes 1572872 | tf_op jit(solution)/shard_map/ppermute | solution.py:87
  436.4 38.7 %collective-permute-start.68 = (bf16[128,2048]{1,0:T(8,128)(2,1)S(1)}, bf16[128,2048]{1,0:T(8,128)(2,1)S(1)}, u32[]{:S(2)}, u32[]{:S(2)}) collective-permute-start(bf16[128,2048]{1,0:T(8,128)(2,1)S(1)} %copy-done.6), channel_id=1, source_target_pairs={{0,2},{1,3},{2,0},{3,1},{4,6},{5,7},{6,4},{7,5},{8,10},{9,11},{10,... | collective-permute-start | bytes 1572872 | tf_op jit(solution)/shard_map/ppermute | solution.py:87
  454.1 18.1 %collective-permute-start.62 = (bf16[256,384]{1,0:T(8,128)(2,1)}, bf16[256,384]{1,0:T(8,128)(2,1)S(1)}, u32[]{:S(2)}, u32[]{:S(2)}) collective-permute-start(bf16[256,384]{1,0:T(8,128)(2,1)} %get-tuple-element.192), channel_id=1, source_target_pairs={{0,12},{4,8},{8,4},{12,0},{16,28},{20,24},{24,20},{28,16},{1,13},{... | collective-permute-start | bytes 589832 | tf_op jit(solution)/shard_map/ppermute | solution.py:124
  454.2 20.2 %collective-permute-start.63 = (bf16[256,384]{1,0:T(8,128)(2,1)}, bf16[256,384]{1,0:T(8,128)(2,1)S(1)}, u32[]{:S(2)}, u32[]{:S(2)}) collective-permute-start(bf16[256,384]{1,0:T(8,128)(2,1)} %get-tuple-element.193), channel_id=1, source_target_pairs={{0,16},{4,20},{8,24},{12,28},{16,0},{20,4},{24,8},{28,12},{1,17},{... | collective-permute-start | bytes 589832 | tf_op jit(solution)/shard_map/ppermute | solution.py:124
  455.9 20.5 %collective-permute-start.64 = (bf16[256,384]{1,0:T(8,128)(2,1)}, bf16[256,384]{1,0:T(8,128)(2,1)S(1)}, u32[]{:S(2)}, u32[]{:S(2)}) collective-permute-start(bf16[256,384]{1,0:T(8,128)(2,1)} %get-tuple-element.194), channel_id=1, source_target_pairs={{0,20},{4,16},{8,28},{12,24},{16,4},{20,0},{24,12},{28,8},{1,21},{... | collective-permute-start | bytes 589832 | tf_op jit(solution)/shard_map/ppermute | solution.py:124
  464.3 18.0 %collective-permute-start.65 = (bf16[256,384]{1,0:T(8,128)(2,1)}, bf16[256,384]{1,0:T(8,128)(2,1)S(1)}, u32[]{:S(2)}, u32[]{:S(2)}) collective-permute-start(bf16[256,384]{1,0:T(8,128)(2,1)} %get-tuple-element.195), channel_id=1, source_target_pairs={{0,24},{4,28},{8,16},{12,20},{16,8},{20,12},{24,0},{28,4},{1,25},{... | collective-permute-start | bytes 589832 | tf_op jit(solution)/shard_map/ppermute | solution.py:124
  472.2 14.9 %collective-permute-start.67 = (bf16[128,2048]{1,0:T(8,128)(2,1)S(1)}, bf16[128,2048]{1,0:T(8,128)(2,1)S(1)}, u32[]{:S(2)}, u32[]{:S(2)}) collective-permute-start(bf16[128,2048]{1,0:T(8,128)(2,1)S(1)} %copy-done.6), channel_id=1, source_target_pairs={{0,1},{1,0},{2,3},{3,2},{4,5},{5,4},{6,7},{7,6},{8,9},{9,8},{10,11... | collective-permute-start | bytes 1572872 | tf_op jit(solution)/shard_map/ppermute | solution.py:87
  475.1 23.3 %collective-permute-start.70 = (bf16[128,2048]{1,0:T(8,128)(2,1)S(1)}, bf16[128,2048]{1,0:T(8,128)(2,1)S(1)}, u32[]{:S(2)}, u32[]{:S(2)}) collective-permute-start(bf16[128,2048]{1,0:T(8,128)(2,1)S(1)} %collective-permute-done.68.refs_2_), channel_id=1, source_target_pairs={{1,0},{2,3},{5,4},{6,7},{9,8},{10,11},{13,12},{14,15},{17,16},{18,... | collective-permute-start | bytes 1572872 | tf_op jit(solution)/shard_map/ppermute | solution.py:87
  507.0 18.4 %collective-permute-start.73 = (f32[5120]{0:T(1024)S(1)}, f32[5120]{0:T(1024)S(1)}, u32[]{:S(2)}, u32[]{:S(2)}) collective-permute-start(f32[5120]{0:T(1024)S(1)} %pad_maximum_fusion.7), channel_id=1, source_target_pairs={{0,3},{1,2},{2,1},{3,0},{4,7},{5,6},{6,5},{7,4},{8,11},{9,10},{10,... | collective-permute-start | bytes 61448 | tf_op jit(solution)/shard_map/ppermute | solution.py:49
  508.5 16.9 %collective-permute-start.72 = (f32[5120]{0:T(1024)S(1)}, f32[5120]{0:T(1024)S(1)}, u32[]{:S(2)}, u32[]{:S(2)}) collective-permute-start(f32[5120]{0:T(1024)S(1)} %pad_maximum_fusion.7), channel_id=1, source_target_pairs={{0,2},{1,3},{2,0},{3,1},{4,6},{5,7},{6,4},{7,5},{8,10},{9,11},{10,... | collective-permute-start | bytes 61448 | tf_op jit(solution)/shard_map/ppermute | solution.py:49
  508.5 17.1 %collective-permute-start.71 = (f32[5120]{0:T(1024)S(1)}, f32[5120]{0:T(1024)S(1)}, u32[]{:S(2)}, u32[]{:S(2)}) collective-permute-start(f32[5120]{0:T(1024)S(1)} %pad_maximum_fusion.7), channel_id=1, source_target_pairs={{0,1},{1,0},{2,3},{3,2},{4,5},{5,4},{6,7},{7,6},{8,9},{9,8},{10,11... | collective-permute-start | bytes 61448 | tf_op jit(solution)/shard_map/ppermute | solution.py:49
  557.7 24.1 %collective-permute-start.82 = (bf16[2,256,1024]{2,1,0:T(8,128)(2,1)S(1)}, bf16[2,256,1024]{2,1,0:T(8,128)(2,1)S(1)}, u32[]{:S(2)}, u32[]{:S(2)}) collective-permute-start(bf16[2,256,1024]{2,1,0:T(8,128)(2,1)S(1)} %pad_maximum_fusion.2), channel_id=1, source_target_pairs={{0,16},{4,20},{8,24},{12,28},{16,0},{20,4},{24,8},{28,12},{1,17},{... | collective-permute-start | bytes 3145736 | tf_op jit(solution)/shard_map/ppermute | solution.py:775
  558.4 23.9 %collective-permute-start.83 = (bf16[2,256,1024]{2,1,0:T(8,128)(2,1)S(1)}, bf16[2,256,1024]{2,1,0:T(8,128)(2,1)S(1)}, u32[]{:S(2)}, u32[]{:S(2)}) collective-permute-start(bf16[2,256,1024]{2,1,0:T(8,128)(2,1)S(1)} %pad_maximum_fusion.3), channel_id=1, source_target_pairs={{0,8},{4,12},{8,0},{12,4},{16,24},{20,28},{24,16},{28,20},{1,9},{5... | collective-permute-start | bytes 3145736 | tf_op jit(solution)/shard_map/ppermute | solution.py:775
  560.7 29.5 %collective-permute-start.75 = (bf16[128,2048]{1,0:T(8,128)(2,1)}, bf16[128,2048]{1,0:T(8,128)(2,1)}, u32[]{:S(2)}, u32[]{:S(2)}) collective-permute-start(bf16[128,2048]{1,0:T(8,128)(2,1)} %get-tuple-element.221), channel_id=1, source_target_pairs={{0,1},{1,0},{2,3},{3,2},{4,5},{5,4},{6,7},{7,6},{8,9},{9,8},{10,11... | collective-permute-start | bytes 1572872 | tf_op jit(solution)/shard_map/ppermute | solution.py:87
  560.8 31.3 %collective-permute-start.76 = (bf16[128,2048]{1,0:T(8,128)(2,1)}, bf16[128,2048]{1,0:T(8,128)(2,1)}, u32[]{:S(2)}, u32[]{:S(2)}) collective-permute-start(bf16[128,2048]{1,0:T(8,128)(2,1)} %get-tuple-element.222), channel_id=1, source_target_pairs={{1,2},{2,1},{5,6},{6,5},{9,10},{10,9},{13,14},{14,13},{17,18},{18,... | collective-permute-start | bytes 1572872 | tf_op jit(solution)/shard_map/ppermute | solution.py:87
  574.3 25.0 %collective-permute-start.78 = (bf16[128,2048]{1,0:T(8,128)(2,1)}, bf16[128,2048]{1,0:T(8,128)(2,1)}, u32[]{:S(2)}, u32[]{:S(2)}) collective-permute-start(bf16[128,2048]{1,0:T(8,128)(2,1)} %add_convert_fusion.1), channel_id=1, source_target_pairs={{0,2},{1,3},{2,0},{3,1},{4,6},{5,7},{6,4},{7,5},{8,10},{9,11},{10,... | collective-permute-start | bytes 1572872 | tf_op jit(solution)/shard_map/ppermute | solution.py:87
  (127 other events, 1239.3 us)
Sparse Core Ops, SparseCore 0:
  10.5 48.3 all-gather.4
  61.4 29.9 all-gather.6
  93.3 133.1 all-gather.8
  252.5 52.4 all-gather.10
  342.8 71.1 reduce-scatter.4
  417.8 133.1 reduce-scatter.2
